TPU v7x, 32 devices: a whole 2x2x4 slice. The times are simulated.
32 devices in a mesh: rows: 8 (over z, y), edges: 4 (over x, core).
Axes of the slice: x: 2, y: 2, z: 4, core: 2. Of those that a mesh axis runs over, the one named last changes fastest.
Arguments:
- features: bfloat16 [40960, 256], P(('rows', 'edges')), may hold values from -6 to 6
- edge_src: int32 [40960], P(('rows', 'edges')), may hold values from 0 to 1023, as said below
- edge_dst: int32 [40960], P(('rows', 'edges')), may hold values from 0 to 1023, as said below
- edge_cell: int32 [40960], P(('rows', 'edges')), may hold values from 0 to 2
- cell_bias: bfloat16 [3, 512], replicated, may hold values from -4 to 4
- w_in: bfloat16 [256, 512], replicated, may hold values from -0.375 to 0.375
- w_out: bfloat16 [256, 256], replicated, may hold values from -0.0068359375 to 0.0068359375
- vectors: float32 [128, 16384], P('edges', 'rows'), may hold values from -6 to 6
- cheb_coef: float32 [5], replicated, may hold values from 0.5 to 1.5
Outputs:
- filtered: float32 [128, 16384], P('edges', 'rows')
Inputs may be any that keep to these rules, and one draw needn't show every extreme that they name: `edge_src`: number the devices d = 0 .. 1024 / 32 - 1 along rows and edges together (rows first) and let quarter q be atoms q * 32 to (q + 1) * 32 - 1. Device d holds 1280 edges in order of source atom (cyclically): first the edges of quarter d - 1 it holds, then edges of quarter d, then edges of quarter d + 1 (cyclically over devices). Between 160 and 320 belong to quarter d - 1 and between 160 and 320 to quarter d + 1; for each kind, some device has exactly 320. `edge_dst`: each source, target pair occurs once. The target's tile (atom // 8) lies within 3 tiles of the source's tile, cyclically over 1024 / 8 tiles.
All inputs are finite; a program needn't handle non-finite values.
Results may differ from a plain program's by a relative error of at most 0.0065.
Values may be sent and summed in bfloat16 or wider, within the bound.
No kernel may reach another device: no remote copies, remote signals or barrier semaphores. Data moves between devices by JAX's collectives and lax.ppermute only.
A program may use at most 64 MiB of HBM per device.

v0:
```python
import jax
import jax.numpy as jnp
from jax import lax
from jax.sharding import PartitionSpec as P

ORB = 16
TILE_ATOMS = 8
BAND = 3
HID = 256
VEC = 128
STEPS = 4
ATOM_Q = 32
SPILL = 320


def with_halo(x, sides, width):
    for axis, dim in sides:
        devices, length = (lax.axis_size(axis), x.shape[dim])
        up = [(i, (i + 1) % devices) for i in range(devices)]
        down = [(j, i) for i, j in up]
        last = lax.slice_in_dim(x, length - width, length, axis=dim)
        leading = lax.slice_in_dim(x, 0, width, axis=dim)
        before = lax.ppermute(last, axis, up)
        after = lax.ppermute(leading, axis, down)
        x = jnp.concatenate([before, x, after], axis=dim)
    return x


def pair_blocks(feat, cell, cell_bias, w_in, w_out):
    onehot = (cell[:, None] == jnp.arange(3, dtype=jnp.int32)[None, :]).astype(jnp.bfloat16)
    pre = jnp.dot(feat, w_in, preferred_element_type=jnp.float32) + jnp.dot(
        onehot, cell_bias, preferred_element_type=jnp.float32
    )
    hidden = (jax.nn.silu(pre[:, :HID]) * pre[:, HID:]).astype(jnp.bfloat16)
    return jnp.dot(hidden, w_out, preferred_element_type=jnp.float32).astype(jnp.bfloat16)


def per_device(features, edge_src, edge_dst, edge_cell, cell_bias, w_in, w_out, vectors, cheb_coef):
    nquart = lax.axis_size("rows") * lax.axis_size("edges")
    quarter = lax.axis_index("rows") * lax.axis_size("edges") + lax.axis_index("edges")
    ntiles = ATOM_Q * nquart // TILE_ATOMS
    nband = 2 * BAND + 1
    trows = ATOM_Q // TILE_ATOMS
    tile_size = TILE_ATOMS * ORB
    window = nband * TILE_ATOMS * TILE_ATOMS
    id_rows = jnp.stack([edge_src, edge_dst, edge_cell])
    wide_ids = with_halo(id_rows, ((("rows", "edges"), 1),), SPILL)
    source = wide_ids[0]
    target = wide_ids[1]
    cells = wide_ids[2]
    wide_feat = with_halo(features, ((("rows", "edges"), 0),), SPILL)
    blocks = pair_blocks(wide_feat, cells, cell_bias, w_in, w_out)
    total_len = source.shape[0]
    owner = source // ATOM_Q
    mine = owner == quarter
    local_atom = source - quarter * ATOM_Q
    shift_tile = (target // TILE_ATOMS - source // TILE_ATOMS + BAND) % ntiles
    within = (shift_tile * TILE_ATOMS + local_atom % TILE_ATOMS) * TILE_ATOMS + target % TILE_ATOMS
    slot_ids = local_atom // TILE_ATOMS * window + within
    ranks = jnp.cumsum(mine.astype(jnp.int32)) - 1
    dest = jnp.where(mine, ranks, total_len + window)
    packed_blocks = (
        jnp.zeros((total_len + window, ORB * ORB), jnp.bfloat16).at[dest].set(blocks, mode="drop")
    )
    packed_ids = jnp.full((total_len + window,), -1, jnp.int32).at[dest].set(slot_ids, mode="drop")
    tile_first = jnp.arange(trows, dtype=jnp.int32) * TILE_ATOMS
    earlier = jnp.logical_and(mine[None, :], local_atom[None, :] < tile_first[:, None])
    starts = jnp.sum(earlier.astype(jnp.int32), axis=1)

    def one_row(tile_row, start):
        piece = lax.dynamic_slice_in_dim(packed_blocks, start, window, 0)
        piece_ids = lax.dynamic_slice_in_dim(packed_ids, start, window, 0)
        wanted = tile_row * window + jnp.arange(window, dtype=jnp.int32)
        onehot = (wanted[:, None] == piece_ids[None, :]).astype(jnp.bfloat16)
        return jnp.dot(onehot, piece, preferred_element_type=jnp.float32).astype(jnp.bfloat16)

    band = jax.vmap(one_row)(jnp.arange(trows, dtype=jnp.int32), starts)
    band = band.reshape(trows, nband, TILE_ATOMS, TILE_ATOMS, ORB, ORB).transpose(0, 1, 2, 4, 3, 5)
    band = band.reshape(trows, nband, tile_size, tile_size).astype(jnp.float32)

    def apply(field):
        wide = with_halo(field, ((("rows", "edges"), 1),), BAND * tile_size)
        wide3 = wide.reshape(VEC, trows + 2 * BAND, tile_size)
        total = jnp.zeros((VEC, trows, tile_size), jnp.float32)
        for diag in range(nband):
            total = total + jnp.einsum(
                "vtc,trc->vtr",
                wide3[:, diag : diag + trows],
                band[:, diag],
                precision=lax.Precision.HIGHEST,
            )
        return total.reshape(VEC, trows * tile_size)

    previous = lax.all_to_all(vectors, "edges", split_axis=1, concat_axis=0, tiled=True)
    current = apply(previous)
    result = cheb_coef[0] * previous + cheb_coef[1] * current
    for step in range(2, STEPS + 1):
        following = 2.0 * apply(current) - previous
        result = result + cheb_coef[step] * following
        previous, current = (current, following)
    return lax.all_to_all(result, "edges", split_axis=0, concat_axis=1, tiled=True)


def solution(mesh):
    placed = (
        P(("rows", "edges"), None),
        P(("rows", "edges")),
        P(("rows", "edges")),
        P(("rows", "edges")),
        P(),
        P(),
        P(),
        P("edges", "rows"),
        P(),
    )
    return jax.shard_map(
        per_device, mesh=mesh, in_specs=placed, out_specs=P("edges", "rows"), check_vma=False
    )
```

profile of v0, /device:TPU:0, one launch (start us, length us, event | category | flops | bytes accessed | tf_op | source)
XLA Modules:
  0.0 142.1 jit_solution(2540325931808539654)
XLA Ops:
  0.0 0.8 stack.12
  0.8 0.7 stack.13
  1.5 0.7 stack.14
  2.7 6.0 %collective-permute-start.1 = (s32[3,320]{1,0:T(4,128)S(1)}, s32[3,320]{1,0:T(4,128)S(1)}, u32[]{:S(2)}, u32[]{:S(2)}) collective-permute-start(s32[3,320]{1,0:T(4,128)S(1)} %get-tuple-element.53), channel_id=1, source_target_pairs={{1,0},{2,1},{3,2},{4,3},{5,4},{6,5},{7,6},{8,7},{9,8},{10,9},{11,1... | collective-permute-start | bytes 11528 | tf_op jit(solution)/shard_map/ppermute | solution.py:24
  8.7 1.0 fusion.85
  9.8 5.3 %collective-permute-start.3 = (bf16[320,256]{1,0:T(8,128)(2,1)S(1)}, bf16[320,256]{1,0:T(8,128)(2,1)S(1)}, u32[]{:S(2)}, u32[]{:S(2)}) collective-permute-start(bf16[320,256]{1,0:T(8,128)(2,1)S(1)} %get-tuple-element.42), channel_id=1, source_target_pairs={{1,0},{2,1},{3,2},{4,3},{5,4},{6,5},{7,6},{8,7},{9,8},{10,9},{11,1... | collective-permute-start | bytes 491528 | tf_op jit(solution)/shard_map/ppermute | solution.py:24
  15.1 1.7 %copy.199 = f32[4,4,8,512]{3,2,0,1:T(8,128)} copy(f32[4,4,8,512]{3,2,1,0:T(8,128)} %bitcast.188) | data formatting | bytes 524288 | tf_op jit(solution)/shard_map/all_to_all | solution.py:94
  16.8 3.4 %all-to-all-start = ((f32[32,4,512]{2,0,1:T(8,128)}), f32[32,4,512]{2,0,1:T(8,128)S(1)}, u32[]{:S(2)}, u32[]{:S(2)}) async-start(f32[32,4,512]{2,0,1:T(8,128)} %bitcast.143), calls=%async_computation | async-start | bytes 524288 | tf_op jit(solution)/shard_map/all_to_all | solution.py:94
  21.5 10.0 %scatter_custom_fusion = s32[2368]{0:T(1024)S(1)} fusion(s32[1920]{0:T(1024)S(1)} %fusion.80, s32[1920]{0:T(1024)S(1)} %fusion.62, s32[]{:T(128)} %constant.89.clone.1), kind=kCustom, calls=%fused_computation.174 | custom fusion | bytes 9476 | tf_op jit(solution)/shard_map/scatter | solution.py:65
  31.5 5.8 %while.2 = (s32[]{:T(128)}, s32[2368]{0:T(1024)S(1)}, s32[4,1]{0,1:T(1,128)S(1)}, s32[4,448]{1,0:T(4,128)S(1)}, s32[]{:T(128)}, /*index=5*/s32[]{:T(128)}) while((s32[]{:T(128)}, s32[2368]{0:T(1024)S(1)}, s32[4,1]{0,1:T(1,128)S(1)}, s32[4,448]{1,0:T(4,128)S(1)}, s32[]{:T(128)}, /*index=5*/s32[]{:T(128)}) %tuple.45), condition=%wide.while_cond, body=%wide.while_body.sunk | while | flops 2 | bytes 7257 | solution.py:72
  31.5 0.6 constant_dynamic-slice_fusion.4
  32.2 0.7 dynamic-slice.15
  33.0 0.6 constant_dynamic-slice_fusion.4
  33.6 0.7 dynamic-slice.15
  34.4 0.6 constant_dynamic-slice_fusion.4
  35.1 0.7 dynamic-slice.15
  35.9 0.6 constant_dynamic-slice_fusion.4
  36.5 0.7 dynamic-slice.15
  37.3 1.2 fusion.17
  38.6 0.7 convolution_add_fusion
  39.4 0.7 convolution_convert_fusion
  40.1 11.0 %scatter_custom_fusion.1 = bf16[2368,256]{1,0:T(8,128)(2,1)S(1)} fusion(s32[1920]{0:T(1024)S(1)} %fusion.80, bf16[1920,256]{1,0:T(8,128)(2,1)S(1)} %convolution_convert_fusion, bf16[]{:T(256)} %constant.105.clone.1), kind=kCustom, calls=%fused_computation.53 | custom fusion | bytes 1212418 | tf_op jit(solution)/shard_map/scatter | solution.py:63
  51.1 8.3 %while.3 = (s32[]{:T(128)}, bf16[2368,256]{1,0:T(8,128)(2,1)S(1)}, s32[4,2]{0,1:T(2,128)S(1)}, bf16[4,448,256]{2,1,0:T(8,128)(2,1)}, s32[]{:T(128)}) while((s32[]{:T(128)}, bf16[2368,256]{1,0:T(8,128)(2,1)S(1)}, s32[4,2]{0,1:T(2,128)S(1)}, bf16[4,448,256]{2,1,0:T(8,128)(2,1)}, s32[]{:T(128)}) %tuple.42), condition=%wide.while_cond.1, body=%wide.while_body.1.sunk | while | flops 2 | bytes 459865 | solution.py:71
  51.2 0.6 slice.453
  51.8 1.4 bitcast_dynamic-update-slice_fusion.2
  53.2 0.6 slice.453
  53.8 1.4 %bitcast_dynamic-update-slice_fusion.2 = bf16[4,448,256]{2,1,0:T(8,128)(2,1)} fusion(bf16[4,448,256]{2,1,0:T(8,128)(2,1)} %get-tuple-element.119, s32[]{:T(128)} %get-tuple-element.116, bf16[2368,256]{1,0:T(8,128)(2,1)S(1)} %get-tuple-element.122, s32[]{:T(128)} %bitcast.151), kind=kLoop, calls=%fused_computation.3.clone.1 | loop fusion | bytes 459776 | tf_op jit(solution)/shard_map/vmap()/gather
  55.3 0.6 slice.453
  55.9 1.4 %bitcast_dynamic-update-slice_fusion.2 = bf16[4,448,256]{2,1,0:T(8,128)(2,1)} fusion(bf16[4,448,256]{2,1,0:T(8,128)(2,1)} %get-tuple-element.119, s32[]{:T(128)} %get-tuple-element.116, bf16[2368,256]{1,0:T(8,128)(2,1)S(1)} %get-tuple-element.122, s32[]{:T(128)} %bitcast.151), kind=kLoop, calls=%fused_computation.3.clone.1 | loop fusion | bytes 459776 | tf_op jit(solution)/shard_map/vmap()/gather
  58.0 1.4 bitcast_dynamic-update-slice_fusion.2
  59.9 4.9 %collective-permute-start.5 = (f32[128,384]{1,0:T(8,128)S(1)}, f32[128,384]{1,0:T(8,128)S(1)}, u32[]{:S(2)}, u32[]{:S(2)}) collective-permute-start(f32[128,384]{1,0:T(8,128)S(1)} %get-tuple-element.52), channel_id=1, source_target_pairs={{1,0},{2,1},{3,2},{4,3},{5,4},{6,5},{7,6},{8,7},{9,8},{10,9},{11,1... | collective-permute-start | bytes 589832 | tf_op jit(solution)/shard_map/ppermute | solution.py:24
  64.8 1.9 %fusion.5 = bf16[4,448,256]{2,1,0:T(8,128)(2,1)S(1)} fusion(bf16[4,448,256]{2,1,0:T(8,128)(2,1)} %get-tuple-element.20, s32[4,448]{1,0:T(4,128)S(1)} %get-tuple-element.12, s32[4,448]{1,0:T(4,128)S(1)} %iota_add_fusion), kind=kOutput, calls=%fused_computation.13 | convolution fusion | flops 412303360 | bytes 1849344 | tf_op jit(solution)/shard_map/vmap()/dot_general | solution.py:75
  66.7 6.8 %reshape.221 = bf16[4,7,8,8,16,16]{5,4,3,2,1,0:T(8,128)(2,1)} reshape(bf16[4,448,256]{2,1,0:T(8,128)(2,1)S(1)} %fusion.5) | data formatting | bytes 1835008 | tf_op jit(solution)/shard_map/reshape | solution.py:78
  73.5 9.8 %copy.129 = bf16[4,7,8,16,8,16]{5,4,3,2,0,1:T(8,128)(2,1)} copy(bf16[4,7,8,16,8,16]{5,3,4,2,1,0:T(8,128)(2,1)} %bitcast.152) | data formatting | bytes 1835008 | tf_op jit(solution)/shard_map/transpose | solution.py:78
  83.3 8.1 %reshape.222 = bf16[4,7,128,128]{3,2,0,1:T(8,128)(2,1)S(1)} reshape(bf16[4,7,8,16,8,16]{5,4,3,2,0,1:T(8,128)(2,1)} %copy.129) | data formatting | bytes 1835008 | tf_op jit(solution)/shard_map/reshape | solution.py:79
  93.9 5.3 %collective-permute-start.7 = (f32[128,384]{0,1:T(8,128)S(1)}, f32[128,384]{0,1:T(8,128)S(1)}, u32[]{:S(2)}, u32[]{:S(2)}) collective-permute-start(f32[128,384]{0,1:T(8,128)S(1)} %get-tuple-element.50), channel_id=1, source_target_pairs={{1,0},{2,1},{3,2},{4,3},{5,4},{6,5},{7,6},{8,7},{9,8},{10,9},{11,1... | collective-permute-start | bytes 589832 | tf_op jit(solution)/shard_map/ppermute | solution.py:24
  99.2 3.3 %collective-permute-done.6 = f32[128,384]{0,1:T(8,128)S(1)} collective-permute-done((f32[128,384]{0,1:T(8,128)S(1)}, f32[128,384]{0,1:T(8,128)S(1)}, u32[]{:S(2)}, u32[]{:S(2)}) %collective-permute-start.6) | collective-permute-done | bytes 196640 | tf_op jit(solution)/shard_map/ppermute | solution.py:23
  104.9 5.7 %collective-permute-start.9 = (f32[128,384]{1,0:T(8,128)S(1)}, f32[128,384]{1,0:T(8,128)S(1)}, u32[]{:S(2)}, u32[]{:S(2)}) collective-permute-start(f32[128,384]{1,0:T(8,128)S(1)} %get-tuple-element.48), channel_id=1, source_target_pairs={{1,0},{2,1},{3,2},{4,3},{5,4},{6,5},{7,6},{8,7},{9,8},{10,9},{11,1... | collective-permute-start | bytes 589832 | tf_op jit(solution)/shard_map/ppermute | solution.py:24
  110.6 0.7 fusion.91
  111.3 2.4 %collective-permute-done.8 = f32[128,384]{1,0:T(8,128)S(1)} collective-permute-done((f32[128,384]{1,0:T(8,128)S(1)}, f32[128,384]{1,0:T(8,128)S(1)}, u32[]{:S(2)}, u32[]{:S(2)}) %collective-permute-start.8) | collective-permute-done | bytes 196640 | tf_op jit(solution)/shard_map/ppermute | solution.py:23
  115.8 1.6 %bitcast_multiply_fusion = (f32[128,4,128]{0,2,1:T(8,128)S(1)}, f32[128,4,128]{0,2,1:T(8,128)S(1)}, f32[4,128,128]{2,1,0:T(8,128)S(1)}) fusion(f32[4,128,128]{2,1,0:T(8,128)S(1)} %convolution_add_fusion.19, f32[]{:T(128)} %bitcast.2, f32[]{:T(128)} %bitcast.22, f32[4,128,128]{2,1,0:T(8,128)S(1)} %convolution_add_fusion.8, ...), kind=kOutput, calls=%fused_computation.92 | convolution fusion | flops 100990976 | bytes 1703944 | tf_op jit(solution)/shard_map/vtc,trc->vtr/dot_general | solution.py:86
  117.5 0.8 fusion.86
  118.3 5.6 %collective-permute-start.11 = (f32[128,384]{0,1:T(8,128)}, f32[128,384]{0,1:T(8,128)}, u32[]{:S(2)}, u32[]{:S(2)}) collective-permute-start(f32[128,384]{0,1:T(8,128)} %get-tuple-element.44), channel_id=1, source_target_pairs={{1,0},{2,1},{3,2},{4,3},{5,4},{6,5},{7,6},{8,7},{9,8},{10,9},{11,1... | collective-permute-start | bytes 589832 | tf_op jit(solution)/shard_map/ppermute | solution.py:24
  124.7 2.9 %collective-permute-done.10 = f32[128,384]{0,1:T(8,128)} collective-permute-done((f32[128,384]{0,1:T(8,128)}, f32[128,384]{0,1:T(8,128)}, u32[]{:S(2)}, u32[]{:S(2)}) %collective-permute-start.10) | collective-permute-done | bytes 196640 | tf_op jit(solution)/shard_map/ppermute | solution.py:23
  127.6 1.1 pad_maximum_fusion.3
  130.9 2.0 %fusion.58 = f32[4,32,512]{2,1,0:T(8,128)S(1)} fusion(f32[4,32,512]{2,1,0:T(8,128)S(1)} %mul.128, f32[4,32,512]{2,1,0:T(8,128)S(1)} %mul.119, f32[32,4,512]{2,0,1:T(8,128)S(1)} %all-to-all-done, f32[4,32,512]{2,1,0:T(8,128)S(1)} %mul.132, f32[4,32,512]{2,1,0:T(8,128)S(1)} %mul.122, f32[]{:T(128)} %bitcast.26, f32[]{:T(128)} %bitcast.17, f32[]{:T(128)} %bitcast), kind=kLoop, calls=%fused_computation.98 | loop fusion | flops 589824 | bytes 1572876 | tf_op jit(solution)/shard_map/add | solution.py:99
  133.0 8.4 %all_to_all.35 = f32[4,32,512]{2,1,0:T(8,128)S(1)} all-to-all(f32[4,32,512]{2,1,0:T(8,128)S(1)} %fusion.58), channel_id=1, replica_groups=mesh['rows'=8,'edges'=4] {'edges'}, dimensions={0} | all-to-all | bytes 524288 | tf_op jit(solution)/shard_map/all_to_all | solution.py:101
  141.4 0.7 copy.195
  (102 shorter events, 13.3 us)
Async XLA Ops:
  0.0 38.6 %copy-start = (bf16[256,512]{1,0:T(8,128)(2,1)S(1)}, bf16[256,512]{1,0:T(8,128)(2,1)}, u32[]{:S(2)}) copy-start(bf16[256,512]{1,0:T(8,128)(2,1)} %param.14) | copy-start | bytes 786436
  0.0 37.3 %copy-start.3 = (bf16[3,512]{1,0:T(4,128)(2,1)S(1)}, bf16[3,512]{1,0:T(4,128)(2,1)}, u32[]{:S(2)}) copy-start(bf16[3,512]{1,0:T(4,128)(2,1)} %param.13) | copy-start | bytes 9220
  2.3 18.0 %collective-permute-start = (s32[3,320]{1,0:T(4,128)S(1)}, s32[3,320]{1,0:T(4,128)S(1)}, u32[]{:S(2)}, u32[]{:S(2)}) collective-permute-start(s32[3,320]{1,0:T(4,128)S(1)} %get-tuple-element.54), channel_id=1, source_target_pairs={{0,1},{1,2},{2,3},{3,4},{4,5},{5,6},{6,7},{7,8},{8,9},{9,10},{10,1... | collective-permute-start | bytes 11528 | tf_op jit(solution)/shard_map/ppermute | solution.py:23
  2.7 17.6 %collective-permute-start.1 = (s32[3,320]{1,0:T(4,128)S(1)}, s32[3,320]{1,0:T(4,128)S(1)}, u32[]{:S(2)}, u32[]{:S(2)}) collective-permute-start(s32[3,320]{1,0:T(4,128)S(1)} %get-tuple-element.53), channel_id=1, source_target_pairs={{1,0},{2,1},{3,2},{4,3},{5,4},{6,5},{7,6},{8,7},{9,8},{10,9},{11,1... | collective-permute-start | bytes 11528 | tf_op jit(solution)/shard_map/ppermute | solution.py:24
  9.7 28.8 %collective-permute-start.2 = (bf16[320,256]{1,0:T(8,128)(2,1)S(1)}, bf16[320,256]{1,0:T(8,128)(2,1)S(1)}, u32[]{:S(2)}, u32[]{:S(2)}) collective-permute-start(bf16[320,256]{1,0:T(8,128)(2,1)S(1)} %get-tuple-element.41), channel_id=1, source_target_pairs={{0,1},{1,2},{2,3},{3,4},{4,5},{5,6},{6,7},{7,8},{8,9},{9,10},{10,1... | collective-permute-start | bytes 491528 | tf_op jit(solution)/shard_map/ppermute | solution.py:23
  9.8 28.8 %collective-permute-start.3 = (bf16[320,256]{1,0:T(8,128)(2,1)S(1)}, bf16[320,256]{1,0:T(8,128)(2,1)S(1)}, u32[]{:S(2)}, u32[]{:S(2)}) collective-permute-start(bf16[320,256]{1,0:T(8,128)(2,1)S(1)} %get-tuple-element.42), channel_id=1, source_target_pairs={{1,0},{2,1},{3,2},{4,3},{5,4},{6,5},{7,6},{8,7},{9,8},{10,9},{11,1... | collective-permute-start | bytes 491528 | tf_op jit(solution)/shard_map/ppermute | solution.py:24
  16.8 42.6 %all-to-all-start = ((f32[32,4,512]{2,0,1:T(8,128)}), f32[32,4,512]{2,0,1:T(8,128)S(1)}, u32[]{:S(2)}, u32[]{:S(2)}) async-start(f32[32,4,512]{2,0,1:T(8,128)} %bitcast.143), calls=%async_computation | async-start | bytes 524288 | tf_op jit(solution)/shard_map/all_to_all | solution.py:94
  37.3 1.3 copy-start.1
  38.5 0.9 copy-start.4
  59.4 32.0 %collective-permute-start.4 = (f32[128,384]{1,0:T(8,128)S(1)}, f32[128,384]{1,0:T(8,128)S(1)}, u32[]{:S(2)}, u32[]{:S(2)}) collective-permute-start(f32[128,384]{1,0:T(8,128)S(1)} %get-tuple-element.51), channel_id=1, source_target_pairs={{0,1},{1,2},{2,3},{3,4},{4,5},{5,6},{6,7},{7,8},{8,9},{9,10},{10,1... | collective-permute-start | bytes 589832 | tf_op jit(solution)/shard_map/ppermute | solution.py:23
  59.9 31.5 %collective-permute-start.5 = (f32[128,384]{1,0:T(8,128)S(1)}, f32[128,384]{1,0:T(8,128)S(1)}, u32[]{:S(2)}, u32[]{:S(2)}) collective-permute-start(f32[128,384]{1,0:T(8,128)S(1)} %get-tuple-element.52), channel_id=1, source_target_pairs={{1,0},{2,1},{3,2},{4,3},{5,4},{6,5},{7,6},{8,7},{9,8},{10,9},{11,1... | collective-permute-start | bytes 589832 | tf_op jit(solution)/shard_map/ppermute | solution.py:24
  93.8 8.7 %collective-permute-start.6 = (f32[128,384]{0,1:T(8,128)S(1)}, f32[128,384]{0,1:T(8,128)S(1)}, u32[]{:S(2)}, u32[]{:S(2)}) collective-permute-start(f32[128,384]{0,1:T(8,128)S(1)} %get-tuple-element.49), channel_id=1, source_target_pairs={{0,1},{1,2},{2,3},{3,4},{4,5},{5,6},{6,7},{7,8},{8,9},{9,10},{10,1... | collective-permute-start | bytes 589832 | tf_op jit(solution)/shard_map/ppermute | solution.py:23
  93.9 8.7 %collective-permute-start.7 = (f32[128,384]{0,1:T(8,128)S(1)}, f32[128,384]{0,1:T(8,128)S(1)}, u32[]{:S(2)}, u32[]{:S(2)}) collective-permute-start(f32[128,384]{0,1:T(8,128)S(1)} %get-tuple-element.50), channel_id=1, source_target_pairs={{1,0},{2,1},{3,2},{4,3},{5,4},{6,5},{7,6},{8,7},{9,8},{10,9},{11,1... | collective-permute-start | bytes 589832 | tf_op jit(solution)/shard_map/ppermute | solution.py:24
  104.1 6.6 %copy-start.2 = (f32[5]{0:T(128)S(1)}, f32[5]{0:T(128)}, u32[]{:S(2)}) copy-start(f32[5]{0:T(128)} %param.17) | copy-start | bytes 64
  104.9 8.8 %collective-permute-start.8 = (f32[128,384]{1,0:T(8,128)S(1)}, f32[128,384]{1,0:T(8,128)S(1)}, u32[]{:S(2)}, u32[]{:S(2)}) collective-permute-start(f32[128,384]{1,0:T(8,128)S(1)} %get-tuple-element.47), channel_id=1, source_target_pairs={{0,1},{1,2},{2,3},{3,4},{4,5},{5,6},{6,7},{7,8},{8,9},{9,10},{10,1... | collective-permute-start | bytes 589832 | tf_op jit(solution)/shard_map/ppermute | solution.py:23
  104.9 8.9 %collective-permute-start.9 = (f32[128,384]{1,0:T(8,128)S(1)}, f32[128,384]{1,0:T(8,128)S(1)}, u32[]{:S(2)}, u32[]{:S(2)}) collective-permute-start(f32[128,384]{1,0:T(8,128)S(1)} %get-tuple-element.48), channel_id=1, source_target_pairs={{1,0},{2,1},{3,2},{4,3},{5,4},{6,5},{7,6},{8,7},{9,8},{10,9},{11,1... | collective-permute-start | bytes 589832 | tf_op jit(solution)/shard_map/ppermute | solution.py:24
  118.3 9.3 %collective-permute-start.10 = (f32[128,384]{0,1:T(8,128)}, f32[128,384]{0,1:T(8,128)}, u32[]{:S(2)}, u32[]{:S(2)}) collective-permute-start(f32[128,384]{0,1:T(8,128)} %get-tuple-element.43), channel_id=1, source_target_pairs={{0,1},{1,2},{2,3},{3,4},{4,5},{5,6},{6,7},{7,8},{8,9},{9,10},{10,1... | collective-permute-start | bytes 589832 | tf_op jit(solution)/shard_map/ppermute | solution.py:23
  118.3 9.3 %collective-permute-start.11 = (f32[128,384]{0,1:T(8,128)}, f32[128,384]{0,1:T(8,128)}, u32[]{:S(2)}, u32[]{:S(2)}) collective-permute-start(f32[128,384]{0,1:T(8,128)} %get-tuple-element.44), channel_id=1, source_target_pairs={{1,0},{2,1},{3,2},{4,3},{5,4},{6,5},{7,6},{8,7},{9,8},{10,9},{11,1... | collective-permute-start | bytes 589832 | tf_op jit(solution)/shard_map/ppermute | solution.py:24
where the time goes:
time: 143 us; the launch traced here: 142 us
  local copies, waits for them, and re-layouts  69 us (48%)
  starting transfers between devices  37.4 us (26%)
  matrix products  13.7 us (10%)
  waiting for transfers between devices  8.74 us (6%)
  blocking collectives  8.42 us (6%)
  other arithmetic  4.28 us (3%)
    ppermute x6, starting transfers between devices, with_halo(): after = lax.ppermute(leading, axis, down)  32.8 us
    gather x24, local copies, waits for them, and re-layouts  14 us
    scatter x1, local copies, waits for them, and re-layouts, per_device(): jnp.zeros((total_len + window, ORB * ORB), jnp.bfloat16).at[dest]  11 us
    scatter x1, local copies, waits for them, and re-layouts, per_device(): jnp.full((total_len + window,), -1, jnp.int32).at[dest]  9.99 us
    transpose x1, local copies, waits for them, and re-layouts, per_device(): band.reshape(trows, nband, TILE_ATOMS, TILE_ATOMS, ORB, ORB)  9.84 us
    dot_general x28, matrix products, apply(): jnp.einsum('vtc,trc->vtr', wide3[:, diag:diag + trows], band[:, diag], pr...  9.23 us
    ppermute x6, waiting for transfers between devices, with_halo(): before = lax.ppermute(last, axis, up)  8.6 us
    all_to_all x1, blocking collectives, per_device(): lax.all_to_all(result, 'edges', split_axis=0, concat_axis=1, tiled=True)  8.42 us
  transfers between devices with their start and end apart: 13, of which 4 were waited for; matrix products, arithmetic and copies ran while one was open for 49% of the time, Pallas kernels for 0%

commit v1 on v0

v1 whole, which is shorter than its diff:
```python
import functools

import jax
import jax.numpy as jnp
from jax import lax
from jax.experimental import pallas as pl
from jax.experimental.pallas import tpu as pltpu
from jax.sharding import PartitionSpec as P

ORB = 16
TILE_ATOMS = 8
BAND = 3
HID = 256
VEC = 128
STEPS = 4
ATOM_Q = 32
SPILL = 320
ID_ROWS = 16
PAIR_ATOMS = 2 * TILE_ATOMS
WIN_ATOMS = (2 * BAND + 2) * TILE_ATOMS
HALO = BAND * TILE_ATOMS * ORB
BF = jnp.bfloat16
F32 = jnp.float32
NT = (((1,), (1,)), ((), ()))


def nt_dot(a, b):
    return lax.dot_general(a, b, NT, preferred_element_type=F32)


def iota(shape, dim):
    return lax.broadcasted_iota(jnp.int32, shape, dim)


def band_kernel(feat, ids, blue, red, cell_bias, w_in, w_out, band, blk, bias8):
    nfeat, width = w_in.shape
    nblk = w_out.shape[1]
    eye = (iota((width, width), 0) == iota((width, width), 1)).astype(BF)
    w_in_t = nt_dot(eye, w_in[...]).astype(BF)
    bias8[...] = jnp.zeros(bias8.shape, F32)
    bias8[0:3, :] = cell_bias[...].astype(F32)
    bias_t = nt_dot(eye, bias8[...].astype(BF)).astype(BF)
    row, col = iota((nblk, nblk), 0), iota((nblk, nblk), 1)
    swap = (col == (row % ORB) * ORB + row // ORB).astype(BF)
    w_out_t = nt_dot(swap, w_out[...]).astype(BF)

    def rows_of(msg, k):
        return msg[SPILL : SPILL + ID_ROWS, :].astype(F32)[2 * k : 2 * k + 2, :]

    parts = []
    own = feat.shape[0]
    for lo in range(0, own, 256):
        parts.append((feat[lo : lo + 256, :], [ids[k : k + 1, lo : lo + 256] for k in range(3)]))
    for msg in (blue, red):
        parts.append((msg[0:256, :], [rows_of(msg, k)[0:1] for k in range(3)]))
    tail = [(rows_of(blue, k)[1:2] + rows_of(red, k)[1:2])[:, :128] for k in range(3)]
    parts.append((jnp.concatenate([blue[256:SPILL, :], red[256:SPILL, :]], axis=0), tail))
    at = 0
    atoms, cols = [], []
    for x, (a, b, c) in parts:
        n = x.shape[0]
        cell1 = (iota((8, n), 0).astype(F32) == c).astype(BF)
        pre = nt_dot(w_in_t, x) + jnp.dot(bias_t, cell1, preferred_element_type=F32)
        gate, up = pre[:HID], pre[HID:]
        hidden = (gate * (0.5 + 0.5 * jnp.tanh(0.5 * gate)) * up).astype(BF)
        blk[:, at : at + n] = jnp.dot(w_out_t, hidden, preferred_element_type=F32).astype(BF)
        atoms.append(a)
        cols.append(b)
        at += n
    atom = jnp.concatenate(atoms, axis=1)
    odd_tile = jnp.floor(atom * (1.0 / TILE_ATOMS)) - 2.0 * jnp.floor(atom * (0.5 / TILE_ATOMS))
    target = jnp.concatenate(cols, axis=1) + TILE_ATOMS * odd_tile
    onehot_t = (iota((WIN_ATOMS, at), 0).astype(F32) == target).astype(BF)
    low = iota((ORB, 128), 1) < WIN_ATOMS
    for first in range(0, ATOM_Q, 4):
        onehot = jnp.concatenate(
            [
                jnp.broadcast_to((atom == float(s)).astype(F32), (WIN_ATOMS, at)).astype(BF) * onehot_t
                for s in range(first, first + 4)
            ],
            axis=0,
        )
        dense = nt_dot(blk[...], onehot)
        for sp in range(2):
            s = first + 2 * sp
            pair, at_row = s // PAIR_ATOMS, s % PAIR_ATOMS * ORB
            for j in range(ORB // 2):
                x = dense[2 * j * ORB : (2 * j + 1) * ORB, sp * 128 : sp * 128 + 128]
                y = dense[(2 * j + 1) * ORB : (2 * j + 2) * ORB, sp * 128 : sp * 128 + 128]
                lanes = slice(j * 128, j * 128 + 128)
                band[pair, at_row : at_row + ORB, lanes] = jnp.where(
                    low, x, pltpu.roll(y, WIN_ATOMS, 1)
                ).astype(BF)
                band[pair, at_row + ORB : at_row + 2 * ORB, lanes] = jnp.where(
                    low, pltpu.roll(x, WIN_ATOMS, 1), y
                ).astype(BF)


def apply_band(band, wide, pair):
    height = PAIR_ATOMS * ORB
    pieces = [
        wide[pl.ds(pair * height + q, WIN_ATOMS, stride=ORB), :] for q in range(ORB)
    ]
    rhs = jnp.concatenate(pieces, axis=0).astype(BF)
    return jnp.dot(band[pair], rhs, preferred_element_type=F32)


def fill_wide(side, own, blue, red, wide):
    rows = own.shape[0]
    end = HALO + rows
    off = pl.multiple_of(side * end, 128)
    wide[pl.ds(off, HALO), :] = blue
    wide[pl.ds(pl.multiple_of(end - off, 128), HALO), :] = red
    wide[HALO:end, :] = own


def put_sends(side, value_ref, to_blue, to_red):
    inner = value_ref.shape[0] - HALO
    off = pl.multiple_of(side * inner, 128)
    to_blue[...] = value_ref[pl.ds(off, HALO), :].astype(BF)
    to_red[...] = value_ref[pl.ds(pl.multiple_of(inner - off, 128), HALO), :].astype(BF)


def first_kernel(side, band, field, blue, red, t0, t1, to_blue, to_red, wide):
    t0[...] = field[...].astype(F32).T
    fill_wide(side[0], t0[...], blue[...].astype(F32).T, red[...].astype(F32).T, wide)
    height = PAIR_ATOMS * ORB
    for pair in range(band.shape[0]):
        t1[pair * height : (pair + 1) * height, :] = apply_band(band, wide, pair)
    put_sends(side[0], t1, to_blue, to_red)


def next_kernel(side, band, before, now, blue, red, after, to_blue, to_red, wide):
    fill_wide(side[0], now[...], blue[...].astype(F32), red[...].astype(F32), wide)
    height = PAIR_ATOMS * ORB
    for pair in range(band.shape[0]):
        span = slice(pair * height, (pair + 1) * height)
        after[span, :] = 2.0 * apply_band(band, wide, pair) - before[span, :]
    put_sends(side[0], after, to_blue, to_red)


def last_kernel(side, coef, band, t0, t1, t2, t3, blue, red, out, wide):
    fill_wide(side[0], t3[...], blue[...].astype(F32), red[...].astype(F32), wide)
    height = PAIR_ATOMS * ORB
    for pair in range(band.shape[0]):
        span = slice(pair * height, (pair + 1) * height)
        t4 = 2.0 * apply_band(band, wide, pair) - t2[span, :]
        total = coef[0] * t0[span, :] + coef[1] * t1[span, :] + coef[2] * t2[span, :]
        total = total + coef[3] * t3[span, :] + coef[4] * t4
        out[:, span] = total.T.astype(BF)


VMEM = pl.BlockSpec(memory_space=pltpu.VMEM)
SMEM = pl.BlockSpec(memory_space=pltpu.SMEM)
PARAMS = pltpu.CompilerParams(vmem_limit_bytes=40 * 1024 * 1024)


def shape(dims, dtype):
    return jax.ShapeDtypeStruct(dims, dtype)


def per_device(features, edge_src, edge_dst, edge_cell, cell_bias, w_in, w_out, vectors, cheb_coef):
    axes = ("rows", "edges")
    ndev = lax.axis_size("rows") * lax.axis_size("edges")
    quarter = lax.axis_index("rows") * lax.axis_size("edges") + lax.axis_index("edges")
    natom = ATOM_Q * ndev
    ntiles = natom // TILE_ATOMS
    side = quarter % 2
    red_pairs = [(i, i ^ 1) for i in range(ndev)]
    blue_pairs = [(i, (i + 1) % ndev if i % 2 else (i - 1) % ndev) for i in range(ndev)]
    nown = features.shape[0]

    rel = edge_src - quarter * ATOM_Q
    rel = jnp.where(rel > natom // 2, rel - natom, jnp.where(rel < -(natom // 2), rel + natom, rel))
    shift_tile = (edge_dst // TILE_ATOMS - edge_src // TILE_ATOMS + BAND + ntiles) % ntiles
    col = shift_tile * TILE_ATOMS + edge_dst % TILE_ATOMS
    ids = jnp.stack([rel, col, edge_cell]).astype(F32)

    def message(first, delta, gap):
        rows = lax.dynamic_slice_in_dim(features, first, SPILL, 0)
        part = lax.dynamic_slice_in_dim(ids, first, SPILL, 1)
        part = part + jnp.array([[1.0], [0.0], [0.0]], F32) * delta
        zeros = jnp.zeros((3, 64), F32)
        tail = [zeros, part[:, 256:]] if gap else [part[:, 256:], zeros]
        block = jnp.concatenate([part[:, :256], *tail, zeros, zeros], axis=1).reshape(6, 256)
        block = jnp.concatenate([block, jnp.zeros((ID_ROWS - 6, 256), F32)], axis=0).astype(BF)
        return jnp.concatenate([rows, block], axis=0)

    low_first, high_first = 0, nown - SPILL
    blue_first = jnp.where(side == 0, low_first, high_first)
    red_first = high_first - blue_first
    sign = (1 - 2 * side).astype(F32) * ATOM_Q
    blue_msg = lax.ppermute(message(blue_first, sign, False), axes, blue_pairs)
    red_msg = lax.ppermute(message(red_first, -sign, True), axes, red_pairs)

    def halo(first, last):
        return (
            lax.ppermute(first, axes, blue_pairs),
            lax.ppermute(last, axes, red_pairs),
        )

    field = lax.all_to_all(vectors.astype(BF), "edges", split_axis=1, concat_axis=0, tiled=True)
    nrow = field.shape[1]
    inner = nrow - HALO
    t0_blue, t0_red = halo(
        lax.dynamic_slice_in_dim(field, side * inner, HALO, 1),
        lax.dynamic_slice_in_dim(field, inner - side * inner, HALO, 1),
    )

    total_len = nown + 2 * SPILL
    band = pl.pallas_call(
        band_kernel,
        name="band",
        out_shape=shape((ATOM_Q // PAIR_ATOMS, PAIR_ATOMS * ORB, WIN_ATOMS * ORB), BF),
        in_specs=[VMEM] * 7,
        out_specs=VMEM,
        scratch_shapes=[
            pltpu.VMEM((ORB * ORB, total_len), BF),
            pltpu.VMEM((8, 2 * HID), F32),
        ],
        compiler_params=PARAMS,
    )(features, ids, blue_msg, red_msg, cell_bias, w_in, w_out)

    side1 = side.reshape(1)
    wide = [pltpu.VMEM((nrow + 2 * HALO, VEC), F32)]
    full, part = shape((nrow, VEC), F32), shape((HALO, VEC), BF)
    t0, t1, to_blue, to_red = pl.pallas_call(
        first_kernel,
        name="first",
        out_shape=(full, full, part, part),
        in_specs=[SMEM] + [VMEM] * 4,
        out_specs=(VMEM,) * 4,
        scratch_shapes=wide,
        compiler_params=PARAMS,
    )(side1, band, field, t0_blue, t0_red)

    fields = [t0, t1]
    for _ in range(2, STEPS):
        blue, red = halo(to_blue, to_red)
        following, to_blue, to_red = pl.pallas_call(
            next_kernel,
            name="next",
            out_shape=(full, part, part),
            in_specs=[SMEM] + [VMEM] * 5,
            out_specs=(VMEM,) * 3,
            scratch_shapes=wide,
            compiler_params=PARAMS,
        )(side1, band, fields[-2], fields[-1], blue, red)
        fields.append(following)
    blue, red = halo(to_blue, to_red)
    result = pl.pallas_call(
        last_kernel,
        name="last",
        out_shape=shape((VEC, nrow), BF),
        in_specs=[SMEM, SMEM] + [VMEM] * 7,
        out_specs=VMEM,
        scratch_shapes=wide,
        compiler_params=PARAMS,
    )(side1, cheb_coef, band, *fields, blue, red)
    result = lax.all_to_all(result, "edges", split_axis=0, concat_axis=1, tiled=True)
    return result.astype(F32)


def solution(mesh):
    placed = (
        P(("rows", "edges"), None),
        P(("rows", "edges")),
        P(("rows", "edges")),
        P(("rows", "edges")),
        P(),
        P(),
        P(),
        P("edges", "rows"),
        P(),
    )
    return jax.shard_map(
        per_device, mesh=mesh, in_specs=placed, out_specs=P("edges", "rows"), check_vma=False
    )
```

time: 143 us -> 58 us (0.41)
  local copies, waits for them, and re-layouts: 69 us -> 2.93 us
  matrix products: 13.7 us -> 0 us
  Pallas kernels: 0 us -> 9.56 us
  starting transfers between devices: 37.4 us -> 27.9 us
  other arithmetic: 4.28 us -> 1.29 us
    scatter x2 -> x0, local copies, waits for them, and re-layouts: 21 us -> none  [the longest x1 11 us: per_device(): jnp.zeros((total_len + window, ORB * ORB), jnp.bfloat16).at[dest]]
    reshape x2, local copies, waits for them, and re-layouts: 14.9 us -> 0.04 us  [message(): jnp.concatenate([part[:, :256], *tail, zeros, zeros], axis=1)]
    gather x24 -> x0, local copies, waits for them, and re-layouts: 14 us -> none
    dot_general x32 -> x0, matrix products: 13.7 us -> none  [the longest x28 9.23 us: apply(): jnp.einsum('vtc,trc->vtr', wide3[:, diag:diag + trows], band[:, diag], pr...]
    ppermute x12 -> x10, starting transfers between devices: 34 us -> 23.7 us  [the longest x4 16.7 us: halo(): lax.ppermute(first, axes, blue_pairs)]
    transpose x1 -> x0, local copies, waits for them, and re-layouts: 9.84 us -> none  [per_device(): band.reshape(trows, nband, TILE_ATOMS, TILE_ATOMS, ORB, ORB)]
    pallas_call x0 -> x5, Pallas kernels: none -> 9.56 us  [the longest x1 6.26 us: per_device(): pl.pallas_call(band_kernel, name='band', out_shape=shape((ATOM_Q // PAIR_...]
    slice x8 -> x2, local copies, waits for them, and re-layouts: 2.69 us -> 0.01 us  [the longest x1 0.01 us: message(): part[:, :256]]
  transfers between devices with their start and end apart: 13 -> 11, of which waited for: 4 -> 4; matrix products, arithmetic and copies ran while one was open for 49% -> 1% of each run, Pallas kernels for 0% -> 11%
where the time goes in v1:
time: 58 us; the launch traced here: 57.7 us
  starting transfers between devices  27.9 us (48%)
  Pallas kernels  9.56 us (16%)
  waiting for transfers between devices  8.72 us (15%)
  blocking collectives  7.02 us (12%)
  local copies, waits for them, and re-layouts  2.93 us (5%)
  other arithmetic  1.29 us (2%)
    ppermute x4, starting transfers between devices, halo(): lax.ppermute(first, axes, blue_pairs)  16.7 us
    ppermute x4, waiting for transfers between devices, halo(): lax.ppermute(first, axes, blue_pairs)  7.22 us
    all_to_all x1, blocking collectives, per_device(): lax.all_to_all(result, 'edges', split_axis=0, concat_axis=1, tiled=True)  7.02 us
    ppermute x1, starting transfers between devices, per_device(): blue_msg = lax.ppermute(message(blue_first, sign, False), axes, blue_pairs)  6.37 us
    pallas_call x1, Pallas kernels, per_device(): pl.pallas_call(band_kernel, name='band', out_shape=shape((ATOM_Q // PAIR_...  6.26 us
    all_to_all x1, starting transfers between devices, per_device(): lax.all_to_all(vectors.astype(BF), 'edges', split_axis=1, concat_axis=0,...  4.21 us
    ppermute x1, waiting for transfers between devices, per_device(): blue_msg = lax.ppermute(message(blue_first, sign, False), axes, blue_pairs)  1.49 us
    unnamed x18, local copies, waits for them, and re-layouts  1.4 us
  transfers between devices with their start and end apart: 11, of which 4 were waited for; matrix products, arithmetic and copies ran while one was open for 1% of the time, Pallas kernels for 11%

profile of v1, /device:TPU:0, one launch (start us, length us, event | category | flops | bytes accessed | tf_op | source)
XLA Modules:
  0.0 57.7 jit_solution(38613642490158799)
XLA Ops:
  0.0 0.0 copy-start
  0.0 1.0 %convert_element_type.22 = bf16[32,2048]{1,0:T(8,128)(2,1)S(1)} convert(f32[32,2048]{1,0:T(8,128)} %param.18) | non-fusion elementwise | flops 65536 | bytes 393216 | tf_op jit(solution)/shard_map/convert_element_type | solution.py:202
  1.0 0.7 %copy.17 = bf16[4,4,8,512]{3,2,0,1:T(8,128)(2,1)} copy(bf16[4,4,8,512]{3,2,1,0:T(8,128)(2,1)S(1)} %bitcast.20) | data formatting | bytes 262144 | tf_op jit(solution)/shard_map/all_to_all | solution.py:202
  1.7 4.2 %all-to-all-start = ((bf16[32,4,512]{2,0,1:T(8,128)(2,1)}), bf16[32,4,512]{2,0,1:T(8,128)(2,1)S(1)}, u32[]{:S(2)}, u32[]{:S(2)}) async-start(bf16[32,4,512]{2,0,1:T(8,128)(2,1)} %bitcast.16), calls=%async_computation | async-start | bytes 262144 | tf_op jit(solution)/shard_map/all_to_all | solution.py:202
  5.9 0.0 copy-start.5
  5.9 0.7 %copy-done.5 = s32[1280]{0:T(1024)S(1)} copy-done((s32[1280]{0:T(1024)S(1)}, s32[1280]{0:T(1024)}, u32[]{:S(2)}) %copy-start.5) | copy-done | bytes 5144
  6.6 0.0 copy-done.6
  6.6 0.0 copy-done.7
  6.7 0.0 copy-start.8
  6.7 0.6 %copy-done.8 = f32[3,1]{0,1:T(1,128)S(1)} copy-done((f32[3,1]{0,1:T(1,128)S(1)}, f32[3,1]{0,1:T(1,128)}, u32[]{:S(2)}) %copy-start.8) | copy-done | bytes 36
  7.4 0.1 add_convert_fusion.1
  7.5 0.0 copy-done
  7.6 6.4 %collective-permute-start = (bf16[336,256]{1,0:T(8,128)(2,1)S(1)}, bf16[336,256]{1,0:T(8,128)(2,1)S(1)}, u32[]{:S(2)}, u32[]{:S(2)}) collective-permute-start(bf16[336,256]{1,0:T(8,128)(2,1)S(1)} %fusion.2), channel_id=1, source_target_pairs={{0,31},{1,2},{2,1},{3,4},{4,3},{5,6},{6,5},{7,8},{8,7},{9,10},{10,... | collective-permute-start | bytes 516104 | tf_op jit(solution)/shard_map/ppermute | solution.py:193
  14.0 0.1 maximum_maximum_fusion
  14.1 0.0 copy-start.1
  14.1 0.1 collective-permute-start.1
  14.2 0.0 all-to-all-done
  14.2 0.0 copy-start.2
  14.2 0.0 copy-start.3
  14.3 0.5 collective-permute-start.3
  14.8 0.8 %collective-permute-start.2 = (bf16[128,384]{1,0:T(8,128)(2,1)S(1)}, bf16[128,384]{1,0:T(8,128)(2,1)S(1)}, u32[]{:S(2)}, u32[]{:S(2)}) collective-permute-start(bf16[128,384]{1,0:T(8,128)(2,1)S(1)} %get-tuple-element.28), channel_id=1, source_target_pairs={{0,31},{1,2},{2,1},{3,4},{4,3},{5,6},{6,5},{7,8},{8,7},{9,10},{10,... | collective-permute-start | bytes 294920 | tf_op jit(solution)/shard_map/ppermute | solution.py:198
  15.6 1.5 %collective-permute-done.blue = bf16[336,256]{1,0:T(8,128)(2,1)S(1)} collective-permute-done((bf16[336,256]{1,0:T(8,128)(2,1)S(1)}, bf16[336,256]{1,0:T(8,128)(2,1)S(1)}, u32[]{:S(2)}, u32[]{:S(2)}) %collective-permute-start) | collective-permute-done | bytes 172064 | tf_op jit(solution)/shard_map/ppermute | solution.py:193
  17.1 0.0 collective-permute-done.1.red
  17.1 0.0 copy-done.1
  17.1 0.0 copy-done.2
  17.1 0.0 copy-done.3
  17.2 6.3 %band.1 = bf16[2,256,1024]{2,1,0:T(8,128)(2,1)S(1)} custom-call(bf16[1280,256]{1,0:T(8,128)(2,1)S(1)} %copy-done, f32[3,1280]{1,0:T(4,128)S(1)} %add_convert_fusion.ids, bf16[336,256]{1,0:T(8,128)(2,1)S(1)} %collective-permute-done.blue, bf16[336,256]{1,0:T(8,128)(2,1)S(1)} %collective-permute-done.1.red, bf16[3,512]{1,0:T(4,128)(2,1)S(1)} %copy-done.3, ...), custom_call_target="tpu_custom_call" | custom-call | tf_op jit(solution)/shard_map/band/pallas_call | solution.py:211
  23.4 0.0 collective-permute-done.3.red
  23.4 0.0 collective-permute-done.2.blue
  23.4 0.8 %first.1 = (f32[512,128]{1,0:T(8,128)S(1)}, f32[512,128]{1,0:T(8,128)S(1)}, bf16[384,128]{1,0:T(8,128)(2,1)S(1)}, bf16[384,128]{1,0:T(8,128)(2,1)S(1)}) custom-call(s32[1]{0:T(128)} %bitcast.side, bf16[2,256,1024]{2,1,0:T(8,128)(2,1)S(1)} %band.1, bf16[128,512]{1,0:T(8,128)(2,1)S(1)} %bitcast.18, bf16[128,384]{1,0:T(8,128)(2,1)S(1)} %collective-permute-done.2.blue, ...), custom_call_target="tpu_custom_call" | custom-call | tf_op jit(solution)/shard_map/first/pallas_call | solution.py:227
  24.2 5.3 %collective-permute-start.4 = (bf16[384,128]{1,0:T(8,128)(2,1)S(1)}, bf16[384,128]{1,0:T(8,128)(2,1)S(1)}, u32[]{:S(2)}, u32[]{:S(2)}) collective-permute-start(bf16[384,128]{1,0:T(8,128)(2,1)S(1)} %get-tuple-element.17), channel_id=1, source_target_pairs={{0,31},{1,2},{2,1},{3,4},{4,3},{5,6},{6,5},{7,8},{8,7},{9,10},{10,... | collective-permute-start | bytes 294920 | tf_op jit(solution)/shard_map/ppermute | solution.py:198
  29.5 0.0 collective-permute-start.5
  29.5 2.4 %collective-permute-done.4.blue = bf16[384,128]{1,0:T(8,128)(2,1)S(1)} collective-permute-done((bf16[384,128]{1,0:T(8,128)(2,1)S(1)}, bf16[384,128]{1,0:T(8,128)(2,1)S(1)}, u32[]{:S(2)}, u32[]{:S(2)}) %collective-permute-start.4) | collective-permute-done | bytes 98336 | tf_op jit(solution)/shard_map/ppermute | solution.py:198
  31.9 0.0 collective-permute-done.5.red
  31.9 0.6 %next.2 = (f32[512,128]{1,0:T(8,128)S(1)}, bf16[384,128]{1,0:T(8,128)(2,1)S(1)}, bf16[384,128]{1,0:T(8,128)(2,1)S(1)}) custom-call(s32[1]{0:T(128)} %bitcast.side, bf16[2,256,1024]{2,1,0:T(8,128)(2,1)S(1)} %band.1, f32[512,128]{1,0:T(8,128)S(1)} %get-tuple-element.15.before.t0, f32[512,128]{1,0:T(8,128)S(1)} %get-tuple-element.16.now.before.t1, ...), custom_call_target="tpu_custom_call" | custom-call | tf_op jit(solution)/shard_map/next/pallas_call | solution.py:240
  32.6 5.3 %collective-permute-start.6 = (bf16[384,128]{1,0:T(8,128)(2,1)S(1)}, bf16[384,128]{1,0:T(8,128)(2,1)S(1)}, u32[]{:S(2)}, u32[]{:S(2)}) collective-permute-start(bf16[384,128]{1,0:T(8,128)(2,1)S(1)} %get-tuple-element.20), channel_id=1, source_target_pairs={{0,31},{1,2},{2,1},{3,4},{4,3},{5,6},{6,5},{7,8},{8,7},{9,10},{10,... | collective-permute-start | bytes 294920 | tf_op jit(solution)/shard_map/ppermute | solution.py:198
  37.9 0.0 collective-permute-start.7
  37.9 2.4 %collective-permute-done.6.blue = bf16[384,128]{1,0:T(8,128)(2,1)S(1)} collective-permute-done((bf16[384,128]{1,0:T(8,128)(2,1)S(1)}, bf16[384,128]{1,0:T(8,128)(2,1)S(1)}, u32[]{:S(2)}, u32[]{:S(2)}) %collective-permute-start.6) | collective-permute-done | bytes 98336 | tf_op jit(solution)/shard_map/ppermute | solution.py:198
  40.3 0.0 collective-permute-done.7.red
  40.3 0.6 %next.3 = (f32[512,128]{1,0:T(8,128)S(1)}, bf16[384,128]{1,0:T(8,128)(2,1)S(1)}, bf16[384,128]{1,0:T(8,128)(2,1)S(1)}) custom-call(s32[1]{0:T(128)} %bitcast.side, bf16[2,256,1024]{2,1,0:T(8,128)(2,1)S(1)} %band.1, f32[512,128]{1,0:T(8,128)S(1)} %get-tuple-element.16.now.before.t1, f32[512,128]{1,0:T(8,128)S(1)} %get-tuple-element.19.now.t2, ...), custom_call_target="tpu_custom_call" | custom-call | tf_op jit(solution)/shard_map/next/pallas_call | solution.py:240
  40.9 5.3 %collective-permute-start.8 = (bf16[384,128]{1,0:T(8,128)(2,1)S(1)}, bf16[384,128]{1,0:T(8,128)(2,1)S(1)}, u32[]{:S(2)}, u32[]{:S(2)}) collective-permute-start(bf16[384,128]{1,0:T(8,128)(2,1)S(1)} %get-tuple-element.23), channel_id=1, source_target_pairs={{0,31},{1,2},{2,1},{3,4},{4,3},{5,6},{6,5},{7,8},{8,7},{9,10},{10,... | collective-permute-start | bytes 294920 | tf_op jit(solution)/shard_map/ppermute | solution.py:198
  46.2 0.0 collective-permute-start.9
  46.2 2.4 %collective-permute-done.8.blue = bf16[384,128]{1,0:T(8,128)(2,1)S(1)} collective-permute-done((bf16[384,128]{1,0:T(8,128)(2,1)S(1)}, bf16[384,128]{1,0:T(8,128)(2,1)S(1)}, u32[]{:S(2)}, u32[]{:S(2)}) %collective-permute-start.8) | collective-permute-done | bytes 98336 | tf_op jit(solution)/shard_map/ppermute | solution.py:198
  48.6 0.0 collective-permute-done.9.red
  48.6 0.0 copy-done.4
  48.6 1.3 %last.1 = bf16[128,512]{1,0:T(8,128)(2,1)S(1)} custom-call(s32[1]{0:T(128)} %bitcast.side, f32[5]{0:T(128)S(1)} %copy-done.4, bf16[2,256,1024]{2,1,0:T(8,128)(2,1)S(1)} %band.1, f32[512,128]{1,0:T(8,128)S(1)} %get-tuple-element.15.before.t0, f32[512,128]{1,0:T(8,128)S(1)} %get-tuple-element.16.now.before.t1, f32[512,128]{1,0:T(8,128)S(1)} %get-tuple-element.19.now.t2, ...), custom_call_target="tpu_custom_call" | custom-call | tf_op jit(solution)/shard_map/last/pallas_call | solution.py:251
  49.9 7.0 %all_to_all.32 = bf16[4,32,512]{2,1,0:T(8,128)(2,1)S(1)} all-to-all(bf16[4,32,512]{2,1,0:T(8,128)(2,1)S(1)} %bitcast.19), channel_id=1, replica_groups=mesh['rows'=8,'edges'=4] {'edges'}, dimensions={0} | all-to-all | bytes 262144 | tf_op jit(solution)/shard_map/all_to_all | solution.py:260
  56.9 0.7 %copy.15 = f32[4,4,8,512]{3,2,0,1:T(8,128)} copy(f32[4,4,8,512]{3,2,1,0:T(8,128)S(1)} %convert_bitcast_fusion) | data formatting | bytes 524288 | tf_op jit(solution)/shard_map/convert_element_type | solution.py:261
  (23 shorter events, 0.3 us)
Async XLA Ops:
  0.0 7.5 %copy-start = (bf16[1280,256]{1,0:T(8,128)(2,1)S(1)}, bf16[1280,256]{1,0:T(8,128)(2,1)}, u32[]{:S(2)}) copy-start(bf16[1280,256]{1,0:T(8,128)(2,1)} %feat.1) | copy-start | bytes 1966084
  1.7 12.5 %all-to-all-start = ((bf16[32,4,512]{2,0,1:T(8,128)(2,1)}), bf16[32,4,512]{2,0,1:T(8,128)(2,1)S(1)}, u32[]{:S(2)}, u32[]{:S(2)}) async-start(bf16[32,4,512]{2,0,1:T(8,128)(2,1)} %bitcast.16), calls=%async_computation | async-start | bytes 262144 | tf_op jit(solution)/shard_map/all_to_all | solution.py:202
  5.9 0.7 %copy-start.5 = (s32[1280]{0:T(1024)S(1)}, s32[1280]{0:T(1024)}, u32[]{:S(2)}) copy-start(s32[1280]{0:T(1024)} %param.14) | copy-start | bytes 15364
  5.9 0.7 %copy-start.6 = (s32[1280]{0:T(1024)S(1)}, s32[1280]{0:T(1024)}, u32[]{:S(2)}) copy-start(s32[1280]{0:T(1024)} %param.12) | copy-start | bytes 15364
  5.9 0.7 %copy-start.7 = (s32[1280]{0:T(1024)S(1)}, s32[1280]{0:T(1024)}, u32[]{:S(2)}) copy-start(s32[1280]{0:T(1024)} %param.13) | copy-start | bytes 15364
  6.7 0.7 %copy-start.8 = (f32[3,1]{0,1:T(1,128)S(1)}, f32[3,1]{0,1:T(1,128)}, u32[]{:S(2)}) copy-start(f32[3,1]{0,1:T(1,128)} %constant.104.clone) | copy-start | bytes 40
  7.6 9.6 %collective-permute-start = (bf16[336,256]{1,0:T(8,128)(2,1)S(1)}, bf16[336,256]{1,0:T(8,128)(2,1)S(1)}, u32[]{:S(2)}, u32[]{:S(2)}) collective-permute-start(bf16[336,256]{1,0:T(8,128)(2,1)S(1)} %fusion.2), channel_id=1, source_target_pairs={{0,31},{1,2},{2,1},{3,4},{4,3},{5,6},{6,5},{7,8},{8,7},{9,10},{10,... | collective-permute-start | bytes 516104 | tf_op jit(solution)/shard_map/ppermute | solution.py:193
  14.1 3.0 %copy-start.1 = (bf16[256,512]{1,0:T(8,128)(2,1)S(1)}, bf16[256,512]{1,0:T(8,128)(2,1)}, u32[]{:S(2)}) copy-start(bf16[256,512]{1,0:T(8,128)(2,1)} %w_in.1) | copy-start | bytes 786436
  14.1 3.0 %collective-permute-start.1 = (bf16[336,256]{1,0:T(8,128)(2,1)S(1)}, bf16[336,256]{1,0:T(8,128)(2,1)S(1)}, u32[]{:S(2)}, u32[]{:S(2)}) collective-permute-start(bf16[336,256]{1,0:T(8,128)(2,1)S(1)} %fusion.3), channel_id=1, source_target_pairs={{0,1},{1,0},{2,3},{3,2},{4,5},{5,4},{6,7},{7,6},{8,9},{9,8},{10,11... | collective-permute-start | bytes 516104 | tf_op jit(solution)/shard_map/ppermute | solution.py:194
  14.2 2.9 %copy-start.2 = (bf16[256,256]{1,0:T(8,128)(2,1)S(1)}, bf16[256,256]{1,0:T(8,128)(2,1)}, u32[]{:S(2)}) copy-start(bf16[256,256]{1,0:T(8,128)(2,1)} %w_out.1) | copy-start | bytes 393220
  14.2 2.9 %copy-start.3 = (bf16[3,512]{1,0:T(4,128)(2,1)S(1)}, bf16[3,512]{1,0:T(4,128)(2,1)}, u32[]{:S(2)}) copy-start(bf16[3,512]{1,0:T(4,128)(2,1)} %cell_bias.1) | copy-start | bytes 9220
  14.3 9.1 %collective-permute-start.3 = (bf16[128,384]{1,0:T(8,128)(2,1)S(1)}, bf16[128,384]{1,0:T(8,128)(2,1)S(1)}, u32[]{:S(2)}, u32[]{:S(2)}) collective-permute-start(bf16[128,384]{1,0:T(8,128)(2,1)S(1)} %get-tuple-element.27), channel_id=1, source_target_pairs={{0,1},{1,0},{2,3},{3,2},{4,5},{5,4},{6,7},{7,6},{8,9},{9,8},{10,11... | collective-permute-start | bytes 294920 | tf_op jit(solution)/shard_map/ppermute | solution.py:199
  14.8 8.6 %collective-permute-start.2 = (bf16[128,384]{1,0:T(8,128)(2,1)S(1)}, bf16[128,384]{1,0:T(8,128)(2,1)S(1)}, u32[]{:S(2)}, u32[]{:S(2)}) collective-permute-start(bf16[128,384]{1,0:T(8,128)(2,1)S(1)} %get-tuple-element.28), channel_id=1, source_target_pairs={{0,31},{1,2},{2,1},{3,4},{4,3},{5,6},{6,5},{7,8},{8,7},{9,10},{10,... | collective-permute-start | bytes 294920 | tf_op jit(solution)/shard_map/ppermute | solution.py:198
  24.2 7.7 %collective-permute-start.4 = (bf16[384,128]{1,0:T(8,128)(2,1)S(1)}, bf16[384,128]{1,0:T(8,128)(2,1)S(1)}, u32[]{:S(2)}, u32[]{:S(2)}) collective-permute-start(bf16[384,128]{1,0:T(8,128)(2,1)S(1)} %get-tuple-element.17), channel_id=1, source_target_pairs={{0,31},{1,2},{2,1},{3,4},{4,3},{5,6},{6,5},{7,8},{8,7},{9,10},{10,... | collective-permute-start | bytes 294920 | tf_op jit(solution)/shard_map/ppermute | solution.py:198
  29.5 2.4 %collective-permute-start.5 = (bf16[384,128]{1,0:T(8,128)(2,1)S(1)}, bf16[384,128]{1,0:T(8,128)(2,1)S(1)}, u32[]{:S(2)}, u32[]{:S(2)}) collective-permute-start(bf16[384,128]{1,0:T(8,128)(2,1)S(1)} %get-tuple-element.18), channel_id=1, source_target_pairs={{0,1},{1,0},{2,3},{3,2},{4,5},{5,4},{6,7},{7,6},{8,9},{9,8},{10,11... | collective-permute-start | bytes 294920 | tf_op jit(solution)/shard_map/ppermute | solution.py:199
  32.6 7.7 %collective-permute-start.6 = (bf16[384,128]{1,0:T(8,128)(2,1)S(1)}, bf16[384,128]{1,0:T(8,128)(2,1)S(1)}, u32[]{:S(2)}, u32[]{:S(2)}) collective-permute-start(bf16[384,128]{1,0:T(8,128)(2,1)S(1)} %get-tuple-element.20), channel_id=1, source_target_pairs={{0,31},{1,2},{2,1},{3,4},{4,3},{5,6},{6,5},{7,8},{8,7},{9,10},{10,... | collective-permute-start | bytes 294920 | tf_op jit(solution)/shard_map/ppermute | solution.py:198
  37.9 2.4 %collective-permute-start.7 = (bf16[384,128]{1,0:T(8,128)(2,1)S(1)}, bf16[384,128]{1,0:T(8,128)(2,1)S(1)}, u32[]{:S(2)}, u32[]{:S(2)}) collective-permute-start(bf16[384,128]{1,0:T(8,128)(2,1)S(1)} %get-tuple-element.21), channel_id=1, source_target_pairs={{0,1},{1,0},{2,3},{3,2},{4,5},{5,4},{6,7},{7,6},{8,9},{9,8},{10,11... | collective-permute-start | bytes 294920 | tf_op jit(solution)/shard_map/ppermute | solution.py:199
  40.9 7.7 %collective-permute-start.8 = (bf16[384,128]{1,0:T(8,128)(2,1)S(1)}, bf16[384,128]{1,0:T(8,128)(2,1)S(1)}, u32[]{:S(2)}, u32[]{:S(2)}) collective-permute-start(bf16[384,128]{1,0:T(8,128)(2,1)S(1)} %get-tuple-element.23), channel_id=1, source_target_pairs={{0,31},{1,2},{2,1},{3,4},{4,3},{5,6},{6,5},{7,8},{8,7},{9,10},{10,... | collective-permute-start | bytes 294920 | tf_op jit(solution)/shard_map/ppermute | solution.py:198
  46.2 2.4 %copy-start.4 = (f32[5]{0:T(128)S(1)}, f32[5]{0:T(128)}, u32[]{:S(2)}) copy-start(f32[5]{0:T(128)} %coef.1) | copy-start | bytes 64
  46.2 2.4 %collective-permute-start.9 = (bf16[384,128]{1,0:T(8,128)(2,1)S(1)}, bf16[384,128]{1,0:T(8,128)(2,1)S(1)}, u32[]{:S(2)}, u32[]{:S(2)}) collective-permute-start(bf16[384,128]{1,0:T(8,128)(2,1)S(1)} %get-tuple-element.24), channel_id=1, source_target_pairs={{0,1},{1,0},{2,3},{3,2},{4,5},{5,4},{6,7},{7,6},{8,9},{9,8},{10,11... | collective-permute-start | bytes 294920 | tf_op jit(solution)/shard_map/ppermute | solution.py:199

commit v2 on v1

v2 whole, which is shorter than its diff:
```python
import functools

import jax
import jax.numpy as jnp
from jax import lax
from jax.experimental import pallas as pl
from jax.experimental.pallas import tpu as pltpu
from jax.sharding import PartitionSpec as P

ORB = 16
TILE_ATOMS = 8
BAND = 3
HID = 256
VEC = 128
STEPS = 4
ATOM_Q = 32
SPILL = 320
ID_ROWS = 16
PAIR_ATOMS = 2 * TILE_ATOMS
WIN_ATOMS = (2 * BAND + 2) * TILE_ATOMS
HALO = BAND * TILE_ATOMS * ORB
BF = jnp.bfloat16
F32 = jnp.float32
NT = (((1,), (1,)), ((), ()))


def nt_dot(a, b):
    return lax.dot_general(a, b, NT, preferred_element_type=F32)


def iota(shape, dim):
    return lax.broadcasted_iota(jnp.int32, shape, dim)


def device_side():
    return (lax.axis_index("rows") * lax.axis_size("edges") + lax.axis_index("edges")) % 2


def prep_kernel(feat, src, dst, cell, vectors, blue, red, ids, p0, p1, p2, p3, sems):
    ndev = lax.axis_size("rows") * lax.axis_size("edges")
    member = lax.axis_index("edges")
    quarter = lax.axis_index("rows") * lax.axis_size("edges") + member
    side = quarter % 2
    high = feat.shape[0] - SPILL
    off = pl.multiple_of(side * high, 64)
    copies = [
        pltpu.make_async_copy(feat.at[pl.ds(off, SPILL)], blue.at[pl.ds(0, SPILL)], sems.at[0]),
        pltpu.make_async_copy(
            feat.at[pl.ds(pl.multiple_of(high - off, 64), SPILL)], red.at[pl.ds(0, SPILL)], sems.at[1]
        ),
    ]
    for copy in copies:
        copy.start()
    natom = ATOM_Q * ndev
    ntiles = natom // TILE_ATOMS
    rel = src[...] - quarter * ATOM_Q
    rel = jnp.where(rel > natom // 2, rel - natom, jnp.where(rel < -(natom // 2), rel + natom, rel))
    shift = (dst[...] >> 3) - (src[...] >> 3) + BAND
    shift = jnp.where(shift < 0, shift + ntiles, jnp.where(shift >= ntiles, shift - ntiles, shift))
    three = [x.astype(F32) for x in (rel, shift * TILE_ATOMS + (dst[...] & 7), cell[...])]
    for k in range(3):
        ids[k] = three[k]
    lane, line = iota((3, 128), 1), iota((3, 128), 0)
    nrow = src.shape[0]
    starts = [x[0:3] for x in three]
    ends = [x[nrow - 3 : nrow] for x in three]
    starts[0] = jnp.where((line == 2) & (lane >= 64), -64.0, starts[0] + ATOM_Q)
    ends[0] = jnp.where((line == 0) & (lane < 64), -64.0, ends[0] - ATOM_Q)
    pad = jnp.zeros((ID_ROWS - 9, 128), F32)
    low_ids = jnp.concatenate(starts + [pad], axis=0)
    high_ids = jnp.concatenate(ends + [pad], axis=0)
    none = jnp.zeros((ID_ROWS, 128), BF)
    for msg, ids_of in (
        (blue, jnp.where(side == 0, low_ids, high_ids)),
        (red, jnp.where(side == 0, high_ids, low_ids)),
    ):
        msg[SPILL : SPILL + ID_ROWS, 0:128] = ids_of.astype(BF)
        msg[SPILL : SPILL + ID_ROWS, 128:256] = none
    for k, piece in enumerate((p0, p1, p2, p3)):
        width = piece.shape[1]
        at = pl.multiple_of((member ^ k) * width, width)
        piece[...] = vectors[:, pl.ds(at, width)].astype(BF)
    for copy in copies:
        copy.wait()


def field_kernel(p0, p1, p2, p3, t0, to_blue, to_red, field):
    member = lax.axis_index("edges")
    for k, piece in enumerate((p0, p1, p2, p3)):
        high = piece.shape[0]
        field[pl.ds(pl.multiple_of((member ^ k) * high, high), high), :] = piece[...].astype(F32)
    t0[...] = field[...].T
    put_sends(t0, to_blue, to_red)


def band_kernel(feat, ids, blue, red, cell_bias, w_in, w_out, band, blk, bias8, spill):
    nfeat, width = w_in.shape
    nblk = w_out.shape[1]
    eye = (iota((width, width), 0) == iota((width, width), 1)).astype(BF)
    w_in_t = nt_dot(eye, w_in[...]).astype(BF)
    bias8[...] = jnp.zeros(bias8.shape, F32)
    bias8[0:3, :] = cell_bias[...].astype(F32)
    bias_t = nt_dot(eye, bias8[...].astype(BF)).astype(BF)
    row, col = iota((nblk, nblk), 0), iota((nblk, nblk), 1)
    swap = (col == (row % ORB) * ORB + row // ORB).astype(BF)
    w_out_t = nt_dot(swap, w_out[...]).astype(BF)

    side = device_side()
    parts = []
    for lo in range(0, feat.shape[0], 256):
        line = lo // 128
        parts.append(
            (
                lambda lo=lo: feat[lo : lo + 256, :],
                [jnp.concatenate([ids[k, line : line + 1], ids[k, line + 1 : line + 2]], axis=1) for k in range(3)],
            )
        )
    rows = spill.shape[0] // 2
    for m, (msg, gap) in enumerate(((blue, side == 0), (red, side == 1))):
        base = m * rows
        spill[base : base + 64, :] = jnp.zeros((64, nfeat), BF)
        spill[base + rows - 64 : base + rows, :] = jnp.zeros((64, nfeat), BF)
        at = pl.multiple_of(base + jnp.where(gap, 64, 0), 64)
        spill[pl.ds(at, SPILL), :] = msg[0:SPILL, :]
    lines = []
    for msg in (blue, red):
        block = msg[SPILL : SPILL + ID_ROWS, 0:128].astype(F32)
        lines.extend([[block[3 * k + n : 3 * k + n + 1] for k in range(3)] for n in range(3)])
    for lo in range(0, 2 * rows, 256):
        first, second = lines[lo // 128], lines[lo // 128 + 1]
        parts.append(
            (
                lambda lo=lo: spill[lo : lo + 256, :],
                [jnp.concatenate([first[k], second[k]], axis=1) for k in range(3)],
            )
        )
    at = 0
    atoms, cols = [], []
    for get, (a, b, c) in parts:
        x = get()
        n = x.shape[0]
        cell1 = (iota((8, n), 0).astype(F32) == c).astype(BF)
        pre = nt_dot(w_in_t, x) + jnp.dot(bias_t, cell1, preferred_element_type=F32)
        gate, up = pre[:HID], pre[HID:]
        hidden = (gate * (0.5 + 0.5 * jnp.tanh(0.5 * gate)) * up).astype(BF)
        blk[:, at : at + n] = jnp.dot(w_out_t, hidden, preferred_element_type=F32).astype(BF)
        atoms.append(a)
        cols.append(b)
        at += n
    atom = jnp.concatenate(atoms, axis=1)
    odd_tile = jnp.floor(atom * (1.0 / TILE_ATOMS)) - 2.0 * jnp.floor(atom * (0.5 / TILE_ATOMS))
    target = jnp.concatenate(cols, axis=1) + TILE_ATOMS * odd_tile
    onehot_t = (iota((WIN_ATOMS, at), 0).astype(F32) == target).astype(BF)
    low = iota((ORB, 128), 1) < WIN_ATOMS
    for first in range(0, ATOM_Q, 4):
        onehot = jnp.concatenate(
            [
                jnp.broadcast_to((atom == float(s)).astype(F32), (WIN_ATOMS, at)).astype(BF) * onehot_t
                for s in range(first, first + 4)
            ],
            axis=0,
        )
        dense = nt_dot(blk[...], onehot)
        for sp in range(2):
            s = first + 2 * sp
            pair, at_row = s // PAIR_ATOMS, s % PAIR_ATOMS * ORB
            for j in range(ORB // 2):
                x = dense[2 * j * ORB : (2 * j + 1) * ORB, sp * 128 : sp * 128 + 128]
                y = dense[(2 * j + 1) * ORB : (2 * j + 2) * ORB, sp * 128 : sp * 128 + 128]
                lanes = slice(j * 128, j * 128 + 128)
                band[pair, at_row : at_row + ORB, lanes] = jnp.where(
                    low, x, pltpu.roll(y, WIN_ATOMS, 1)
                ).astype(BF)
                band[pair, at_row + ORB : at_row + 2 * ORB, lanes] = jnp.where(
                    low, pltpu.roll(x, WIN_ATOMS, 1), y
                ).astype(BF)


def apply_band(band, wide, pair):
    height = PAIR_ATOMS * ORB
    pieces = [
        wide[pl.ds(pair * height + q, WIN_ATOMS, stride=ORB), :] for q in range(ORB)
    ]
    rhs = jnp.concatenate(pieces, axis=0).astype(BF)
    return jnp.dot(band[pair], rhs, preferred_element_type=F32)


def fill_wide(own, blue, red, wide):
    side = device_side()
    rows = own.shape[0]
    end = HALO + rows
    off = pl.multiple_of(side * end, 128)
    wide[pl.ds(off, HALO), :] = blue
    wide[pl.ds(pl.multiple_of(end - off, 128), HALO), :] = red
    wide[HALO:end, :] = own


def put_sends(value_ref, to_blue, to_red):
    side = device_side()
    inner = value_ref.shape[0] - HALO
    off = pl.multiple_of(side * inner, 128)
    to_blue[...] = value_ref[pl.ds(off, HALO), :].astype(BF)
    to_red[...] = value_ref[pl.ds(pl.multiple_of(inner - off, 128), HALO), :].astype(BF)


def first_kernel(band, t0, blue, red, t1, to_blue, to_red, wide):
    fill_wide(t0[...], blue[...].astype(F32), red[...].astype(F32), wide)
    height = PAIR_ATOMS * ORB
    for pair in range(band.shape[0]):
        t1[pair * height : (pair + 1) * height, :] = apply_band(band, wide, pair)
    put_sends(t1, to_blue, to_red)


def next_kernel(band, before, now, blue, red, after, to_blue, to_red, wide):
    fill_wide(now[...], blue[...].astype(F32), red[...].astype(F32), wide)
    height = PAIR_ATOMS * ORB
    for pair in range(band.shape[0]):
        span = slice(pair * height, (pair + 1) * height)
        after[span, :] = 2.0 * apply_band(band, wide, pair) - before[span, :]
    put_sends(after, to_blue, to_red)


def last_kernel(coef, band, t0, t1, t2, t3, blue, red, p0, p1, p2, p3, wide, out):
    member = lax.axis_index("edges")
    fill_wide(t3[...], blue[...].astype(F32), red[...].astype(F32), wide)
    height = PAIR_ATOMS * ORB
    for pair in range(band.shape[0]):
        span = slice(pair * height, (pair + 1) * height)
        t4 = 2.0 * apply_band(band, wide, pair) - t2[span, :]
        total = coef[0] * t0[span, :] + coef[1] * t1[span, :] + coef[2] * t2[span, :]
        total = total + coef[3] * t3[span, :] + coef[4] * t4
        out[:, span] = total.T
    for k, piece in enumerate((p0, p1, p2, p3)):
        high = piece.shape[0]
        piece[...] = out[pl.ds(pl.multiple_of((member ^ k) * high, high), high), :].astype(BF)


def join_kernel(p0, p1, p2, p3, out):
    member = lax.axis_index("edges")
    for k, piece in enumerate((p0, p1, p2, p3)):
        width = piece.shape[1]
        at = pl.multiple_of((member ^ k) * width, width)
        out[:, pl.ds(at, width)] = piece[...].astype(F32)


VMEM = pl.BlockSpec(memory_space=pltpu.VMEM)
SMEM = pl.BlockSpec(memory_space=pltpu.SMEM)
ANYWHERE = pl.BlockSpec(memory_space=pl.ANY)
PARAMS = pltpu.CompilerParams(vmem_limit_bytes=40 * 1024 * 1024)


def shape(dims, dtype):
    return jax.ShapeDtypeStruct(dims, dtype)


def call(kernel, name, outs, scratch, *args, smem=(), anywhere=()):
    spaces = [SMEM if k in smem else ANYWHERE if k in anywhere else VMEM for k in range(len(args))]
    return pl.pallas_call(
        kernel,
        name=name,
        out_shape=outs,
        in_specs=spaces,
        out_specs=(VMEM,) * len(outs),
        scratch_shapes=scratch,
        compiler_params=PARAMS,
    )(*args)


def per_device(features, edge_src, edge_dst, edge_cell, cell_bias, w_in, w_out, vectors, cheb_coef):
    axes = ("rows", "edges")
    nedge = lax.axis_size("edges")
    ndev = lax.axis_size("rows") * nedge
    red_pairs = [(i, i ^ 1) for i in range(ndev)]
    blue_pairs = [(i, (i + 1) % ndev if i % 2 else (i - 1) % ndev) for i in range(ndev)]
    nown, nfeat = features.shape
    high, ncol = vectors.shape
    nrow = ncol // nedge

    def swap(first, last):
        return (
            lax.ppermute(first, axes, blue_pairs),
            lax.ppermute(last, axes, red_pairs),
        )

    def exchange(pieces):
        return [pieces[0]] + [
            lax.ppermute(pieces[k], "edges", [(i, i ^ k) for i in range(nedge)]) for k in (1, 2, 3)
        ]

    msg = shape((SPILL + ID_ROWS, nfeat), BF)
    piece = shape((high, nrow), BF)
    lines = (nown // 128, 128)
    blue_msg, red_msg, ids, *pieces = call(
        prep_kernel,
        "prep",
        (msg, msg, shape((3,) + lines, F32)) + (piece,) * 4,
        [pltpu.SemaphoreType.DMA((2,))],
        features,
        edge_src.reshape(lines),
        edge_dst.reshape(lines),
        edge_cell.reshape(lines),
        vectors,
        anywhere=(0,),
    )
    blue_msg, red_msg = swap(blue_msg, red_msg)
    pieces = exchange(pieces)
    full, part = shape((nrow, VEC), F32), shape((HALO, VEC), BF)
    t0, to_blue, to_red = call(
        field_kernel, "field", (full, part, part), [pltpu.VMEM((VEC, nrow), F32)], *pieces
    )
    blue, red = swap(to_blue, to_red)

    spill_len = 2 * (SPILL + 64)
    (band,) = call(
        band_kernel,
        "band",
        (shape((ATOM_Q // PAIR_ATOMS, PAIR_ATOMS * ORB, WIN_ATOMS * ORB), BF),),
        [
            pltpu.VMEM((ORB * ORB, nown + spill_len), BF),
            pltpu.VMEM((8, 2 * HID), F32),
            pltpu.VMEM((spill_len, nfeat), BF),
        ],
        features,
        ids,
        blue_msg,
        red_msg,
        cell_bias,
        w_in,
        w_out,
    )

    wide = pltpu.VMEM((nrow + 2 * HALO, VEC), F32)
    t1, to_blue, to_red = call(first_kernel, "first", (full, part, part), [wide], band, t0, blue, red)
    fields = [t0, t1]
    for _ in range(2, STEPS):
        blue, red = swap(to_blue, to_red)
        following, to_blue, to_red = call(
            next_kernel, "next", (full, part, part), [wide], band, fields[-2], fields[-1], blue, red
        )
        fields.append(following)
    blue, red = swap(to_blue, to_red)
    pieces = call(
        last_kernel,
        "last",
        (piece,) * 4,
        [wide, pltpu.VMEM((VEC, nrow), F32)],
        cheb_coef,
        band,
        *fields,
        blue,
        red,
        smem=(0,),
    )
    (result,) = call(join_kernel, "join", (shape((high, ncol), F32),), [], *exchange(pieces))
    return result


def solution(mesh):
    placed = (
        P(("rows", "edges"), None),
        P(("rows", "edges")),
        P(("rows", "edges")),
        P(("rows", "edges")),
        P(),
        P(),
        P(),
        P("edges", "rows"),
        P(),
    )
    return jax.shard_map(
        per_device, mesh=mesh, in_specs=placed, out_specs=P("edges", "rows"), check_vma=False
    )
```

time: 58 us -> 57.9 us (level)
  waiting for transfers between devices: 8.72 us -> 23.5 us
  starting transfers between devices: 27.9 us -> 18.7 us
  blocking collectives: 7.02 us -> 0 us
  Pallas kernels: 9.56 us -> 11.1 us
  other arithmetic: 1.29 us -> 0 us
  local copies, waits for them, and re-layouts: 2.93 us -> 4.15 us
    ppermute x10 -> x16, waiting for transfers between devices: 8.72 us -> 23.5 us  [the longest x5 18.6 us: swap(): lax.ppermute(first, axes, blue_pairs)]
    all_to_all x1 -> x0, blocking collectives: 7.02 us -> none  [per_device(): lax.all_to_all(result, 'edges', split_axis=0, concat_axis=1, tiled=True)]
    ppermute x10 -> x16, starting transfers between devices: 23.7 us -> 18.7 us  [the longest x5 14.9 us: swap(): lax.ppermute(first, axes, blue_pairs)]
    all_to_all x1 -> x0, starting transfers between devices: 4.21 us -> none  [per_device(): lax.all_to_all(vectors.astype(BF), 'edges', split_axis=1, concat_axis=0,...]
    unnamed x18 -> x20, local copies, waits for them, and re-layouts: 1.4 us -> 4.15 us
    pallas_call x5 -> x8, Pallas kernels: 9.56 us -> 11.1 us  [call(): pl.pallas_call(kernel, name=name, out_shape=outs, in_specs=spaces, out_sp...]
    convert_element_type x2 -> x0, other arithmetic: 1.05 us -> none  [the longest x1 1.03 us: per_device(): vectors.astype(BF)]
    convert_element_type x1 -> x0, local copies, waits for them, and re-layouts: 0.72 us -> none  [per_device(): return result.astype(F32)]
  transfers between devices with their start and end apart: 11 -> 16, of which waited for: 4 -> 5; matrix products, arithmetic and copies ran while one was open for 1% -> 0% of each run, Pallas kernels for 11% -> 11%
where the time goes in v2:
time: 57.9 us; the launch traced here: 57.6 us
  waiting for transfers between devices  23.5 us (41%)
  starting transfers between devices  18.7 us (32%)
  Pallas kernels  11.1 us (19%)
  local copies, waits for them, and re-layouts  4.15 us (7%)
    ppermute x5, waiting for transfers between devices, swap(): lax.ppermute(first, axes, blue_pairs)  18.6 us
    ppermute x5, starting transfers between devices, swap(): lax.ppermute(first, axes, blue_pairs)  14.9 us
    pallas_call x8, Pallas kernels, call(): pl.pallas_call(kernel, name=name, out_shape=outs, in_specs=spaces, out_sp...  11.1 us
    ppermute x6, waiting for transfers between devices, exchange(): lax.ppermute(pieces[k], 'edges', [(i, i ^ k) for i in range(nedge)])  4.86 us
    unnamed x20, local copies, waits for them, and re-layouts  4.15 us
    ppermute x6, starting transfers between devices, exchange(): lax.ppermute(pieces[k], 'edges', [(i, i ^ k) for i in range(nedge)])  3.79 us
  transfers between devices with their start and end apart: 16, of which 5 were waited for; matrix products, arithmetic and copies ran while one was open for 0% of the time, Pallas kernels for 11%

profile of v2, /device:TPU:0, one launch (start us, length us, event | category | flops | bytes accessed | tf_op | source)
XLA Modules:
  0.0 57.6 jit_solution(9069813639693320482)
XLA Ops:
  0.0 1.1 %copy-done = bf16[1280,256]{1,0:T(8,128)(2,1)S(1)} copy-done((bf16[1280,256]{1,0:T(8,128)(2,1)S(1)}, bf16[1280,256]{1,0:T(8,128)(2,1)}, u32[]{:S(2)}) %copy-start) | copy-done | bytes 655384
  1.1 0.9 %copy-done.2 = f32[32,2048]{1,0:T(8,128)S(1)} copy-done((f32[32,2048]{1,0:T(8,128)S(1)}, f32[32,2048]{1,0:T(8,128)}, u32[]{:S(2)}) %copy-start.2) | copy-done | bytes 262168
  2.0 0.7 %copy-done.5 = s32[1280]{0:T(1024)S(1)} copy-done((s32[1280]{0:T(1024)S(1)}, s32[1280]{0:T(1024)}, u32[]{:S(2)}) %copy-start.5) | copy-done | bytes 5144
  2.7 0.7 %copy-done.6 = s32[1280]{0:T(1024)S(1)} copy-done((s32[1280]{0:T(1024)S(1)}, s32[1280]{0:T(1024)}, u32[]{:S(2)}) %copy-start.6) | copy-done | bytes 5144
  3.4 0.7 %copy-done.7 = s32[1280]{0:T(1024)S(1)} copy-done((s32[1280]{0:T(1024)S(1)}, s32[1280]{0:T(1024)}, u32[]{:S(2)}) %copy-start.7) | copy-done | bytes 5144
  4.1 0.4 prep.1
  4.6 0.0 copy-start.4
  4.6 6.4 %collective-permute-start = (bf16[336,256]{1,0:T(8,128)(2,1)S(1)}, bf16[336,256]{1,0:T(8,128)(2,1)S(1)}, u32[]{:S(2)}, u32[]{:S(2)}) collective-permute-start(bf16[336,256]{1,0:T(8,128)(2,1)S(1)} %get-tuple-element.29), channel_id=1, source_target_pairs={{0,31},{1,2},{2,1},{3,4},{4,3},{5,6},{6,5},{7,8},{8,7},{9,10},{10,... | collective-permute-start | bytes 516104 | tf_op jit(solution)/shard_map/ppermute | solution.py:281
  11.0 0.0 collective-permute-start.1
  11.0 0.5 collective-permute-start.2
  11.6 0.0 collective-permute-start.3
  11.6 1.4 %collective-permute-start.4 = (bf16[32,512]{1,0:T(8,128)(2,1)S(1)}, bf16[32,512]{1,0:T(8,128)(2,1)S(1)}, u32[]{:S(2)}, u32[]{:S(2)}) collective-permute-start(bf16[32,512]{1,0:T(8,128)(2,1)S(1)} %get-tuple-element.34), channel_id=1, source_target_pairs={{0,3},{1,2},{2,1},{3,0},{4,7},{5,6},{6,5},{7,4},{8,11},{9,10},{10,... | collective-permute-start | bytes 98312 | tf_op jit(solution)/shard_map/ppermute | solution.py:287
  12.9 0.0 collective-permute-done.2.p1
  12.9 2.6 %collective-permute-done.3.p2 = bf16[32,512]{1,0:T(8,128)(2,1)S(1)} collective-permute-done((bf16[32,512]{1,0:T(8,128)(2,1)S(1)}, bf16[32,512]{1,0:T(8,128)(2,1)S(1)}, u32[]{:S(2)}, u32[]{:S(2)}) %collective-permute-start.3) | collective-permute-done | bytes 32800 | tf_op jit(solution)/shard_map/ppermute | solution.py:287
  15.5 0.0 collective-permute-done.4.p3
  15.5 0.2 field.1
  15.7 0.0 copy-start.8
  15.7 3.9 %collective-permute-start.5 = (bf16[384,128]{1,0:T(8,128)(2,1)S(1)}, bf16[384,128]{1,0:T(8,128)(2,1)S(1)}, u32[]{:S(2)}, u32[]{:S(2)}) collective-permute-start(bf16[384,128]{1,0:T(8,128)(2,1)S(1)} %get-tuple-element.36), channel_id=1, source_target_pairs={{0,31},{1,2},{2,1},{3,4},{4,3},{5,6},{6,5},{7,8},{8,7},{9,10},{10,... | collective-permute-start | bytes 294920 | tf_op jit(solution)/shard_map/ppermute | solution.py:281
  19.6 0.0 collective-permute-start.6
  19.6 0.0 collective-permute-done.blue
  19.6 0.0 collective-permute-done.1.red
  19.6 0.0 copy-done.1
  19.6 6.4 %band.1 = bf16[2,256,1024]{2,1,0:T(8,128)(2,1)S(1)} custom-call(bf16[1280,256]{1,0:T(8,128)(2,1)S(1)} %copy-done.1, f32[3,10,128]{2,1,0:T(8,128)S(1)} %get-tuple-element.28.ids, bf16[336,256]{1,0:T(8,128)(2,1)S(1)} %collective-permute-done.blue, bf16[336,256]{1,0:T(8,128)(2,1)S(1)} %collective-permute-done.1.red, bf16[3,512]{1,0:T(4,128)(2,1)S(1)} %copy-done.8, ...), custom_call_target="tpu_custom_call" | custom-call | tf_op jit(solution)/shard_map/band/pallas_call | solution.py:258
  26.0 0.0 collective-permute-done.5.blue
  26.1 0.0 collective-permute-done.6.red
  26.1 0.7 %first.1 = (f32[512,128]{1,0:T(8,128)S(1)}, bf16[384,128]{1,0:T(8,128)(2,1)S(1)}, bf16[384,128]{1,0:T(8,128)(2,1)S(1)}) custom-call(bf16[2,256,1024]{2,1,0:T(8,128)(2,1)S(1)} %band.1, f32[512,128]{1,0:T(8,128)S(1)} %get-tuple-element.35.t0.before, bf16[384,128]{1,0:T(8,128)(2,1)S(1)} %collective-permute-done.5.blue, ...), custom_call_target="tpu_custom_call" | custom-call | tf_op jit(solution)/shard_map/first/pallas_call | solution.py:258
  26.8 1.6 %collective-permute-start.7 = (bf16[384,128]{1,0:T(8,128)(2,1)S(1)}, bf16[384,128]{1,0:T(8,128)(2,1)S(1)}, u32[]{:S(2)}, u32[]{:S(2)}) collective-permute-start(bf16[384,128]{1,0:T(8,128)(2,1)S(1)} %get-tuple-element.39), channel_id=1, source_target_pairs={{0,31},{1,2},{2,1},{3,4},{4,3},{5,6},{6,5},{7,8},{8,7},{9,10},{10,... | collective-permute-start | bytes 294920 | tf_op jit(solution)/shard_map/ppermute | solution.py:281
  28.3 0.0 collective-permute-start.8
  28.3 6.2 %collective-permute-done.7.blue = bf16[384,128]{1,0:T(8,128)(2,1)S(1)} collective-permute-done((bf16[384,128]{1,0:T(8,128)(2,1)S(1)}, bf16[384,128]{1,0:T(8,128)(2,1)S(1)}, u32[]{:S(2)}, u32[]{:S(2)}) %collective-permute-start.7) | collective-permute-done | bytes 98336 | tf_op jit(solution)/shard_map/ppermute | solution.py:281
  34.5 0.0 collective-permute-done.8.red
  34.5 0.7 %next.2 = (f32[512,128]{1,0:T(8,128)S(1)}, bf16[384,128]{1,0:T(8,128)(2,1)S(1)}, bf16[384,128]{1,0:T(8,128)(2,1)S(1)}) custom-call(bf16[2,256,1024]{2,1,0:T(8,128)(2,1)S(1)} %band.1, f32[512,128]{1,0:T(8,128)S(1)} %get-tuple-element.35.t0.before, f32[512,128]{1,0:T(8,128)S(1)} %get-tuple-element.38.now.before.t1, ...), custom_call_target="tpu_custom_call" | custom-call | tf_op jit(solution)/shard_map/next/pallas_call | solution.py:258
  35.2 1.5 %collective-permute-start.9 = (bf16[384,128]{1,0:T(8,128)(2,1)S(1)}, bf16[384,128]{1,0:T(8,128)(2,1)S(1)}, u32[]{:S(2)}, u32[]{:S(2)}) collective-permute-start(bf16[384,128]{1,0:T(8,128)(2,1)S(1)} %get-tuple-element.42), channel_id=1, source_target_pairs={{0,31},{1,2},{2,1},{3,4},{4,3},{5,6},{6,5},{7,8},{8,7},{9,10},{10,... | collective-permute-start | bytes 294920 | tf_op jit(solution)/shard_map/ppermute | solution.py:281
  36.7 0.0 collective-permute-start.10
  36.7 6.2 %collective-permute-done.9.blue = bf16[384,128]{1,0:T(8,128)(2,1)S(1)} collective-permute-done((bf16[384,128]{1,0:T(8,128)(2,1)S(1)}, bf16[384,128]{1,0:T(8,128)(2,1)S(1)}, u32[]{:S(2)}, u32[]{:S(2)}) %collective-permute-start.9) | collective-permute-done | bytes 98336 | tf_op jit(solution)/shard_map/ppermute | solution.py:281
  42.9 0.0 collective-permute-done.10.red
  42.9 0.7 %next.3 = (f32[512,128]{1,0:T(8,128)S(1)}, bf16[384,128]{1,0:T(8,128)(2,1)S(1)}, bf16[384,128]{1,0:T(8,128)(2,1)S(1)}) custom-call(bf16[2,256,1024]{2,1,0:T(8,128)(2,1)S(1)} %band.1, f32[512,128]{1,0:T(8,128)S(1)} %get-tuple-element.38.now.before.t1, f32[512,128]{1,0:T(8,128)S(1)} %get-tuple-element.41.now.t2, ...), custom_call_target="tpu_custom_call" | custom-call | tf_op jit(solution)/shard_map/next/pallas_call | solution.py:258
  43.6 1.5 %collective-permute-start.11 = (bf16[384,128]{1,0:T(8,128)(2,1)S(1)}, bf16[384,128]{1,0:T(8,128)(2,1)S(1)}, u32[]{:S(2)}, u32[]{:S(2)}) collective-permute-start(bf16[384,128]{1,0:T(8,128)(2,1)S(1)} %get-tuple-element.45), channel_id=1, source_target_pairs={{0,31},{1,2},{2,1},{3,4},{4,3},{5,6},{6,5},{7,8},{8,7},{9,10},{10,... | collective-permute-start | bytes 294920 | tf_op jit(solution)/shard_map/ppermute | solution.py:281
  45.1 0.0 collective-permute-start.12
  45.1 6.2 %collective-permute-done.11.blue = bf16[384,128]{1,0:T(8,128)(2,1)S(1)} collective-permute-done((bf16[384,128]{1,0:T(8,128)(2,1)S(1)}, bf16[384,128]{1,0:T(8,128)(2,1)S(1)}, u32[]{:S(2)}, u32[]{:S(2)}) %collective-permute-start.11) | collective-permute-done | bytes 98336 | tf_op jit(solution)/shard_map/ppermute | solution.py:281
  51.3 0.0 collective-permute-done.12.red
  51.3 1.3 %last.1 = (bf16[32,512]{1,0:T(8,128)(2,1)S(1)}, bf16[32,512]{1,0:T(8,128)(2,1)S(1)}, bf16[32,512]{1,0:T(8,128)(2,1)S(1)}, bf16[32,512]{1,0:T(8,128)(2,1)S(1)}) custom-call(f32[5]{0:T(128)S(1)} %copy-done.9, bf16[2,256,1024]{2,1,0:T(8,128)(2,1)S(1)} %band.1, f32[512,128]{1,0:T(8,128)S(1)} %get-tuple-element.35.t0.before, ...), custom_call_target="tpu_custom_call" | custom-call | tf_op jit(solution)/shard_map/last/pallas_call | solution.py:258
  52.6 0.1 collective-permute-start.13
  52.7 0.1 collective-permute-start.14
  52.8 1.8 %collective-permute-start.15 = (bf16[32,512]{1,0:T(8,128)(2,1)S(1)}, bf16[32,512]{1,0:T(8,128)(2,1)S(1)}, u32[]{:S(2)}, u32[]{:S(2)}) collective-permute-start(bf16[32,512]{1,0:T(8,128)(2,1)S(1)} %get-tuple-element.50), channel_id=1, source_target_pairs={{0,3},{1,2},{2,1},{3,0},{4,7},{5,6},{6,5},{7,4},{8,11},{9,10},{10,... | collective-permute-start | bytes 98312 | tf_op jit(solution)/shard_map/ppermute | solution.py:287
  54.6 0.0 collective-permute-done.13.p1
  54.6 2.3 %collective-permute-done.14.p2 = bf16[32,512]{1,0:T(8,128)(2,1)S(1)} collective-permute-done((bf16[32,512]{1,0:T(8,128)(2,1)S(1)}, bf16[32,512]{1,0:T(8,128)(2,1)S(1)}, u32[]{:S(2)}, u32[]{:S(2)}) %collective-permute-start.14) | collective-permute-done | bytes 32800 | tf_op jit(solution)/shard_map/ppermute | solution.py:287
  56.9 0.0 collective-permute-done.15.p3
  56.9 0.7 %join.1 = f32[32,2048]{1,0:T(8,128)} custom-call(bf16[32,512]{1,0:T(8,128)(2,1)S(1)} %get-tuple-element.47.p0, bf16[32,512]{1,0:T(8,128)(2,1)S(1)} %collective-permute-done.13.p1, bf16[32,512]{1,0:T(8,128)(2,1)S(1)} %collective-permute-done.14.p2, bf16[32,512]{1,0:T(8,128)(2,1)S(1)} %collective-permute-done.15.p3), custom_call_target="tpu_custom_call" | custom-call | tf_op jit(solution)/shard_map/join/pallas_call | solution.py:258
  (12 shorter events, 0.0 us)
Async XLA Ops:
  0.0 1.1 %copy-start = (bf16[1280,256]{1,0:T(8,128)(2,1)S(1)}, bf16[1280,256]{1,0:T(8,128)(2,1)}, u32[]{:S(2)}) copy-start(bf16[1280,256]{1,0:T(8,128)(2,1)} %feat.3) | copy-start | bytes 1966084
  1.1 0.9 %copy-start.2 = (f32[32,2048]{1,0:T(8,128)S(1)}, f32[32,2048]{1,0:T(8,128)}, u32[]{:S(2)}) copy-start(f32[32,2048]{1,0:T(8,128)} %vectors.1) | copy-start | bytes 786436
  2.0 0.7 %copy-start.5 = (s32[1280]{0:T(1024)S(1)}, s32[1280]{0:T(1024)}, u32[]{:S(2)}) copy-start(s32[1280]{0:T(1024)} %param.10) | copy-start | bytes 15364
  2.7 0.7 %copy-start.6 = (s32[1280]{0:T(1024)S(1)}, s32[1280]{0:T(1024)}, u32[]{:S(2)}) copy-start(s32[1280]{0:T(1024)} %param.11) | copy-start | bytes 15364
  3.4 0.7 %copy-start.7 = (s32[1280]{0:T(1024)S(1)}, s32[1280]{0:T(1024)}, u32[]{:S(2)}) copy-start(s32[1280]{0:T(1024)} %param.12) | copy-start | bytes 15364
  4.1 15.5 %copy-start.1 = (bf16[1280,256]{1,0:T(8,128)(2,1)S(1)}, bf16[1280,256]{1,0:T(8,128)(2,1)}, u32[]{:S(2)}) copy-start(bf16[1280,256]{1,0:T(8,128)(2,1)} %feat.3) | copy-start | bytes 1966084
  4.1 15.5 %copy-start.3 = (bf16[256,512]{1,0:T(8,128)(2,1)S(1)}, bf16[256,512]{1,0:T(8,128)(2,1)}, u32[]{:S(2)}) copy-start(bf16[256,512]{1,0:T(8,128)(2,1)} %w_in.1) | copy-start | bytes 786436
  4.6 15.0 %copy-start.4 = (bf16[256,256]{1,0:T(8,128)(2,1)S(1)}, bf16[256,256]{1,0:T(8,128)(2,1)}, u32[]{:S(2)}) copy-start(bf16[256,256]{1,0:T(8,128)(2,1)} %w_out.1) | copy-start | bytes 393220
  4.6 15.0 %collective-permute-start = (bf16[336,256]{1,0:T(8,128)(2,1)S(1)}, bf16[336,256]{1,0:T(8,128)(2,1)S(1)}, u32[]{:S(2)}, u32[]{:S(2)}) collective-permute-start(bf16[336,256]{1,0:T(8,128)(2,1)S(1)} %get-tuple-element.29), channel_id=1, source_target_pairs={{0,31},{1,2},{2,1},{3,4},{4,3},{5,6},{6,5},{7,8},{8,7},{9,10},{10,... | collective-permute-start | bytes 516104 | tf_op jit(solution)/shard_map/ppermute | solution.py:281
  11.0 8.6 %collective-permute-start.1 = (bf16[336,256]{1,0:T(8,128)(2,1)S(1)}, bf16[336,256]{1,0:T(8,128)(2,1)S(1)}, u32[]{:S(2)}, u32[]{:S(2)}) collective-permute-start(bf16[336,256]{1,0:T(8,128)(2,1)S(1)} %get-tuple-element.30), channel_id=1, source_target_pairs={{0,1},{1,0},{2,3},{3,2},{4,5},{5,4},{6,7},{7,6},{8,9},{9,8},{10,11... | collective-permute-start | bytes 516104 | tf_op jit(solution)/shard_map/ppermute | solution.py:282
  11.0 1.9 %collective-permute-start.2 = (bf16[32,512]{1,0:T(8,128)(2,1)S(1)}, bf16[32,512]{1,0:T(8,128)(2,1)S(1)}, u32[]{:S(2)}, u32[]{:S(2)}) collective-permute-start(bf16[32,512]{1,0:T(8,128)(2,1)S(1)} %get-tuple-element.32), channel_id=1, source_target_pairs={{0,1},{1,0},{2,3},{3,2},{4,5},{5,4},{6,7},{7,6},{8,9},{9,8},{10,11... | collective-permute-start | bytes 98312 | tf_op jit(solution)/shard_map/ppermute | solution.py:287
  11.6 3.9 %collective-permute-start.3 = (bf16[32,512]{1,0:T(8,128)(2,1)S(1)}, bf16[32,512]{1,0:T(8,128)(2,1)S(1)}, u32[]{:S(2)}, u32[]{:S(2)}) collective-permute-start(bf16[32,512]{1,0:T(8,128)(2,1)S(1)} %get-tuple-element.33), channel_id=1, source_target_pairs={{0,2},{1,3},{2,0},{3,1},{4,6},{5,7},{6,4},{7,5},{8,10},{9,11},{10,... | collective-permute-start | bytes 98312 | tf_op jit(solution)/shard_map/ppermute | solution.py:287
  11.6 3.9 %collective-permute-start.4 = (bf16[32,512]{1,0:T(8,128)(2,1)S(1)}, bf16[32,512]{1,0:T(8,128)(2,1)S(1)}, u32[]{:S(2)}, u32[]{:S(2)}) collective-permute-start(bf16[32,512]{1,0:T(8,128)(2,1)S(1)} %get-tuple-element.34), channel_id=1, source_target_pairs={{0,3},{1,2},{2,1},{3,0},{4,7},{5,6},{6,5},{7,4},{8,11},{9,10},{10,... | collective-permute-start | bytes 98312 | tf_op jit(solution)/shard_map/ppermute | solution.py:287
  15.7 4.0 %copy-start.8 = (bf16[3,512]{1,0:T(4,128)(2,1)S(1)}, bf16[3,512]{1,0:T(4,128)(2,1)}, u32[]{:S(2)}) copy-start(bf16[3,512]{1,0:T(4,128)(2,1)} %cell_bias.1) | copy-start | bytes 9220
  15.7 10.4 %collective-permute-start.5 = (bf16[384,128]{1,0:T(8,128)(2,1)S(1)}, bf16[384,128]{1,0:T(8,128)(2,1)S(1)}, u32[]{:S(2)}, u32[]{:S(2)}) collective-permute-start(bf16[384,128]{1,0:T(8,128)(2,1)S(1)} %get-tuple-element.36), channel_id=1, source_target_pairs={{0,31},{1,2},{2,1},{3,4},{4,3},{5,6},{6,5},{7,8},{8,7},{9,10},{10,... | collective-permute-start | bytes 294920 | tf_op jit(solution)/shard_map/ppermute | solution.py:281
  19.6 6.5 %collective-permute-start.6 = (bf16[384,128]{1,0:T(8,128)(2,1)S(1)}, bf16[384,128]{1,0:T(8,128)(2,1)S(1)}, u32[]{:S(2)}, u32[]{:S(2)}) collective-permute-start(bf16[384,128]{1,0:T(8,128)(2,1)S(1)} %get-tuple-element.37), channel_id=1, source_target_pairs={{0,1},{1,0},{2,3},{3,2},{4,5},{5,4},{6,7},{7,6},{8,9},{9,8},{10,11... | collective-permute-start | bytes 294920 | tf_op jit(solution)/shard_map/ppermute | solution.py:282
  26.8 7.8 %collective-permute-start.7 = (bf16[384,128]{1,0:T(8,128)(2,1)S(1)}, bf16[384,128]{1,0:T(8,128)(2,1)S(1)}, u32[]{:S(2)}, u32[]{:S(2)}) collective-permute-start(bf16[384,128]{1,0:T(8,128)(2,1)S(1)} %get-tuple-element.39), channel_id=1, source_target_pairs={{0,31},{1,2},{2,1},{3,4},{4,3},{5,6},{6,5},{7,8},{8,7},{9,10},{10,... | collective-permute-start | bytes 294920 | tf_op jit(solution)/shard_map/ppermute | solution.py:281
  28.3 6.2 %collective-permute-start.8 = (bf16[384,128]{1,0:T(8,128)(2,1)S(1)}, bf16[384,128]{1,0:T(8,128)(2,1)S(1)}, u32[]{:S(2)}, u32[]{:S(2)}) collective-permute-start(bf16[384,128]{1,0:T(8,128)(2,1)S(1)} %get-tuple-element.40), channel_id=1, source_target_pairs={{0,1},{1,0},{2,3},{3,2},{4,5},{5,4},{6,7},{7,6},{8,9},{9,8},{10,11... | collective-permute-start | bytes 294920 | tf_op jit(solution)/shard_map/ppermute | solution.py:282
  35.2 7.7 %collective-permute-start.9 = (bf16[384,128]{1,0:T(8,128)(2,1)S(1)}, bf16[384,128]{1,0:T(8,128)(2,1)S(1)}, u32[]{:S(2)}, u32[]{:S(2)}) collective-permute-start(bf16[384,128]{1,0:T(8,128)(2,1)S(1)} %get-tuple-element.42), channel_id=1, source_target_pairs={{0,31},{1,2},{2,1},{3,4},{4,3},{5,6},{6,5},{7,8},{8,7},{9,10},{10,... | collective-permute-start | bytes 294920 | tf_op jit(solution)/shard_map/ppermute | solution.py:281
  36.7 6.2 %collective-permute-start.10 = (bf16[384,128]{1,0:T(8,128)(2,1)S(1)}, bf16[384,128]{1,0:T(8,128)(2,1)S(1)}, u32[]{:S(2)}, u32[]{:S(2)}) collective-permute-start(bf16[384,128]{1,0:T(8,128)(2,1)S(1)} %get-tuple-element.43), channel_id=1, source_target_pairs={{0,1},{1,0},{2,3},{3,2},{4,5},{5,4},{6,7},{7,6},{8,9},{9,8},{10,11... | collective-permute-start | bytes 294920 | tf_op jit(solution)/shard_map/ppermute | solution.py:282
  43.6 7.7 %collective-permute-start.11 = (bf16[384,128]{1,0:T(8,128)(2,1)S(1)}, bf16[384,128]{1,0:T(8,128)(2,1)S(1)}, u32[]{:S(2)}, u32[]{:S(2)}) collective-permute-start(bf16[384,128]{1,0:T(8,128)(2,1)S(1)} %get-tuple-element.45), channel_id=1, source_target_pairs={{0,31},{1,2},{2,1},{3,4},{4,3},{5,6},{6,5},{7,8},{8,7},{9,10},{10,... | collective-permute-start | bytes 294920 | tf_op jit(solution)/shard_map/ppermute | solution.py:281
  45.1 6.2 %copy-start.9 = (f32[5]{0:T(128)S(1)}, f32[5]{0:T(128)}, u32[]{:S(2)}) copy-start(f32[5]{0:T(128)} %coef.1) | copy-start | bytes 64
  45.1 6.2 %collective-permute-start.12 = (bf16[384,128]{1,0:T(8,128)(2,1)S(1)}, bf16[384,128]{1,0:T(8,128)(2,1)S(1)}, u32[]{:S(2)}, u32[]{:S(2)}) collective-permute-start(bf16[384,128]{1,0:T(8,128)(2,1)S(1)} %get-tuple-element.46), channel_id=1, source_target_pairs={{0,1},{1,0},{2,3},{3,2},{4,5},{5,4},{6,7},{7,6},{8,9},{9,8},{10,11... | collective-permute-start | bytes 294920 | tf_op jit(solution)/shard_map/ppermute | solution.py:282
  52.6 1.9 %collective-permute-start.13 = (bf16[32,512]{1,0:T(8,128)(2,1)S(1)}, bf16[32,512]{1,0:T(8,128)(2,1)S(1)}, u32[]{:S(2)}, u32[]{:S(2)}) collective-permute-start(bf16[32,512]{1,0:T(8,128)(2,1)S(1)} %get-tuple-element.48), channel_id=1, source_target_pairs={{0,1},{1,0},{2,3},{3,2},{4,5},{5,4},{6,7},{7,6},{8,9},{9,8},{10,11... | collective-permute-start | bytes 98312 | tf_op jit(solution)/shard_map/ppermute | solution.py:287
  52.7 4.2 %collective-permute-start.14 = (bf16[32,512]{1,0:T(8,128)(2,1)S(1)}, bf16[32,512]{1,0:T(8,128)(2,1)S(1)}, u32[]{:S(2)}, u32[]{:S(2)}) collective-permute-start(bf16[32,512]{1,0:T(8,128)(2,1)S(1)} %get-tuple-element.49), channel_id=1, source_target_pairs={{0,2},{1,3},{2,0},{3,1},{4,6},{5,7},{6,4},{7,5},{8,10},{9,11},{10,... | collective-permute-start | bytes 98312 | tf_op jit(solution)/shard_map/ppermute | solution.py:287
  52.8 4.1 %collective-permute-start.15 = (bf16[32,512]{1,0:T(8,128)(2,1)S(1)}, bf16[32,512]{1,0:T(8,128)(2,1)S(1)}, u32[]{:S(2)}, u32[]{:S(2)}) collective-permute-start(bf16[32,512]{1,0:T(8,128)(2,1)S(1)} %get-tuple-element.50), channel_id=1, source_target_pairs={{0,3},{1,2},{2,1},{3,0},{4,7},{5,6},{6,5},{7,4},{8,11},{9,10},{10,... | collective-permute-start | bytes 98312 | tf_op jit(solution)/shard_map/ppermute | solution.py:287

commit v3 on v2

--- a/solution.py
+++ b/solution.py
@@ -19,6 +19,8 @@
 PAIR_ATOMS = 2 * TILE_ATOMS
 WIN_ATOMS = (2 * BAND + 2) * TILE_ATOMS
 HALO = BAND * TILE_ATOMS * ORB
+GROUP = 4
+GROUP_SPAN = 384
 BF = jnp.bfloat16
 F32 = jnp.float32
 NT = (((1,), (1,)), ((), ()))
@@ -36,10 +38,20 @@
     return (lax.axis_index("rows") * lax.axis_size("edges") + lax.axis_index("edges")) % 2
 
 
-def prep_kernel(feat, src, dst, cell, vectors, blue, red, ids, p0, p1, p2, p3, sems):
+def split_kernel(vec_hbm, p0, p1, p2, p3, vectors, sem):
+    member = lax.axis_index("edges")
+    load = pltpu.make_async_copy(vec_hbm, vectors, sem)
+    load.start()
+    load.wait()
+    for k, piece in enumerate((p0, p1, p2, p3)):
+        width = piece.shape[1]
+        at = pl.multiple_of((member ^ k) * width, width)
+        piece[...] = vectors[:, pl.ds(at, width)].astype(BF)
+
+
+def message_kernel(feat, src_hbm, dst_hbm, cell_hbm, _, blue, red, ids, src, dst, cell, sems):
     ndev = lax.axis_size("rows") * lax.axis_size("edges")
-    member = lax.axis_index("edges")
-    quarter = lax.axis_index("rows") * lax.axis_size("edges") + member
+    quarter = lax.axis_index("rows") * lax.axis_size("edges") + lax.axis_index("edges")
     side = quarter % 2
     high = feat.shape[0] - SPILL
     off = pl.multiple_of(side * high, 64)
@@ -49,8 +61,14 @@
             feat.at[pl.ds(pl.multiple_of(high - off, 64), SPILL)], red.at[pl.ds(0, SPILL)], sems.at[1]
         ),
     ]
-    for copy in copies:
+    loads = [
+        pltpu.make_async_copy(x, y, sems.at[2 + n])
+        for n, (x, y) in enumerate(((src_hbm, src), (dst_hbm, dst), (cell_hbm, cell)))
+    ]
+    for copy in loads + copies:
         copy.start()
+    for copy in loads:
+        copy.wait()
     natom = ATOM_Q * ndev
     ntiles = natom // TILE_ATOMS
     rel = src[...] - quarter * ATOM_Q
@@ -76,10 +94,6 @@
     ):
         msg[SPILL : SPILL + ID_ROWS, 0:128] = ids_of.astype(BF)
         msg[SPILL : SPILL + ID_ROWS, 128:256] = none
-    for k, piece in enumerate((p0, p1, p2, p3)):
-        width = piece.shape[1]
-        at = pl.multiple_of((member ^ k) * width, width)
-        piece[...] = vectors[:, pl.ds(at, width)].astype(BF)
     for copy in copies:
         copy.wait()
 
@@ -93,28 +107,79 @@
     put_sends(t0, to_blue, to_red)
 
 
-def band_kernel(feat, ids, blue, red, cell_bias, w_in, w_out, band, blk, bias8, spill):
+def pair_blocks(x, cell, w_in_t, bias_t, w_out_t):
+    cell1 = (iota((8, x.shape[0]), 0).astype(F32) == cell).astype(BF)
+    pre = nt_dot(w_in_t, x) + jnp.dot(bias_t, cell1, preferred_element_type=F32)
+    gate, up = pre[:HID], pre[HID:]
+    hidden = (gate * (0.5 + 0.5 * jnp.tanh(0.5 * gate)) * up).astype(BF)
+    return jnp.dot(w_out_t, hidden, preferred_element_type=F32).astype(BF)
+
+
+def dense_of(blocks, atom, target, first):
+    span = atom.shape[1]
+    column = (iota((WIN_ATOMS, span), 0).astype(F32) == target).astype(BF)
+    onehot = [
+        jnp.broadcast_to((atom == float(s)).astype(F32), (WIN_ATOMS, span)).astype(BF) * column
+        for s in range(first, first + GROUP)
+    ]
+    return nt_dot(blocks, jnp.concatenate(onehot, axis=0))
+
+
+def put_dense(band, dense, first, add):
+    low = iota((ORB, 128), 1) < WIN_ATOMS
+    for sp in range(GROUP // 2):
+        s = first + 2 * sp
+        pair, at_row = s // PAIR_ATOMS, s % PAIR_ATOMS * ORB
+        for j in range(ORB // 2):
+            x = dense[2 * j * ORB : (2 * j + 1) * ORB, sp * 128 : sp * 128 + 128]
+            y = dense[(2 * j + 1) * ORB : (2 * j + 2) * ORB, sp * 128 : sp * 128 + 128]
+            lanes = slice(j * 128, j * 128 + 128)
+            both = (
+                jnp.where(low, x, pltpu.roll(y, WIN_ATOMS, 1)),
+                jnp.where(low, pltpu.roll(x, WIN_ATOMS, 1), y),
+            )
+            for n, value in enumerate(both):
+                rows = slice(at_row + n * ORB, at_row + (n + 1) * ORB)
+                if add:
+                    value = value + band[pair, rows, lanes].astype(F32)
+                band[pair, rows, lanes] = value.astype(BF)
+
+
+def odd_tile(atom):
+    return jnp.floor(atom * (1.0 / TILE_ATOMS)) - 2.0 * jnp.floor(atom * (0.5 / TILE_ATOMS))
+
+
+def own_kernel(feat, ids, cell_bias, w_in, w_out, band, w_in_t, bias_t, w_out_t, blk, bias8, rows):
     nfeat, width = w_in.shape
     nblk = w_out.shape[1]
     eye = (iota((width, width), 0) == iota((width, width), 1)).astype(BF)
-    w_in_t = nt_dot(eye, w_in[...]).astype(BF)
+    w_in_t[...] = nt_dot(eye, w_in[...]).astype(BF)
     bias8[...] = jnp.zeros(bias8.shape, F32)
     bias8[0:3, :] = cell_bias[...].astype(F32)
-    bias_t = nt_dot(eye, bias8[...].astype(BF)).astype(BF)
+    bias_t[...] = nt_dot(eye, bias8[...].astype(BF)).astype(BF)
     row, col = iota((nblk, nblk), 0), iota((nblk, nblk), 1)
     swap = (col == (row % ORB) * ORB + row // ORB).astype(BF)
-    w_out_t = nt_dot(swap, w_out[...]).astype(BF)
-
+    w_out_t[...] = nt_dot(swap, w_out[...]).astype(BF)
+    own = feat.shape[0]
+    for lo in range(0, own, 256):
+        span = slice(lo, lo + 256)
+        line = lo // 128
+        a, b, c = [
+            jnp.concatenate([ids[k, line : line + 1], ids[k, line + 1 : line + 2]], axis=1) for k in range(3)
+        ]
+        blk[:, span] = pair_blocks(feat[span, :], c, w_in_t[...], bias_t[...], w_out_t[...])
+        rows[0:1, span] = a
+        rows[1:2, span] = b + TILE_ATOMS * odd_tile(a)
+    for first in range(0, ATOM_Q, GROUP):
+        start = jnp.sum((ids[0] < float(first)).astype(F32)).astype(jnp.int32)
+        at = pl.multiple_of(jnp.minimum(start // 128 * 128, own - GROUP_SPAN), 128)
+        span = pl.ds(at, GROUP_SPAN)
+        put_dense(band, dense_of(blk[:, span], rows[0:1, span], rows[1:2, span], first), first, False)
+
+
+def spill_kernel(own_band, blue, red, w_in_t, bias_t, w_out_t, band, blk, spill):
     side = device_side()
-    parts = []
-    for lo in range(0, feat.shape[0], 256):
-        line = lo // 128
-        parts.append(
-            (
-                lambda lo=lo: feat[lo : lo + 256, :],
-                [jnp.concatenate([ids[k, line : line + 1], ids[k, line + 1 : line + 2]], axis=1) for k in range(3)],
-            )
-        )
+    nfeat = spill.shape[1]
     rows = spill.shape[0] // 2
     for m, (msg, gap) in enumerate(((blue, side == 0), (red, side == 1))):
         base = m * rows
@@ -122,58 +187,36 @@
         spill[base + rows - 64 : base + rows, :] = jnp.zeros((64, nfeat), BF)
         at = pl.multiple_of(base + jnp.where(gap, 64, 0), 64)
         spill[pl.ds(at, SPILL), :] = msg[0:SPILL, :]
-    lines = []
+    lines, ends = [], []
     for msg in (blue, red):
         block = msg[SPILL : SPILL + ID_ROWS, 0:128].astype(F32)
         lines.extend([[block[3 * k + n : 3 * k + n + 1] for k in range(3)] for n in range(3)])
-    for lo in range(0, 2 * rows, 256):
-        first, second = lines[lo // 128], lines[lo // 128 + 1]
-        parts.append(
+        a = block[0:3]
+        mine = (a >= 0.0) & (a < float(ATOM_Q))
+        ends.append(
             (
-                lambda lo=lo: spill[lo : lo + 256, :],
-                [jnp.concatenate([first[k], second[k]], axis=1) for k in range(3)],
+                jnp.min(jnp.where(mine, a, float(ATOM_Q))).astype(jnp.int32),
+                jnp.max(jnp.where(mine, a, -1.0)).astype(jnp.int32),
             )
         )
-    at = 0
-    atoms, cols = [], []
-    for get, (a, b, c) in parts:
-        x = get()
-        n = x.shape[0]
-        cell1 = (iota((8, n), 0).astype(F32) == c).astype(BF)
-        pre = nt_dot(w_in_t, x) + jnp.dot(bias_t, cell1, preferred_element_type=F32)
-        gate, up = pre[:HID], pre[HID:]
-        hidden = (gate * (0.5 + 0.5 * jnp.tanh(0.5 * gate)) * up).astype(BF)
-        blk[:, at : at + n] = jnp.dot(w_out_t, hidden, preferred_element_type=F32).astype(BF)
-        atoms.append(a)
-        cols.append(b)
-        at += n
-    atom = jnp.concatenate(atoms, axis=1)
-    odd_tile = jnp.floor(atom * (1.0 / TILE_ATOMS)) - 2.0 * jnp.floor(atom * (0.5 / TILE_ATOMS))
-    target = jnp.concatenate(cols, axis=1) + TILE_ATOMS * odd_tile
-    onehot_t = (iota((WIN_ATOMS, at), 0).astype(F32) == target).astype(BF)
-    low = iota((ORB, 128), 1) < WIN_ATOMS
-    for first in range(0, ATOM_Q, 4):
-        onehot = jnp.concatenate(
-            [
-                jnp.broadcast_to((atom == float(s)).astype(F32), (WIN_ATOMS, at)).astype(BF) * onehot_t
-                for s in range(first, first + 4)
-            ],
-            axis=0,
+    for lo in range(0, 2 * rows, 256):
+        both = lines[lo // 128 : lo // 128 + 2]
+        cell = jnp.concatenate([x[2] for x in both], axis=1)
+        blk[:, lo : lo + 256] = pair_blocks(
+            spill[lo : lo + 256, :], cell, w_in_t[...], bias_t[...], w_out_t[...]
         )
-        dense = nt_dot(blk[...], onehot)
-        for sp in range(2):
-            s = first + 2 * sp
-            pair, at_row = s // PAIR_ATOMS, s % PAIR_ATOMS * ORB
-            for j in range(ORB // 2):
-                x = dense[2 * j * ORB : (2 * j + 1) * ORB, sp * 128 : sp * 128 + 128]
-                y = dense[(2 * j + 1) * ORB : (2 * j + 2) * ORB, sp * 128 : sp * 128 + 128]
-                lanes = slice(j * 128, j * 128 + 128)
-                band[pair, at_row : at_row + ORB, lanes] = jnp.where(
-                    low, x, pltpu.roll(y, WIN_ATOMS, 1)
-                ).astype(BF)
-                band[pair, at_row + ORB : at_row + 2 * ORB, lanes] = jnp.where(
-                    low, pltpu.roll(x, WIN_ATOMS, 1), y
-                ).astype(BF)
+    band[...] = own_band[...]
+    for m in range(2):
+        mine = lines[3 * m : 3 * m + 3]
+        atom = jnp.concatenate([x[0] for x in mine], axis=1)
+        target = jnp.concatenate([x[1] for x in mine], axis=1) + TILE_ATOMS * odd_tile(atom)
+        lowest, highest = ends[m]
+        for first in range(0, ATOM_Q, GROUP):
+
+            @pl.when((lowest < first + GROUP) & (highest >= first))
+            def _(m=m, first=first, atom=atom, target=target):
+                dense = dense_of(blk[:, m * rows : (m + 1) * rows], atom, target, first)
+                put_dense(band, dense, first, True)
 
 
 def apply_band(band, wide, pair):
@@ -220,16 +263,18 @@
     put_sends(after, to_blue, to_red)
 
 
-def last_kernel(coef, band, t0, t1, t2, t3, blue, red, p0, p1, p2, p3, wide, out):
+def mix_kernel(coef, t0, t1, t2, t3, base):
+    total = coef[0] * t0[...] + coef[1] * t1[...] + (coef[2] - coef[4]) * t2[...] + coef[3] * t3[...]
+    base[...] = total.T
+
+
+def last_kernel(coef, band, base, t3, blue, red, p0, p1, p2, p3, wide, out):
     member = lax.axis_index("edges")
     fill_wide(t3[...], blue[...].astype(F32), red[...].astype(F32), wide)
     height = PAIR_ATOMS * ORB
     for pair in range(band.shape[0]):
         span = slice(pair * height, (pair + 1) * height)
-        t4 = 2.0 * apply_band(band, wide, pair) - t2[span, :]
-        total = coef[0] * t0[span, :] + coef[1] * t1[span, :] + coef[2] * t2[span, :]
-        total = total + coef[3] * t3[span, :] + coef[4] * t4
-        out[:, span] = total.T
+        out[:, span] = base[:, span] + (2.0 * coef[4] * apply_band(band, wide, pair)).T
     for k, piece in enumerate((p0, p1, p2, p3)):
         high = piece.shape[0]
         piece[...] = out[pl.ds(pl.multiple_of((member ^ k) * high, high), high), :].astype(BF)
@@ -245,16 +290,16 @@
 
 VMEM = pl.BlockSpec(memory_space=pltpu.VMEM)
 SMEM = pl.BlockSpec(memory_space=pltpu.SMEM)
-ANYWHERE = pl.BlockSpec(memory_space=pl.ANY)
-PARAMS = pltpu.CompilerParams(vmem_limit_bytes=40 * 1024 * 1024)
+IN_HBM = pl.BlockSpec(memory_space=pltpu.HBM)
+FULL, PART = 60 * 1024 * 1024, 32 * 1024 * 1024
 
 
 def shape(dims, dtype):
     return jax.ShapeDtypeStruct(dims, dtype)
 
 
-def call(kernel, name, outs, scratch, *args, smem=(), anywhere=()):
-    spaces = [SMEM if k in smem else ANYWHERE if k in anywhere else VMEM for k in range(len(args))]
+def call(kernel, name, outs, scratch, *args, smem=(), in_hbm=(), alias=None, limit=PART):
+    spaces = [SMEM if k in smem else IN_HBM if k in in_hbm else VMEM for k in range(len(args))]
     return pl.pallas_call(
         kernel,
         name=name,
@@ -262,7 +307,8 @@
         in_specs=spaces,
         out_specs=(VMEM,) * len(outs),
         scratch_shapes=scratch,
-        compiler_params=PARAMS,
+        input_output_aliases=alias or {},
+        compiler_params=pltpu.CompilerParams(vmem_limit_bytes=limit),
     )(*args)
 
 
@@ -290,43 +336,60 @@
     msg = shape((SPILL + ID_ROWS, nfeat), BF)
     piece = shape((high, nrow), BF)
     lines = (nown // 128, 128)
-    blue_msg, red_msg, ids, *pieces = call(
-        prep_kernel,
-        "prep",
-        (msg, msg, shape((3,) + lines, F32)) + (piece,) * 4,
-        [pltpu.SemaphoreType.DMA((2,))],
+    pieces = call(
+        split_kernel,
+        "split",
+        (piece,) * 4,
+        [pltpu.VMEM((high, ncol), F32), pltpu.SemaphoreType.DMA],
+        vectors,
+        in_hbm=(0,),
+        limit=FULL,
+    )
+    pieces = exchange(pieces)
+    blue_msg, red_msg, ids = call(
+        message_kernel,
+        "message",
+        (msg, msg, shape((3,) + lines, F32)),
+        [pltpu.VMEM(lines, jnp.int32)] * 3 + [pltpu.SemaphoreType.DMA((5,))],
         features,
         edge_src.reshape(lines),
         edge_dst.reshape(lines),
         edge_cell.reshape(lines),
-        vectors,
-        anywhere=(0,),
+        pieces[0],
+        in_hbm=range(5),
+        limit=FULL,
     )
     blue_msg, red_msg = swap(blue_msg, red_msg)
-    pieces = exchange(pieces)
     full, part = shape((nrow, VEC), F32), shape((HALO, VEC), BF)
     t0, to_blue, to_red = call(
         field_kernel, "field", (full, part, part), [pltpu.VMEM((VEC, nrow), F32)], *pieces
     )
     blue, red = swap(to_blue, to_red)
 
-    spill_len = 2 * (SPILL + 64)
-    (band,) = call(
-        band_kernel,
-        "band",
-        (shape((ATOM_Q // PAIR_ATOMS, PAIR_ATOMS * ORB, WIN_ATOMS * ORB), BF),),
-        [
-            pltpu.VMEM((ORB * ORB, nown + spill_len), BF),
-            pltpu.VMEM((8, 2 * HID), F32),
-            pltpu.VMEM((spill_len, nfeat), BF),
-        ],
+    band_shape = shape((ATOM_Q // PAIR_ATOMS, PAIR_ATOMS * ORB, WIN_ATOMS * ORB), BF)
+    width = w_in.shape[1]
+    band, *weights = call(
+        own_kernel,
+        "own",
+        (band_shape, shape((width, nfeat), BF), shape((width, 8), BF), shape((ORB * ORB, HID), BF)),
+        [pltpu.VMEM((ORB * ORB, nown), BF), pltpu.VMEM((8, width), F32), pltpu.VMEM((8, nown), F32)],
         features,
         ids,
-        blue_msg,
-        red_msg,
         cell_bias,
         w_in,
         w_out,
+    )
+    spill_len = 2 * (SPILL + 64)
+    (band,) = call(
+        spill_kernel,
+        "spill",
+        (band_shape,),
+        [pltpu.VMEM((ORB * ORB, spill_len), BF), pltpu.VMEM((spill_len, nfeat), BF)],
+        band,
+        blue_msg,
+        red_msg,
+        *weights,
+        alias={0: 0},
     )
 
     wide = pltpu.VMEM((nrow + 2 * HALO, VEC), F32)
@@ -339,6 +402,7 @@
         )
         fields.append(following)
     blue, red = swap(to_blue, to_red)
+    (base,) = call(mix_kernel, "mix", (shape((VEC, nrow), F32),), [], cheb_coef, *fields, smem=(0,))
     pieces = call(
         last_kernel,
         "last",
@@ -346,7 +410,8 @@
         [wide, pltpu.VMEM((VEC, nrow), F32)],
         cheb_coef,
         band,
-        *fields,
+        base,
+        fields[-1],
         blue,
         red,
         smem=(0,),

time: 57.9 us -> 58.1 us (level)
  Pallas kernels: 11.1 us -> 15.2 us
  local copies, waits for them, and re-layouts: 4.15 us -> 1.41 us
  starting transfers between devices: 18.7 us -> 18 us
    pallas_call x8 -> x11, Pallas kernels: 11.1 us -> 15.2 us  [call(): pl.pallas_call(kernel, name=name, out_shape=outs, in_specs=spaces, out_sp...]
    unnamed x20 -> x16, local copies, waits for them, and re-layouts: 4.15 us -> 1.41 us
    ppermute x5, starting transfers between devices: 14.9 us -> 14.1 us  [swap(): lax.ppermute(first, axes, blue_pairs)]
    ppermute x5, waiting for transfers between devices: 18.6 us -> 17.9 us  [swap(): lax.ppermute(first, axes, blue_pairs)]
  transfers between devices with their start and end apart: 16 -> 16, of which waited for: 5 -> 6; matrix products, arithmetic and copies ran while one was open for 0% -> 0% of each run, Pallas kernels for 11% -> 13%
where the time goes in v3:
time: 58.1 us; the launch traced here: 57.9 us
  waiting for transfers between devices  23 us (40%)
  starting transfers between devices  18 us (31%)
  Pallas kernels  15.2 us (26%)
  local copies, waits for them, and re-layouts  1.41 us (2%)
    ppermute x5, waiting for transfers between devices, swap(): lax.ppermute(first, axes, blue_pairs)  17.9 us
    pallas_call x11, Pallas kernels, call(): pl.pallas_call(kernel, name=name, out_shape=outs, in_specs=spaces, out_sp...  15.2 us
    ppermute x5, starting transfers between devices, swap(): lax.ppermute(first, axes, blue_pairs)  14.1 us
    ppermute x6, waiting for transfers between devices, exchange(): lax.ppermute(pieces[k], 'edges', [(i, i ^ k) for i in range(nedge)])  5.07 us
    ppermute x6, starting transfers between devices, exchange(): lax.ppermute(pieces[k], 'edges', [(i, i ^ k) for i in range(nedge)])  3.79 us
    unnamed x16, local copies, waits for them, and re-layouts  1.41 us
  transfers between devices with their start and end apart: 16, of which 6 were waited for; matrix products, arithmetic and copies ran while one was open for 0% of the time, Pallas kernels for 13%

profile of v3, /device:TPU:0, one launch (start us, length us, event | category | flops | bytes accessed | tf_op | source)
XLA Modules:
  0.0 57.9 jit_solution(13427867313916343384)
XLA Ops:
  0.0 1.7 %split.1 = (bf16[32,512]{1,0:T(8,128)(2,1)}, bf16[32,512]{1,0:T(8,128)(2,1)}, bf16[32,512]{1,0:T(8,128)(2,1)}, bf16[32,512]{1,0:T(8,128)(2,1)}) custom-call(f32[32,2048]{1,0:T(8,128)} %vec_hbm.1), custom_call_target="tpu_custom_call" | custom-call | tf_op jit(solution)/shard_map/split/pallas_call | solution.py:303
  1.7 0.0 copy-start.1
  1.7 1.9 %message.1 = (bf16[336,256]{1,0:T(8,128)(2,1)}, bf16[336,256]{1,0:T(8,128)(2,1)}, f32[3,10,128]{2,1,0:T(8,128)}) custom-call(bf16[1280,256]{1,0:T(8,128)(2,1)} %feat.3, s32[10,128]{1,0:T(8,128)} %bitcast.3, s32[10,128]{1,0:T(8,128)} %bitcast.4, s32[10,128]{1,0:T(8,128)} %bitcast.5, bf16[32,512]{1,0:T(8,128)(2,1)} %get-tuple-element.32._.p0), custom_call_target="tpu_custom_call" | custom-call | tf_op jit(solution)/shard_map/message/pallas_call | solution.py:303
  3.6 0.0 copy-start.2
  3.6 6.4 %collective-permute-start = (bf16[336,256]{1,0:T(8,128)(2,1)}, bf16[336,256]{1,0:T(8,128)(2,1)S(1)}, u32[]{:S(2)}, u32[]{:S(2)}) collective-permute-start(bf16[336,256]{1,0:T(8,128)(2,1)} %get-tuple-element.35), channel_id=1, source_target_pairs={{0,31},{1,2},{2,1},{3,4},{4,3},{5,6},{6,5},{7,8},{8,7},{9,10},{10,... | collective-permute-start | bytes 516104 | tf_op jit(solution)/shard_map/ppermute | solution.py:327
  10.0 0.0 collective-permute-start.1
  10.0 0.5 collective-permute-start.2
  10.6 0.0 collective-permute-start.3
  10.6 1.4 %collective-permute-start.4 = (bf16[32,512]{1,0:T(8,128)(2,1)S(1)}, bf16[32,512]{1,0:T(8,128)(2,1)S(1)}, u32[]{:S(2)}, u32[]{:S(2)}) collective-permute-start(bf16[32,512]{1,0:T(8,128)(2,1)S(1)} %copy-done.7), channel_id=1, source_target_pairs={{0,3},{1,2},{2,1},{3,0},{4,7},{5,6},{6,5},{7,4},{8,11},{9,10},{10,... | collective-permute-start | bytes 98312 | tf_op jit(solution)/shard_map/ppermute | solution.py:333
  11.9 0.0 collective-permute-done.2.p1
  11.9 2.8 %collective-permute-done.3.p2 = bf16[32,512]{1,0:T(8,128)(2,1)S(1)} collective-permute-done((bf16[32,512]{1,0:T(8,128)(2,1)}, bf16[32,512]{1,0:T(8,128)(2,1)S(1)}, u32[]{:S(2)}, u32[]{:S(2)}) %collective-permute-start.3) | collective-permute-done | bytes 32800 | tf_op jit(solution)/shard_map/ppermute | solution.py:333
  14.7 0.0 collective-permute-done.4.p3
  14.7 0.2 field.1
  14.9 0.0 copy-start.5
  14.9 3.9 %collective-permute-start.5 = (bf16[384,128]{1,0:T(8,128)(2,1)S(1)}, bf16[384,128]{1,0:T(8,128)(2,1)S(1)}, u32[]{:S(2)}, u32[]{:S(2)}) collective-permute-start(bf16[384,128]{1,0:T(8,128)(2,1)S(1)} %get-tuple-element.44), channel_id=1, source_target_pairs={{0,31},{1,2},{2,1},{3,4},{4,3},{5,6},{6,5},{7,8},{8,7},{9,10},{10,... | collective-permute-start | bytes 294920 | tf_op jit(solution)/shard_map/ppermute | solution.py:327
  18.8 0.0 collective-permute-start.6
  18.8 0.7 %copy-done.4 = f32[3,10,128]{2,1,0:T(8,128)S(1)} copy-done((f32[3,10,128]{2,1,0:T(8,128)S(1)}, f32[3,10,128]{2,1,0:T(8,128)}, u32[]{:S(2)}) %copy-start.4) | copy-done | bytes 15384
  19.6 3.8 %own.1 = (bf16[2,256,1024]{2,1,0:T(8,128)(2,1)S(1)}, bf16[512,256]{1,0:T(8,128)(2,1)S(1)}, bf16[512,8]{1,0:T(8,128)(2,1)S(1)}, bf16[256,256]{1,0:T(8,128)(2,1)S(1)}) custom-call(bf16[1280,256]{1,0:T(8,128)(2,1)S(1)} %copy-done, f32[3,10,128]{2,1,0:T(8,128)S(1)} %copy-done.4, bf16[3,512]{1,0:T(4,128)(2,1)S(1)} %copy-done.5, bf16[256,512]{1,0:T(8,128)(2,1)S(1)} %copy-done.1, ...), custom_call_target="tpu_custom_call" | custom-call | tf_op jit(solution)/shard_map/own/pallas_call | solution.py:303
  23.3 0.0 collective-permute-done.blue
  23.3 0.0 collective-permute-done.1.red
  23.4 2.9 %spill.1.band = bf16[2,256,1024]{2,1,0:T(8,128)(2,1)S(1)} custom-call(bf16[2,256,1024]{2,1,0:T(8,128)(2,1)S(1)} %get-tuple-element.34.own_band, bf16[336,256]{1,0:T(8,128)(2,1)S(1)} %collective-permute-done.blue, bf16[336,256]{1,0:T(8,128)(2,1)S(1)} %collective-permute-done.1.red, ...), custom_call_target="tpu_custom_call", output_to_operand_aliasing={{}: (0, {})} | custom-call | tf_op jit(solution)/shard_map/spill/pallas_call | solution.py:303
  26.3 0.0 collective-permute-done.5.blue
  26.3 0.0 collective-permute-done.6.red
  26.3 0.7 %first.1 = (f32[512,128]{1,0:T(8,128)S(1)}, bf16[384,128]{1,0:T(8,128)(2,1)S(1)}, bf16[384,128]{1,0:T(8,128)(2,1)S(1)}) custom-call(bf16[2,256,1024]{2,1,0:T(8,128)(2,1)S(1)} %spill.1.band, f32[512,128]{1,0:T(8,128)S(1)} %get-tuple-element.43.t0.before, bf16[384,128]{1,0:T(8,128)(2,1)S(1)} %collective-permute-done.5.blue, ...), custom_call_target="tpu_custom_call" | custom-call | tf_op jit(solution)/shard_map/first/pallas_call | solution.py:303
  27.0 1.2 %collective-permute-start.7 = (bf16[384,128]{1,0:T(8,128)(2,1)S(1)}, bf16[384,128]{1,0:T(8,128)(2,1)S(1)}, u32[]{:S(2)}, u32[]{:S(2)}) collective-permute-start(bf16[384,128]{1,0:T(8,128)(2,1)S(1)} %get-tuple-element.47), channel_id=1, source_target_pairs={{0,31},{1,2},{2,1},{3,4},{4,3},{5,6},{6,5},{7,8},{8,7},{9,10},{10,... | collective-permute-start | bytes 294920 | tf_op jit(solution)/shard_map/ppermute | solution.py:327
  28.2 0.0 collective-permute-start.8
  28.2 6.5 %collective-permute-done.7.blue = bf16[384,128]{1,0:T(8,128)(2,1)S(1)} collective-permute-done((bf16[384,128]{1,0:T(8,128)(2,1)S(1)}, bf16[384,128]{1,0:T(8,128)(2,1)S(1)}, u32[]{:S(2)}, u32[]{:S(2)}) %collective-permute-start.7) | collective-permute-done | bytes 98336 | tf_op jit(solution)/shard_map/ppermute | solution.py:327
  34.7 0.0 collective-permute-done.8.red
  34.7 0.7 %next.2 = (f32[512,128]{1,0:T(8,128)S(1)}, bf16[384,128]{1,0:T(8,128)(2,1)S(1)}, bf16[384,128]{1,0:T(8,128)(2,1)S(1)}) custom-call(bf16[2,256,1024]{2,1,0:T(8,128)(2,1)S(1)} %spill.1.band, f32[512,128]{1,0:T(8,128)S(1)} %get-tuple-element.43.t0.before, f32[512,128]{1,0:T(8,128)S(1)} %get-tuple-element.46.now.before.t1, ...), custom_call_target="tpu_custom_call" | custom-call | tf_op jit(solution)/shard_map/next/pallas_call | solution.py:303
  35.4 0.1 collective-permute-start.10
  35.5 1.2 %collective-permute-start.9 = (bf16[384,128]{1,0:T(8,128)(2,1)S(1)}, bf16[384,128]{1,0:T(8,128)(2,1)S(1)}, u32[]{:S(2)}, u32[]{:S(2)}) collective-permute-start(bf16[384,128]{1,0:T(8,128)(2,1)S(1)} %get-tuple-element.50), channel_id=1, source_target_pairs={{0,31},{1,2},{2,1},{3,4},{4,3},{5,6},{6,5},{7,8},{8,7},{9,10},{10,... | collective-permute-start | bytes 294920 | tf_op jit(solution)/shard_map/ppermute | solution.py:327
  36.7 0.1 collective-permute-done.10.red
  36.8 6.4 %collective-permute-done.9.blue = bf16[384,128]{1,0:T(8,128)(2,1)S(1)} collective-permute-done((bf16[384,128]{1,0:T(8,128)(2,1)S(1)}, bf16[384,128]{1,0:T(8,128)(2,1)S(1)}, u32[]{:S(2)}, u32[]{:S(2)}) %collective-permute-start.9) | collective-permute-done | bytes 98336 | tf_op jit(solution)/shard_map/ppermute | solution.py:327
  43.2 0.7 %next.3 = (f32[512,128]{1,0:T(8,128)S(1)}, bf16[384,128]{1,0:T(8,128)(2,1)S(1)}, bf16[384,128]{1,0:T(8,128)(2,1)S(1)}) custom-call(bf16[2,256,1024]{2,1,0:T(8,128)(2,1)S(1)} %spill.1.band, f32[512,128]{1,0:T(8,128)S(1)} %get-tuple-element.46.now.before.t1, f32[512,128]{1,0:T(8,128)S(1)} %get-tuple-element.49.now.t2, ...), custom_call_target="tpu_custom_call" | custom-call | tf_op jit(solution)/shard_map/next/pallas_call | solution.py:303
  43.9 1.3 %collective-permute-start.11 = (bf16[384,128]{1,0:T(8,128)(2,1)S(1)}, bf16[384,128]{1,0:T(8,128)(2,1)S(1)}, u32[]{:S(2)}, u32[]{:S(2)}) collective-permute-start(bf16[384,128]{1,0:T(8,128)(2,1)S(1)} %get-tuple-element.53), channel_id=1, source_target_pairs={{0,31},{1,2},{2,1},{3,4},{4,3},{5,6},{6,5},{7,8},{8,7},{9,10},{10,... | collective-permute-start | bytes 294920 | tf_op jit(solution)/shard_map/ppermute | solution.py:327
  45.2 0.0 collective-permute-start.12
  45.2 0.7 %copy-done.6 = f32[5]{0:T(128)S(1)} copy-done((f32[5]{0:T(128)S(1)}, f32[5]{0:T(128)}, u32[]{:S(2)}) %copy-start.6) | copy-done | bytes 44
  45.9 0.7 %mix.1.base = f32[128,512]{1,0:T(8,128)S(1)} custom-call(f32[5]{0:T(128)S(1)} %copy-done.6, f32[512,128]{1,0:T(8,128)S(1)} %get-tuple-element.43.t0.before, f32[512,128]{1,0:T(8,128)S(1)} %get-tuple-element.46.now.before.t1, f32[512,128]{1,0:T(8,128)S(1)} %get-tuple-element.49.now.t2, f32[512,128]{1,0:T(8,128)S(1)} %get-tuple-element.52.t3), custom_call_target="tpu_custom_call" | custom-call | tf_op jit(solution)/shard_map/mix/pallas_call | solution.py:303
  46.6 5.0 %collective-permute-done.11.blue = bf16[384,128]{1,0:T(8,128)(2,1)S(1)} collective-permute-done((bf16[384,128]{1,0:T(8,128)(2,1)S(1)}, bf16[384,128]{1,0:T(8,128)(2,1)S(1)}, u32[]{:S(2)}, u32[]{:S(2)}) %collective-permute-start.11) | collective-permute-done | bytes 98336 | tf_op jit(solution)/shard_map/ppermute | solution.py:327
  51.6 0.0 collective-permute-done.12.red
  51.6 1.3 %last.1 = (bf16[32,512]{1,0:T(8,128)(2,1)S(1)}, bf16[32,512]{1,0:T(8,128)(2,1)S(1)}, bf16[32,512]{1,0:T(8,128)(2,1)S(1)}, bf16[32,512]{1,0:T(8,128)(2,1)S(1)}) custom-call(f32[5]{0:T(128)S(1)} %copy-done.6, bf16[2,256,1024]{2,1,0:T(8,128)(2,1)S(1)} %spill.1.band, f32[128,512]{1,0:T(8,128)S(1)} %mix.1.base, f32[512,128]{1,0:T(8,128)S(1)} %get-tuple-element.52.t3, ...), custom_call_target="tpu_custom_call" | custom-call | tf_op jit(solution)/shard_map/last/pallas_call | solution.py:303
  52.9 0.1 collective-permute-start.13
  53.0 0.1 collective-permute-start.14
  53.0 1.8 %collective-permute-start.15 = (bf16[32,512]{1,0:T(8,128)(2,1)S(1)}, bf16[32,512]{1,0:T(8,128)(2,1)S(1)}, u32[]{:S(2)}, u32[]{:S(2)}) collective-permute-start(bf16[32,512]{1,0:T(8,128)(2,1)S(1)} %get-tuple-element.58), channel_id=1, source_target_pairs={{0,3},{1,2},{2,1},{3,0},{4,7},{5,6},{6,5},{7,4},{8,11},{9,10},{10,... | collective-permute-start | bytes 98312 | tf_op jit(solution)/shard_map/ppermute | solution.py:333
  54.8 0.0 collective-permute-done.13.p1
  54.8 2.3 %collective-permute-done.14.p2 = bf16[32,512]{1,0:T(8,128)(2,1)S(1)} collective-permute-done((bf16[32,512]{1,0:T(8,128)(2,1)S(1)}, bf16[32,512]{1,0:T(8,128)(2,1)S(1)}, u32[]{:S(2)}, u32[]{:S(2)}) %collective-permute-start.14) | collective-permute-done | bytes 32800 | tf_op jit(solution)/shard_map/ppermute | solution.py:333
  57.1 0.0 collective-permute-done.15.p3
  57.1 0.7 %join.1 = f32[32,2048]{1,0:T(8,128)} custom-call(bf16[32,512]{1,0:T(8,128)(2,1)S(1)} %get-tuple-element.55.p0, bf16[32,512]{1,0:T(8,128)(2,1)S(1)} %collective-permute-done.13.p1, bf16[32,512]{1,0:T(8,128)(2,1)S(1)} %collective-permute-done.14.p2, bf16[32,512]{1,0:T(8,128)(2,1)S(1)} %collective-permute-done.15.p3), custom_call_target="tpu_custom_call" | custom-call | tf_op jit(solution)/shard_map/join/pallas_call | solution.py:303
  (11 shorter events, 0.0 us)
Async XLA Ops:
  0.0 18.8 %copy-start = (bf16[1280,256]{1,0:T(8,128)(2,1)S(1)}, bf16[1280,256]{1,0:T(8,128)(2,1)}, u32[]{:S(2)}) copy-start(bf16[1280,256]{1,0:T(8,128)(2,1)} %feat.3) | copy-start | bytes 1966084
  1.7 8.9 %copy-start.7 = (bf16[32,512]{1,0:T(8,128)(2,1)S(1)}, bf16[32,512]{1,0:T(8,128)(2,1)}, u32[]{:S(2)}) copy-start(bf16[32,512]{1,0:T(8,128)(2,1)} %get-tuple-element.42) | copy-start | bytes 98308
  1.7 13.0 %copy-start.3 = (bf16[32,512]{1,0:T(8,128)(2,1)S(1)}, bf16[32,512]{1,0:T(8,128)(2,1)}, u32[]{:S(2)}) copy-start(bf16[32,512]{1,0:T(8,128)(2,1)} %get-tuple-element.32._.p0) | copy-start | bytes 98308
  1.7 17.1 %copy-start.1 = (bf16[256,512]{1,0:T(8,128)(2,1)S(1)}, bf16[256,512]{1,0:T(8,128)(2,1)}, u32[]{:S(2)}) copy-start(bf16[256,512]{1,0:T(8,128)(2,1)} %w_in.1) | copy-start | bytes 786436
  3.6 15.2 %copy-start.2 = (bf16[256,256]{1,0:T(8,128)(2,1)S(1)}, bf16[256,256]{1,0:T(8,128)(2,1)}, u32[]{:S(2)}) copy-start(bf16[256,256]{1,0:T(8,128)(2,1)} %w_out.1) | copy-start | bytes 393220
  3.6 19.7 %collective-permute-start = (bf16[336,256]{1,0:T(8,128)(2,1)}, bf16[336,256]{1,0:T(8,128)(2,1)S(1)}, u32[]{:S(2)}, u32[]{:S(2)}) collective-permute-start(bf16[336,256]{1,0:T(8,128)(2,1)} %get-tuple-element.35), channel_id=1, source_target_pairs={{0,31},{1,2},{2,1},{3,4},{4,3},{5,6},{6,5},{7,8},{8,7},{9,10},{10,... | collective-permute-start | bytes 516104 | tf_op jit(solution)/shard_map/ppermute | solution.py:327
  10.0 13.3 %collective-permute-start.1 = (bf16[336,256]{1,0:T(8,128)(2,1)}, bf16[336,256]{1,0:T(8,128)(2,1)S(1)}, u32[]{:S(2)}, u32[]{:S(2)}) collective-permute-start(bf16[336,256]{1,0:T(8,128)(2,1)} %get-tuple-element.36), channel_id=1, source_target_pairs={{0,1},{1,0},{2,3},{3,2},{4,5},{5,4},{6,7},{7,6},{8,9},{9,8},{10,11... | collective-permute-start | bytes 516104 | tf_op jit(solution)/shard_map/ppermute | solution.py:328
  10.0 1.9 %collective-permute-start.2 = (bf16[32,512]{1,0:T(8,128)(2,1)}, bf16[32,512]{1,0:T(8,128)(2,1)S(1)}, u32[]{:S(2)}, u32[]{:S(2)}) collective-permute-start(bf16[32,512]{1,0:T(8,128)(2,1)} %get-tuple-element.40), channel_id=1, source_target_pairs={{0,1},{1,0},{2,3},{3,2},{4,5},{5,4},{6,7},{7,6},{8,9},{9,8},{10,11... | collective-permute-start | bytes 98312 | tf_op jit(solution)/shard_map/ppermute | solution.py:333
  10.6 4.1 %collective-permute-start.3 = (bf16[32,512]{1,0:T(8,128)(2,1)}, bf16[32,512]{1,0:T(8,128)(2,1)S(1)}, u32[]{:S(2)}, u32[]{:S(2)}) collective-permute-start(bf16[32,512]{1,0:T(8,128)(2,1)} %get-tuple-element.41), channel_id=1, source_target_pairs={{0,2},{1,3},{2,0},{3,1},{4,6},{5,7},{6,4},{7,5},{8,10},{9,11},{10,... | collective-permute-start | bytes 98312 | tf_op jit(solution)/shard_map/ppermute | solution.py:333
  10.6 4.1 %collective-permute-start.4 = (bf16[32,512]{1,0:T(8,128)(2,1)S(1)}, bf16[32,512]{1,0:T(8,128)(2,1)S(1)}, u32[]{:S(2)}, u32[]{:S(2)}) collective-permute-start(bf16[32,512]{1,0:T(8,128)(2,1)S(1)} %copy-done.7), channel_id=1, source_target_pairs={{0,3},{1,2},{2,1},{3,0},{4,7},{5,6},{6,5},{7,4},{8,11},{9,10},{10,... | collective-permute-start | bytes 98312 | tf_op jit(solution)/shard_map/ppermute | solution.py:333
  14.9 3.9 %copy-start.5 = (bf16[3,512]{1,0:T(4,128)(2,1)S(1)}, bf16[3,512]{1,0:T(4,128)(2,1)}, u32[]{:S(2)}) copy-start(bf16[3,512]{1,0:T(4,128)(2,1)} %cell_bias.1) | copy-start | bytes 9220
  14.9 11.4 %collective-permute-start.5 = (bf16[384,128]{1,0:T(8,128)(2,1)S(1)}, bf16[384,128]{1,0:T(8,128)(2,1)S(1)}, u32[]{:S(2)}, u32[]{:S(2)}) collective-permute-start(bf16[384,128]{1,0:T(8,128)(2,1)S(1)} %get-tuple-element.44), channel_id=1, source_target_pairs={{0,31},{1,2},{2,1},{3,4},{4,3},{5,6},{6,5},{7,8},{8,7},{9,10},{10,... | collective-permute-start | bytes 294920 | tf_op jit(solution)/shard_map/ppermute | solution.py:327
  18.8 7.5 %collective-permute-start.6 = (bf16[384,128]{1,0:T(8,128)(2,1)S(1)}, bf16[384,128]{1,0:T(8,128)(2,1)S(1)}, u32[]{:S(2)}, u32[]{:S(2)}) collective-permute-start(bf16[384,128]{1,0:T(8,128)(2,1)S(1)} %get-tuple-element.45), channel_id=1, source_target_pairs={{0,1},{1,0},{2,3},{3,2},{4,5},{5,4},{6,7},{7,6},{8,9},{9,8},{10,11... | collective-permute-start | bytes 294920 | tf_op jit(solution)/shard_map/ppermute | solution.py:328
  18.8 0.7 %copy-start.4 = (f32[3,10,128]{2,1,0:T(8,128)S(1)}, f32[3,10,128]{2,1,0:T(8,128)}, u32[]{:S(2)}) copy-start(f32[3,10,128]{2,1,0:T(8,128)} %get-tuple-element.33.ids) | copy-start | bytes 46084
  27.0 7.7 %collective-permute-start.7 = (bf16[384,128]{1,0:T(8,128)(2,1)S(1)}, bf16[384,128]{1,0:T(8,128)(2,1)S(1)}, u32[]{:S(2)}, u32[]{:S(2)}) collective-permute-start(bf16[384,128]{1,0:T(8,128)(2,1)S(1)} %get-tuple-element.47), channel_id=1, source_target_pairs={{0,31},{1,2},{2,1},{3,4},{4,3},{5,6},{6,5},{7,8},{8,7},{9,10},{10,... | collective-permute-start | bytes 294920 | tf_op jit(solution)/shard_map/ppermute | solution.py:327
  28.2 6.5 %collective-permute-start.8 = (bf16[384,128]{1,0:T(8,128)(2,1)S(1)}, bf16[384,128]{1,0:T(8,128)(2,1)S(1)}, u32[]{:S(2)}, u32[]{:S(2)}) collective-permute-start(bf16[384,128]{1,0:T(8,128)(2,1)S(1)} %get-tuple-element.48), channel_id=1, source_target_pairs={{0,1},{1,0},{2,3},{3,2},{4,5},{5,4},{6,7},{7,6},{8,9},{9,8},{10,11... | collective-permute-start | bytes 294920 | tf_op jit(solution)/shard_map/ppermute | solution.py:328
  35.4 1.4 %collective-permute-start.10 = (bf16[384,128]{1,0:T(8,128)(2,1)S(1)}, bf16[384,128]{1,0:T(8,128)(2,1)S(1)}, u32[]{:S(2)}, u32[]{:S(2)}) collective-permute-start(bf16[384,128]{1,0:T(8,128)(2,1)S(1)} %get-tuple-element.51), channel_id=1, source_target_pairs={{0,1},{1,0},{2,3},{3,2},{4,5},{5,4},{6,7},{7,6},{8,9},{9,8},{10,11... | collective-permute-start | bytes 294920 | tf_op jit(solution)/shard_map/ppermute | solution.py:328
  35.5 7.7 %collective-permute-start.9 = (bf16[384,128]{1,0:T(8,128)(2,1)S(1)}, bf16[384,128]{1,0:T(8,128)(2,1)S(1)}, u32[]{:S(2)}, u32[]{:S(2)}) collective-permute-start(bf16[384,128]{1,0:T(8,128)(2,1)S(1)} %get-tuple-element.50), channel_id=1, source_target_pairs={{0,31},{1,2},{2,1},{3,4},{4,3},{5,6},{6,5},{7,8},{8,7},{9,10},{10,... | collective-permute-start | bytes 294920 | tf_op jit(solution)/shard_map/ppermute | solution.py:327
  43.9 7.7 %collective-permute-start.11 = (bf16[384,128]{1,0:T(8,128)(2,1)S(1)}, bf16[384,128]{1,0:T(8,128)(2,1)S(1)}, u32[]{:S(2)}, u32[]{:S(2)}) collective-permute-start(bf16[384,128]{1,0:T(8,128)(2,1)S(1)} %get-tuple-element.53), channel_id=1, source_target_pairs={{0,31},{1,2},{2,1},{3,4},{4,3},{5,6},{6,5},{7,8},{8,7},{9,10},{10,... | collective-permute-start | bytes 294920 | tf_op jit(solution)/shard_map/ppermute | solution.py:327
  45.2 0.7 %copy-start.6 = (f32[5]{0:T(128)S(1)}, f32[5]{0:T(128)}, u32[]{:S(2)}) copy-start(f32[5]{0:T(128)} %coef.3) | copy-start | bytes 64
  45.2 6.4 %collective-permute-start.12 = (bf16[384,128]{1,0:T(8,128)(2,1)S(1)}, bf16[384,128]{1,0:T(8,128)(2,1)S(1)}, u32[]{:S(2)}, u32[]{:S(2)}) collective-permute-start(bf16[384,128]{1,0:T(8,128)(2,1)S(1)} %get-tuple-element.54), channel_id=1, source_target_pairs={{0,1},{1,0},{2,3},{3,2},{4,5},{5,4},{6,7},{7,6},{8,9},{9,8},{10,11... | collective-permute-start | bytes 294920 | tf_op jit(solution)/shard_map/ppermute | solution.py:328
  52.9 1.9 %collective-permute-start.13 = (bf16[32,512]{1,0:T(8,128)(2,1)S(1)}, bf16[32,512]{1,0:T(8,128)(2,1)S(1)}, u32[]{:S(2)}, u32[]{:S(2)}) collective-permute-start(bf16[32,512]{1,0:T(8,128)(2,1)S(1)} %get-tuple-element.56), channel_id=1, source_target_pairs={{0,1},{1,0},{2,3},{3,2},{4,5},{5,4},{6,7},{7,6},{8,9},{9,8},{10,11... | collective-permute-start | bytes 98312 | tf_op jit(solution)/shard_map/ppermute | solution.py:333
  53.0 4.2 %collective-permute-start.14 = (bf16[32,512]{1,0:T(8,128)(2,1)S(1)}, bf16[32,512]{1,0:T(8,128)(2,1)S(1)}, u32[]{:S(2)}, u32[]{:S(2)}) collective-permute-start(bf16[32,512]{1,0:T(8,128)(2,1)S(1)} %get-tuple-element.57), channel_id=1, source_target_pairs={{0,2},{1,3},{2,0},{3,1},{4,6},{5,7},{6,4},{7,5},{8,10},{9,11},{10,... | collective-permute-start | bytes 98312 | tf_op jit(solution)/shard_map/ppermute | solution.py:333
  53.0 4.1 %collective-permute-start.15 = (bf16[32,512]{1,0:T(8,128)(2,1)S(1)}, bf16[32,512]{1,0:T(8,128)(2,1)S(1)}, u32[]{:S(2)}, u32[]{:S(2)}) collective-permute-start(bf16[32,512]{1,0:T(8,128)(2,1)S(1)} %get-tuple-element.58), channel_id=1, source_target_pairs={{0,3},{1,2},{2,1},{3,0},{4,7},{5,6},{6,5},{7,4},{8,11},{9,10},{10,... | collective-permute-start | bytes 98312 | tf_op jit(solution)/shard_map/ppermute | solution.py:333

commit v4 on v3

--- a/solution.py
+++ b/solution.py
@@ -38,18 +38,22 @@
     return (lax.axis_index("rows") * lax.axis_size("edges") + lax.axis_index("edges")) % 2
 
 
-def split_kernel(vec_hbm, p0, p1, p2, p3, vectors, sem):
+def split_kernel(vec_hbm, p0, p1, p2, p3, vectors, sems):
     member = lax.axis_index("edges")
-    load = pltpu.make_async_copy(vec_hbm, vectors, sem)
-    load.start()
-    load.wait()
-    for k, piece in enumerate((p0, p1, p2, p3)):
+    pieces = (p0, p1, p2, p3)
+    loads = []
+    for k, piece in enumerate(pieces):
         width = piece.shape[1]
         at = pl.multiple_of((member ^ k) * width, width)
-        piece[...] = vectors[:, pl.ds(at, width)].astype(BF)
-
-
-def message_kernel(feat, src_hbm, dst_hbm, cell_hbm, _, blue, red, ids, src, dst, cell, sems):
+        loads.append(pltpu.make_async_copy(vec_hbm.at[:, pl.ds(at, width)], vectors.at[k], sems.at[k]))
+    for k in (2, 3, 1, 0):
+        loads[k].start()
+    for k in (2, 3, 1, 0):
+        loads[k].wait()
+        pieces[k][...] = vectors[k].astype(BF)
+
+
+def message_kernel(feat, src_hbm, dst_hbm, cell_hbm, _, blue, red, ids, src, dst, cell, lines, sems):
     ndev = lax.axis_size("rows") * lax.axis_size("edges")
     quarter = lax.axis_index("rows") * lax.axis_size("edges") + lax.axis_index("edges")
     side = quarter % 2
@@ -88,17 +92,22 @@
     low_ids = jnp.concatenate(starts + [pad], axis=0)
     high_ids = jnp.concatenate(ends + [pad], axis=0)
     none = jnp.zeros((ID_ROWS, 128), BF)
-    for msg, ids_of in (
-        (blue, jnp.where(side == 0, low_ids, high_ids)),
-        (red, jnp.where(side == 0, high_ids, low_ids)),
+    for m, (msg, ids_of) in enumerate(
+        (
+            (blue, jnp.where(side == 0, low_ids, high_ids)),
+            (red, jnp.where(side == 0, high_ids, low_ids)),
+        )
     ):
-        msg[SPILL : SPILL + ID_ROWS, 0:128] = ids_of.astype(BF)
-        msg[SPILL : SPILL + ID_ROWS, 128:256] = none
+        lines[m, :, 0:128] = ids_of.astype(BF)
+        lines[m, :, 128:256] = none
+        copy = pltpu.make_async_copy(lines.at[m], msg.at[pl.ds(SPILL, ID_ROWS)], sems.at[5 + m])
+        copy.start()
+        copies.append(copy)
     for copy in copies:
         copy.wait()
 
 
-def field_kernel(p0, p1, p2, p3, t0, to_blue, to_red, field):
+def field_kernel(p0, p1, p2, p3, _, t0, to_blue, to_red, field):
     member = lax.axis_index("edges")
     for k, piece in enumerate((p0, p1, p2, p3)):
         high = piece.shape[0]
@@ -263,18 +272,19 @@
     put_sends(after, to_blue, to_red)
 
 
-def mix_kernel(coef, t0, t1, t2, t3, base):
+def mix_kernel(coef, t0, t1, t2, t3, base, final):
     total = coef[0] * t0[...] + coef[1] * t1[...] + (coef[2] - coef[4]) * t2[...] + coef[3] * t3[...]
     base[...] = total.T
-
-
-def last_kernel(coef, band, base, t3, blue, red, p0, p1, p2, p3, wide, out):
+    final[...] = jnp.full(final.shape, 2.0 * coef[4], F32)
+
+
+def last_kernel(final, band, base, t3, blue, red, p0, p1, p2, p3, wide, out):
     member = lax.axis_index("edges")
     fill_wide(t3[...], blue[...].astype(F32), red[...].astype(F32), wide)
     height = PAIR_ATOMS * ORB
     for pair in range(band.shape[0]):
         span = slice(pair * height, (pair + 1) * height)
-        out[:, span] = base[:, span] + (2.0 * coef[4] * apply_band(band, wide, pair)).T
+        out[:, span] = base[:, span] + (final[0:1, :] * apply_band(band, wide, pair)).T
     for k, piece in enumerate((p0, p1, p2, p3)):
         high = piece.shape[0]
         piece[...] = out[pl.ds(pl.multiple_of((member ^ k) * high, high), high), :].astype(BF)
@@ -298,16 +308,17 @@
     return jax.ShapeDtypeStruct(dims, dtype)
 
 
-def call(kernel, name, outs, scratch, *args, smem=(), in_hbm=(), alias=None, limit=PART):
+def call(kernel, name, outs, scratch, *args, smem=(), in_hbm=(), out_hbm=(), alias=None, limit=PART, micros=1):
     spaces = [SMEM if k in smem else IN_HBM if k in in_hbm else VMEM for k in range(len(args))]
     return pl.pallas_call(
         kernel,
         name=name,
         out_shape=outs,
         in_specs=spaces,
-        out_specs=(VMEM,) * len(outs),
+        out_specs=tuple(IN_HBM if k in out_hbm else VMEM for k in range(len(outs))),
         scratch_shapes=scratch,
         input_output_aliases=alias or {},
+        cost_estimate=pl.CostEstimate(flops=micros * 10**9, bytes_accessed=0, transcendentals=0),
         compiler_params=pltpu.CompilerParams(vmem_limit_bytes=limit),
     )(*args)
 
@@ -340,7 +351,7 @@
         split_kernel,
         "split",
         (piece,) * 4,
-        [pltpu.VMEM((high, ncol), F32), pltpu.SemaphoreType.DMA],
+        [pltpu.VMEM((nedge, high, nrow), F32), pltpu.SemaphoreType.DMA((4,))],
         vectors,
         in_hbm=(0,),
         limit=FULL,
@@ -350,22 +361,20 @@
         message_kernel,
         "message",
         (msg, msg, shape((3,) + lines, F32)),
-        [pltpu.VMEM(lines, jnp.int32)] * 3 + [pltpu.SemaphoreType.DMA((5,))],
+        [pltpu.VMEM(lines, jnp.int32)] * 3
+        + [pltpu.VMEM((2, ID_ROWS, nfeat), BF), pltpu.SemaphoreType.DMA((7,))],
         features,
         edge_src.reshape(lines),
         edge_dst.reshape(lines),
         edge_cell.reshape(lines),
         pieces[0],
         in_hbm=range(5),
+        out_hbm=(0, 1),
         limit=FULL,
+        micros=3,
     )
     blue_msg, red_msg = swap(blue_msg, red_msg)
     full, part = shape((nrow, VEC), F32), shape((HALO, VEC), BF)
-    t0, to_blue, to_red = call(
-        field_kernel, "field", (full, part, part), [pltpu.VMEM((VEC, nrow), F32)], *pieces
-    )
-    blue, red = swap(to_blue, to_red)
-
     band_shape = shape((ATOM_Q // PAIR_ATOMS, PAIR_ATOMS * ORB, WIN_ATOMS * ORB), BF)
     width = w_in.shape[1]
     band, *weights = call(
@@ -378,7 +387,13 @@
         cell_bias,
         w_in,
         w_out,
-    )
+        micros=4,
+    )
+    t0, to_blue, to_red = call(
+        field_kernel, "field", (full, part, part), [pltpu.VMEM((VEC, nrow), F32)], *pieces, weights[1], in_hbm=(4,)
+    )
+    blue, red = swap(to_blue, to_red)
+
     spill_len = 2 * (SPILL + 64)
     (band,) = call(
         spill_kernel,
@@ -402,19 +417,20 @@
         )
         fields.append(following)
     blue, red = swap(to_blue, to_red)
-    (base,) = call(mix_kernel, "mix", (shape((VEC, nrow), F32),), [], cheb_coef, *fields, smem=(0,))
+    base, final = call(
+        mix_kernel, "mix", (shape((VEC, nrow), F32), shape((8, VEC), F32)), [], cheb_coef, *fields, smem=(0,)
+    )
     pieces = call(
         last_kernel,
         "last",
         (piece,) * 4,
         [wide, pltpu.VMEM((VEC, nrow), F32)],
-        cheb_coef,
+        final,
         band,
         base,
         fields[-1],
         blue,
         red,
-        smem=(0,),
     )
     (result,) = call(join_kernel, "join", (shape((high, ncol), F32),), [], *exchange(pieces))
     return result

time: 58.1 us -> 66 us (1.14)
  Pallas kernels: 15.2 us -> 24.4 us
  starting transfers between devices: 18 us -> 13.6 us
  waiting for transfers between devices: 23 us -> 26.1 us
    pallas_call x11, Pallas kernels: 15.2 us -> 24.4 us  [call(): pl.pallas_call(kernel, name=name, out_shape=outs, in_specs=spaces, out_sp...]
    ppermute x5, waiting for transfers between devices: 17.9 us -> 23.8 us  [swap(): lax.ppermute(first, axes, blue_pairs)]
    ppermute x5, starting transfers between devices: 14.1 us -> 8.52 us  [swap(): lax.ppermute(first, axes, blue_pairs)]
    ppermute x6, waiting for transfers between devices: 5.07 us -> 2.31 us  [exchange(): lax.ppermute(pieces[k], 'edges', [(i, i ^ k) for i in range(nedge)])]
    ppermute x6, starting transfers between devices: 3.79 us -> 5.08 us  [exchange(): lax.ppermute(pieces[k], 'edges', [(i, i ^ k) for i in range(nedge)])]
    unnamed x16 -> x14, local copies, waits for them, and re-layouts: 1.41 us -> 1.4 us
  transfers between devices with their start and end apart: 16 -> 16, of which waited for: 6 -> 5; matrix products, arithmetic and copies ran while one was open for 0% -> 0% of each run, Pallas kernels for 13% -> 29%
where the time goes in v4:
time: 66 us; the launch traced here: 65.8 us
  waiting for transfers between devices  26.1 us (40%)
  Pallas kernels  24.4 us (37%)
  starting transfers between devices  13.6 us (21%)
  local copies, waits for them, and re-layouts  1.4 us (2%)
    pallas_call x11, Pallas kernels, call(): pl.pallas_call(kernel, name=name, out_shape=outs, in_specs=spaces, out_sp...  24.4 us
    ppermute x5, waiting for transfers between devices, swap(): lax.ppermute(first, axes, blue_pairs)  23.8 us
    ppermute x5, starting transfers between devices, swap(): lax.ppermute(first, axes, blue_pairs)  8.52 us
    ppermute x6, starting transfers between devices, exchange(): lax.ppermute(pieces[k], 'edges', [(i, i ^ k) for i in range(nedge)])  5.08 us
    ppermute x6, waiting for transfers between devices, exchange(): lax.ppermute(pieces[k], 'edges', [(i, i ^ k) for i in range(nedge)])  2.31 us
    unnamed x14, local copies, waits for them, and re-layouts  1.4 us
  transfers between devices with their start and end apart: 16, of which 5 were waited for; matrix products, arithmetic and copies ran while one was open for 0% of the time, Pallas kernels for 29%

profile of v4, /device:TPU:0, one launch (start us, length us, event | category | flops | bytes accessed | tf_op | source)
XLA Modules:
  0.0 65.8 jit_solution(17574445234418441334)
XLA Ops:
  0.0 1.6 %split.1 = (bf16[32,512]{1,0:T(8,128)(2,1)}, bf16[32,512]{1,0:T(8,128)(2,1)}, bf16[32,512]{1,0:T(8,128)(2,1)}, bf16[32,512]{1,0:T(8,128)(2,1)}) custom-call(f32[32,2048]{1,0:T(8,128)} %vec_hbm.1), custom_call_target="tpu_custom_call" | custom-call | flops 1000000000 | tf_op jit(solution)/shard_map/split/pallas_call | solution.py:313
  1.6 0.5 collective-permute-start
  2.1 2.6 %collective-permute-start.1 = (bf16[32,512]{1,0:T(8,128)(2,1)}, bf16[32,512]{1,0:T(8,128)(2,1)S(1)}, u32[]{:S(2)}, u32[]{:S(2)}) collective-permute-start(bf16[32,512]{1,0:T(8,128)(2,1)} %get-tuple-element.36), channel_id=1, source_target_pairs={{0,2},{1,3},{2,0},{3,1},{4,6},{5,7},{6,4},{7,5},{8,10},{9,11},{10,... | collective-permute-start | bytes 98312 | tf_op jit(solution)/shard_map/ppermute | solution.py:344
  4.7 0.1 collective-permute-start.2
  4.8 11.7 %message.1 = (bf16[336,256]{1,0:T(8,128)(2,1)}, bf16[336,256]{1,0:T(8,128)(2,1)}, f32[3,10,128]{2,1,0:T(8,128)}) custom-call(bf16[1280,256]{1,0:T(8,128)(2,1)} %feat.3, s32[10,128]{1,0:T(8,128)} %bitcast.3, s32[10,128]{1,0:T(8,128)} %bitcast.4, s32[10,128]{1,0:T(8,128)} %bitcast.5, bf16[32,512]{1,0:T(8,128)(2,1)} %get-tuple-element.34._.p0), custom_call_target="tpu_custom_call" | custom-call | flops 3000000000 | tf_op jit(solution)/shard_map/message/pallas_call | solution.py:313
  16.5 0.0 copy-start.3
  16.5 5.7 %collective-permute-start.3 = (bf16[336,256]{1,0:T(8,128)(2,1)}, bf16[336,256]{1,0:T(8,128)(2,1)S(1)}, u32[]{:S(2)}, u32[]{:S(2)}) collective-permute-start(bf16[336,256]{1,0:T(8,128)(2,1)} %get-tuple-element.42), channel_id=1, source_target_pairs={{0,31},{1,2},{2,1},{3,4},{4,3},{5,6},{6,5},{7,8},{8,7},{9,10},{10,... | collective-permute-start | bytes 516104 | tf_op jit(solution)/shard_map/ppermute | solution.py:338
  22.3 0.0 collective-permute-start.4
  22.3 0.0 copy-done
  22.3 0.0 copy-done.1
  22.3 0.7 %copy-done.6 = f32[3,10,128]{2,1,0:T(8,128)S(1)} copy-done((f32[3,10,128]{2,1,0:T(8,128)S(1)}, f32[3,10,128]{2,1,0:T(8,128)}, u32[]{:S(2)}) %copy-start.6) | copy-done | bytes 15384
  23.0 3.7 %own.1 = (bf16[2,256,1024]{2,1,0:T(8,128)(2,1)S(1)}, bf16[512,256]{1,0:T(8,128)(2,1)S(1)}, bf16[512,8]{1,0:T(8,128)(2,1)S(1)}, bf16[256,256]{1,0:T(8,128)(2,1)S(1)}) custom-call(bf16[1280,256]{1,0:T(8,128)(2,1)S(1)} %copy-done, f32[3,10,128]{2,1,0:T(8,128)S(1)} %copy-done.6, bf16[3,512]{1,0:T(4,128)(2,1)S(1)} %copy-done.3, bf16[256,512]{1,0:T(8,128)(2,1)S(1)} %copy-done.1, ...), custom_call_target="tpu_custom_call" | custom-call | flops 4000000000 | tf_op jit(solution)/shard_map/own/pallas_call | solution.py:313
  26.8 0.0 collective-permute-done.p1
  26.8 0.0 collective-permute-done.1.p2
  26.8 0.0 collective-permute-done.2.p3
  26.8 0.2 field.1
  27.0 0.7 %collective-permute-start.5 = (bf16[384,128]{1,0:T(8,128)(2,1)S(1)}, bf16[384,128]{1,0:T(8,128)(2,1)S(1)}, u32[]{:S(2)}, u32[]{:S(2)}) collective-permute-start(bf16[384,128]{1,0:T(8,128)(2,1)S(1)} %get-tuple-element.46), channel_id=1, source_target_pairs={{0,31},{1,2},{2,1},{3,4},{4,3},{5,6},{6,5},{7,8},{8,7},{9,10},{10,... | collective-permute-start | bytes 294920 | tf_op jit(solution)/shard_map/ppermute | solution.py:338
  27.7 0.0 collective-permute-start.6
  27.7 0.0 collective-permute-done.3.blue
  27.7 0.0 collective-permute-done.4.red
  27.7 2.9 %spill.1.band = bf16[2,256,1024]{2,1,0:T(8,128)(2,1)S(1)} custom-call(bf16[2,256,1024]{2,1,0:T(8,128)(2,1)S(1)} %get-tuple-element.41.own_band, bf16[336,256]{1,0:T(8,128)(2,1)S(1)} %collective-permute-done.3.blue, bf16[336,256]{1,0:T(8,128)(2,1)S(1)} %collective-permute-done.4.red, ...), custom_call_target="tpu_custom_call", output_to_operand_aliasing={{}: (0, {})} | custom-call | flops 1000000000 | tf_op jit(solution)/shard_map/spill/pallas_call | solution.py:313
  30.7 4.2 %collective-permute-done.5.blue = bf16[384,128]{1,0:T(8,128)(2,1)S(1)} collective-permute-done((bf16[384,128]{1,0:T(8,128)(2,1)S(1)}, bf16[384,128]{1,0:T(8,128)(2,1)S(1)}, u32[]{:S(2)}, u32[]{:S(2)}) %collective-permute-start.5) | collective-permute-done | bytes 98336 | tf_op jit(solution)/shard_map/ppermute | solution.py:338
  34.8 0.0 collective-permute-done.6.red
  34.8 0.7 %first.1 = (f32[512,128]{1,0:T(8,128)S(1)}, bf16[384,128]{1,0:T(8,128)(2,1)S(1)}, bf16[384,128]{1,0:T(8,128)(2,1)S(1)}) custom-call(bf16[2,256,1024]{2,1,0:T(8,128)(2,1)S(1)} %spill.1.band, f32[512,128]{1,0:T(8,128)S(1)} %get-tuple-element.40.t0.before, bf16[384,128]{1,0:T(8,128)(2,1)S(1)} %collective-permute-done.5.blue, ...), custom_call_target="tpu_custom_call" | custom-call | flops 1000000000 | tf_op jit(solution)/shard_map/first/pallas_call | solution.py:313
  35.5 0.6 collective-permute-start.7
  36.2 0.0 collective-permute-start.8
  36.2 7.1 %collective-permute-done.7.blue = bf16[384,128]{1,0:T(8,128)(2,1)S(1)} collective-permute-done((bf16[384,128]{1,0:T(8,128)(2,1)S(1)}, bf16[384,128]{1,0:T(8,128)(2,1)S(1)}, u32[]{:S(2)}, u32[]{:S(2)}) %collective-permute-start.7) | collective-permute-done | bytes 98336 | tf_op jit(solution)/shard_map/ppermute | solution.py:338
  43.2 0.0 collective-permute-done.8.red
  43.2 0.7 %next.2 = (f32[512,128]{1,0:T(8,128)S(1)}, bf16[384,128]{1,0:T(8,128)(2,1)S(1)}, bf16[384,128]{1,0:T(8,128)(2,1)S(1)}) custom-call(bf16[2,256,1024]{2,1,0:T(8,128)(2,1)S(1)} %spill.1.band, f32[512,128]{1,0:T(8,128)S(1)} %get-tuple-element.40.t0.before, f32[512,128]{1,0:T(8,128)S(1)} %get-tuple-element.48.now.before.t1, ...), custom_call_target="tpu_custom_call" | custom-call | flops 1000000000 | tf_op jit(solution)/shard_map/next/pallas_call | solution.py:313
  43.9 0.7 %collective-permute-start.9 = (bf16[384,128]{1,0:T(8,128)(2,1)S(1)}, bf16[384,128]{1,0:T(8,128)(2,1)S(1)}, u32[]{:S(2)}, u32[]{:S(2)}) collective-permute-start(bf16[384,128]{1,0:T(8,128)(2,1)S(1)} %get-tuple-element.52), channel_id=1, source_target_pairs={{0,31},{1,2},{2,1},{3,4},{4,3},{5,6},{6,5},{7,8},{8,7},{9,10},{10,... | collective-permute-start | bytes 294920 | tf_op jit(solution)/shard_map/ppermute | solution.py:338
  44.7 0.0 collective-permute-start.10
  44.7 7.0 %collective-permute-done.9.blue = bf16[384,128]{1,0:T(8,128)(2,1)S(1)} collective-permute-done((bf16[384,128]{1,0:T(8,128)(2,1)S(1)}, bf16[384,128]{1,0:T(8,128)(2,1)S(1)}, u32[]{:S(2)}, u32[]{:S(2)}) %collective-permute-start.9) | collective-permute-done | bytes 98336 | tf_op jit(solution)/shard_map/ppermute | solution.py:338
  51.6 0.0 collective-permute-done.10.red
  51.6 0.7 %next.3 = (f32[512,128]{1,0:T(8,128)S(1)}, bf16[384,128]{1,0:T(8,128)(2,1)S(1)}, bf16[384,128]{1,0:T(8,128)(2,1)S(1)}) custom-call(bf16[2,256,1024]{2,1,0:T(8,128)(2,1)S(1)} %spill.1.band, f32[512,128]{1,0:T(8,128)S(1)} %get-tuple-element.48.now.before.t1, f32[512,128]{1,0:T(8,128)S(1)} %get-tuple-element.51.now.t2, ...), custom_call_target="tpu_custom_call" | custom-call | flops 1000000000 | tf_op jit(solution)/shard_map/next/pallas_call | solution.py:313
  52.3 0.7 %collective-permute-start.11 = (bf16[384,128]{1,0:T(8,128)(2,1)S(1)}, bf16[384,128]{1,0:T(8,128)(2,1)S(1)}, u32[]{:S(2)}, u32[]{:S(2)}) collective-permute-start(bf16[384,128]{1,0:T(8,128)(2,1)S(1)} %get-tuple-element.57), channel_id=1, source_target_pairs={{0,31},{1,2},{2,1},{3,4},{4,3},{5,6},{6,5},{7,8},{8,7},{9,10},{10,... | collective-permute-start | bytes 294920 | tf_op jit(solution)/shard_map/ppermute | solution.py:338
  53.1 0.0 collective-permute-start.12
  53.1 0.7 copy-done.4
  53.7 0.7 %mix.1 = (f32[128,512]{1,0:T(8,128)S(1)}, f32[8,128]{1,0:T(8,128)S(1)}) custom-call(f32[5]{0:T(128)S(1)} %copy-done.4, f32[512,128]{1,0:T(8,128)S(1)} %get-tuple-element.40.t0.before, f32[512,128]{1,0:T(8,128)S(1)} %get-tuple-element.48.now.before.t1, f32[512,128]{1,0:T(8,128)S(1)} %get-tuple-element.51.now.t2, f32[512,128]{1,0:T(8,128)S(1)} %get-tuple-element.54.t3), custom_call_target="tpu_custom_call" | custom-call | flops 1000000000 | tf_op jit(solution)/shard_map/mix/pallas_call | solution.py:313
  54.4 5.6 %collective-permute-done.11.blue = bf16[384,128]{1,0:T(8,128)(2,1)S(1)} collective-permute-done((bf16[384,128]{1,0:T(8,128)(2,1)S(1)}, bf16[384,128]{1,0:T(8,128)(2,1)S(1)}, u32[]{:S(2)}, u32[]{:S(2)}) %collective-permute-start.11) | collective-permute-done | bytes 98336 | tf_op jit(solution)/shard_map/ppermute | solution.py:338
  60.0 0.0 collective-permute-done.12.red
  60.0 0.7 %last.1 = (bf16[32,512]{1,0:T(8,128)(2,1)S(1)}, bf16[32,512]{1,0:T(8,128)(2,1)S(1)}, bf16[32,512]{1,0:T(8,128)(2,1)S(1)}, bf16[32,512]{1,0:T(8,128)(2,1)S(1)}) custom-call(f32[8,128]{1,0:T(8,128)S(1)} %get-tuple-element.55.final, bf16[2,256,1024]{2,1,0:T(8,128)(2,1)S(1)} %spill.1.band, f32[128,512]{1,0:T(8,128)S(1)} %get-tuple-element.56.base, ...), custom_call_target="tpu_custom_call" | custom-call | flops 1000000000 | tf_op jit(solution)/shard_map/last/pallas_call | solution.py:313
  60.8 0.1 collective-permute-start.13
  60.9 0.1 collective-permute-start.14
  61.0 1.8 %collective-permute-start.15 = (bf16[32,512]{1,0:T(8,128)(2,1)S(1)}, bf16[32,512]{1,0:T(8,128)(2,1)S(1)}, u32[]{:S(2)}, u32[]{:S(2)}) collective-permute-start(bf16[32,512]{1,0:T(8,128)(2,1)S(1)} %get-tuple-element.62), channel_id=1, source_target_pairs={{0,3},{1,2},{2,1},{3,0},{4,7},{5,6},{6,5},{7,4},{8,11},{9,10},{10,... | collective-permute-start | bytes 98312 | tf_op jit(solution)/shard_map/ppermute | solution.py:344
  62.7 0.0 collective-permute-done.13.p1
  62.7 2.3 %collective-permute-done.14.p2 = bf16[32,512]{1,0:T(8,128)(2,1)S(1)} collective-permute-done((bf16[32,512]{1,0:T(8,128)(2,1)S(1)}, bf16[32,512]{1,0:T(8,128)(2,1)S(1)}, u32[]{:S(2)}, u32[]{:S(2)}) %collective-permute-start.14) | collective-permute-done | bytes 32800 | tf_op jit(solution)/shard_map/ppermute | solution.py:344
  65.0 0.0 collective-permute-done.15.p3
  65.0 0.7 %join.1 = f32[32,2048]{1,0:T(8,128)} custom-call(bf16[32,512]{1,0:T(8,128)(2,1)S(1)} %get-tuple-element.59.p0, bf16[32,512]{1,0:T(8,128)(2,1)S(1)} %collective-permute-done.13.p1, bf16[32,512]{1,0:T(8,128)(2,1)S(1)} %collective-permute-done.14.p2, bf16[32,512]{1,0:T(8,128)(2,1)S(1)} %collective-permute-done.15.p3), custom_call_target="tpu_custom_call" | custom-call | flops 1000000000 | tf_op jit(solution)/shard_map/join/pallas_call | solution.py:313
  (9 shorter events, 0.0 us)
Async XLA Ops:
  1.6 25.2 %collective-permute-start = (bf16[32,512]{1,0:T(8,128)(2,1)}, bf16[32,512]{1,0:T(8,128)(2,1)S(1)}, u32[]{:S(2)}, u32[]{:S(2)}) collective-permute-start(bf16[32,512]{1,0:T(8,128)(2,1)} %get-tuple-element.35), channel_id=1, source_target_pairs={{0,1},{1,0},{2,3},{3,2},{4,5},{5,4},{6,7},{7,6},{8,9},{9,8},{10,11... | collective-permute-start | bytes 98312 | tf_op jit(solution)/shard_map/ppermute | solution.py:344
  2.1 24.6 %collective-permute-start.1 = (bf16[32,512]{1,0:T(8,128)(2,1)}, bf16[32,512]{1,0:T(8,128)(2,1)S(1)}, u32[]{:S(2)}, u32[]{:S(2)}) collective-permute-start(bf16[32,512]{1,0:T(8,128)(2,1)} %get-tuple-element.36), channel_id=1, source_target_pairs={{0,2},{1,3},{2,0},{3,1},{4,6},{5,7},{6,4},{7,5},{8,10},{9,11},{10,... | collective-permute-start | bytes 98312 | tf_op jit(solution)/shard_map/ppermute | solution.py:344
  4.7 22.1 %collective-permute-start.2 = (bf16[32,512]{1,0:T(8,128)(2,1)}, bf16[32,512]{1,0:T(8,128)(2,1)S(1)}, u32[]{:S(2)}, u32[]{:S(2)}) collective-permute-start(bf16[32,512]{1,0:T(8,128)(2,1)} %get-tuple-element.37), channel_id=1, source_target_pairs={{0,3},{1,2},{2,1},{3,0},{4,7},{5,6},{6,5},{7,4},{8,11},{9,10},{10,... | collective-permute-start | bytes 98312 | tf_op jit(solution)/shard_map/ppermute | solution.py:344
  4.8 17.5 %copy-start = (bf16[1280,256]{1,0:T(8,128)(2,1)S(1)}, bf16[1280,256]{1,0:T(8,128)(2,1)}, u32[]{:S(2)}) copy-start(bf16[1280,256]{1,0:T(8,128)(2,1)} %feat.3) | copy-start | bytes 1966084
  4.8 17.5 %copy-start.1 = (bf16[256,512]{1,0:T(8,128)(2,1)S(1)}, bf16[256,512]{1,0:T(8,128)(2,1)}, u32[]{:S(2)}) copy-start(bf16[256,512]{1,0:T(8,128)(2,1)} %w_in.1) | copy-start | bytes 786436
  4.8 17.5 %copy-start.2 = (bf16[256,256]{1,0:T(8,128)(2,1)S(1)}, bf16[256,256]{1,0:T(8,128)(2,1)}, u32[]{:S(2)}) copy-start(bf16[256,256]{1,0:T(8,128)(2,1)} %w_out.1) | copy-start | bytes 393220
  16.5 5.8 %copy-start.3 = (bf16[3,512]{1,0:T(4,128)(2,1)S(1)}, bf16[3,512]{1,0:T(4,128)(2,1)}, u32[]{:S(2)}) copy-start(bf16[3,512]{1,0:T(4,128)(2,1)} %cell_bias.1) | copy-start | bytes 9220
  16.5 11.2 %collective-permute-start.3 = (bf16[336,256]{1,0:T(8,128)(2,1)}, bf16[336,256]{1,0:T(8,128)(2,1)S(1)}, u32[]{:S(2)}, u32[]{:S(2)}) collective-permute-start(bf16[336,256]{1,0:T(8,128)(2,1)} %get-tuple-element.42), channel_id=1, source_target_pairs={{0,31},{1,2},{2,1},{3,4},{4,3},{5,6},{6,5},{7,8},{8,7},{9,10},{10,... | collective-permute-start | bytes 516104 | tf_op jit(solution)/shard_map/ppermute | solution.py:338
  22.3 5.5 %collective-permute-start.4 = (bf16[336,256]{1,0:T(8,128)(2,1)}, bf16[336,256]{1,0:T(8,128)(2,1)S(1)}, u32[]{:S(2)}, u32[]{:S(2)}) collective-permute-start(bf16[336,256]{1,0:T(8,128)(2,1)} %get-tuple-element.43), channel_id=1, source_target_pairs={{0,1},{1,0},{2,3},{3,2},{4,5},{5,4},{6,7},{7,6},{8,9},{9,8},{10,11... | collective-permute-start | bytes 516104 | tf_op jit(solution)/shard_map/ppermute | solution.py:339
  22.3 0.7 %copy-start.6 = (f32[3,10,128]{2,1,0:T(8,128)S(1)}, f32[3,10,128]{2,1,0:T(8,128)}, u32[]{:S(2)}) copy-start(f32[3,10,128]{2,1,0:T(8,128)} %get-tuple-element.38.ids) | copy-start | bytes 46084
  23.0 3.8 %copy-start.5 = (bf16[32,512]{1,0:T(8,128)(2,1)S(1)}, bf16[32,512]{1,0:T(8,128)(2,1)}, u32[]{:S(2)}) copy-start(bf16[32,512]{1,0:T(8,128)(2,1)} %get-tuple-element.34._.p0) | copy-start | bytes 98308
  27.0 7.8 %collective-permute-start.5 = (bf16[384,128]{1,0:T(8,128)(2,1)S(1)}, bf16[384,128]{1,0:T(8,128)(2,1)S(1)}, u32[]{:S(2)}, u32[]{:S(2)}) collective-permute-start(bf16[384,128]{1,0:T(8,128)(2,1)S(1)} %get-tuple-element.46), channel_id=1, source_target_pairs={{0,31},{1,2},{2,1},{3,4},{4,3},{5,6},{6,5},{7,8},{8,7},{9,10},{10,... | collective-permute-start | bytes 294920 | tf_op jit(solution)/shard_map/ppermute | solution.py:338
  27.7 7.1 %collective-permute-start.6 = (bf16[384,128]{1,0:T(8,128)(2,1)S(1)}, bf16[384,128]{1,0:T(8,128)(2,1)S(1)}, u32[]{:S(2)}, u32[]{:S(2)}) collective-permute-start(bf16[384,128]{1,0:T(8,128)(2,1)S(1)} %get-tuple-element.47), channel_id=1, source_target_pairs={{0,1},{1,0},{2,3},{3,2},{4,5},{5,4},{6,7},{7,6},{8,9},{9,8},{10,11... | collective-permute-start | bytes 294920 | tf_op jit(solution)/shard_map/ppermute | solution.py:339
  35.5 7.7 %collective-permute-start.7 = (bf16[384,128]{1,0:T(8,128)(2,1)S(1)}, bf16[384,128]{1,0:T(8,128)(2,1)S(1)}, u32[]{:S(2)}, u32[]{:S(2)}) collective-permute-start(bf16[384,128]{1,0:T(8,128)(2,1)S(1)} %get-tuple-element.49), channel_id=1, source_target_pairs={{0,31},{1,2},{2,1},{3,4},{4,3},{5,6},{6,5},{7,8},{8,7},{9,10},{10,... | collective-permute-start | bytes 294920 | tf_op jit(solution)/shard_map/ppermute | solution.py:338
  36.2 7.1 %collective-permute-start.8 = (bf16[384,128]{1,0:T(8,128)(2,1)S(1)}, bf16[384,128]{1,0:T(8,128)(2,1)S(1)}, u32[]{:S(2)}, u32[]{:S(2)}) collective-permute-start(bf16[384,128]{1,0:T(8,128)(2,1)S(1)} %get-tuple-element.50), channel_id=1, source_target_pairs={{0,1},{1,0},{2,3},{3,2},{4,5},{5,4},{6,7},{7,6},{8,9},{9,8},{10,11... | collective-permute-start | bytes 294920 | tf_op jit(solution)/shard_map/ppermute | solution.py:339
  43.9 7.7 %collective-permute-start.9 = (bf16[384,128]{1,0:T(8,128)(2,1)S(1)}, bf16[384,128]{1,0:T(8,128)(2,1)S(1)}, u32[]{:S(2)}, u32[]{:S(2)}) collective-permute-start(bf16[384,128]{1,0:T(8,128)(2,1)S(1)} %get-tuple-element.52), channel_id=1, source_target_pairs={{0,31},{1,2},{2,1},{3,4},{4,3},{5,6},{6,5},{7,8},{8,7},{9,10},{10,... | collective-permute-start | bytes 294920 | tf_op jit(solution)/shard_map/ppermute | solution.py:338
  44.7 7.0 %collective-permute-start.10 = (bf16[384,128]{1,0:T(8,128)(2,1)S(1)}, bf16[384,128]{1,0:T(8,128)(2,1)S(1)}, u32[]{:S(2)}, u32[]{:S(2)}) collective-permute-start(bf16[384,128]{1,0:T(8,128)(2,1)S(1)} %get-tuple-element.53), channel_id=1, source_target_pairs={{0,1},{1,0},{2,3},{3,2},{4,5},{5,4},{6,7},{7,6},{8,9},{9,8},{10,11... | collective-permute-start | bytes 294920 | tf_op jit(solution)/shard_map/ppermute | solution.py:339
  52.3 7.7 %collective-permute-start.11 = (bf16[384,128]{1,0:T(8,128)(2,1)S(1)}, bf16[384,128]{1,0:T(8,128)(2,1)S(1)}, u32[]{:S(2)}, u32[]{:S(2)}) collective-permute-start(bf16[384,128]{1,0:T(8,128)(2,1)S(1)} %get-tuple-element.57), channel_id=1, source_target_pairs={{0,31},{1,2},{2,1},{3,4},{4,3},{5,6},{6,5},{7,8},{8,7},{9,10},{10,... | collective-permute-start | bytes 294920 | tf_op jit(solution)/shard_map/ppermute | solution.py:338
  53.1 0.7 copy-start.4
  53.1 7.0 %collective-permute-start.12 = (bf16[384,128]{1,0:T(8,128)(2,1)S(1)}, bf16[384,128]{1,0:T(8,128)(2,1)S(1)}, u32[]{:S(2)}, u32[]{:S(2)}) collective-permute-start(bf16[384,128]{1,0:T(8,128)(2,1)S(1)} %get-tuple-element.58), channel_id=1, source_target_pairs={{0,1},{1,0},{2,3},{3,2},{4,5},{5,4},{6,7},{7,6},{8,9},{9,8},{10,11... | collective-permute-start | bytes 294920 | tf_op jit(solution)/shard_map/ppermute | solution.py:339
  60.8 1.9 %collective-permute-start.13 = (bf16[32,512]{1,0:T(8,128)(2,1)S(1)}, bf16[32,512]{1,0:T(8,128)(2,1)S(1)}, u32[]{:S(2)}, u32[]{:S(2)}) collective-permute-start(bf16[32,512]{1,0:T(8,128)(2,1)S(1)} %get-tuple-element.60), channel_id=1, source_target_pairs={{0,1},{1,0},{2,3},{3,2},{4,5},{5,4},{6,7},{7,6},{8,9},{9,8},{10,11... | collective-permute-start | bytes 98312 | tf_op jit(solution)/shard_map/ppermute | solution.py:344
  60.9 4.2 %collective-permute-start.14 = (bf16[32,512]{1,0:T(8,128)(2,1)S(1)}, bf16[32,512]{1,0:T(8,128)(2,1)S(1)}, u32[]{:S(2)}, u32[]{:S(2)}) collective-permute-start(bf16[32,512]{1,0:T(8,128)(2,1)S(1)} %get-tuple-element.61), channel_id=1, source_target_pairs={{0,2},{1,3},{2,0},{3,1},{4,6},{5,7},{6,4},{7,5},{8,10},{9,11},{10,... | collective-permute-start | bytes 98312 | tf_op jit(solution)/shard_map/ppermute | solution.py:344
  61.0 4.1 %collective-permute-start.15 = (bf16[32,512]{1,0:T(8,128)(2,1)S(1)}, bf16[32,512]{1,0:T(8,128)(2,1)S(1)}, u32[]{:S(2)}, u32[]{:S(2)}) collective-permute-start(bf16[32,512]{1,0:T(8,128)(2,1)S(1)} %get-tuple-element.62), channel_id=1, source_target_pairs={{0,3},{1,2},{2,1},{3,0},{4,7},{5,6},{6,5},{7,4},{8,11},{9,10},{10,... | collective-permute-start | bytes 98312 | tf_op jit(solution)/shard_map/ppermute | solution.py:344

commit v5 on v4

--- a/solution.py
+++ b/solution.py
@@ -38,6 +38,18 @@
     return (lax.axis_index("rows") * lax.axis_size("edges") + lax.axis_index("edges")) % 2
 
 
+def edge_ids(src, dst, cell):
+    ndev = lax.axis_size("rows") * lax.axis_size("edges")
+    quarter = lax.axis_index("rows") * lax.axis_size("edges") + lax.axis_index("edges")
+    natom = ATOM_Q * ndev
+    ntiles = natom // TILE_ATOMS
+    rel = src - quarter * ATOM_Q
+    rel = jnp.where(rel > natom // 2, rel - natom, jnp.where(rel < -(natom // 2), rel + natom, rel))
+    shift = (dst >> 3) - (src >> 3) + BAND
+    shift = jnp.where(shift < 0, shift + ntiles, jnp.where(shift >= ntiles, shift - ntiles, shift))
+    return [x.astype(F32) for x in (rel, shift * TILE_ATOMS + (dst & 7), cell)]
+
+
 def split_kernel(vec_hbm, p0, p1, p2, p3, vectors, sems):
     member = lax.axis_index("edges")
     pieces = (p0, p1, p2, p3)
@@ -53,10 +65,8 @@
         pieces[k][...] = vectors[k].astype(BF)
 
 
-def message_kernel(feat, src_hbm, dst_hbm, cell_hbm, _, blue, red, ids, src, dst, cell, lines, sems):
-    ndev = lax.axis_size("rows") * lax.axis_size("edges")
-    quarter = lax.axis_index("rows") * lax.axis_size("edges") + lax.axis_index("edges")
-    side = quarter % 2
+def message_kernel(feat, src_hbm, dst_hbm, cell_hbm, _, blue, red, src, dst, cell, sems):
+    side = device_side()
     high = feat.shape[0] - SPILL
     off = pl.multiple_of(side * high, 64)
     copies = [
@@ -73,15 +83,7 @@
         copy.start()
     for copy in loads:
         copy.wait()
-    natom = ATOM_Q * ndev
-    ntiles = natom // TILE_ATOMS
-    rel = src[...] - quarter * ATOM_Q
-    rel = jnp.where(rel > natom // 2, rel - natom, jnp.where(rel < -(natom // 2), rel + natom, rel))
-    shift = (dst[...] >> 3) - (src[...] >> 3) + BAND
-    shift = jnp.where(shift < 0, shift + ntiles, jnp.where(shift >= ntiles, shift - ntiles, shift))
-    three = [x.astype(F32) for x in (rel, shift * TILE_ATOMS + (dst[...] & 7), cell[...])]
-    for k in range(3):
-        ids[k] = three[k]
+    three = edge_ids(src[...], dst[...], cell[...])
     lane, line = iota((3, 128), 1), iota((3, 128), 0)
     nrow = src.shape[0]
     starts = [x[0:3] for x in three]
@@ -92,22 +94,17 @@
     low_ids = jnp.concatenate(starts + [pad], axis=0)
     high_ids = jnp.concatenate(ends + [pad], axis=0)
     none = jnp.zeros((ID_ROWS, 128), BF)
-    for m, (msg, ids_of) in enumerate(
-        (
-            (blue, jnp.where(side == 0, low_ids, high_ids)),
-            (red, jnp.where(side == 0, high_ids, low_ids)),
-        )
+    for msg, ids_of in (
+        (blue, jnp.where(side == 0, low_ids, high_ids)),
+        (red, jnp.where(side == 0, high_ids, low_ids)),
     ):
-        lines[m, :, 0:128] = ids_of.astype(BF)
-        lines[m, :, 128:256] = none
-        copy = pltpu.make_async_copy(lines.at[m], msg.at[pl.ds(SPILL, ID_ROWS)], sems.at[5 + m])
-        copy.start()
-        copies.append(copy)
+        msg[SPILL : SPILL + ID_ROWS, 0:128] = ids_of.astype(BF)
+        msg[SPILL : SPILL + ID_ROWS, 128:256] = none
     for copy in copies:
         copy.wait()
 
 
-def field_kernel(p0, p1, p2, p3, _, t0, to_blue, to_red, field):
+def field_kernel(p0, p1, p2, p3, t0, to_blue, to_red, field):
     member = lax.axis_index("edges")
     for k, piece in enumerate((p0, p1, p2, p3)):
         high = piece.shape[0]
@@ -117,11 +114,16 @@
 
 
 def pair_blocks(x, cell, w_in_t, bias_t, w_out_t):
-    cell1 = (iota((8, x.shape[0]), 0).astype(F32) == cell).astype(BF)
-    pre = nt_dot(w_in_t, x) + jnp.dot(bias_t, cell1, preferred_element_type=F32)
+    bias = [bias_t[:, k : k + 1].astype(F32) for k in range(3)]
+    pre = nt_dot(w_in_t[...], x)
+    pre = pre + jnp.where(cell == 1.0, bias[1], jnp.where(cell == 2.0, bias[2], bias[0]))
     gate, up = pre[:HID], pre[HID:]
     hidden = (gate * (0.5 + 0.5 * jnp.tanh(0.5 * gate)) * up).astype(BF)
-    return jnp.dot(w_out_t, hidden, preferred_element_type=F32).astype(BF)
+    return jnp.dot(w_out_t[...], hidden, preferred_element_type=F32).astype(BF)
+
+
+def row_of(x):
+    return jnp.concatenate([x[k : k + 1] for k in range(x.shape[0])], axis=1)
 
 
 def dense_of(blocks, atom, target, first):
@@ -158,7 +160,7 @@
     return jnp.floor(atom * (1.0 / TILE_ATOMS)) - 2.0 * jnp.floor(atom * (0.5 / TILE_ATOMS))
 
 
-def own_kernel(feat, ids, cell_bias, w_in, w_out, band, w_in_t, bias_t, w_out_t, blk, bias8, rows):
+def own_kernel(feat, src, dst, cell, cell_bias, w_in, w_out, band, w_in_t, bias_t, w_out_t, blk, bias8, rows):
     nfeat, width = w_in.shape
     nblk = w_out.shape[1]
     eye = (iota((width, width), 0) == iota((width, width), 1)).astype(BF)
@@ -170,15 +172,11 @@
     swap = (col == (row % ORB) * ORB + row // ORB).astype(BF)
     w_out_t[...] = nt_dot(swap, w_out[...]).astype(BF)
     own = feat.shape[0]
-    for lo in range(0, own, 256):
-        span = slice(lo, lo + 256)
-        line = lo // 128
-        a, b, c = [
-            jnp.concatenate([ids[k, line : line + 1], ids[k, line + 1 : line + 2]], axis=1) for k in range(3)
-        ]
-        blk[:, span] = pair_blocks(feat[span, :], c, w_in_t[...], bias_t[...], w_out_t[...])
-        rows[0:1, span] = a
-        rows[1:2, span] = b + TILE_ATOMS * odd_tile(a)
+    ids = edge_ids(src[...], dst[...], cell[...])
+    atom = row_of(ids[0])
+    rows[0:1, :] = atom
+    rows[1:2, :] = row_of(ids[1]) + TILE_ATOMS * odd_tile(atom)
+    blk[...] = pair_blocks(feat[...], row_of(ids[2]), w_in_t, bias_t, w_out_t)
     for first in range(0, ATOM_Q, GROUP):
         start = jnp.sum((ids[0] < float(first)).astype(F32)).astype(jnp.int32)
         at = pl.multiple_of(jnp.minimum(start // 128 * 128, own - GROUP_SPAN), 128)
@@ -196,29 +194,23 @@
         spill[base + rows - 64 : base + rows, :] = jnp.zeros((64, nfeat), BF)
         at = pl.multiple_of(base + jnp.where(gap, 64, 0), 64)
         spill[pl.ds(at, SPILL), :] = msg[0:SPILL, :]
-    lines, ends = [], []
+    ids, ends = [], []
     for msg in (blue, red):
         block = msg[SPILL : SPILL + ID_ROWS, 0:128].astype(F32)
-        lines.extend([[block[3 * k + n : 3 * k + n + 1] for k in range(3)] for n in range(3)])
         a = block[0:3]
         mine = (a >= 0.0) & (a < float(ATOM_Q))
+        ids.append([row_of(block[3 * k : 3 * k + 3]) for k in range(3)])
         ends.append(
             (
                 jnp.min(jnp.where(mine, a, float(ATOM_Q))).astype(jnp.int32),
                 jnp.max(jnp.where(mine, a, -1.0)).astype(jnp.int32),
             )
         )
-    for lo in range(0, 2 * rows, 256):
-        both = lines[lo // 128 : lo // 128 + 2]
-        cell = jnp.concatenate([x[2] for x in both], axis=1)
-        blk[:, lo : lo + 256] = pair_blocks(
-            spill[lo : lo + 256, :], cell, w_in_t[...], bias_t[...], w_out_t[...]
-        )
+    cells = jnp.concatenate([x[2] for x in ids], axis=1)
+    blk[...] = pair_blocks(spill[...], cells, w_in_t, bias_t, w_out_t)
     band[...] = own_band[...]
     for m in range(2):
-        mine = lines[3 * m : 3 * m + 3]
-        atom = jnp.concatenate([x[0] for x in mine], axis=1)
-        target = jnp.concatenate([x[1] for x in mine], axis=1) + TILE_ATOMS * odd_tile(atom)
+        atom, target = ids[m][0], ids[m][1] + TILE_ATOMS * odd_tile(ids[m][0])
         lowest, highest = ends[m]
         for first in range(0, ATOM_Q, GROUP):
 
@@ -347,6 +339,7 @@
     msg = shape((SPILL + ID_ROWS, nfeat), BF)
     piece = shape((high, nrow), BF)
     lines = (nown // 128, 128)
+    edges = [x.reshape(lines) for x in (edge_src, edge_dst, edge_cell)]
     pieces = call(
         split_kernel,
         "split",
@@ -357,19 +350,16 @@
         limit=FULL,
     )
     pieces = exchange(pieces)
-    blue_msg, red_msg, ids = call(
+    blue_msg, red_msg = call(
         message_kernel,
         "message",
-        (msg, msg, shape((3,) + lines, F32)),
+        (msg, msg),
         [pltpu.VMEM(lines, jnp.int32)] * 3
-        + [pltpu.VMEM((2, ID_ROWS, nfeat), BF), pltpu.SemaphoreType.DMA((7,))],
+        + [pltpu.SemaphoreType.DMA((5,))],
         features,
-        edge_src.reshape(lines),
-        edge_dst.reshape(lines),
-        edge_cell.reshape(lines),
+        *edges,
         pieces[0],
         in_hbm=range(5),
-        out_hbm=(0, 1),
         limit=FULL,
         micros=3,
     )
@@ -383,14 +373,14 @@
         (band_shape, shape((width, nfeat), BF), shape((width, 8), BF), shape((ORB * ORB, HID), BF)),
         [pltpu.VMEM((ORB * ORB, nown), BF), pltpu.VMEM((8, width), F32), pltpu.VMEM((8, nown), F32)],
         features,
-        ids,
+        *edges,
         cell_bias,
         w_in,
         w_out,
         micros=4,
     )
     t0, to_blue, to_red = call(
-        field_kernel, "field", (full, part, part), [pltpu.VMEM((VEC, nrow), F32)], *pieces, weights[1], in_hbm=(4,)
+        field_kernel, "field", (full, part, part), [pltpu.VMEM((VEC, nrow), F32)], *pieces
     )
     blue, red = swap(to_blue, to_red)
 

time: 66 us -> 51.7 us (0.78)
  Pallas kernels: 24.4 us -> 12.3 us
  waiting for transfers between devices: 26.1 us -> 17.8 us
  starting transfers between devices: 13.6 us -> 20.5 us
    pallas_call x11, Pallas kernels: 24.4 us -> 12.3 us  [call(): pl.pallas_call(kernel, name=name, out_shape=outs, in_specs=spaces, out_sp...]
    ppermute x5, waiting for transfers between devices: 23.8 us -> 15.4 us  [swap(): lax.ppermute(first, axes, blue_pairs)]
    ppermute x5, starting transfers between devices: 8.52 us -> 15.2 us  [swap(): lax.ppermute(first, axes, blue_pairs)]
    unnamed x14 -> x18, local copies, waits for them, and re-layouts: 1.4 us -> 0.81 us
  transfers between devices with their start and end apart: 16 -> 16, of which waited for: 5 -> 6; matrix products, arithmetic and copies ran while one was open for 0% -> 0% of each run, Pallas kernels for 29% -> 14%
where the time goes in v5:
time: 51.7 us; the launch traced here: 51.5 us
  starting transfers between devices  20.5 us (40%)
  waiting for transfers between devices  17.8 us (34%)
  Pallas kernels  12.3 us (24%)
  local copies, waits for them, and re-layouts  0.81 us (2%)
    ppermute x5, waiting for transfers between devices, swap(): lax.ppermute(first, axes, blue_pairs)  15.4 us
    ppermute x5, starting transfers between devices, swap(): lax.ppermute(first, axes, blue_pairs)  15.2 us
    pallas_call x11, Pallas kernels, call(): pl.pallas_call(kernel, name=name, out_shape=outs, in_specs=spaces, out_sp...  12.3 us
    ppermute x6, starting transfers between devices, exchange(): lax.ppermute(pieces[k], 'edges', [(i, i ^ k) for i in range(nedge)])  5.08 us
    ppermute x6, waiting for transfers between devices, exchange(): lax.ppermute(pieces[k], 'edges', [(i, i ^ k) for i in range(nedge)])  2.31 us
  transfers between devices with their start and end apart: 16, of which 6 were waited for; matrix products, arithmetic and copies ran while one was open for 0% of the time, Pallas kernels for 14%

profile of v5, /device:TPU:0, one launch (start us, length us, event | category | flops | bytes accessed | tf_op | source)
XLA Modules:
  0.0 51.5 jit_solution(2290563606638027039)
XLA Ops:
  0.0 1.6 %split.1 = (bf16[32,512]{1,0:T(8,128)(2,1)}, bf16[32,512]{1,0:T(8,128)(2,1)}, bf16[32,512]{1,0:T(8,128)(2,1)}, bf16[32,512]{1,0:T(8,128)(2,1)}) custom-call(f32[32,2048]{1,0:T(8,128)} %vec_hbm.1), custom_call_target="tpu_custom_call" | custom-call | flops 1000000000 | tf_op jit(solution)/shard_map/split/pallas_call | solution.py:305
  1.6 0.5 %collective-permute-start = (bf16[32,512]{1,0:T(8,128)(2,1)}, bf16[32,512]{1,0:T(8,128)(2,1)S(1)}, u32[]{:S(2)}, u32[]{:S(2)}) collective-permute-start(bf16[32,512]{1,0:T(8,128)(2,1)} %get-tuple-element.34), channel_id=1, source_target_pairs={{0,1},{1,0},{2,3},{3,2},{4,5},{5,4},{6,7},{7,6},{8,9},{9,8},{10,11... | collective-permute-start | bytes 98312 | tf_op jit(solution)/shard_map/ppermute | solution.py:336
  2.1 2.6 %collective-permute-start.1 = (bf16[32,512]{1,0:T(8,128)(2,1)}, bf16[32,512]{1,0:T(8,128)(2,1)S(1)}, u32[]{:S(2)}, u32[]{:S(2)}) collective-permute-start(bf16[32,512]{1,0:T(8,128)(2,1)} %get-tuple-element.35), channel_id=1, source_target_pairs={{0,2},{1,3},{2,0},{3,1},{4,6},{5,7},{6,4},{7,5},{8,10},{9,11},{10,... | collective-permute-start | bytes 98312 | tf_op jit(solution)/shard_map/ppermute | solution.py:336
  4.7 0.1 collective-permute-start.2
  4.8 1.8 %message.1 = (bf16[336,256]{1,0:T(8,128)(2,1)}, bf16[336,256]{1,0:T(8,128)(2,1)}) custom-call(bf16[1280,256]{1,0:T(8,128)(2,1)} %feat.3, s32[10,128]{1,0:T(8,128)} %bitcast.3, s32[10,128]{1,0:T(8,128)} %bitcast.5, s32[10,128]{1,0:T(8,128)} %bitcast.7, bf16[32,512]{1,0:T(8,128)(2,1)} %get-tuple-element.33.p0._), custom_call_target="tpu_custom_call" | custom-call | flops 3000000000 | tf_op jit(solution)/shard_map/message/pallas_call | solution.py:305
  6.6 5.7 %collective-permute-start.3 = (bf16[336,256]{1,0:T(8,128)(2,1)}, bf16[336,256]{1,0:T(8,128)(2,1)S(1)}, u32[]{:S(2)}, u32[]{:S(2)}) collective-permute-start(bf16[336,256]{1,0:T(8,128)(2,1)} %get-tuple-element.39), channel_id=1, source_target_pairs={{0,31},{1,2},{2,1},{3,4},{4,3},{5,6},{6,5},{7,8},{8,7},{9,10},{10,... | collective-permute-start | bytes 516104 | tf_op jit(solution)/shard_map/ppermute | solution.py:330
  12.3 0.0 copy-start.4
  12.4 0.0 copy-start.5
  12.4 0.0 copy-start.6
  12.4 0.1 collective-permute-start.4
  12.5 0.0 collective-permute-done.p1
  12.5 0.0 collective-permute-done.1.p2
  12.5 0.0 collective-permute-done.2.p3
  12.5 0.2 field.1
  12.7 0.7 %collective-permute-start.5 = (bf16[384,128]{1,0:T(8,128)(2,1)S(1)}, bf16[384,128]{1,0:T(8,128)(2,1)S(1)}, u32[]{:S(2)}, u32[]{:S(2)}) collective-permute-start(bf16[384,128]{1,0:T(8,128)(2,1)S(1)} %get-tuple-element.44), channel_id=1, source_target_pairs={{0,31},{1,2},{2,1},{3,4},{4,3},{5,6},{6,5},{7,8},{8,7},{9,10},{10,... | collective-permute-start | bytes 294920 | tf_op jit(solution)/shard_map/ppermute | solution.py:330
  13.4 0.0 collective-permute-start.6
  13.4 0.0 copy-done
  13.4 0.1 copy-done.1
  13.5 0.0 copy-done.2
  13.5 2.1 %own.1 = (bf16[2,256,1024]{2,1,0:T(8,128)(2,1)S(1)}, bf16[512,256]{1,0:T(8,128)(2,1)S(1)}, bf16[512,8]{1,0:T(8,128)(2,1)S(1)}, bf16[256,256]{1,0:T(8,128)(2,1)S(1)}) custom-call(bf16[1280,256]{1,0:T(8,128)(2,1)S(1)} %copy-done, s32[10,128]{1,0:T(8,128)S(1)} %bitcast.4, s32[10,128]{1,0:T(8,128)S(1)} %bitcast.6, s32[10,128]{1,0:T(8,128)S(1)} %bitcast.8, ...), custom_call_target="tpu_custom_call" | custom-call | flops 4000000000 | tf_op jit(solution)/shard_map/own/pallas_call | solution.py:305
  15.6 0.1 collective-permute-done.3.blue
  15.7 0.0 collective-permute-done.4.red
  15.7 2.3 %spill.1.band = bf16[2,256,1024]{2,1,0:T(8,128)(2,1)S(1)} custom-call(bf16[2,256,1024]{2,1,0:T(8,128)(2,1)S(1)} %get-tuple-element.38.own_band, bf16[336,256]{1,0:T(8,128)(2,1)S(1)} %collective-permute-done.3.blue, bf16[336,256]{1,0:T(8,128)(2,1)S(1)} %collective-permute-done.4.red, ...), custom_call_target="tpu_custom_call", output_to_operand_aliasing={{}: (0, {})} | custom-call | flops 1000000000 | tf_op jit(solution)/shard_map/spill/pallas_call | solution.py:305
  18.1 2.3 %collective-permute-done.5.blue = bf16[384,128]{1,0:T(8,128)(2,1)S(1)} collective-permute-done((bf16[384,128]{1,0:T(8,128)(2,1)S(1)}, bf16[384,128]{1,0:T(8,128)(2,1)S(1)}, u32[]{:S(2)}, u32[]{:S(2)}) %collective-permute-start.5) | collective-permute-done | bytes 98336 | tf_op jit(solution)/shard_map/ppermute | solution.py:330
  20.4 0.0 collective-permute-done.6.red
  20.4 0.7 %first.1 = (f32[512,128]{1,0:T(8,128)S(1)}, bf16[384,128]{1,0:T(8,128)(2,1)S(1)}, bf16[384,128]{1,0:T(8,128)(2,1)S(1)}) custom-call(bf16[2,256,1024]{2,1,0:T(8,128)(2,1)S(1)} %spill.1.band, f32[512,128]{1,0:T(8,128)S(1)} %get-tuple-element.37.t0.before, bf16[384,128]{1,0:T(8,128)(2,1)S(1)} %collective-permute-done.5.blue, ...), custom_call_target="tpu_custom_call" | custom-call | flops 1000000000 | tf_op jit(solution)/shard_map/first/pallas_call | solution.py:305
  21.1 3.0 %collective-permute-start.7 = (bf16[384,128]{1,0:T(8,128)(2,1)S(1)}, bf16[384,128]{1,0:T(8,128)(2,1)S(1)}, u32[]{:S(2)}, u32[]{:S(2)}) collective-permute-start(bf16[384,128]{1,0:T(8,128)(2,1)S(1)} %get-tuple-element.47), channel_id=1, source_target_pairs={{0,31},{1,2},{2,1},{3,4},{4,3},{5,6},{6,5},{7,8},{8,7},{9,10},{10,... | collective-permute-start | bytes 294920 | tf_op jit(solution)/shard_map/ppermute | solution.py:330
  24.1 0.0 collective-permute-start.8
  24.1 4.8 %collective-permute-done.7.blue = bf16[384,128]{1,0:T(8,128)(2,1)S(1)} collective-permute-done((bf16[384,128]{1,0:T(8,128)(2,1)S(1)}, bf16[384,128]{1,0:T(8,128)(2,1)S(1)}, u32[]{:S(2)}, u32[]{:S(2)}) %collective-permute-start.7) | collective-permute-done | bytes 98336 | tf_op jit(solution)/shard_map/ppermute | solution.py:330
  28.9 0.0 collective-permute-done.8.red
  28.9 0.7 %next.2 = (f32[512,128]{1,0:T(8,128)S(1)}, bf16[384,128]{1,0:T(8,128)(2,1)S(1)}, bf16[384,128]{1,0:T(8,128)(2,1)S(1)}) custom-call(bf16[2,256,1024]{2,1,0:T(8,128)(2,1)S(1)} %spill.1.band, f32[512,128]{1,0:T(8,128)S(1)} %get-tuple-element.37.t0.before, f32[512,128]{1,0:T(8,128)S(1)} %get-tuple-element.46.now.before.t1, ...), custom_call_target="tpu_custom_call" | custom-call | flops 1000000000 | tf_op jit(solution)/shard_map/next/pallas_call | solution.py:305
  29.6 0.1 collective-permute-start.10
  29.7 2.9 %collective-permute-start.9 = (bf16[384,128]{1,0:T(8,128)(2,1)S(1)}, bf16[384,128]{1,0:T(8,128)(2,1)S(1)}, u32[]{:S(2)}, u32[]{:S(2)}) collective-permute-start(bf16[384,128]{1,0:T(8,128)(2,1)S(1)} %get-tuple-element.50), channel_id=1, source_target_pairs={{0,31},{1,2},{2,1},{3,4},{4,3},{5,6},{6,5},{7,8},{8,7},{9,10},{10,... | collective-permute-start | bytes 294920 | tf_op jit(solution)/shard_map/ppermute | solution.py:330
  32.6 0.0 collective-permute-done.10.red
  32.6 4.8 %collective-permute-done.9.blue = bf16[384,128]{1,0:T(8,128)(2,1)S(1)} collective-permute-done((bf16[384,128]{1,0:T(8,128)(2,1)S(1)}, bf16[384,128]{1,0:T(8,128)(2,1)S(1)}, u32[]{:S(2)}, u32[]{:S(2)}) %collective-permute-start.9) | collective-permute-done | bytes 98336 | tf_op jit(solution)/shard_map/ppermute | solution.py:330
  37.4 0.7 %next.3 = (f32[512,128]{1,0:T(8,128)S(1)}, bf16[384,128]{1,0:T(8,128)(2,1)S(1)}, bf16[384,128]{1,0:T(8,128)(2,1)S(1)}) custom-call(bf16[2,256,1024]{2,1,0:T(8,128)(2,1)S(1)} %spill.1.band, f32[512,128]{1,0:T(8,128)S(1)} %get-tuple-element.46.now.before.t1, f32[512,128]{1,0:T(8,128)S(1)} %get-tuple-element.49.now.t2, ...), custom_call_target="tpu_custom_call" | custom-call | flops 1000000000 | tf_op jit(solution)/shard_map/next/pallas_call | solution.py:305
  38.0 2.9 %collective-permute-start.11 = (bf16[384,128]{1,0:T(8,128)(2,1)S(1)}, bf16[384,128]{1,0:T(8,128)(2,1)S(1)}, u32[]{:S(2)}, u32[]{:S(2)}) collective-permute-start(bf16[384,128]{1,0:T(8,128)(2,1)S(1)} %get-tuple-element.55), channel_id=1, source_target_pairs={{0,31},{1,2},{2,1},{3,4},{4,3},{5,6},{6,5},{7,8},{8,7},{9,10},{10,... | collective-permute-start | bytes 294920 | tf_op jit(solution)/shard_map/ppermute | solution.py:330
  41.0 0.7 %copy-done.7 = f32[5]{0:T(128)S(1)} copy-done((f32[5]{0:T(128)S(1)}, f32[5]{0:T(128)}, u32[]{:S(2)}) %copy-start.7) | copy-done | bytes 44
  41.6 0.7 %mix.1 = (f32[128,512]{1,0:T(8,128)S(1)}, f32[8,128]{1,0:T(8,128)S(1)}) custom-call(f32[5]{0:T(128)S(1)} %copy-done.7, f32[512,128]{1,0:T(8,128)S(1)} %get-tuple-element.37.t0.before, f32[512,128]{1,0:T(8,128)S(1)} %get-tuple-element.46.now.before.t1, f32[512,128]{1,0:T(8,128)S(1)} %get-tuple-element.49.now.t2, f32[512,128]{1,0:T(8,128)S(1)} %get-tuple-element.52.t3), custom_call_target="tpu_custom_call" | custom-call | flops 1000000000 | tf_op jit(solution)/shard_map/mix/pallas_call | solution.py:305
  42.3 3.4 %collective-permute-done.11.blue = bf16[384,128]{1,0:T(8,128)(2,1)S(1)} collective-permute-done((bf16[384,128]{1,0:T(8,128)(2,1)S(1)}, bf16[384,128]{1,0:T(8,128)(2,1)S(1)}, u32[]{:S(2)}, u32[]{:S(2)}) %collective-permute-start.11) | collective-permute-done | bytes 98336 | tf_op jit(solution)/shard_map/ppermute | solution.py:330
  45.8 0.0 collective-permute-done.12.red
  45.8 0.7 %last.1 = (bf16[32,512]{1,0:T(8,128)(2,1)S(1)}, bf16[32,512]{1,0:T(8,128)(2,1)S(1)}, bf16[32,512]{1,0:T(8,128)(2,1)S(1)}, bf16[32,512]{1,0:T(8,128)(2,1)S(1)}) custom-call(f32[8,128]{1,0:T(8,128)S(1)} %get-tuple-element.53.final, bf16[2,256,1024]{2,1,0:T(8,128)(2,1)S(1)} %spill.1.band, f32[128,512]{1,0:T(8,128)S(1)} %get-tuple-element.54.base, ...), custom_call_target="tpu_custom_call" | custom-call | flops 1000000000 | tf_op jit(solution)/shard_map/last/pallas_call | solution.py:305
  46.5 0.1 collective-permute-start.13
  46.6 0.1 collective-permute-start.14
  46.7 1.8 %collective-permute-start.15 = (bf16[32,512]{1,0:T(8,128)(2,1)S(1)}, bf16[32,512]{1,0:T(8,128)(2,1)S(1)}, u32[]{:S(2)}, u32[]{:S(2)}) collective-permute-start(bf16[32,512]{1,0:T(8,128)(2,1)S(1)} %get-tuple-element.60), channel_id=1, source_target_pairs={{0,3},{1,2},{2,1},{3,0},{4,7},{5,6},{6,5},{7,4},{8,11},{9,10},{10,... | collective-permute-start | bytes 98312 | tf_op jit(solution)/shard_map/ppermute | solution.py:336
  48.4 2.3 %collective-permute-done.14.p2 = bf16[32,512]{1,0:T(8,128)(2,1)S(1)} collective-permute-done((bf16[32,512]{1,0:T(8,128)(2,1)S(1)}, bf16[32,512]{1,0:T(8,128)(2,1)S(1)}, u32[]{:S(2)}, u32[]{:S(2)}) %collective-permute-start.14) | collective-permute-done | bytes 32800 | tf_op jit(solution)/shard_map/ppermute | solution.py:336
  50.7 0.0 collective-permute-done.15.p3
  50.7 0.7 %join.1 = f32[32,2048]{1,0:T(8,128)} custom-call(bf16[32,512]{1,0:T(8,128)(2,1)S(1)} %get-tuple-element.57.p0, bf16[32,512]{1,0:T(8,128)(2,1)S(1)} %collective-permute-done.13.p1, bf16[32,512]{1,0:T(8,128)(2,1)S(1)} %collective-permute-done.14.p2, bf16[32,512]{1,0:T(8,128)(2,1)S(1)} %collective-permute-done.15.p3), custom_call_target="tpu_custom_call" | custom-call | flops 1000000000 | tf_op jit(solution)/shard_map/join/pallas_call | solution.py:305
  (13 shorter events, 0.0 us)
Async XLA Ops:
  1.6 10.8 %collective-permute-start = (bf16[32,512]{1,0:T(8,128)(2,1)}, bf16[32,512]{1,0:T(8,128)(2,1)S(1)}, u32[]{:S(2)}, u32[]{:S(2)}) collective-permute-start(bf16[32,512]{1,0:T(8,128)(2,1)} %get-tuple-element.34), channel_id=1, source_target_pairs={{0,1},{1,0},{2,3},{3,2},{4,5},{5,4},{6,7},{7,6},{8,9},{9,8},{10,11... | collective-permute-start | bytes 98312 | tf_op jit(solution)/shard_map/ppermute | solution.py:336
  2.1 10.3 %collective-permute-start.1 = (bf16[32,512]{1,0:T(8,128)(2,1)}, bf16[32,512]{1,0:T(8,128)(2,1)S(1)}, u32[]{:S(2)}, u32[]{:S(2)}) collective-permute-start(bf16[32,512]{1,0:T(8,128)(2,1)} %get-tuple-element.35), channel_id=1, source_target_pairs={{0,2},{1,3},{2,0},{3,1},{4,6},{5,7},{6,4},{7,5},{8,10},{9,11},{10,... | collective-permute-start | bytes 98312 | tf_op jit(solution)/shard_map/ppermute | solution.py:336
  4.7 7.8 %collective-permute-start.2 = (bf16[32,512]{1,0:T(8,128)(2,1)}, bf16[32,512]{1,0:T(8,128)(2,1)S(1)}, u32[]{:S(2)}, u32[]{:S(2)}) collective-permute-start(bf16[32,512]{1,0:T(8,128)(2,1)} %get-tuple-element.36), channel_id=1, source_target_pairs={{0,3},{1,2},{2,1},{3,0},{4,7},{5,6},{6,5},{7,4},{8,11},{9,10},{10,... | collective-permute-start | bytes 98312 | tf_op jit(solution)/shard_map/ppermute | solution.py:336
  4.8 7.7 %copy-start.8 = (bf16[32,512]{1,0:T(8,128)(2,1)S(1)}, bf16[32,512]{1,0:T(8,128)(2,1)}, u32[]{:S(2)}) copy-start(bf16[32,512]{1,0:T(8,128)(2,1)} %get-tuple-element.33.p0._) | copy-start | bytes 98308
  6.6 9.1 %collective-permute-start.3 = (bf16[336,256]{1,0:T(8,128)(2,1)}, bf16[336,256]{1,0:T(8,128)(2,1)S(1)}, u32[]{:S(2)}, u32[]{:S(2)}) collective-permute-start(bf16[336,256]{1,0:T(8,128)(2,1)} %get-tuple-element.39), channel_id=1, source_target_pairs={{0,31},{1,2},{2,1},{3,4},{4,3},{5,6},{6,5},{7,8},{8,7},{9,10},{10,... | collective-permute-start | bytes 516104 | tf_op jit(solution)/shard_map/ppermute | solution.py:330
  12.3 1.1 %copy-start = (bf16[1280,256]{1,0:T(8,128)(2,1)S(1)}, bf16[1280,256]{1,0:T(8,128)(2,1)}, u32[]{:S(2)}) copy-start(bf16[1280,256]{1,0:T(8,128)(2,1)} %feat.3) | copy-start | bytes 1966084
  12.3 1.1 %copy-start.1 = (bf16[256,512]{1,0:T(8,128)(2,1)S(1)}, bf16[256,512]{1,0:T(8,128)(2,1)}, u32[]{:S(2)}) copy-start(bf16[256,512]{1,0:T(8,128)(2,1)} %w_in.1) | copy-start | bytes 786436
  12.3 1.2 %copy-start.2 = (bf16[256,256]{1,0:T(8,128)(2,1)S(1)}, bf16[256,256]{1,0:T(8,128)(2,1)}, u32[]{:S(2)}) copy-start(bf16[256,256]{1,0:T(8,128)(2,1)} %w_out.1) | copy-start | bytes 393220
  12.3 1.2 %copy-start.3 = (s32[1280]{0:T(1024)S(1)}, s32[1280]{0:T(1024)}, u32[]{:S(2)}) copy-start(s32[1280]{0:T(1024)} %param.10) | copy-start | bytes 15364
  12.3 1.2 %copy-start.4 = (s32[1280]{0:T(1024)S(1)}, s32[1280]{0:T(1024)}, u32[]{:S(2)}) copy-start(s32[1280]{0:T(1024)} %param.11) | copy-start | bytes 15364
  12.4 1.2 %copy-start.5 = (s32[1280]{0:T(1024)S(1)}, s32[1280]{0:T(1024)}, u32[]{:S(2)}) copy-start(s32[1280]{0:T(1024)} %param.12) | copy-start | bytes 15364
  12.4 1.2 %copy-start.6 = (bf16[3,512]{1,0:T(4,128)(2,1)S(1)}, bf16[3,512]{1,0:T(4,128)(2,1)}, u32[]{:S(2)}) copy-start(bf16[3,512]{1,0:T(4,128)(2,1)} %cell_bias.1) | copy-start | bytes 9220
  12.4 3.4 %collective-permute-start.4 = (bf16[336,256]{1,0:T(8,128)(2,1)}, bf16[336,256]{1,0:T(8,128)(2,1)S(1)}, u32[]{:S(2)}, u32[]{:S(2)}) collective-permute-start(bf16[336,256]{1,0:T(8,128)(2,1)} %get-tuple-element.40), channel_id=1, source_target_pairs={{0,1},{1,0},{2,3},{3,2},{4,5},{5,4},{6,7},{7,6},{8,9},{9,8},{10,11... | collective-permute-start | bytes 516104 | tf_op jit(solution)/shard_map/ppermute | solution.py:331
  12.7 7.7 %collective-permute-start.5 = (bf16[384,128]{1,0:T(8,128)(2,1)S(1)}, bf16[384,128]{1,0:T(8,128)(2,1)S(1)}, u32[]{:S(2)}, u32[]{:S(2)}) collective-permute-start(bf16[384,128]{1,0:T(8,128)(2,1)S(1)} %get-tuple-element.44), channel_id=1, source_target_pairs={{0,31},{1,2},{2,1},{3,4},{4,3},{5,6},{6,5},{7,8},{8,7},{9,10},{10,... | collective-permute-start | bytes 294920 | tf_op jit(solution)/shard_map/ppermute | solution.py:330
  13.4 7.0 %collective-permute-start.6 = (bf16[384,128]{1,0:T(8,128)(2,1)S(1)}, bf16[384,128]{1,0:T(8,128)(2,1)S(1)}, u32[]{:S(2)}, u32[]{:S(2)}) collective-permute-start(bf16[384,128]{1,0:T(8,128)(2,1)S(1)} %get-tuple-element.45), channel_id=1, source_target_pairs={{0,1},{1,0},{2,3},{3,2},{4,5},{5,4},{6,7},{7,6},{8,9},{9,8},{10,11... | collective-permute-start | bytes 294920 | tf_op jit(solution)/shard_map/ppermute | solution.py:331
  21.1 7.8 %collective-permute-start.7 = (bf16[384,128]{1,0:T(8,128)(2,1)S(1)}, bf16[384,128]{1,0:T(8,128)(2,1)S(1)}, u32[]{:S(2)}, u32[]{:S(2)}) collective-permute-start(bf16[384,128]{1,0:T(8,128)(2,1)S(1)} %get-tuple-element.47), channel_id=1, source_target_pairs={{0,31},{1,2},{2,1},{3,4},{4,3},{5,6},{6,5},{7,8},{8,7},{9,10},{10,... | collective-permute-start | bytes 294920 | tf_op jit(solution)/shard_map/ppermute | solution.py:330
  24.1 4.8 %collective-permute-start.8 = (bf16[384,128]{1,0:T(8,128)(2,1)S(1)}, bf16[384,128]{1,0:T(8,128)(2,1)S(1)}, u32[]{:S(2)}, u32[]{:S(2)}) collective-permute-start(bf16[384,128]{1,0:T(8,128)(2,1)S(1)} %get-tuple-element.48), channel_id=1, source_target_pairs={{0,1},{1,0},{2,3},{3,2},{4,5},{5,4},{6,7},{7,6},{8,9},{9,8},{10,11... | collective-permute-start | bytes 294920 | tf_op jit(solution)/shard_map/ppermute | solution.py:331
  29.6 3.0 %collective-permute-start.10 = (bf16[384,128]{1,0:T(8,128)(2,1)S(1)}, bf16[384,128]{1,0:T(8,128)(2,1)S(1)}, u32[]{:S(2)}, u32[]{:S(2)}) collective-permute-start(bf16[384,128]{1,0:T(8,128)(2,1)S(1)} %get-tuple-element.51), channel_id=1, source_target_pairs={{0,1},{1,0},{2,3},{3,2},{4,5},{5,4},{6,7},{7,6},{8,9},{9,8},{10,11... | collective-permute-start | bytes 294920 | tf_op jit(solution)/shard_map/ppermute | solution.py:331
  29.7 7.7 %collective-permute-start.9 = (bf16[384,128]{1,0:T(8,128)(2,1)S(1)}, bf16[384,128]{1,0:T(8,128)(2,1)S(1)}, u32[]{:S(2)}, u32[]{:S(2)}) collective-permute-start(bf16[384,128]{1,0:T(8,128)(2,1)S(1)} %get-tuple-element.50), channel_id=1, source_target_pairs={{0,31},{1,2},{2,1},{3,4},{4,3},{5,6},{6,5},{7,8},{8,7},{9,10},{10,... | collective-permute-start | bytes 294920 | tf_op jit(solution)/shard_map/ppermute | solution.py:330
  38.0 7.7 %collective-permute-start.11 = (bf16[384,128]{1,0:T(8,128)(2,1)S(1)}, bf16[384,128]{1,0:T(8,128)(2,1)S(1)}, u32[]{:S(2)}, u32[]{:S(2)}) collective-permute-start(bf16[384,128]{1,0:T(8,128)(2,1)S(1)} %get-tuple-element.55), channel_id=1, source_target_pairs={{0,31},{1,2},{2,1},{3,4},{4,3},{5,6},{6,5},{7,8},{8,7},{9,10},{10,... | collective-permute-start | bytes 294920 | tf_op jit(solution)/shard_map/ppermute | solution.py:330
  41.0 0.7 %copy-start.7 = (f32[5]{0:T(128)S(1)}, f32[5]{0:T(128)}, u32[]{:S(2)}) copy-start(f32[5]{0:T(128)} %coef.1) | copy-start | bytes 64
  41.0 4.8 %collective-permute-start.12 = (bf16[384,128]{1,0:T(8,128)(2,1)S(1)}, bf16[384,128]{1,0:T(8,128)(2,1)S(1)}, u32[]{:S(2)}, u32[]{:S(2)}) collective-permute-start(bf16[384,128]{1,0:T(8,128)(2,1)S(1)} %get-tuple-element.56), channel_id=1, source_target_pairs={{0,1},{1,0},{2,3},{3,2},{4,5},{5,4},{6,7},{7,6},{8,9},{9,8},{10,11... | collective-permute-start | bytes 294920 | tf_op jit(solution)/shard_map/ppermute | solution.py:331
  46.5 1.9 %collective-permute-start.13 = (bf16[32,512]{1,0:T(8,128)(2,1)S(1)}, bf16[32,512]{1,0:T(8,128)(2,1)S(1)}, u32[]{:S(2)}, u32[]{:S(2)}) collective-permute-start(bf16[32,512]{1,0:T(8,128)(2,1)S(1)} %get-tuple-element.58), channel_id=1, source_target_pairs={{0,1},{1,0},{2,3},{3,2},{4,5},{5,4},{6,7},{7,6},{8,9},{9,8},{10,11... | collective-permute-start | bytes 98312 | tf_op jit(solution)/shard_map/ppermute | solution.py:336
  46.6 4.2 %collective-permute-start.14 = (bf16[32,512]{1,0:T(8,128)(2,1)S(1)}, bf16[32,512]{1,0:T(8,128)(2,1)S(1)}, u32[]{:S(2)}, u32[]{:S(2)}) collective-permute-start(bf16[32,512]{1,0:T(8,128)(2,1)S(1)} %get-tuple-element.59), channel_id=1, source_target_pairs={{0,2},{1,3},{2,0},{3,1},{4,6},{5,7},{6,4},{7,5},{8,10},{9,11},{10,... | collective-permute-start | bytes 98312 | tf_op jit(solution)/shard_map/ppermute | solution.py:336
  46.7 4.1 %collective-permute-start.15 = (bf16[32,512]{1,0:T(8,128)(2,1)S(1)}, bf16[32,512]{1,0:T(8,128)(2,1)S(1)}, u32[]{:S(2)}, u32[]{:S(2)}) collective-permute-start(bf16[32,512]{1,0:T(8,128)(2,1)S(1)} %get-tuple-element.60), channel_id=1, source_target_pairs={{0,3},{1,2},{2,1},{3,0},{4,7},{5,6},{6,5},{7,4},{8,11},{9,10},{10,... | collective-permute-start | bytes 98312 | tf_op jit(solution)/shard_map/ppermute | solution.py:336

commit v6 on v5

--- a/solution.py
+++ b/solution.py
@@ -50,38 +50,31 @@
     return [x.astype(F32) for x in (rel, shift * TILE_ATOMS + (dst & 7), cell)]
 
 
-def split_kernel(vec_hbm, p0, p1, p2, p3, vectors, sems):
-    member = lax.axis_index("edges")
+def prep_kernel(
+    vec_hbm, feat, src_hbm, dst_hbm, cell_hbm, p0, p1, p2, p3, blue, red, vectors, src, dst, cell, sems
+):
+    member, side = lax.axis_index("edges"), device_side()
     pieces = (p0, p1, p2, p3)
     loads = []
     for k, piece in enumerate(pieces):
         width = piece.shape[1]
         at = pl.multiple_of((member ^ k) * width, width)
         loads.append(pltpu.make_async_copy(vec_hbm.at[:, pl.ds(at, width)], vectors.at[k], sems.at[k]))
-    for k in (2, 3, 1, 0):
-        loads[k].start()
-    for k in (2, 3, 1, 0):
-        loads[k].wait()
-        pieces[k][...] = vectors[k].astype(BF)
-
-
-def message_kernel(feat, src_hbm, dst_hbm, cell_hbm, _, blue, red, src, dst, cell, sems):
-    side = device_side()
     high = feat.shape[0] - SPILL
     off = pl.multiple_of(side * high, 64)
     copies = [
-        pltpu.make_async_copy(feat.at[pl.ds(off, SPILL)], blue.at[pl.ds(0, SPILL)], sems.at[0]),
+        pltpu.make_async_copy(feat.at[pl.ds(off, SPILL)], blue.at[pl.ds(0, SPILL)], sems.at[4]),
         pltpu.make_async_copy(
-            feat.at[pl.ds(pl.multiple_of(high - off, 64), SPILL)], red.at[pl.ds(0, SPILL)], sems.at[1]
+            feat.at[pl.ds(pl.multiple_of(high - off, 64), SPILL)], red.at[pl.ds(0, SPILL)], sems.at[5]
         ),
     ]
-    loads = [
-        pltpu.make_async_copy(x, y, sems.at[2 + n])
+    lists = [
+        pltpu.make_async_copy(x, y, sems.at[6 + n])
         for n, (x, y) in enumerate(((src_hbm, src), (dst_hbm, dst), (cell_hbm, cell)))
     ]
-    for copy in loads + copies:
+    for copy in lists + loads + copies:
         copy.start()
-    for copy in loads:
+    for copy in lists:
         copy.wait()
     three = edge_ids(src[...], dst[...], cell[...])
     lane, line = iota((3, 128), 1), iota((3, 128), 0)
@@ -100,6 +93,9 @@
     ):
         msg[SPILL : SPILL + ID_ROWS, 0:128] = ids_of.astype(BF)
         msg[SPILL : SPILL + ID_ROWS, 128:256] = none
+    for k, piece in enumerate(pieces):
+        loads[k].wait()
+        piece[...] = vectors[k].astype(BF)
     for copy in copies:
         copy.wait()
 
@@ -340,29 +336,20 @@
     piece = shape((high, nrow), BF)
     lines = (nown // 128, 128)
     edges = [x.reshape(lines) for x in (edge_src, edge_dst, edge_cell)]
-    pieces = call(
-        split_kernel,
-        "split",
-        (piece,) * 4,
-        [pltpu.VMEM((nedge, high, nrow), F32), pltpu.SemaphoreType.DMA((4,))],
+    *pieces, blue_msg, red_msg = call(
+        prep_kernel,
+        "prep",
+        (piece,) * 4 + (msg, msg),
+        [pltpu.VMEM((nedge, high, nrow), F32)]
+        + [pltpu.VMEM(lines, jnp.int32)] * 3
+        + [pltpu.SemaphoreType.DMA((9,))],
         vectors,
-        in_hbm=(0,),
-        limit=FULL,
-    )
-    pieces = exchange(pieces)
-    blue_msg, red_msg = call(
-        message_kernel,
-        "message",
-        (msg, msg),
-        [pltpu.VMEM(lines, jnp.int32)] * 3
-        + [pltpu.SemaphoreType.DMA((5,))],
         features,
         *edges,
-        pieces[0],
         in_hbm=range(5),
         limit=FULL,
-        micros=3,
-    )
+    )
+    pieces = exchange(pieces)
     blue_msg, red_msg = swap(blue_msg, red_msg)
     full, part = shape((nrow, VEC), F32), shape((HALO, VEC), BF)
     band_shape = shape((ATOM_Q // PAIR_ATOMS, PAIR_ATOMS * ORB, WIN_ATOMS * ORB), BF)
@@ -395,6 +382,7 @@
         red_msg,
         *weights,
         alias={0: 0},
+        micros=0,
     )
 
     wide = pltpu.VMEM((nrow + 2 * HALO, VEC), F32)

time: 51.7 us -> 50.9 us (0.985)
  Pallas kernels: 12.3 us -> 10.9 us
  local copies, waits for them, and re-layouts: 0.81 us -> 1.44 us
    pallas_call x11 -> x10, Pallas kernels: 12.3 us -> 10.9 us  [call(): pl.pallas_call(kernel, name=name, out_shape=outs, in_specs=spaces, out_sp...]
    unnamed x18, local copies, waits for them, and re-layouts: 0.81 us -> 1.44 us
  transfers between devices with their start and end apart: 16 -> 16, of which waited for: 6 -> 5; matrix products, arithmetic and copies ran while one was open for 0% -> 0% of each run, Pallas kernels for 14% -> 11%
where the time goes in v6:
time: 50.9 us; the launch traced here: 50.7 us
  starting transfers between devices  20.8 us (41%)
  waiting for transfers between devices  17.4 us (34%)
  Pallas kernels  10.9 us (21%)
  local copies, waits for them, and re-layouts  1.44 us (3%)
    ppermute x5, starting transfers between devices, swap(): lax.ppermute(first, axes, blue_pairs)  15.6 us
    ppermute x5, waiting for transfers between devices, swap(): lax.ppermute(first, axes, blue_pairs)  15.1 us
    pallas_call x10, Pallas kernels, call(): pl.pallas_call(kernel, name=name, out_shape=outs, in_specs=spaces, out_sp...  10.9 us
    ppermute x6, starting transfers between devices, exchange(): lax.ppermute(pieces[k], 'edges', [(i, i ^ k) for i in range(nedge)])  5.08 us
    ppermute x6, waiting for transfers between devices, exchange(): lax.ppermute(pieces[k], 'edges', [(i, i ^ k) for i in range(nedge)])  2.31 us
    unnamed x18, local copies, waits for them, and re-layouts  1.44 us
  transfers between devices with their start and end apart: 16, of which 5 were waited for; matrix products, arithmetic and copies ran while one was open for 0% of the time, Pallas kernels for 11%

profile of v6, /device:TPU:0, one launch (start us, length us, event | category | flops | bytes accessed | tf_op | source)
XLA Modules:
  0.0 50.7 jit_solution(15674181726550778826)
XLA Ops:
  0.0 2.0 %prep.1 = (bf16[32,512]{1,0:T(8,128)(2,1)}, bf16[32,512]{1,0:T(8,128)(2,1)}, bf16[32,512]{1,0:T(8,128)(2,1)}, bf16[32,512]{1,0:T(8,128)(2,1)}, bf16[336,256]{1,0:T(8,128)(2,1)}, /*index=5*/bf16[336,256]{1,0:T(8,128)(2,1)}) custom-call(f32[32,2048]{1,0:T(8,128)} %vec_hbm.1, bf16[1280,256]{1,0:T(8,128)(2,1)} %feat.3, s32[10,128]{1,0:T(8,128)} %bitcast.3, ...), custom_call_target="tpu_custom_call" | custom-call | flops 1000000000 | tf_op jit(solution)/shard_map/prep/pallas_call | solution.py:301
  2.0 0.5 %collective-permute-start = (bf16[32,512]{1,0:T(8,128)(2,1)}, bf16[32,512]{1,0:T(8,128)(2,1)S(1)}, u32[]{:S(2)}, u32[]{:S(2)}) collective-permute-start(bf16[32,512]{1,0:T(8,128)(2,1)} %get-tuple-element.34), channel_id=1, source_target_pairs={{0,1},{1,0},{2,3},{3,2},{4,5},{5,4},{6,7},{7,6},{8,9},{9,8},{10,11... | collective-permute-start | bytes 98312 | tf_op jit(solution)/shard_map/ppermute | solution.py:332
  2.5 2.6 %collective-permute-start.1 = (bf16[32,512]{1,0:T(8,128)(2,1)}, bf16[32,512]{1,0:T(8,128)(2,1)S(1)}, u32[]{:S(2)}, u32[]{:S(2)}) collective-permute-start(bf16[32,512]{1,0:T(8,128)(2,1)} %get-tuple-element.35), channel_id=1, source_target_pairs={{0,2},{1,3},{2,0},{3,1},{4,6},{5,7},{6,4},{7,5},{8,10},{9,11},{10,... | collective-permute-start | bytes 98312 | tf_op jit(solution)/shard_map/ppermute | solution.py:332
  5.1 0.1 collective-permute-start.2
  5.2 5.7 %collective-permute-start.3 = (bf16[336,256]{1,0:T(8,128)(2,1)}, bf16[336,256]{1,0:T(8,128)(2,1)S(1)}, u32[]{:S(2)}, u32[]{:S(2)}) collective-permute-start(bf16[336,256]{1,0:T(8,128)(2,1)} %get-tuple-element.39), channel_id=1, source_target_pairs={{0,31},{1,2},{2,1},{3,4},{4,3},{5,6},{6,5},{7,8},{8,7},{9,10},{10,... | collective-permute-start | bytes 516104 | tf_op jit(solution)/shard_map/ppermute | solution.py:326
  10.9 0.0 collective-permute-start.4
  10.9 0.0 collective-permute-done.p1
  10.9 0.0 collective-permute-done.1.p2
  10.9 0.0 collective-permute-done.2.p3
  10.9 0.7 %copy-done.8 = bf16[32,512]{1,0:T(8,128)(2,1)S(1)} copy-done((bf16[32,512]{1,0:T(8,128)(2,1)S(1)}, bf16[32,512]{1,0:T(8,128)(2,1)}, u32[]{:S(2)}) %copy-start.8) | copy-done | bytes 32792
  11.6 0.0 copy-start.4
  11.7 0.0 copy-start.5
  11.7 0.0 copy-start.6
  11.7 0.2 field.1
  11.9 2.5 %collective-permute-start.5 = (bf16[384,128]{1,0:T(8,128)(2,1)S(1)}, bf16[384,128]{1,0:T(8,128)(2,1)S(1)}, u32[]{:S(2)}, u32[]{:S(2)}) collective-permute-start(bf16[384,128]{1,0:T(8,128)(2,1)S(1)} %get-tuple-element.44), channel_id=1, source_target_pairs={{0,31},{1,2},{2,1},{3,4},{4,3},{5,6},{6,5},{7,8},{8,7},{9,10},{10,... | collective-permute-start | bytes 294920 | tf_op jit(solution)/shard_map/ppermute | solution.py:326
  14.4 0.0 collective-permute-start.6
  14.4 0.0 copy-done.2
  14.5 2.1 %own.1 = (bf16[2,256,1024]{2,1,0:T(8,128)(2,1)S(1)}, bf16[512,256]{1,0:T(8,128)(2,1)S(1)}, bf16[512,8]{1,0:T(8,128)(2,1)S(1)}, bf16[256,256]{1,0:T(8,128)(2,1)S(1)}) custom-call(bf16[1280,256]{1,0:T(8,128)(2,1)S(1)} %copy-done, s32[10,128]{1,0:T(8,128)S(1)} %bitcast.4, s32[10,128]{1,0:T(8,128)S(1)} %bitcast.6, s32[10,128]{1,0:T(8,128)S(1)} %bitcast.8, ...), custom_call_target="tpu_custom_call" | custom-call | flops 4000000000 | tf_op jit(solution)/shard_map/own/pallas_call | solution.py:301
  16.6 0.0 collective-permute-done.3.blue
  16.6 0.0 collective-permute-done.4.red
  16.6 2.3 %spill.1.band = bf16[2,256,1024]{2,1,0:T(8,128)(2,1)S(1)} custom-call(bf16[2,256,1024]{2,1,0:T(8,128)(2,1)S(1)} %get-tuple-element.38.own_band, bf16[336,256]{1,0:T(8,128)(2,1)S(1)} %collective-permute-done.3.blue, bf16[336,256]{1,0:T(8,128)(2,1)S(1)} %collective-permute-done.4.red, ...), custom_call_target="tpu_custom_call", output_to_operand_aliasing={{}: (0, {})} | custom-call | tf_op jit(solution)/shard_map/spill/pallas_call | solution.py:301
  18.9 0.7 %collective-permute-done.5.blue = bf16[384,128]{1,0:T(8,128)(2,1)S(1)} collective-permute-done((bf16[384,128]{1,0:T(8,128)(2,1)S(1)}, bf16[384,128]{1,0:T(8,128)(2,1)S(1)}, u32[]{:S(2)}, u32[]{:S(2)}) %collective-permute-start.5) | collective-permute-done | bytes 98336 | tf_op jit(solution)/shard_map/ppermute | solution.py:326
  19.6 0.0 collective-permute-done.6.red
  19.6 0.7 %first.1 = (f32[512,128]{1,0:T(8,128)S(1)}, bf16[384,128]{1,0:T(8,128)(2,1)S(1)}, bf16[384,128]{1,0:T(8,128)(2,1)S(1)}) custom-call(bf16[2,256,1024]{2,1,0:T(8,128)(2,1)S(1)} %spill.1.band, f32[512,128]{1,0:T(8,128)S(1)} %get-tuple-element.37.t0.before, bf16[384,128]{1,0:T(8,128)(2,1)S(1)} %collective-permute-done.5.blue, ...), custom_call_target="tpu_custom_call" | custom-call | flops 1000000000 | tf_op jit(solution)/shard_map/first/pallas_call | solution.py:301
  20.3 2.5 %collective-permute-start.7 = (bf16[384,128]{1,0:T(8,128)(2,1)S(1)}, bf16[384,128]{1,0:T(8,128)(2,1)S(1)}, u32[]{:S(2)}, u32[]{:S(2)}) collective-permute-start(bf16[384,128]{1,0:T(8,128)(2,1)S(1)} %get-tuple-element.47), channel_id=1, source_target_pairs={{0,31},{1,2},{2,1},{3,4},{4,3},{5,6},{6,5},{7,8},{8,7},{9,10},{10,... | collective-permute-start | bytes 294920 | tf_op jit(solution)/shard_map/ppermute | solution.py:326
  22.8 0.0 collective-permute-start.8
  22.8 5.3 %collective-permute-done.7.blue = bf16[384,128]{1,0:T(8,128)(2,1)S(1)} collective-permute-done((bf16[384,128]{1,0:T(8,128)(2,1)S(1)}, bf16[384,128]{1,0:T(8,128)(2,1)S(1)}, u32[]{:S(2)}, u32[]{:S(2)}) %collective-permute-start.7) | collective-permute-done | bytes 98336 | tf_op jit(solution)/shard_map/ppermute | solution.py:326
  28.1 0.0 collective-permute-done.8.red
  28.1 0.7 %next.2 = (f32[512,128]{1,0:T(8,128)S(1)}, bf16[384,128]{1,0:T(8,128)(2,1)S(1)}, bf16[384,128]{1,0:T(8,128)(2,1)S(1)}) custom-call(bf16[2,256,1024]{2,1,0:T(8,128)(2,1)S(1)} %spill.1.band, f32[512,128]{1,0:T(8,128)S(1)} %get-tuple-element.37.t0.before, f32[512,128]{1,0:T(8,128)S(1)} %get-tuple-element.46.now.before.t1, ...), custom_call_target="tpu_custom_call" | custom-call | flops 1000000000 | tf_op jit(solution)/shard_map/next/pallas_call | solution.py:301
  28.8 0.1 collective-permute-start.10
  28.8 2.5 %collective-permute-start.9 = (bf16[384,128]{1,0:T(8,128)(2,1)S(1)}, bf16[384,128]{1,0:T(8,128)(2,1)S(1)}, u32[]{:S(2)}, u32[]{:S(2)}) collective-permute-start(bf16[384,128]{1,0:T(8,128)(2,1)S(1)} %get-tuple-element.50), channel_id=1, source_target_pairs={{0,31},{1,2},{2,1},{3,4},{4,3},{5,6},{6,5},{7,8},{8,7},{9,10},{10,... | collective-permute-start | bytes 294920 | tf_op jit(solution)/shard_map/ppermute | solution.py:326
  31.3 0.0 collective-permute-done.10.red
  31.3 5.2 %collective-permute-done.9.blue = bf16[384,128]{1,0:T(8,128)(2,1)S(1)} collective-permute-done((bf16[384,128]{1,0:T(8,128)(2,1)S(1)}, bf16[384,128]{1,0:T(8,128)(2,1)S(1)}, u32[]{:S(2)}, u32[]{:S(2)}) %collective-permute-start.9) | collective-permute-done | bytes 98336 | tf_op jit(solution)/shard_map/ppermute | solution.py:326
  36.5 0.7 %next.3 = (f32[512,128]{1,0:T(8,128)S(1)}, bf16[384,128]{1,0:T(8,128)(2,1)S(1)}, bf16[384,128]{1,0:T(8,128)(2,1)S(1)}) custom-call(bf16[2,256,1024]{2,1,0:T(8,128)(2,1)S(1)} %spill.1.band, f32[512,128]{1,0:T(8,128)S(1)} %get-tuple-element.46.now.before.t1, f32[512,128]{1,0:T(8,128)S(1)} %get-tuple-element.49.now.t2, ...), custom_call_target="tpu_custom_call" | custom-call | flops 1000000000 | tf_op jit(solution)/shard_map/next/pallas_call | solution.py:301
  37.2 2.5 %collective-permute-start.11 = (bf16[384,128]{1,0:T(8,128)(2,1)S(1)}, bf16[384,128]{1,0:T(8,128)(2,1)S(1)}, u32[]{:S(2)}, u32[]{:S(2)}) collective-permute-start(bf16[384,128]{1,0:T(8,128)(2,1)S(1)} %get-tuple-element.55), channel_id=1, source_target_pairs={{0,31},{1,2},{2,1},{3,4},{4,3},{5,6},{6,5},{7,8},{8,7},{9,10},{10,... | collective-permute-start | bytes 294920 | tf_op jit(solution)/shard_map/ppermute | solution.py:326
  39.7 0.0 collective-permute-start.12
  39.7 0.7 %copy-done.7 = f32[5]{0:T(128)S(1)} copy-done((f32[5]{0:T(128)S(1)}, f32[5]{0:T(128)}, u32[]{:S(2)}) %copy-start.7) | copy-done | bytes 44
  40.3 0.7 %mix.1 = (f32[128,512]{1,0:T(8,128)S(1)}, f32[8,128]{1,0:T(8,128)S(1)}) custom-call(f32[5]{0:T(128)S(1)} %copy-done.7, f32[512,128]{1,0:T(8,128)S(1)} %get-tuple-element.37.t0.before, f32[512,128]{1,0:T(8,128)S(1)} %get-tuple-element.46.now.before.t1, f32[512,128]{1,0:T(8,128)S(1)} %get-tuple-element.49.now.t2, f32[512,128]{1,0:T(8,128)S(1)} %get-tuple-element.52.t3), custom_call_target="tpu_custom_call" | custom-call | flops 1000000000 | tf_op jit(solution)/shard_map/mix/pallas_call | solution.py:301
  41.0 3.9 %collective-permute-done.11.blue = bf16[384,128]{1,0:T(8,128)(2,1)S(1)} collective-permute-done((bf16[384,128]{1,0:T(8,128)(2,1)S(1)}, bf16[384,128]{1,0:T(8,128)(2,1)S(1)}, u32[]{:S(2)}, u32[]{:S(2)}) %collective-permute-start.11) | collective-permute-done | bytes 98336 | tf_op jit(solution)/shard_map/ppermute | solution.py:326
  44.9 0.0 collective-permute-done.12.red
  44.9 0.7 %last.1 = (bf16[32,512]{1,0:T(8,128)(2,1)S(1)}, bf16[32,512]{1,0:T(8,128)(2,1)S(1)}, bf16[32,512]{1,0:T(8,128)(2,1)S(1)}, bf16[32,512]{1,0:T(8,128)(2,1)S(1)}) custom-call(f32[8,128]{1,0:T(8,128)S(1)} %get-tuple-element.53.final, bf16[2,256,1024]{2,1,0:T(8,128)(2,1)S(1)} %spill.1.band, f32[128,512]{1,0:T(8,128)S(1)} %get-tuple-element.54.base, ...), custom_call_target="tpu_custom_call" | custom-call | flops 1000000000 | tf_op jit(solution)/shard_map/last/pallas_call | solution.py:301
  45.7 0.1 collective-permute-start.13
  45.8 0.1 collective-permute-start.14
  45.8 1.8 %collective-permute-start.15 = (bf16[32,512]{1,0:T(8,128)(2,1)S(1)}, bf16[32,512]{1,0:T(8,128)(2,1)S(1)}, u32[]{:S(2)}, u32[]{:S(2)}) collective-permute-start(bf16[32,512]{1,0:T(8,128)(2,1)S(1)} %get-tuple-element.60), channel_id=1, source_target_pairs={{0,3},{1,2},{2,1},{3,0},{4,7},{5,6},{6,5},{7,4},{8,11},{9,10},{10,... | collective-permute-start | bytes 98312 | tf_op jit(solution)/shard_map/ppermute | solution.py:332
  47.6 0.0 collective-permute-done.13.p1
  47.6 2.3 %collective-permute-done.14.p2 = bf16[32,512]{1,0:T(8,128)(2,1)S(1)} collective-permute-done((bf16[32,512]{1,0:T(8,128)(2,1)S(1)}, bf16[32,512]{1,0:T(8,128)(2,1)S(1)}, u32[]{:S(2)}, u32[]{:S(2)}) %collective-permute-start.14) | collective-permute-done | bytes 32800 | tf_op jit(solution)/shard_map/ppermute | solution.py:332
  49.9 0.0 collective-permute-done.15.p3
  49.9 0.7 %join.1 = f32[32,2048]{1,0:T(8,128)} custom-call(bf16[32,512]{1,0:T(8,128)(2,1)S(1)} %get-tuple-element.57.p0, bf16[32,512]{1,0:T(8,128)(2,1)S(1)} %collective-permute-done.13.p1, bf16[32,512]{1,0:T(8,128)(2,1)S(1)} %collective-permute-done.14.p2, bf16[32,512]{1,0:T(8,128)(2,1)S(1)} %collective-permute-done.15.p3), custom_call_target="tpu_custom_call" | custom-call | flops 1000000000 | tf_op jit(solution)/shard_map/join/pallas_call | solution.py:301
  (12 shorter events, 0.0 us)
Async XLA Ops:
  2.0 8.8 %collective-permute-start = (bf16[32,512]{1,0:T(8,128)(2,1)}, bf16[32,512]{1,0:T(8,128)(2,1)S(1)}, u32[]{:S(2)}, u32[]{:S(2)}) collective-permute-start(bf16[32,512]{1,0:T(8,128)(2,1)} %get-tuple-element.34), channel_id=1, source_target_pairs={{0,1},{1,0},{2,3},{3,2},{4,5},{5,4},{6,7},{7,6},{8,9},{9,8},{10,11... | collective-permute-start | bytes 98312 | tf_op jit(solution)/shard_map/ppermute | solution.py:332
  2.5 8.3 %collective-permute-start.1 = (bf16[32,512]{1,0:T(8,128)(2,1)}, bf16[32,512]{1,0:T(8,128)(2,1)S(1)}, u32[]{:S(2)}, u32[]{:S(2)}) collective-permute-start(bf16[32,512]{1,0:T(8,128)(2,1)} %get-tuple-element.35), channel_id=1, source_target_pairs={{0,2},{1,3},{2,0},{3,1},{4,6},{5,7},{6,4},{7,5},{8,10},{9,11},{10,... | collective-permute-start | bytes 98312 | tf_op jit(solution)/shard_map/ppermute | solution.py:332
  5.1 5.8 %collective-permute-start.2 = (bf16[32,512]{1,0:T(8,128)(2,1)}, bf16[32,512]{1,0:T(8,128)(2,1)S(1)}, u32[]{:S(2)}, u32[]{:S(2)}) collective-permute-start(bf16[32,512]{1,0:T(8,128)(2,1)} %get-tuple-element.36), channel_id=1, source_target_pairs={{0,3},{1,2},{2,1},{3,0},{4,7},{5,6},{6,5},{7,4},{8,11},{9,10},{10,... | collective-permute-start | bytes 98312 | tf_op jit(solution)/shard_map/ppermute | solution.py:332
  5.2 11.4 %collective-permute-start.3 = (bf16[336,256]{1,0:T(8,128)(2,1)}, bf16[336,256]{1,0:T(8,128)(2,1)S(1)}, u32[]{:S(2)}, u32[]{:S(2)}) collective-permute-start(bf16[336,256]{1,0:T(8,128)(2,1)} %get-tuple-element.39), channel_id=1, source_target_pairs={{0,31},{1,2},{2,1},{3,4},{4,3},{5,6},{6,5},{7,8},{8,7},{9,10},{10,... | collective-permute-start | bytes 516104 | tf_op jit(solution)/shard_map/ppermute | solution.py:326
  10.9 5.7 %collective-permute-start.4 = (bf16[336,256]{1,0:T(8,128)(2,1)}, bf16[336,256]{1,0:T(8,128)(2,1)S(1)}, u32[]{:S(2)}, u32[]{:S(2)}) collective-permute-start(bf16[336,256]{1,0:T(8,128)(2,1)} %get-tuple-element.40), channel_id=1, source_target_pairs={{0,1},{1,0},{2,3},{3,2},{4,5},{5,4},{6,7},{7,6},{8,9},{9,8},{10,11... | collective-permute-start | bytes 516104 | tf_op jit(solution)/shard_map/ppermute | solution.py:327
  10.9 0.8 %copy-start.8 = (bf16[32,512]{1,0:T(8,128)(2,1)S(1)}, bf16[32,512]{1,0:T(8,128)(2,1)}, u32[]{:S(2)}) copy-start(bf16[32,512]{1,0:T(8,128)(2,1)} %get-tuple-element.33.p0) | copy-start | bytes 98308
  11.6 2.8 %copy-start = (bf16[1280,256]{1,0:T(8,128)(2,1)S(1)}, bf16[1280,256]{1,0:T(8,128)(2,1)}, u32[]{:S(2)}) copy-start(bf16[1280,256]{1,0:T(8,128)(2,1)} %feat.3) | copy-start | bytes 1966084
  11.6 2.8 %copy-start.1 = (bf16[256,512]{1,0:T(8,128)(2,1)S(1)}, bf16[256,512]{1,0:T(8,128)(2,1)}, u32[]{:S(2)}) copy-start(bf16[256,512]{1,0:T(8,128)(2,1)} %w_in.1) | copy-start | bytes 786436
  11.6 2.8 %copy-start.2 = (bf16[256,256]{1,0:T(8,128)(2,1)S(1)}, bf16[256,256]{1,0:T(8,128)(2,1)}, u32[]{:S(2)}) copy-start(bf16[256,256]{1,0:T(8,128)(2,1)} %w_out.1) | copy-start | bytes 393220
  11.6 2.8 %copy-start.3 = (s32[1280]{0:T(1024)S(1)}, s32[1280]{0:T(1024)}, u32[]{:S(2)}) copy-start(s32[1280]{0:T(1024)} %param.10) | copy-start | bytes 15364
  11.6 2.8 %copy-start.4 = (s32[1280]{0:T(1024)S(1)}, s32[1280]{0:T(1024)}, u32[]{:S(2)}) copy-start(s32[1280]{0:T(1024)} %param.11) | copy-start | bytes 15364
  11.7 2.8 %copy-start.5 = (s32[1280]{0:T(1024)S(1)}, s32[1280]{0:T(1024)}, u32[]{:S(2)}) copy-start(s32[1280]{0:T(1024)} %param.12) | copy-start | bytes 15364
  11.7 2.8 %copy-start.6 = (bf16[3,512]{1,0:T(4,128)(2,1)S(1)}, bf16[3,512]{1,0:T(4,128)(2,1)}, u32[]{:S(2)}) copy-start(bf16[3,512]{1,0:T(4,128)(2,1)} %cell_bias.1) | copy-start | bytes 9220
  11.9 7.7 %collective-permute-start.5 = (bf16[384,128]{1,0:T(8,128)(2,1)S(1)}, bf16[384,128]{1,0:T(8,128)(2,1)S(1)}, u32[]{:S(2)}, u32[]{:S(2)}) collective-permute-start(bf16[384,128]{1,0:T(8,128)(2,1)S(1)} %get-tuple-element.44), channel_id=1, source_target_pairs={{0,31},{1,2},{2,1},{3,4},{4,3},{5,6},{6,5},{7,8},{8,7},{9,10},{10,... | collective-permute-start | bytes 294920 | tf_op jit(solution)/shard_map/ppermute | solution.py:326
  14.4 5.2 %collective-permute-start.6 = (bf16[384,128]{1,0:T(8,128)(2,1)S(1)}, bf16[384,128]{1,0:T(8,128)(2,1)S(1)}, u32[]{:S(2)}, u32[]{:S(2)}) collective-permute-start(bf16[384,128]{1,0:T(8,128)(2,1)S(1)} %get-tuple-element.45), channel_id=1, source_target_pairs={{0,1},{1,0},{2,3},{3,2},{4,5},{5,4},{6,7},{7,6},{8,9},{9,8},{10,11... | collective-permute-start | bytes 294920 | tf_op jit(solution)/shard_map/ppermute | solution.py:327
  20.3 7.8 %collective-permute-start.7 = (bf16[384,128]{1,0:T(8,128)(2,1)S(1)}, bf16[384,128]{1,0:T(8,128)(2,1)S(1)}, u32[]{:S(2)}, u32[]{:S(2)}) collective-permute-start(bf16[384,128]{1,0:T(8,128)(2,1)S(1)} %get-tuple-element.47), channel_id=1, source_target_pairs={{0,31},{1,2},{2,1},{3,4},{4,3},{5,6},{6,5},{7,8},{8,7},{9,10},{10,... | collective-permute-start | bytes 294920 | tf_op jit(solution)/shard_map/ppermute | solution.py:326
  22.8 5.3 %collective-permute-start.8 = (bf16[384,128]{1,0:T(8,128)(2,1)S(1)}, bf16[384,128]{1,0:T(8,128)(2,1)S(1)}, u32[]{:S(2)}, u32[]{:S(2)}) collective-permute-start(bf16[384,128]{1,0:T(8,128)(2,1)S(1)} %get-tuple-element.48), channel_id=1, source_target_pairs={{0,1},{1,0},{2,3},{3,2},{4,5},{5,4},{6,7},{7,6},{8,9},{9,8},{10,11... | collective-permute-start | bytes 294920 | tf_op jit(solution)/shard_map/ppermute | solution.py:327
  28.8 2.5 %collective-permute-start.10 = (bf16[384,128]{1,0:T(8,128)(2,1)S(1)}, bf16[384,128]{1,0:T(8,128)(2,1)S(1)}, u32[]{:S(2)}, u32[]{:S(2)}) collective-permute-start(bf16[384,128]{1,0:T(8,128)(2,1)S(1)} %get-tuple-element.51), channel_id=1, source_target_pairs={{0,1},{1,0},{2,3},{3,2},{4,5},{5,4},{6,7},{7,6},{8,9},{9,8},{10,11... | collective-permute-start | bytes 294920 | tf_op jit(solution)/shard_map/ppermute | solution.py:327
  28.8 7.7 %collective-permute-start.9 = (bf16[384,128]{1,0:T(8,128)(2,1)S(1)}, bf16[384,128]{1,0:T(8,128)(2,1)S(1)}, u32[]{:S(2)}, u32[]{:S(2)}) collective-permute-start(bf16[384,128]{1,0:T(8,128)(2,1)S(1)} %get-tuple-element.50), channel_id=1, source_target_pairs={{0,31},{1,2},{2,1},{3,4},{4,3},{5,6},{6,5},{7,8},{8,7},{9,10},{10,... | collective-permute-start | bytes 294920 | tf_op jit(solution)/shard_map/ppermute | solution.py:326
  37.2 7.7 %collective-permute-start.11 = (bf16[384,128]{1,0:T(8,128)(2,1)S(1)}, bf16[384,128]{1,0:T(8,128)(2,1)S(1)}, u32[]{:S(2)}, u32[]{:S(2)}) collective-permute-start(bf16[384,128]{1,0:T(8,128)(2,1)S(1)} %get-tuple-element.55), channel_id=1, source_target_pairs={{0,31},{1,2},{2,1},{3,4},{4,3},{5,6},{6,5},{7,8},{8,7},{9,10},{10,... | collective-permute-start | bytes 294920 | tf_op jit(solution)/shard_map/ppermute | solution.py:326
  39.7 0.7 %copy-start.7 = (f32[5]{0:T(128)S(1)}, f32[5]{0:T(128)}, u32[]{:S(2)}) copy-start(f32[5]{0:T(128)} %coef.1) | copy-start | bytes 64
  39.7 5.3 %collective-permute-start.12 = (bf16[384,128]{1,0:T(8,128)(2,1)S(1)}, bf16[384,128]{1,0:T(8,128)(2,1)S(1)}, u32[]{:S(2)}, u32[]{:S(2)}) collective-permute-start(bf16[384,128]{1,0:T(8,128)(2,1)S(1)} %get-tuple-element.56), channel_id=1, source_target_pairs={{0,1},{1,0},{2,3},{3,2},{4,5},{5,4},{6,7},{7,6},{8,9},{9,8},{10,11... | collective-permute-start | bytes 294920 | tf_op jit(solution)/shard_map/ppermute | solution.py:327
  45.7 1.9 %collective-permute-start.13 = (bf16[32,512]{1,0:T(8,128)(2,1)S(1)}, bf16[32,512]{1,0:T(8,128)(2,1)S(1)}, u32[]{:S(2)}, u32[]{:S(2)}) collective-permute-start(bf16[32,512]{1,0:T(8,128)(2,1)S(1)} %get-tuple-element.58), channel_id=1, source_target_pairs={{0,1},{1,0},{2,3},{3,2},{4,5},{5,4},{6,7},{7,6},{8,9},{9,8},{10,11... | collective-permute-start | bytes 98312 | tf_op jit(solution)/shard_map/ppermute | solution.py:332
  45.8 4.2 %collective-permute-start.14 = (bf16[32,512]{1,0:T(8,128)(2,1)S(1)}, bf16[32,512]{1,0:T(8,128)(2,1)S(1)}, u32[]{:S(2)}, u32[]{:S(2)}) collective-permute-start(bf16[32,512]{1,0:T(8,128)(2,1)S(1)} %get-tuple-element.59), channel_id=1, source_target_pairs={{0,2},{1,3},{2,0},{3,1},{4,6},{5,7},{6,4},{7,5},{8,10},{9,11},{10,... | collective-permute-start | bytes 98312 | tf_op jit(solution)/shard_map/ppermute | solution.py:332
  45.8 4.1 %collective-permute-start.15 = (bf16[32,512]{1,0:T(8,128)(2,1)S(1)}, bf16[32,512]{1,0:T(8,128)(2,1)S(1)}, u32[]{:S(2)}, u32[]{:S(2)}) collective-permute-start(bf16[32,512]{1,0:T(8,128)(2,1)S(1)} %get-tuple-element.60), channel_id=1, source_target_pairs={{0,3},{1,2},{2,1},{3,0},{4,7},{5,6},{6,5},{7,4},{8,11},{9,10},{10,... | collective-permute-start | bytes 98312 | tf_op jit(solution)/shard_map/ppermute | solution.py:332

commit v7 on v6

--- a/solution.py
+++ b/solution.py
@@ -21,6 +21,8 @@
 HALO = BAND * TILE_ATOMS * ORB
 GROUP = 4
 GROUP_SPAN = 384
+HALF = ATOM_Q * ORB
+NEAR = 3
 BF = jnp.bfloat16
 F32 = jnp.float32
 NT = (((1,), (1,)), ((), ()))
@@ -132,28 +134,32 @@
     return nt_dot(blocks, jnp.concatenate(onehot, axis=0))
 
 
-def put_dense(band, dense, first, add):
-    low = iota((ORB, 128), 1) < WIN_ATOMS
+def put_dense(band, dense, first, base=None):
+    quarter_lane = iota((ORB, 128), 1) // ATOM_Q
     for sp in range(GROUP // 2):
         s = first + 2 * sp
         pair, at_row = s // PAIR_ATOMS, s % PAIR_ATOMS * ORB
-        for j in range(ORB // 2):
-            x = dense[2 * j * ORB : (2 * j + 1) * ORB, sp * 128 : sp * 128 + 128]
-            y = dense[(2 * j + 1) * ORB : (2 * j + 2) * ORB, sp * 128 : sp * 128 + 128]
-            lanes = slice(j * 128, j * 128 + 128)
-            both = (
-                jnp.where(low, x, pltpu.roll(y, WIN_ATOMS, 1)),
-                jnp.where(low, pltpu.roll(x, WIN_ATOMS, 1), y),
-            )
-            for n, value in enumerate(both):
-                rows = slice(at_row + n * ORB, at_row + (n + 1) * ORB)
-                if add:
-                    value = value + band[pair, rows, lanes].astype(F32)
-                band[pair, rows, lanes] = value.astype(BF)
-
-
-def odd_tile(atom):
-    return jnp.floor(atom * (1.0 / TILE_ATOMS)) - 2.0 * jnp.floor(atom * (0.5 / TILE_ATOMS))
+        for m in range(ORB // 4):
+            x = [
+                dense[(4 * m + i) * ORB : (4 * m + i + 1) * ORB, sp * 128 : sp * 128 + 128] for i in range(4)
+            ]
+            for c in range(4):
+                turned = [pltpu.roll(x[i], (i - c) % 4 * ATOM_Q, 1) if i != c else x[i] for i in range(4)]
+                value = turned[0]
+                for i in range(1, 4):
+                    value = jnp.where(quarter_lane == i, turned[i], value)
+                rows = slice(at_row + c // 2 * ORB, at_row + (c // 2 + 1) * ORB)
+                lo = c % 2 * HALF + m * 128
+                if base is not None:
+                    value = value + base[pair, rows, lo : lo + 128].astype(F32)
+                band[pair, rows, lo : lo + 128] = value.astype(BF)
+
+
+def column_of(atom, offset):
+    target = TILE_ATOMS * (jnp.floor(atom * (1.0 / TILE_ATOMS)) - BAND) + offset
+    base = BAND * TILE_ATOMS - PAIR_ATOMS * jnp.floor(atom * (1.0 / PAIR_ATOMS))
+    outside = jnp.where(target < 0.0, target + (base + ATOM_Q), target + base)
+    return jnp.where((target >= 0.0) & (target < float(ATOM_Q)), target, outside)
 
 
 def own_kernel(feat, src, dst, cell, cell_bias, w_in, w_out, band, w_in_t, bias_t, w_out_t, blk, bias8, rows):
@@ -171,68 +177,75 @@
     ids = edge_ids(src[...], dst[...], cell[...])
     atom = row_of(ids[0])
     rows[0:1, :] = atom
-    rows[1:2, :] = row_of(ids[1]) + TILE_ATOMS * odd_tile(atom)
+    rows[1:2, :] = column_of(atom, row_of(ids[1]))
     blk[...] = pair_blocks(feat[...], row_of(ids[2]), w_in_t, bias_t, w_out_t)
     for first in range(0, ATOM_Q, GROUP):
         start = jnp.sum((ids[0] < float(first)).astype(F32)).astype(jnp.int32)
         at = pl.multiple_of(jnp.minimum(start // 128 * 128, own - GROUP_SPAN), 128)
         span = pl.ds(at, GROUP_SPAN)
-        put_dense(band, dense_of(blk[:, span], rows[0:1, span], rows[1:2, span], first), first, False)
+        put_dense(band, dense_of(blk[:, span], rows[0:1, span], rows[1:2, span], first), first)
 
 
 def spill_kernel(own_band, blue, red, w_in_t, bias_t, w_out_t, band, blk, spill):
-    side = device_side()
+    even = device_side() == 0
     nfeat = spill.shape[1]
     rows = spill.shape[0] // 2
-    for m, (msg, gap) in enumerate(((blue, side == 0), (red, side == 1))):
-        base = m * rows
-        spill[base : base + 64, :] = jnp.zeros((64, nfeat), BF)
-        spill[base + rows - 64 : base + rows, :] = jnp.zeros((64, nfeat), BF)
-        at = pl.multiple_of(base + jnp.where(gap, 64, 0), 64)
-        spill[pl.ds(at, SPILL), :] = msg[0:SPILL, :]
-    ids, ends = [], []
-    for msg in (blue, red):
+    left, right = [jnp.where(even, x, y) for x, y in ((blue[...], red[...]), (red[...], blue[...]))]
+    spill[0:64, :] = jnp.zeros((64, nfeat), BF)
+    spill[64 : rows + SPILL, :] = jnp.concatenate([left[0:SPILL], right[0:SPILL]], axis=0)
+    spill[rows + SPILL :, :] = jnp.zeros((64, nfeat), BF)
+    ids = []
+    for msg in (left, right):
         block = msg[SPILL : SPILL + ID_ROWS, 0:128].astype(F32)
-        a = block[0:3]
-        mine = (a >= 0.0) & (a < float(ATOM_Q))
         ids.append([row_of(block[3 * k : 3 * k + 3]) for k in range(3)])
-        ends.append(
-            (
-                jnp.min(jnp.where(mine, a, float(ATOM_Q))).astype(jnp.int32),
-                jnp.max(jnp.where(mine, a, -1.0)).astype(jnp.int32),
-            )
-        )
+    atoms = [x[0] for x in ids]
+    cols = [column_of(x[0], x[1]) for x in ids]
+    mine = [(a >= 0.0) & (a < float(ATOM_Q)) for a in atoms]
+    highest = jnp.max(jnp.where(mine[0], atoms[0], -1.0)).astype(jnp.int32)
+    lowest = jnp.min(jnp.where(mine[1], atoms[1], float(ATOM_Q))).astype(jnp.int32)
     cells = jnp.concatenate([x[2] for x in ids], axis=1)
     blk[...] = pair_blocks(spill[...], cells, w_in_t, bias_t, w_out_t)
-    band[...] = own_band[...]
-    for m in range(2):
-        atom, target = ids[m][0], ids[m][1] + TILE_ATOMS * odd_tile(ids[m][0])
-        lowest, highest = ends[m]
-        for first in range(0, ATOM_Q, GROUP):
-
-            @pl.when((lowest < first + GROUP) & (highest >= first))
-            def _(m=m, first=first, atom=atom, target=target):
-                dense = dense_of(blk[:, m * rows : (m + 1) * rows], atom, target, first)
-                put_dense(band, dense, first, True)
-
-
-def apply_band(band, wide, pair):
-    height = PAIR_ATOMS * ORB
-    pieces = [
-        wide[pl.ds(pair * height + q, WIN_ATOMS, stride=ORB), :] for q in range(ORB)
+    spans = [slice(0, rows), slice(rows, 2 * rows)]
+    ngroup = ATOM_Q // GROUP
+    for g in range(ngroup):
+        first = g * GROUP
+        sides = [m for m in range(2) if (g < NEAR, g >= ngroup - NEAR)[m]]
+        if sides:
+            (m,) = sides
+            put_dense(band, dense_of(blk[:, spans[m]], atoms[m], cols[m], first), first, own_band)
+        else:
+            pair, at = first // PAIR_ATOMS, first % PAIR_ATOMS * ORB
+            band[pair, at : at + GROUP * ORB, :] = own_band[pair, at : at + GROUP * ORB, :]
+    for m, far in ((0, range(NEAR, ngroup)), (1, range(ngroup - NEAR))):
+        for g in far:
+            first = g * GROUP
+
+            @pl.when(highest >= first if m == 0 else lowest < first + GROUP)
+            def _(m=m, first=first):
+                put_dense(band, dense_of(blk[:, spans[m]], atoms[m], cols[m], first), first, band)
+
+
+def own_part(band, field):
+    pieces = [field[pl.ds(q, ATOM_Q, stride=ORB), :].astype(BF) for q in range(ORB)]
+    rhs = jnp.concatenate(pieces, axis=0)
+    return [jnp.dot(band[k, :, :HALF], rhs, preferred_element_type=F32) for k in range(band.shape[0])]
+
+
+def halo_part(band, blue, red, wide):
+    even = device_side() == 0
+    wide[0:HALO, :] = jnp.where(even, blue[...], red[...]).astype(F32)
+    wide[HALO : 2 * HALO, :] = jnp.where(even, red[...], blue[...]).astype(F32)
+    atoms = BAND * TILE_ATOMS
+    pieces = [[], []]
+    for q in range(ORB):
+        left = wide[pl.ds(q, atoms, stride=ORB), :]
+        right = wide[pl.ds(HALO + q, atoms, stride=ORB), :]
+        pieces[0].append(jnp.concatenate([left, right[:TILE_ATOMS]], axis=0).astype(BF))
+        pieces[1].append(jnp.concatenate([left[atoms - TILE_ATOMS :], right], axis=0).astype(BF))
+    return [
+        jnp.dot(band[k, :, HALF:], jnp.concatenate(pieces[k], axis=0), preferred_element_type=F32)
+        for k in range(band.shape[0])
     ]
-    rhs = jnp.concatenate(pieces, axis=0).astype(BF)
-    return jnp.dot(band[pair], rhs, preferred_element_type=F32)
-
-
-def fill_wide(own, blue, red, wide):
-    side = device_side()
-    rows = own.shape[0]
-    end = HALO + rows
-    off = pl.multiple_of(side * end, 128)
-    wide[pl.ds(off, HALO), :] = blue
-    wide[pl.ds(pl.multiple_of(end - off, 128), HALO), :] = red
-    wide[HALO:end, :] = own
 
 
 def put_sends(value_ref, to_blue, to_red):
@@ -243,36 +256,45 @@
     to_red[...] = value_ref[pl.ds(pl.multiple_of(inner - off, 128), HALO), :].astype(BF)
 
 
+def spans_of(band):
+    height = band.shape[1]
+    return [slice(k * height, (k + 1) * height) for k in range(band.shape[0])]
+
+
 def first_kernel(band, t0, blue, red, t1, to_blue, to_red, wide):
-    fill_wide(t0[...], blue[...].astype(F32), red[...].astype(F32), wide)
-    height = PAIR_ATOMS * ORB
-    for pair in range(band.shape[0]):
-        t1[pair * height : (pair + 1) * height, :] = apply_band(band, wide, pair)
+    inner, outer = own_part(band, t0), halo_part(band, blue, red, wide)
+    for k, span in enumerate(spans_of(band)):
+        t1[span, :] = inner[k] + outer[k]
     put_sends(t1, to_blue, to_red)
 
 
-def next_kernel(band, before, now, blue, red, after, to_blue, to_red, wide):
-    fill_wide(now[...], blue[...].astype(F32), red[...].astype(F32), wide)
-    height = PAIR_ATOMS * ORB
-    for pair in range(band.shape[0]):
-        span = slice(pair * height, (pair + 1) * height)
-        after[span, :] = 2.0 * apply_band(band, wide, pair) - before[span, :]
+def inner_kernel(band, before, now, part):
+    inner = own_part(band, now)
+    for k, span in enumerate(spans_of(band)):
+        part[span, :] = 2.0 * inner[k] - before[span, :]
+
+
+def outer_kernel(band, part, blue, red, after, to_blue, to_red, wide):
+    outer = halo_part(band, blue, red, wide)
+    for k, span in enumerate(spans_of(band)):
+        after[span, :] = 2.0 * outer[k] + part[span, :]
     put_sends(after, to_blue, to_red)
 
 
-def mix_kernel(coef, t0, t1, t2, t3, base, final):
-    total = coef[0] * t0[...] + coef[1] * t1[...] + (coef[2] - coef[4]) * t2[...] + coef[3] * t3[...]
-    base[...] = total.T
+def mix_kernel(coef, band, t0, t1, t2, t3, base, final):
+    inner = own_part(band, t3)
+    for k, span in enumerate(spans_of(band)):
+        total = coef[0] * t0[span, :] + coef[1] * t1[span, :] + (coef[2] - coef[4]) * t2[span, :]
+        total = total + coef[3] * t3[span, :] + 2.0 * coef[4] * inner[k]
+        base[:, span] = total.T
     final[...] = jnp.full(final.shape, 2.0 * coef[4], F32)
 
 
-def last_kernel(final, band, base, t3, blue, red, p0, p1, p2, p3, wide, out):
+def last_kernel(final, band, base, blue, red, p0, p1, p2, p3, wide, out):
     member = lax.axis_index("edges")
-    fill_wide(t3[...], blue[...].astype(F32), red[...].astype(F32), wide)
-    height = PAIR_ATOMS * ORB
-    for pair in range(band.shape[0]):
-        span = slice(pair * height, (pair + 1) * height)
-        out[:, span] = base[:, span] + (final[0:1, :] * apply_band(band, wide, pair)).T
+    outer = halo_part(band, blue, red, wide)
+    for k, span in enumerate(spans_of(band)):
+        out[:, span] = base[:, span] + (final[0:1, :] * outer[k]).T
     for k, piece in enumerate((p0, p1, p2, p3)):
         high = piece.shape[0]
         piece[...] = out[pl.ds(pl.multiple_of((member ^ k) * high, high), high), :].astype(BF)
@@ -385,18 +407,26 @@
         micros=0,
     )
 
-    wide = pltpu.VMEM((nrow + 2 * HALO, VEC), F32)
+    wide = pltpu.VMEM((2 * HALO, VEC), F32)
     t1, to_blue, to_red = call(first_kernel, "first", (full, part, part), [wide], band, t0, blue, red)
     fields = [t0, t1]
     for _ in range(2, STEPS):
         blue, red = swap(to_blue, to_red)
+        (inner,) = call(inner_kernel, "inner", (full,), [], band, fields[-2], fields[-1])
         following, to_blue, to_red = call(
-            next_kernel, "next", (full, part, part), [wide], band, fields[-2], fields[-1], blue, red
+            outer_kernel, "outer", (full, part, part), [wide], band, inner, blue, red
         )
         fields.append(following)
     blue, red = swap(to_blue, to_red)
     base, final = call(
-        mix_kernel, "mix", (shape((VEC, nrow), F32), shape((8, VEC), F32)), [], cheb_coef, *fields, smem=(0,)
+        mix_kernel,
+        "mix",
+        (shape((VEC, nrow), F32), shape((8, VEC), F32)),
+        [],
+        cheb_coef,
+        band,
+        *fields,
+        smem=(0,),
     )
     pieces = call(
         last_kernel,
@@ -406,7 +436,6 @@
         final,
         band,
         base,
-        fields[-1],
         blue,
         red,
     )

time: 50.9 us -> 50.2 us (0.986)
  waiting for transfers between devices: 17.4 us -> 14.4 us
  starting transfers between devices: 20.8 us -> 22.1 us
  Pallas kernels: 10.9 us -> 11.9 us
    ppermute x5, waiting for transfers between devices: 15.1 us -> 12 us  [swap(): lax.ppermute(first, axes, blue_pairs)]
    ppermute x5, starting transfers between devices: 15.6 us -> 17 us  [swap(): lax.ppermute(first, axes, blue_pairs)]
    pallas_call x10 -> x12, Pallas kernels: 10.9 us -> 11.9 us  [call(): pl.pallas_call(kernel, name=name, out_shape=outs, in_specs=spaces, out_sp...]
  transfers between devices with their start and end apart: 16 -> 16, of which waited for: 5 -> 4; matrix products, arithmetic and copies ran while one was open for 0% -> 0% of each run, Pallas kernels for 11% -> 14%
where the time goes in v7:
time: 50.2 us; the launch traced here: 50 us
  starting transfers between devices  22.1 us (44%)
  waiting for transfers between devices  14.4 us (29%)
  Pallas kernels  11.9 us (24%)
  local copies, waits for them, and re-layouts  1.44 us (3%)
    ppermute x5, starting transfers between devices, swap(): lax.ppermute(first, axes, blue_pairs)  17 us
    ppermute x5, waiting for transfers between devices, swap(): lax.ppermute(first, axes, blue_pairs)  12 us
    pallas_call x12, Pallas kernels, call(): pl.pallas_call(kernel, name=name, out_shape=outs, in_specs=spaces, out_sp...  11.9 us
    ppermute x6, starting transfers between devices, exchange(): lax.ppermute(pieces[k], 'edges', [(i, i ^ k) for i in range(nedge)])  5.08 us
    ppermute x6, waiting for transfers between devices, exchange(): lax.ppermute(pieces[k], 'edges', [(i, i ^ k) for i in range(nedge)])  2.31 us
    unnamed x18, local copies, waits for them, and re-layouts  1.44 us
  transfers between devices with their start and end apart: 16, of which 4 were waited for; matrix products, arithmetic and copies ran while one was open for 0% of the time, Pallas kernels for 14%

profile of v7, /device:TPU:0, one launch (start us, length us, event | category | flops | bytes accessed | tf_op | source)
XLA Modules:
  0.0 50.0 jit_solution(12884175713179376520)
XLA Ops:
  0.0 2.0 %prep.1 = (bf16[32,512]{1,0:T(8,128)(2,1)}, bf16[32,512]{1,0:T(8,128)(2,1)}, bf16[32,512]{1,0:T(8,128)(2,1)}, bf16[32,512]{1,0:T(8,128)(2,1)}, bf16[336,256]{1,0:T(8,128)(2,1)}, /*index=5*/bf16[336,256]{1,0:T(8,128)(2,1)}) custom-call(f32[32,2048]{1,0:T(8,128)} %vec_hbm.1, bf16[1280,256]{1,0:T(8,128)(2,1)} %feat.3, s32[10,128]{1,0:T(8,128)} %bitcast.3, ...), custom_call_target="tpu_custom_call" | custom-call | flops 1000000000 | tf_op jit(solution)/shard_map/prep/pallas_call | solution.py:323
  2.0 0.5 %collective-permute-start.2 = (bf16[32,512]{1,0:T(8,128)(2,1)}, bf16[32,512]{1,0:T(8,128)(2,1)S(1)}, u32[]{:S(2)}, u32[]{:S(2)}) collective-permute-start(bf16[32,512]{1,0:T(8,128)(2,1)} %get-tuple-element.40), channel_id=1, source_target_pairs={{0,1},{1,0},{2,3},{3,2},{4,5},{5,4},{6,7},{7,6},{8,9},{9,8},{10,11... | collective-permute-start | bytes 98312 | tf_op jit(solution)/shard_map/ppermute | solution.py:354
  2.5 2.6 %collective-permute-start.3 = (bf16[32,512]{1,0:T(8,128)(2,1)}, bf16[32,512]{1,0:T(8,128)(2,1)S(1)}, u32[]{:S(2)}, u32[]{:S(2)}) collective-permute-start(bf16[32,512]{1,0:T(8,128)(2,1)} %get-tuple-element.41), channel_id=1, source_target_pairs={{0,2},{1,3},{2,0},{3,1},{4,6},{5,7},{6,4},{7,5},{8,10},{9,11},{10,... | collective-permute-start | bytes 98312 | tf_op jit(solution)/shard_map/ppermute | solution.py:354
  5.1 0.1 collective-permute-start.4
  5.2 5.7 %collective-permute-start = (bf16[336,256]{1,0:T(8,128)(2,1)}, bf16[336,256]{1,0:T(8,128)(2,1)S(1)}, u32[]{:S(2)}, u32[]{:S(2)}) collective-permute-start(bf16[336,256]{1,0:T(8,128)(2,1)} %get-tuple-element.34), channel_id=1, source_target_pairs={{0,31},{1,2},{2,1},{3,4},{4,3},{5,6},{6,5},{7,8},{8,7},{9,10},{10,... | collective-permute-start | bytes 516104 | tf_op jit(solution)/shard_map/ppermute | solution.py:348
  10.9 0.0 collective-permute-start.1
  10.9 0.0 collective-permute-done.2.p1
  10.9 0.0 collective-permute-done.3.p2
  10.9 0.0 collective-permute-done.4.p3
  10.9 0.7 %copy-done.8 = bf16[32,512]{1,0:T(8,128)(2,1)S(1)} copy-done((bf16[32,512]{1,0:T(8,128)(2,1)S(1)}, bf16[32,512]{1,0:T(8,128)(2,1)}, u32[]{:S(2)}) %copy-start.8) | copy-done | bytes 32792
  11.6 0.0 copy-start.4
  11.7 0.0 copy-start.5
  11.7 0.0 copy-start.6
  11.7 0.2 field.1
  11.9 2.5 %collective-permute-start.5 = (bf16[384,128]{1,0:T(8,128)(2,1)S(1)}, bf16[384,128]{1,0:T(8,128)(2,1)S(1)}, u32[]{:S(2)}, u32[]{:S(2)}) collective-permute-start(bf16[384,128]{1,0:T(8,128)(2,1)S(1)} %get-tuple-element.44), channel_id=1, source_target_pairs={{0,31},{1,2},{2,1},{3,4},{4,3},{5,6},{6,5},{7,8},{8,7},{9,10},{10,... | collective-permute-start | bytes 294920 | tf_op jit(solution)/shard_map/ppermute | solution.py:348
  14.4 0.0 collective-permute-start.6
  14.5 2.5 %own.1 = (bf16[2,256,1024]{2,1,0:T(8,128)(2,1)S(1)}, bf16[512,256]{1,0:T(8,128)(2,1)S(1)}, bf16[512,8]{1,0:T(8,128)(2,1)S(1)}, bf16[256,256]{1,0:T(8,128)(2,1)S(1)}) custom-call(bf16[1280,256]{1,0:T(8,128)(2,1)S(1)} %copy-done, s32[10,128]{1,0:T(8,128)S(1)} %bitcast.4, s32[10,128]{1,0:T(8,128)S(1)} %bitcast.6, s32[10,128]{1,0:T(8,128)S(1)} %bitcast.8, ...), custom_call_target="tpu_custom_call" | custom-call | flops 4000000000 | tf_op jit(solution)/shard_map/own/pallas_call | solution.py:323
  16.9 0.0 collective-permute-done.blue
  17.0 0.0 collective-permute-done.1.red
  17.0 2.8 %spill.1.band = bf16[2,256,1024]{2,1,0:T(8,128)(2,1)S(1)} custom-call(bf16[2,256,1024]{2,1,0:T(8,128)(2,1)S(1)} %get-tuple-element.33.own_band, bf16[336,256]{1,0:T(8,128)(2,1)S(1)} %collective-permute-done.blue, bf16[336,256]{1,0:T(8,128)(2,1)S(1)} %collective-permute-done.1.red, ...), custom_call_target="tpu_custom_call", output_to_operand_aliasing={{}: (0, {})} | custom-call | tf_op jit(solution)/shard_map/spill/pallas_call | solution.py:323
  19.8 0.0 collective-permute-done.5.blue
  19.8 0.0 collective-permute-done.6.red
  19.8 0.6 %first.1 = (f32[512,128]{1,0:T(8,128)S(1)}, bf16[384,128]{1,0:T(8,128)(2,1)S(1)}, bf16[384,128]{1,0:T(8,128)(2,1)S(1)}) custom-call(bf16[2,256,1024]{2,1,0:T(8,128)(2,1)S(1)} %spill.1.band, f32[512,128]{1,0:T(8,128)S(1)} %get-tuple-element.43.t0.before, bf16[384,128]{1,0:T(8,128)(2,1)S(1)} %collective-permute-done.5.blue, ...), custom_call_target="tpu_custom_call" | custom-call | flops 1000000000 | tf_op jit(solution)/shard_map/first/pallas_call | solution.py:323
  20.5 2.9 %collective-permute-start.7 = (bf16[384,128]{1,0:T(8,128)(2,1)S(1)}, bf16[384,128]{1,0:T(8,128)(2,1)S(1)}, u32[]{:S(2)}, u32[]{:S(2)}) collective-permute-start(bf16[384,128]{1,0:T(8,128)(2,1)S(1)} %get-tuple-element.47), channel_id=1, source_target_pairs={{0,31},{1,2},{2,1},{3,4},{4,3},{5,6},{6,5},{7,8},{8,7},{9,10},{10,... | collective-permute-start | bytes 294920 | tf_op jit(solution)/shard_map/ppermute | solution.py:348
  23.4 0.0 collective-permute-start.8
  23.4 0.3 inner.2.part
  23.7 4.4 %collective-permute-done.7.blue = bf16[384,128]{1,0:T(8,128)(2,1)S(1)} collective-permute-done((bf16[384,128]{1,0:T(8,128)(2,1)S(1)}, bf16[384,128]{1,0:T(8,128)(2,1)S(1)}, u32[]{:S(2)}, u32[]{:S(2)}) %collective-permute-start.7) | collective-permute-done | bytes 98336 | tf_op jit(solution)/shard_map/ppermute | solution.py:348
  28.2 0.0 collective-permute-done.8.red
  28.2 0.4 outer.2
  28.6 0.1 collective-permute-start.10
  28.7 2.9 %collective-permute-start.9 = (bf16[384,128]{1,0:T(8,128)(2,1)S(1)}, bf16[384,128]{1,0:T(8,128)(2,1)S(1)}, u32[]{:S(2)}, u32[]{:S(2)}) collective-permute-start(bf16[384,128]{1,0:T(8,128)(2,1)S(1)} %get-tuple-element.50), channel_id=1, source_target_pairs={{0,31},{1,2},{2,1},{3,4},{4,3},{5,6},{6,5},{7,8},{8,7},{9,10},{10,... | collective-permute-start | bytes 294920 | tf_op jit(solution)/shard_map/ppermute | solution.py:348
  31.6 0.3 inner.3.part
  32.0 0.0 collective-permute-done.10.red
  32.0 4.4 %collective-permute-done.9.blue = bf16[384,128]{1,0:T(8,128)(2,1)S(1)} collective-permute-done((bf16[384,128]{1,0:T(8,128)(2,1)S(1)}, bf16[384,128]{1,0:T(8,128)(2,1)S(1)}, u32[]{:S(2)}, u32[]{:S(2)}) %collective-permute-start.9) | collective-permute-done | bytes 98336 | tf_op jit(solution)/shard_map/ppermute | solution.py:348
  36.4 0.4 outer.3
  36.8 2.9 %collective-permute-start.11 = (bf16[384,128]{1,0:T(8,128)(2,1)S(1)}, bf16[384,128]{1,0:T(8,128)(2,1)S(1)}, u32[]{:S(2)}, u32[]{:S(2)}) collective-permute-start(bf16[384,128]{1,0:T(8,128)(2,1)S(1)} %get-tuple-element.55), channel_id=1, source_target_pairs={{0,31},{1,2},{2,1},{3,4},{4,3},{5,6},{6,5},{7,8},{8,7},{9,10},{10,... | collective-permute-start | bytes 294920 | tf_op jit(solution)/shard_map/ppermute | solution.py:348
  39.8 0.0 collective-permute-start.12
  39.8 0.7 %copy-done.7 = f32[5]{0:T(128)S(1)} copy-done((f32[5]{0:T(128)S(1)}, f32[5]{0:T(128)}, u32[]{:S(2)}) %copy-start.7) | copy-done | bytes 44
  40.4 0.9 %mix.1 = (f32[128,512]{1,0:T(8,128)S(1)}, f32[8,128]{1,0:T(8,128)S(1)}) custom-call(f32[5]{0:T(128)S(1)} %copy-done.7, bf16[2,256,1024]{2,1,0:T(8,128)(2,1)S(1)} %spill.1.band, f32[512,128]{1,0:T(8,128)S(1)} %get-tuple-element.43.t0.before, f32[512,128]{1,0:T(8,128)S(1)} %get-tuple-element.46.now.before.t1, f32[512,128]{1,0:T(8,128)S(1)} %get-tuple-element.49.now.t2, ...), custom_call_target="tpu_custom_call" | custom-call | flops 1000000000 | tf_op jit(solution)/shard_map/mix/pallas_call | solution.py:323
  41.4 3.2 %collective-permute-done.11.blue = bf16[384,128]{1,0:T(8,128)(2,1)S(1)} collective-permute-done((bf16[384,128]{1,0:T(8,128)(2,1)S(1)}, bf16[384,128]{1,0:T(8,128)(2,1)S(1)}, u32[]{:S(2)}, u32[]{:S(2)}) %collective-permute-start.11) | collective-permute-done | bytes 98336 | tf_op jit(solution)/shard_map/ppermute | solution.py:348
  44.6 0.0 collective-permute-done.12.red
  44.6 0.5 last.1
  45.0 0.1 collective-permute-start.13
  45.1 0.1 collective-permute-start.14
  45.2 1.8 %collective-permute-start.15 = (bf16[32,512]{1,0:T(8,128)(2,1)S(1)}, bf16[32,512]{1,0:T(8,128)(2,1)S(1)}, u32[]{:S(2)}, u32[]{:S(2)}) collective-permute-start(bf16[32,512]{1,0:T(8,128)(2,1)S(1)} %get-tuple-element.60), channel_id=1, source_target_pairs={{0,3},{1,2},{2,1},{3,0},{4,7},{5,6},{6,5},{7,4},{8,11},{9,10},{10,... | collective-permute-start | bytes 98312 | tf_op jit(solution)/shard_map/ppermute | solution.py:354
  47.0 0.0 collective-permute-done.13.p1
  47.0 2.3 %collective-permute-done.14.p2 = bf16[32,512]{1,0:T(8,128)(2,1)S(1)} collective-permute-done((bf16[32,512]{1,0:T(8,128)(2,1)S(1)}, bf16[32,512]{1,0:T(8,128)(2,1)S(1)}, u32[]{:S(2)}, u32[]{:S(2)}) %collective-permute-start.14) | collective-permute-done | bytes 32800 | tf_op jit(solution)/shard_map/ppermute | solution.py:354
  49.3 0.7 %join.1 = f32[32,2048]{1,0:T(8,128)} custom-call(bf16[32,512]{1,0:T(8,128)(2,1)S(1)} %get-tuple-element.57.p0, bf16[32,512]{1,0:T(8,128)(2,1)S(1)} %collective-permute-done.13.p1, bf16[32,512]{1,0:T(8,128)(2,1)S(1)} %collective-permute-done.14.p2, bf16[32,512]{1,0:T(8,128)(2,1)S(1)} %collective-permute-done.15.p3), custom_call_target="tpu_custom_call" | custom-call | flops 1000000000 | tf_op jit(solution)/shard_map/join/pallas_call | solution.py:323
  (14 shorter events, 0.0 us)
Async XLA Ops:
  2.0 8.8 %collective-permute-start.2 = (bf16[32,512]{1,0:T(8,128)(2,1)}, bf16[32,512]{1,0:T(8,128)(2,1)S(1)}, u32[]{:S(2)}, u32[]{:S(2)}) collective-permute-start(bf16[32,512]{1,0:T(8,128)(2,1)} %get-tuple-element.40), channel_id=1, source_target_pairs={{0,1},{1,0},{2,3},{3,2},{4,5},{5,4},{6,7},{7,6},{8,9},{9,8},{10,11... | collective-permute-start | bytes 98312 | tf_op jit(solution)/shard_map/ppermute | solution.py:354
  2.5 8.3 %collective-permute-start.3 = (bf16[32,512]{1,0:T(8,128)(2,1)}, bf16[32,512]{1,0:T(8,128)(2,1)S(1)}, u32[]{:S(2)}, u32[]{:S(2)}) collective-permute-start(bf16[32,512]{1,0:T(8,128)(2,1)} %get-tuple-element.41), channel_id=1, source_target_pairs={{0,2},{1,3},{2,0},{3,1},{4,6},{5,7},{6,4},{7,5},{8,10},{9,11},{10,... | collective-permute-start | bytes 98312 | tf_op jit(solution)/shard_map/ppermute | solution.py:354
  5.1 5.8 %collective-permute-start.4 = (bf16[32,512]{1,0:T(8,128)(2,1)}, bf16[32,512]{1,0:T(8,128)(2,1)S(1)}, u32[]{:S(2)}, u32[]{:S(2)}) collective-permute-start(bf16[32,512]{1,0:T(8,128)(2,1)} %get-tuple-element.42), channel_id=1, source_target_pairs={{0,3},{1,2},{2,1},{3,0},{4,7},{5,6},{6,5},{7,4},{8,11},{9,10},{10,... | collective-permute-start | bytes 98312 | tf_op jit(solution)/shard_map/ppermute | solution.py:354
  5.2 11.8 %collective-permute-start = (bf16[336,256]{1,0:T(8,128)(2,1)}, bf16[336,256]{1,0:T(8,128)(2,1)S(1)}, u32[]{:S(2)}, u32[]{:S(2)}) collective-permute-start(bf16[336,256]{1,0:T(8,128)(2,1)} %get-tuple-element.34), channel_id=1, source_target_pairs={{0,31},{1,2},{2,1},{3,4},{4,3},{5,6},{6,5},{7,8},{8,7},{9,10},{10,... | collective-permute-start | bytes 516104 | tf_op jit(solution)/shard_map/ppermute | solution.py:348
  10.9 6.1 %collective-permute-start.1 = (bf16[336,256]{1,0:T(8,128)(2,1)}, bf16[336,256]{1,0:T(8,128)(2,1)S(1)}, u32[]{:S(2)}, u32[]{:S(2)}) collective-permute-start(bf16[336,256]{1,0:T(8,128)(2,1)} %get-tuple-element.35), channel_id=1, source_target_pairs={{0,1},{1,0},{2,3},{3,2},{4,5},{5,4},{6,7},{7,6},{8,9},{9,8},{10,11... | collective-permute-start | bytes 516104 | tf_op jit(solution)/shard_map/ppermute | solution.py:349
  10.9 0.8 %copy-start.8 = (bf16[32,512]{1,0:T(8,128)(2,1)S(1)}, bf16[32,512]{1,0:T(8,128)(2,1)}, u32[]{:S(2)}) copy-start(bf16[32,512]{1,0:T(8,128)(2,1)} %get-tuple-element.39.p0) | copy-start | bytes 98308
  11.6 2.8 %copy-start = (bf16[1280,256]{1,0:T(8,128)(2,1)S(1)}, bf16[1280,256]{1,0:T(8,128)(2,1)}, u32[]{:S(2)}) copy-start(bf16[1280,256]{1,0:T(8,128)(2,1)} %feat.3) | copy-start | bytes 1966084
  11.6 2.8 %copy-start.1 = (bf16[256,512]{1,0:T(8,128)(2,1)S(1)}, bf16[256,512]{1,0:T(8,128)(2,1)}, u32[]{:S(2)}) copy-start(bf16[256,512]{1,0:T(8,128)(2,1)} %w_in.1) | copy-start | bytes 786436
  11.6 2.8 %copy-start.2 = (bf16[256,256]{1,0:T(8,128)(2,1)S(1)}, bf16[256,256]{1,0:T(8,128)(2,1)}, u32[]{:S(2)}) copy-start(bf16[256,256]{1,0:T(8,128)(2,1)} %w_out.1) | copy-start | bytes 393220
  11.6 2.8 %copy-start.3 = (s32[1280]{0:T(1024)S(1)}, s32[1280]{0:T(1024)}, u32[]{:S(2)}) copy-start(s32[1280]{0:T(1024)} %param.10) | copy-start | bytes 15364
  11.6 2.8 %copy-start.4 = (s32[1280]{0:T(1024)S(1)}, s32[1280]{0:T(1024)}, u32[]{:S(2)}) copy-start(s32[1280]{0:T(1024)} %param.11) | copy-start | bytes 15364
  11.7 2.8 %copy-start.5 = (s32[1280]{0:T(1024)S(1)}, s32[1280]{0:T(1024)}, u32[]{:S(2)}) copy-start(s32[1280]{0:T(1024)} %param.12) | copy-start | bytes 15364
  11.7 2.8 %copy-start.6 = (bf16[3,512]{1,0:T(4,128)(2,1)S(1)}, bf16[3,512]{1,0:T(4,128)(2,1)}, u32[]{:S(2)}) copy-start(bf16[3,512]{1,0:T(4,128)(2,1)} %cell_bias.1) | copy-start | bytes 9220
  11.9 7.9 %collective-permute-start.5 = (bf16[384,128]{1,0:T(8,128)(2,1)S(1)}, bf16[384,128]{1,0:T(8,128)(2,1)S(1)}, u32[]{:S(2)}, u32[]{:S(2)}) collective-permute-start(bf16[384,128]{1,0:T(8,128)(2,1)S(1)} %get-tuple-element.44), channel_id=1, source_target_pairs={{0,31},{1,2},{2,1},{3,4},{4,3},{5,6},{6,5},{7,8},{8,7},{9,10},{10,... | collective-permute-start | bytes 294920 | tf_op jit(solution)/shard_map/ppermute | solution.py:348
  14.4 5.4 %collective-permute-start.6 = (bf16[384,128]{1,0:T(8,128)(2,1)S(1)}, bf16[384,128]{1,0:T(8,128)(2,1)S(1)}, u32[]{:S(2)}, u32[]{:S(2)}) collective-permute-start(bf16[384,128]{1,0:T(8,128)(2,1)S(1)} %get-tuple-element.45), channel_id=1, source_target_pairs={{0,1},{1,0},{2,3},{3,2},{4,5},{5,4},{6,7},{7,6},{8,9},{9,8},{10,11... | collective-permute-start | bytes 294920 | tf_op jit(solution)/shard_map/ppermute | solution.py:349
  20.5 7.7 %collective-permute-start.7 = (bf16[384,128]{1,0:T(8,128)(2,1)S(1)}, bf16[384,128]{1,0:T(8,128)(2,1)S(1)}, u32[]{:S(2)}, u32[]{:S(2)}) collective-permute-start(bf16[384,128]{1,0:T(8,128)(2,1)S(1)} %get-tuple-element.47), channel_id=1, source_target_pairs={{0,31},{1,2},{2,1},{3,4},{4,3},{5,6},{6,5},{7,8},{8,7},{9,10},{10,... | collective-permute-start | bytes 294920 | tf_op jit(solution)/shard_map/ppermute | solution.py:348
  23.4 4.8 %collective-permute-start.8 = (bf16[384,128]{1,0:T(8,128)(2,1)S(1)}, bf16[384,128]{1,0:T(8,128)(2,1)S(1)}, u32[]{:S(2)}, u32[]{:S(2)}) collective-permute-start(bf16[384,128]{1,0:T(8,128)(2,1)S(1)} %get-tuple-element.48), channel_id=1, source_target_pairs={{0,1},{1,0},{2,3},{3,2},{4,5},{5,4},{6,7},{7,6},{8,9},{9,8},{10,11... | collective-permute-start | bytes 294920 | tf_op jit(solution)/shard_map/ppermute | solution.py:349
  28.6 3.3 %collective-permute-start.10 = (bf16[384,128]{1,0:T(8,128)(2,1)S(1)}, bf16[384,128]{1,0:T(8,128)(2,1)S(1)}, u32[]{:S(2)}, u32[]{:S(2)}) collective-permute-start(bf16[384,128]{1,0:T(8,128)(2,1)S(1)} %get-tuple-element.51), channel_id=1, source_target_pairs={{0,1},{1,0},{2,3},{3,2},{4,5},{5,4},{6,7},{7,6},{8,9},{9,8},{10,11... | collective-permute-start | bytes 294920 | tf_op jit(solution)/shard_map/ppermute | solution.py:349
  28.7 7.7 %collective-permute-start.9 = (bf16[384,128]{1,0:T(8,128)(2,1)S(1)}, bf16[384,128]{1,0:T(8,128)(2,1)S(1)}, u32[]{:S(2)}, u32[]{:S(2)}) collective-permute-start(bf16[384,128]{1,0:T(8,128)(2,1)S(1)} %get-tuple-element.50), channel_id=1, source_target_pairs={{0,31},{1,2},{2,1},{3,4},{4,3},{5,6},{6,5},{7,8},{8,7},{9,10},{10,... | collective-permute-start | bytes 294920 | tf_op jit(solution)/shard_map/ppermute | solution.py:348
  36.8 7.7 %collective-permute-start.11 = (bf16[384,128]{1,0:T(8,128)(2,1)S(1)}, bf16[384,128]{1,0:T(8,128)(2,1)S(1)}, u32[]{:S(2)}, u32[]{:S(2)}) collective-permute-start(bf16[384,128]{1,0:T(8,128)(2,1)S(1)} %get-tuple-element.55), channel_id=1, source_target_pairs={{0,31},{1,2},{2,1},{3,4},{4,3},{5,6},{6,5},{7,8},{8,7},{9,10},{10,... | collective-permute-start | bytes 294920 | tf_op jit(solution)/shard_map/ppermute | solution.py:348
  39.8 0.7 %copy-start.7 = (f32[5]{0:T(128)S(1)}, f32[5]{0:T(128)}, u32[]{:S(2)}) copy-start(f32[5]{0:T(128)} %coef.1) | copy-start | bytes 64
  39.8 4.8 %collective-permute-start.12 = (bf16[384,128]{1,0:T(8,128)(2,1)S(1)}, bf16[384,128]{1,0:T(8,128)(2,1)S(1)}, u32[]{:S(2)}, u32[]{:S(2)}) collective-permute-start(bf16[384,128]{1,0:T(8,128)(2,1)S(1)} %get-tuple-element.56), channel_id=1, source_target_pairs={{0,1},{1,0},{2,3},{3,2},{4,5},{5,4},{6,7},{7,6},{8,9},{9,8},{10,11... | collective-permute-start | bytes 294920 | tf_op jit(solution)/shard_map/ppermute | solution.py:349
  45.0 1.9 %collective-permute-start.13 = (bf16[32,512]{1,0:T(8,128)(2,1)S(1)}, bf16[32,512]{1,0:T(8,128)(2,1)S(1)}, u32[]{:S(2)}, u32[]{:S(2)}) collective-permute-start(bf16[32,512]{1,0:T(8,128)(2,1)S(1)} %get-tuple-element.58), channel_id=1, source_target_pairs={{0,1},{1,0},{2,3},{3,2},{4,5},{5,4},{6,7},{7,6},{8,9},{9,8},{10,11... | collective-permute-start | bytes 98312 | tf_op jit(solution)/shard_map/ppermute | solution.py:354
  45.1 4.2 %collective-permute-start.14 = (bf16[32,512]{1,0:T(8,128)(2,1)S(1)}, bf16[32,512]{1,0:T(8,128)(2,1)S(1)}, u32[]{:S(2)}, u32[]{:S(2)}) collective-permute-start(bf16[32,512]{1,0:T(8,128)(2,1)S(1)} %get-tuple-element.59), channel_id=1, source_target_pairs={{0,2},{1,3},{2,0},{3,1},{4,6},{5,7},{6,4},{7,5},{8,10},{9,11},{10,... | collective-permute-start | bytes 98312 | tf_op jit(solution)/shard_map/ppermute | solution.py:354
  45.2 4.1 %collective-permute-start.15 = (bf16[32,512]{1,0:T(8,128)(2,1)S(1)}, bf16[32,512]{1,0:T(8,128)(2,1)S(1)}, u32[]{:S(2)}, u32[]{:S(2)}) collective-permute-start(bf16[32,512]{1,0:T(8,128)(2,1)S(1)} %get-tuple-element.60), channel_id=1, source_target_pairs={{0,3},{1,2},{2,1},{3,0},{4,7},{5,6},{6,5},{7,4},{8,11},{9,10},{10,... | collective-permute-start | bytes 98312 | tf_op jit(solution)/shard_map/ppermute | solution.py:354

commit v8 on v7

--- a/solution.py
+++ b/solution.py
@@ -53,13 +53,13 @@
 
 
 def prep_kernel(
-    vec_hbm, feat, src_hbm, dst_hbm, cell_hbm, p0, p1, p2, p3, blue, red, vectors, src, dst, cell, sems
+    vec_hbm, feat, src_hbm, dst_hbm, cell_hbm, p0, p1, far, blue, red, vectors, src, dst, cell, sems
 ):
     member, side = lax.axis_index("edges"), device_side()
-    pieces = (p0, p1, p2, p3)
+    pieces = (p0, p1, far.at[0], far.at[1])
     loads = []
-    for k, piece in enumerate(pieces):
-        width = piece.shape[1]
+    width = p0.shape[1]
+    for k in range(4):
         at = pl.multiple_of((member ^ k) * width, width)
         loads.append(pltpu.make_async_copy(vec_hbm.at[:, pl.ds(at, width)], vectors.at[k], sems.at[k]))
     high = feat.shape[0] - SPILL
@@ -102,12 +102,17 @@
         copy.wait()
 
 
-def field_kernel(p0, p1, p2, p3, t0, to_blue, to_red, field):
+def relay_kernel(far, onward):
+    onward[...] = far[1]
+
+
+def field_kernel(p0, p1, far, p3, t0, to_blue, to_red, token, field):
     member = lax.axis_index("edges")
-    for k, piece in enumerate((p0, p1, p2, p3)):
+    for k, piece in enumerate((p0, p1, far.at[0], p3)):
         high = piece.shape[0]
         field[pl.ds(pl.multiple_of((member ^ k) * high, high), high), :] = piece[...].astype(F32)
     t0[...] = field[...].T
+    token[...] = jnp.zeros(token.shape, F32)
     put_sends(t0, to_blue, to_red)
 
 
@@ -135,24 +140,31 @@
 
 
 def put_dense(band, dense, first, base=None):
-    quarter_lane = iota((ORB, 128), 1) // ATOM_Q
+    lane = iota((ORB, 128), 1)
+    low, even = lane < 64, lane % 64 < ATOM_Q
     for sp in range(GROUP // 2):
         s = first + 2 * sp
         pair, at_row = s // PAIR_ATOMS, s % PAIR_ATOMS * ORB
         for m in range(ORB // 4):
             x = [
-                dense[(4 * m + i) * ORB : (4 * m + i + 1) * ORB, sp * 128 : sp * 128 + 128] for i in range(4)
+                dense[(4 * m + i) * ORB : (4 * m + i + 1) * ORB, sp * 128 : sp * 128 + 128].astype(BF)
+                for i in range(4)
             ]
-            for c in range(4):
-                turned = [pltpu.roll(x[i], (i - c) % 4 * ATOM_Q, 1) if i != c else x[i] for i in range(4)]
-                value = turned[0]
-                for i in range(1, 4):
-                    value = jnp.where(quarter_lane == i, turned[i], value)
-                rows = slice(at_row + c // 2 * ORB, at_row + (c // 2 + 1) * ORB)
-                lo = c % 2 * HALF + m * 128
-                if base is not None:
-                    value = value + base[pair, rows, lo : lo + 128].astype(F32)
-                band[pair, rows, lo : lo + 128] = value.astype(BF)
+            for half in range(2):
+                if half == 0:
+                    u = [jnp.where(low, x[i], pltpu.roll(x[i + 2], 64, 1)) for i in range(2)]
+                else:
+                    u = [jnp.where(low, pltpu.roll(x[i], 64, 1), x[i + 2]) for i in range(2)]
+                both = (
+                    jnp.where(even, u[0], pltpu.roll(u[1], ATOM_Q, 1)),
+                    jnp.where(even, pltpu.roll(u[0], 128 - ATOM_Q, 1), u[1]),
+                )
+                rows = slice(at_row + half * ORB, at_row + (half + 1) * ORB)
+                for n, value in enumerate(both):
+                    lo = n * HALF + m * 128
+                    if base is not None:
+                        value = value + base[pair, rows, lo : lo + 128]
+                    band[pair, rows, lo : lo + 128] = value
 
 
 def column_of(atom, offset):
@@ -162,7 +174,7 @@
     return jnp.where((target >= 0.0) & (target < float(ATOM_Q)), target, outside)
 
 
-def own_kernel(feat, src, dst, cell, cell_bias, w_in, w_out, band, w_in_t, bias_t, w_out_t, blk, bias8, rows):
+def own_kernel(feat, src, dst, cell, cell_bias, w_in, w_out, _, band, w_in_t, bias_t, w_out_t, blk, bias8, rows):
     nfeat, width = w_in.shape
     nblk = w_out.shape[1]
     eye = (iota((width, width), 0) == iota((width, width), 1)).astype(BF)
@@ -351,17 +363,17 @@
 
     def exchange(pieces):
         return [pieces[0]] + [
-            lax.ppermute(pieces[k], "edges", [(i, i ^ k) for i in range(nedge)]) for k in (1, 2, 3)
-        ]
+            lax.ppermute(pieces[k], "edges", [(i, i ^ k) for i in range(nedge)]) for k in (3, 2, 1)
+        ][::-1]
 
     msg = shape((SPILL + ID_ROWS, nfeat), BF)
     piece = shape((high, nrow), BF)
     lines = (nown // 128, 128)
     edges = [x.reshape(lines) for x in (edge_src, edge_dst, edge_cell)]
-    *pieces, blue_msg, red_msg = call(
+    own_piece, near, far, blue_msg, red_msg = call(
         prep_kernel,
         "prep",
-        (piece,) * 4 + (msg, msg),
+        (piece, piece, shape((2, high, nrow), BF), msg, msg),
         [pltpu.VMEM((nedge, high, nrow), F32)]
         + [pltpu.VMEM(lines, jnp.int32)] * 3
         + [pltpu.SemaphoreType.DMA((9,))],
@@ -371,9 +383,18 @@
         in_hbm=range(5),
         limit=FULL,
     )
-    pieces = exchange(pieces)
+    far = lax.ppermute(far, "edges", [(i, i ^ 2) for i in range(nedge)])
     blue_msg, red_msg = swap(blue_msg, red_msg)
+    near = lax.ppermute(near, "edges", [(i, i ^ 1) for i in range(nedge)])
+    (onward,) = call(relay_kernel, "relay", (piece,), [], far, micros=0)
+    onward = lax.ppermute(onward, "edges", [(i, i ^ 1) for i in range(nedge)])
+    pieces = [own_piece, near, far, onward]
     full, part = shape((nrow, VEC), F32), shape((HALO, VEC), BF)
+    t0, to_blue, to_red, token = call(
+        field_kernel, "field", (full, part, part, shape((8, VEC), F32)), [pltpu.VMEM((VEC, nrow), F32)], *pieces
+    )
+    blue, red = swap(to_blue, to_red)
+
     band_shape = shape((ATOM_Q // PAIR_ATOMS, PAIR_ATOMS * ORB, WIN_ATOMS * ORB), BF)
     width = w_in.shape[1]
     band, *weights = call(
@@ -386,13 +407,9 @@
         cell_bias,
         w_in,
         w_out,
-        micros=4,
-    )
-    t0, to_blue, to_red = call(
-        field_kernel, "field", (full, part, part), [pltpu.VMEM((VEC, nrow), F32)], *pieces
-    )
-    blue, red = swap(to_blue, to_red)
-
+        token,
+        micros=0,
+    )
     spill_len = 2 * (SPILL + 64)
     (band,) = call(
         spill_kernel,
@@ -404,7 +421,7 @@
         red_msg,
         *weights,
         alias={0: 0},
-        micros=0,
+        micros=3,
     )
 
     wide = pltpu.VMEM((2 * HALO, VEC), F32)

time: 50.2 us -> 49.8 us (level)
  starting transfers between devices: 22.1 us -> 25.1 us
  Pallas kernels: 11.9 us -> 10.5 us
  waiting for transfers between devices: 14.4 us -> 13.2 us
  local copies, waits for them, and re-layouts: 1.44 us -> 0.69 us
    ppermute x0 -> x3, starting transfers between devices: none -> 3.59 us  [the longest x1 3 us: per_device(): far = lax.ppermute(far, 'edges', [(i, i ^ 2) for i in range(nedge)])]
    ppermute x6 -> x3, starting transfers between devices: 5.08 us -> 1.93 us  [exchange(): lax.ppermute(pieces[k], 'edges', [(i, i ^ k) for i in range(nedge)])]
    ppermute x5, starting transfers between devices: 17 us -> 19.6 us  [swap(): lax.ppermute(first, axes, blue_pairs)]
    ppermute x5, waiting for transfers between devices: 12 us -> 9.72 us  [swap(): lax.ppermute(first, axes, blue_pairs)]
    pallas_call x12 -> x13, Pallas kernels: 11.9 us -> 10.5 us  [call(): pl.pallas_call(kernel, name=name, out_shape=outs, in_specs=spaces, out_sp...]
    ppermute x0 -> x3, waiting for transfers between devices: none -> 1.13 us  [the longest x1 1.06 us: per_device(): near = lax.ppermute(near, 'edges', [(i, i ^ 1) for i in range(nedge)])]
    unnamed x18, local copies, waits for them, and re-layouts: 1.44 us -> 0.69 us
    ppermute x6 -> x3, waiting for transfers between devices: 2.31 us -> 2.3 us  [exchange(): lax.ppermute(pieces[k], 'edges', [(i, i ^ k) for i in range(nedge)])]
  transfers between devices with their start and end apart: 16 -> 16, of which waited for: 4 -> 6; matrix products, arithmetic and copies ran while one was open for 0% -> 0% of each run, Pallas kernels for 14% -> 12%
where the time goes in v8:
time: 49.8 us; the launch traced here: 49.6 us
  starting transfers between devices  25.1 us (50%)
  waiting for transfers between devices  13.2 us (27%)
  Pallas kernels  10.5 us (21%)
  local copies, waits for them, and re-layouts  0.69 us (1%)
    ppermute x5, starting transfers between devices, swap(): lax.ppermute(first, axes, blue_pairs)  19.6 us
    pallas_call x13, Pallas kernels, call(): pl.pallas_call(kernel, name=name, out_shape=outs, in_specs=spaces, out_sp...  10.5 us
    ppermute x5, waiting for transfers between devices, swap(): lax.ppermute(first, axes, blue_pairs)  9.72 us
    ppermute x1, starting transfers between devices, per_device(): far = lax.ppermute(far, 'edges', [(i, i ^ 2) for i in range(nedge)])  3 us
    ppermute x3, waiting for transfers between devices, exchange(): lax.ppermute(pieces[k], 'edges', [(i, i ^ k) for i in range(nedge)])  2.3 us
    ppermute x3, starting transfers between devices, exchange(): lax.ppermute(pieces[k], 'edges', [(i, i ^ k) for i in range(nedge)])  1.93 us
    ppermute x1, waiting for transfers between devices, per_device(): near = lax.ppermute(near, 'edges', [(i, i ^ 1) for i in range(nedge)])  1.06 us
  transfers between devices with their start and end apart: 16, of which 6 were waited for; matrix products, arithmetic and copies ran while one was open for 0% of the time, Pallas kernels for 12%

profile of v8, /device:TPU:0, one launch (start us, length us, event | category | flops | bytes accessed | tf_op | source)
XLA Modules:
  0.0 49.6 jit_solution(1929687103627755548)
XLA Ops:
  0.0 2.0 %prep.1 = (bf16[32,512]{1,0:T(8,128)(2,1)}, bf16[32,512]{1,0:T(8,128)(2,1)}, bf16[2,32,512]{2,1,0:T(8,128)(2,1)}, bf16[336,256]{1,0:T(8,128)(2,1)}, bf16[336,256]{1,0:T(8,128)(2,1)}) custom-call(f32[32,2048]{1,0:T(8,128)} %vec_hbm.1, bf16[1280,256]{1,0:T(8,128)(2,1)} %feat.3, s32[10,128]{1,0:T(8,128)} %bitcast.3, s32[10,128]{1,0:T(8,128)} %bitcast.5, ...), custom_call_target="tpu_custom_call" | custom-call | flops 1000000000 | tf_op jit(solution)/shard_map/prep/pallas_call | solution.py:335
  2.0 3.0 %collective-permute-start.1 = (bf16[2,32,512]{2,1,0:T(8,128)(2,1)}, bf16[2,32,512]{2,1,0:T(8,128)(2,1)S(1)}, u32[]{:S(2)}, u32[]{:S(2)}) collective-permute-start(bf16[2,32,512]{2,1,0:T(8,128)(2,1)} %get-tuple-element.35), channel_id=1, source_target_pairs={{0,2},{1,3},{2,0},{3,1},{4,6},{5,7},{6,4},{7,5},{8,10},{9,11},{10,... | collective-permute-start | bytes 196616 | tf_op jit(solution)/shard_map/ppermute | solution.py:386
  5.0 3.7 %collective-permute-start.3 = (bf16[336,256]{1,0:T(8,128)(2,1)}, bf16[336,256]{1,0:T(8,128)(2,1)S(1)}, u32[]{:S(2)}, u32[]{:S(2)}) collective-permute-start(bf16[336,256]{1,0:T(8,128)(2,1)} %get-tuple-element.38), channel_id=1, source_target_pairs={{0,31},{1,2},{2,1},{3,4},{4,3},{5,6},{6,5},{7,8},{8,7},{9,10},{10,... | collective-permute-start | bytes 516104 | tf_op jit(solution)/shard_map/ppermute | solution.py:360
  8.7 0.0 collective-permute-start.4
  8.7 0.5 %collective-permute-start = (bf16[32,512]{1,0:T(8,128)(2,1)}, bf16[32,512]{1,0:T(8,128)(2,1)S(1)}, u32[]{:S(2)}, u32[]{:S(2)}) collective-permute-start(bf16[32,512]{1,0:T(8,128)(2,1)} %get-tuple-element.34), channel_id=1, source_target_pairs={{0,1},{1,0},{2,3},{3,2},{4,5},{5,4},{6,7},{7,6},{8,9},{9,8},{10,11... | collective-permute-start | bytes 98312 | tf_op jit(solution)/shard_map/ppermute | solution.py:388
  9.2 0.0 collective-permute-done.1.far
  9.2 0.1 collective-permute-start.2
  9.3 1.1 %collective-permute-done.p1 = bf16[32,512]{1,0:T(8,128)(2,1)S(1)} collective-permute-done((bf16[32,512]{1,0:T(8,128)(2,1)}, bf16[32,512]{1,0:T(8,128)(2,1)S(1)}, u32[]{:S(2)}, u32[]{:S(2)}) %collective-permute-start) | collective-permute-done | bytes 32800 | tf_op jit(solution)/shard_map/ppermute | solution.py:388
  10.4 0.1 collective-permute-done.2.p3
  10.5 0.0 copy-start.3
  10.5 0.0 copy-start.4
  10.5 0.0 copy-start.5
  10.5 0.2 field.1
  10.7 0.0 copy-start.6
  10.7 4.8 %collective-permute-start.5 = (bf16[384,128]{1,0:T(8,128)(2,1)S(1)}, bf16[384,128]{1,0:T(8,128)(2,1)S(1)}, u32[]{:S(2)}, u32[]{:S(2)}) collective-permute-start(bf16[384,128]{1,0:T(8,128)(2,1)S(1)} %get-tuple-element.44), channel_id=1, source_target_pairs={{0,31},{1,2},{2,1},{3,4},{4,3},{5,6},{6,5},{7,8},{8,7},{9,10},{10,... | collective-permute-start | bytes 294920 | tf_op jit(solution)/shard_map/ppermute | solution.py:360
  15.5 0.0 collective-permute-start.6
  15.6 2.2 %own.1 = (bf16[2,256,1024]{2,1,0:T(8,128)(2,1)S(1)}, bf16[512,256]{1,0:T(8,128)(2,1)S(1)}, bf16[512,8]{1,0:T(8,128)(2,1)S(1)}, bf16[256,256]{1,0:T(8,128)(2,1)S(1)}) custom-call(bf16[1280,256]{1,0:T(8,128)(2,1)S(1)} %copy-done, s32[10,128]{1,0:T(8,128)S(1)} %bitcast.4, s32[10,128]{1,0:T(8,128)S(1)} %bitcast.6, s32[10,128]{1,0:T(8,128)S(1)} %bitcast.8, ...), custom_call_target="tpu_custom_call" | custom-call | tf_op jit(solution)/shard_map/own/pallas_call | solution.py:335
  17.8 0.0 collective-permute-done.3.blue
  17.8 0.0 collective-permute-done.4.red
  17.8 1.8 %spill.1.band = bf16[2,256,1024]{2,1,0:T(8,128)(2,1)S(1)} custom-call(bf16[2,256,1024]{2,1,0:T(8,128)(2,1)S(1)} %get-tuple-element.37.own_band, bf16[336,256]{1,0:T(8,128)(2,1)S(1)} %collective-permute-done.3.blue, bf16[336,256]{1,0:T(8,128)(2,1)S(1)} %collective-permute-done.4.red, ...), custom_call_target="tpu_custom_call", output_to_operand_aliasing={{}: (0, {})} | custom-call | flops 3000000000 | tf_op jit(solution)/shard_map/spill/pallas_call | solution.py:335
  19.6 0.0 collective-permute-done.5.blue
  19.6 0.0 collective-permute-done.6.red
  19.6 0.6 %first.1 = (f32[512,128]{1,0:T(8,128)S(1)}, bf16[384,128]{1,0:T(8,128)(2,1)S(1)}, bf16[384,128]{1,0:T(8,128)(2,1)S(1)}) custom-call(bf16[2,256,1024]{2,1,0:T(8,128)(2,1)S(1)} %spill.1.band, f32[512,128]{1,0:T(8,128)S(1)} %get-tuple-element.43.t0.before, bf16[384,128]{1,0:T(8,128)(2,1)S(1)} %collective-permute-done.5.blue, ...), custom_call_target="tpu_custom_call" | custom-call | flops 1000000000 | tf_op jit(solution)/shard_map/first/pallas_call | solution.py:335
  20.2 3.6 %collective-permute-start.7 = (bf16[384,128]{1,0:T(8,128)(2,1)S(1)}, bf16[384,128]{1,0:T(8,128)(2,1)S(1)}, u32[]{:S(2)}, u32[]{:S(2)}) collective-permute-start(bf16[384,128]{1,0:T(8,128)(2,1)S(1)} %get-tuple-element.47), channel_id=1, source_target_pairs={{0,31},{1,2},{2,1},{3,4},{4,3},{5,6},{6,5},{7,8},{8,7},{9,10},{10,... | collective-permute-start | bytes 294920 | tf_op jit(solution)/shard_map/ppermute | solution.py:360
  23.8 0.0 collective-permute-start.8
  23.8 0.3 inner.2.part
  24.2 3.7 %collective-permute-done.7.blue = bf16[384,128]{1,0:T(8,128)(2,1)S(1)} collective-permute-done((bf16[384,128]{1,0:T(8,128)(2,1)S(1)}, bf16[384,128]{1,0:T(8,128)(2,1)S(1)}, u32[]{:S(2)}, u32[]{:S(2)}) %collective-permute-start.7) | collective-permute-done | bytes 98336 | tf_op jit(solution)/shard_map/ppermute | solution.py:360
  27.9 0.0 collective-permute-done.8.red
  27.9 0.4 outer.2
  28.3 3.7 %collective-permute-start.9 = (bf16[384,128]{1,0:T(8,128)(2,1)S(1)}, bf16[384,128]{1,0:T(8,128)(2,1)S(1)}, u32[]{:S(2)}, u32[]{:S(2)}) collective-permute-start(bf16[384,128]{1,0:T(8,128)(2,1)S(1)} %get-tuple-element.50), channel_id=1, source_target_pairs={{0,31},{1,2},{2,1},{3,4},{4,3},{5,6},{6,5},{7,8},{8,7},{9,10},{10,... | collective-permute-start | bytes 294920 | tf_op jit(solution)/shard_map/ppermute | solution.py:360
  32.1 0.0 collective-permute-start.10
  32.1 0.3 inner.3.part
  32.4 3.6 %collective-permute-done.9.blue = bf16[384,128]{1,0:T(8,128)(2,1)S(1)} collective-permute-done((bf16[384,128]{1,0:T(8,128)(2,1)S(1)}, bf16[384,128]{1,0:T(8,128)(2,1)S(1)}, u32[]{:S(2)}, u32[]{:S(2)}) %collective-permute-start.9) | collective-permute-done | bytes 98336 | tf_op jit(solution)/shard_map/ppermute | solution.py:360
  36.0 0.0 collective-permute-done.10.red
  36.0 0.4 outer.3
  36.5 3.7 %collective-permute-start.11 = (bf16[384,128]{1,0:T(8,128)(2,1)S(1)}, bf16[384,128]{1,0:T(8,128)(2,1)S(1)}, u32[]{:S(2)}, u32[]{:S(2)}) collective-permute-start(bf16[384,128]{1,0:T(8,128)(2,1)S(1)} %get-tuple-element.55), channel_id=1, source_target_pairs={{0,31},{1,2},{2,1},{3,4},{4,3},{5,6},{6,5},{7,8},{8,7},{9,10},{10,... | collective-permute-start | bytes 294920 | tf_op jit(solution)/shard_map/ppermute | solution.py:360
  40.2 0.0 collective-permute-start.12
  40.2 0.7 %copy-done.7 = f32[5]{0:T(128)S(1)} copy-done((f32[5]{0:T(128)S(1)}, f32[5]{0:T(128)}, u32[]{:S(2)}) %copy-start.7) | copy-done | bytes 44
  40.9 1.0 %mix.1 = (f32[128,512]{1,0:T(8,128)S(1)}, f32[8,128]{1,0:T(8,128)S(1)}) custom-call(f32[5]{0:T(128)S(1)} %copy-done.7, bf16[2,256,1024]{2,1,0:T(8,128)(2,1)S(1)} %spill.1.band, f32[512,128]{1,0:T(8,128)S(1)} %get-tuple-element.43.t0.before, f32[512,128]{1,0:T(8,128)S(1)} %get-tuple-element.46.now.before.t1, f32[512,128]{1,0:T(8,128)S(1)} %get-tuple-element.49.now.t2, ...), custom_call_target="tpu_custom_call" | custom-call | flops 1000000000 | tf_op jit(solution)/shard_map/mix/pallas_call | solution.py:335
  41.8 2.4 %collective-permute-done.11.blue = bf16[384,128]{1,0:T(8,128)(2,1)S(1)} collective-permute-done((bf16[384,128]{1,0:T(8,128)(2,1)S(1)}, bf16[384,128]{1,0:T(8,128)(2,1)S(1)}, u32[]{:S(2)}, u32[]{:S(2)}) %collective-permute-start.11) | collective-permute-done | bytes 98336 | tf_op jit(solution)/shard_map/ppermute | solution.py:360
  44.2 0.0 collective-permute-done.12.red
  44.2 0.5 last.1
  44.7 0.1 collective-permute-start.13
  44.7 0.1 collective-permute-start.14
  44.8 1.8 %collective-permute-start.15 = (bf16[32,512]{1,0:T(8,128)(2,1)S(1)}, bf16[32,512]{1,0:T(8,128)(2,1)S(1)}, u32[]{:S(2)}, u32[]{:S(2)}) collective-permute-start(bf16[32,512]{1,0:T(8,128)(2,1)S(1)} %get-tuple-element.60), channel_id=1, source_target_pairs={{0,3},{1,2},{2,1},{3,0},{4,7},{5,6},{6,5},{7,4},{8,11},{9,10},{10,... | collective-permute-start | bytes 98312 | tf_op jit(solution)/shard_map/ppermute | solution.py:366
  46.6 0.0 collective-permute-done.13.p1
  46.6 2.3 %collective-permute-done.14.p2 = bf16[32,512]{1,0:T(8,128)(2,1)S(1)} collective-permute-done((bf16[32,512]{1,0:T(8,128)(2,1)S(1)}, bf16[32,512]{1,0:T(8,128)(2,1)S(1)}, u32[]{:S(2)}, u32[]{:S(2)}) %collective-permute-start.14) | collective-permute-done | bytes 32800 | tf_op jit(solution)/shard_map/ppermute | solution.py:366
  48.9 0.7 %join.1 = f32[32,2048]{1,0:T(8,128)} custom-call(bf16[32,512]{1,0:T(8,128)(2,1)S(1)} %get-tuple-element.57.p0, bf16[32,512]{1,0:T(8,128)(2,1)S(1)} %collective-permute-done.13.p1, bf16[32,512]{1,0:T(8,128)(2,1)S(1)} %collective-permute-done.14.p2, bf16[32,512]{1,0:T(8,128)(2,1)S(1)} %collective-permute-done.15.p3), custom_call_target="tpu_custom_call" | custom-call | flops 1000000000 | tf_op jit(solution)/shard_map/join/pallas_call | solution.py:335
  (15 shorter events, 0.0 us)
Async XLA Ops:
  2.0 7.2 %collective-permute-start.1 = (bf16[2,32,512]{2,1,0:T(8,128)(2,1)}, bf16[2,32,512]{2,1,0:T(8,128)(2,1)S(1)}, u32[]{:S(2)}, u32[]{:S(2)}) collective-permute-start(bf16[2,32,512]{2,1,0:T(8,128)(2,1)} %get-tuple-element.35), channel_id=1, source_target_pairs={{0,2},{1,3},{2,0},{3,1},{4,6},{5,7},{6,4},{7,5},{8,10},{9,11},{10,... | collective-permute-start | bytes 196616 | tf_op jit(solution)/shard_map/ppermute | solution.py:386
  5.0 12.7 %collective-permute-start.3 = (bf16[336,256]{1,0:T(8,128)(2,1)}, bf16[336,256]{1,0:T(8,128)(2,1)S(1)}, u32[]{:S(2)}, u32[]{:S(2)}) collective-permute-start(bf16[336,256]{1,0:T(8,128)(2,1)} %get-tuple-element.38), channel_id=1, source_target_pairs={{0,31},{1,2},{2,1},{3,4},{4,3},{5,6},{6,5},{7,8},{8,7},{9,10},{10,... | collective-permute-start | bytes 516104 | tf_op jit(solution)/shard_map/ppermute | solution.py:360
  8.7 9.1 %collective-permute-start.4 = (bf16[336,256]{1,0:T(8,128)(2,1)}, bf16[336,256]{1,0:T(8,128)(2,1)S(1)}, u32[]{:S(2)}, u32[]{:S(2)}) collective-permute-start(bf16[336,256]{1,0:T(8,128)(2,1)} %get-tuple-element.39), channel_id=1, source_target_pairs={{0,1},{1,0},{2,3},{3,2},{4,5},{5,4},{6,7},{7,6},{8,9},{9,8},{10,11... | collective-permute-start | bytes 516104 | tf_op jit(solution)/shard_map/ppermute | solution.py:361
  8.7 1.7 %copy-start.8 = (bf16[32,512]{1,0:T(8,128)(2,1)S(1)}, bf16[32,512]{1,0:T(8,128)(2,1)}, u32[]{:S(2)}) copy-start(bf16[32,512]{1,0:T(8,128)(2,1)} %get-tuple-element.33.p0) | copy-start | bytes 98308
  8.7 1.7 %collective-permute-start = (bf16[32,512]{1,0:T(8,128)(2,1)}, bf16[32,512]{1,0:T(8,128)(2,1)S(1)}, u32[]{:S(2)}, u32[]{:S(2)}) collective-permute-start(bf16[32,512]{1,0:T(8,128)(2,1)} %get-tuple-element.34), channel_id=1, source_target_pairs={{0,1},{1,0},{2,3},{3,2},{4,5},{5,4},{6,7},{7,6},{8,9},{9,8},{10,11... | collective-permute-start | bytes 98312 | tf_op jit(solution)/shard_map/ppermute | solution.py:388
  9.2 1.2 %collective-permute-start.2 = (bf16[32,512]{1,0:T(8,128)(2,1)S(1)}, bf16[32,512]{1,0:T(8,128)(2,1)S(1)}, u32[]{:S(2)}, u32[]{:S(2)}) collective-permute-start(bf16[32,512]{1,0:T(8,128)(2,1)S(1)} %relay.1), channel_id=1, source_target_pairs={{0,1},{1,0},{2,3},{3,2},{4,5},{5,4},{6,7},{7,6},{8,9},{9,8},{10,11... | collective-permute-start | bytes 98312 | tf_op jit(solution)/shard_map/ppermute | solution.py:390
  10.5 5.1 %copy-start = (bf16[1280,256]{1,0:T(8,128)(2,1)S(1)}, bf16[1280,256]{1,0:T(8,128)(2,1)}, u32[]{:S(2)}) copy-start(bf16[1280,256]{1,0:T(8,128)(2,1)} %feat.3) | copy-start | bytes 1966084
  10.5 5.1 %copy-start.1 = (bf16[256,512]{1,0:T(8,128)(2,1)S(1)}, bf16[256,512]{1,0:T(8,128)(2,1)}, u32[]{:S(2)}) copy-start(bf16[256,512]{1,0:T(8,128)(2,1)} %w_in.1) | copy-start | bytes 786436
  10.5 5.1 %copy-start.2 = (bf16[256,256]{1,0:T(8,128)(2,1)S(1)}, bf16[256,256]{1,0:T(8,128)(2,1)}, u32[]{:S(2)}) copy-start(bf16[256,256]{1,0:T(8,128)(2,1)} %w_out.1) | copy-start | bytes 393220
  10.5 5.1 %copy-start.3 = (s32[1280]{0:T(1024)S(1)}, s32[1280]{0:T(1024)}, u32[]{:S(2)}) copy-start(s32[1280]{0:T(1024)} %param.10) | copy-start | bytes 15364
  10.5 5.1 %copy-start.4 = (s32[1280]{0:T(1024)S(1)}, s32[1280]{0:T(1024)}, u32[]{:S(2)}) copy-start(s32[1280]{0:T(1024)} %param.11) | copy-start | bytes 15364
  10.5 5.1 %copy-start.5 = (s32[1280]{0:T(1024)S(1)}, s32[1280]{0:T(1024)}, u32[]{:S(2)}) copy-start(s32[1280]{0:T(1024)} %param.12) | copy-start | bytes 15364
  10.7 4.9 %copy-start.6 = (bf16[3,512]{1,0:T(4,128)(2,1)S(1)}, bf16[3,512]{1,0:T(4,128)(2,1)}, u32[]{:S(2)}) copy-start(bf16[3,512]{1,0:T(4,128)(2,1)} %cell_bias.1) | copy-start | bytes 9220
  10.7 8.9 %collective-permute-start.5 = (bf16[384,128]{1,0:T(8,128)(2,1)S(1)}, bf16[384,128]{1,0:T(8,128)(2,1)S(1)}, u32[]{:S(2)}, u32[]{:S(2)}) collective-permute-start(bf16[384,128]{1,0:T(8,128)(2,1)S(1)} %get-tuple-element.44), channel_id=1, source_target_pairs={{0,31},{1,2},{2,1},{3,4},{4,3},{5,6},{6,5},{7,8},{8,7},{9,10},{10,... | collective-permute-start | bytes 294920 | tf_op jit(solution)/shard_map/ppermute | solution.py:360
  15.5 4.1 %collective-permute-start.6 = (bf16[384,128]{1,0:T(8,128)(2,1)S(1)}, bf16[384,128]{1,0:T(8,128)(2,1)S(1)}, u32[]{:S(2)}, u32[]{:S(2)}) collective-permute-start(bf16[384,128]{1,0:T(8,128)(2,1)S(1)} %get-tuple-element.45), channel_id=1, source_target_pairs={{0,1},{1,0},{2,3},{3,2},{4,5},{5,4},{6,7},{7,6},{8,9},{9,8},{10,11... | collective-permute-start | bytes 294920 | tf_op jit(solution)/shard_map/ppermute | solution.py:361
  20.2 7.7 %collective-permute-start.7 = (bf16[384,128]{1,0:T(8,128)(2,1)S(1)}, bf16[384,128]{1,0:T(8,128)(2,1)S(1)}, u32[]{:S(2)}, u32[]{:S(2)}) collective-permute-start(bf16[384,128]{1,0:T(8,128)(2,1)S(1)} %get-tuple-element.47), channel_id=1, source_target_pairs={{0,31},{1,2},{2,1},{3,4},{4,3},{5,6},{6,5},{7,8},{8,7},{9,10},{10,... | collective-permute-start | bytes 294920 | tf_op jit(solution)/shard_map/ppermute | solution.py:360
  23.8 4.1 %collective-permute-start.8 = (bf16[384,128]{1,0:T(8,128)(2,1)S(1)}, bf16[384,128]{1,0:T(8,128)(2,1)S(1)}, u32[]{:S(2)}, u32[]{:S(2)}) collective-permute-start(bf16[384,128]{1,0:T(8,128)(2,1)S(1)} %get-tuple-element.48), channel_id=1, source_target_pairs={{0,1},{1,0},{2,3},{3,2},{4,5},{5,4},{6,7},{7,6},{8,9},{9,8},{10,11... | collective-permute-start | bytes 294920 | tf_op jit(solution)/shard_map/ppermute | solution.py:361
  28.3 7.7 %collective-permute-start.9 = (bf16[384,128]{1,0:T(8,128)(2,1)S(1)}, bf16[384,128]{1,0:T(8,128)(2,1)S(1)}, u32[]{:S(2)}, u32[]{:S(2)}) collective-permute-start(bf16[384,128]{1,0:T(8,128)(2,1)S(1)} %get-tuple-element.50), channel_id=1, source_target_pairs={{0,31},{1,2},{2,1},{3,4},{4,3},{5,6},{6,5},{7,8},{8,7},{9,10},{10,... | collective-permute-start | bytes 294920 | tf_op jit(solution)/shard_map/ppermute | solution.py:360
  32.1 4.0 %collective-permute-start.10 = (bf16[384,128]{1,0:T(8,128)(2,1)S(1)}, bf16[384,128]{1,0:T(8,128)(2,1)S(1)}, u32[]{:S(2)}, u32[]{:S(2)}) collective-permute-start(bf16[384,128]{1,0:T(8,128)(2,1)S(1)} %get-tuple-element.51), channel_id=1, source_target_pairs={{0,1},{1,0},{2,3},{3,2},{4,5},{5,4},{6,7},{7,6},{8,9},{9,8},{10,11... | collective-permute-start | bytes 294920 | tf_op jit(solution)/shard_map/ppermute | solution.py:361
  36.5 7.7 %collective-permute-start.11 = (bf16[384,128]{1,0:T(8,128)(2,1)S(1)}, bf16[384,128]{1,0:T(8,128)(2,1)S(1)}, u32[]{:S(2)}, u32[]{:S(2)}) collective-permute-start(bf16[384,128]{1,0:T(8,128)(2,1)S(1)} %get-tuple-element.55), channel_id=1, source_target_pairs={{0,31},{1,2},{2,1},{3,4},{4,3},{5,6},{6,5},{7,8},{8,7},{9,10},{10,... | collective-permute-start | bytes 294920 | tf_op jit(solution)/shard_map/ppermute | solution.py:360
  40.2 0.7 %copy-start.7 = (f32[5]{0:T(128)S(1)}, f32[5]{0:T(128)}, u32[]{:S(2)}) copy-start(f32[5]{0:T(128)} %coef.1) | copy-start | bytes 64
  40.2 4.0 %collective-permute-start.12 = (bf16[384,128]{1,0:T(8,128)(2,1)S(1)}, bf16[384,128]{1,0:T(8,128)(2,1)S(1)}, u32[]{:S(2)}, u32[]{:S(2)}) collective-permute-start(bf16[384,128]{1,0:T(8,128)(2,1)S(1)} %get-tuple-element.56), channel_id=1, source_target_pairs={{0,1},{1,0},{2,3},{3,2},{4,5},{5,4},{6,7},{7,6},{8,9},{9,8},{10,11... | collective-permute-start | bytes 294920 | tf_op jit(solution)/shard_map/ppermute | solution.py:361
  44.7 1.9 %collective-permute-start.13 = (bf16[32,512]{1,0:T(8,128)(2,1)S(1)}, bf16[32,512]{1,0:T(8,128)(2,1)S(1)}, u32[]{:S(2)}, u32[]{:S(2)}) collective-permute-start(bf16[32,512]{1,0:T(8,128)(2,1)S(1)} %get-tuple-element.58), channel_id=1, source_target_pairs={{0,1},{1,0},{2,3},{3,2},{4,5},{5,4},{6,7},{7,6},{8,9},{9,8},{10,11... | collective-permute-start | bytes 98312 | tf_op jit(solution)/shard_map/ppermute | solution.py:366
  44.7 4.2 %collective-permute-start.14 = (bf16[32,512]{1,0:T(8,128)(2,1)S(1)}, bf16[32,512]{1,0:T(8,128)(2,1)S(1)}, u32[]{:S(2)}, u32[]{:S(2)}) collective-permute-start(bf16[32,512]{1,0:T(8,128)(2,1)S(1)} %get-tuple-element.59), channel_id=1, source_target_pairs={{0,2},{1,3},{2,0},{3,1},{4,6},{5,7},{6,4},{7,5},{8,10},{9,11},{10,... | collective-permute-start | bytes 98312 | tf_op jit(solution)/shard_map/ppermute | solution.py:366
  44.8 4.1 %collective-permute-start.15 = (bf16[32,512]{1,0:T(8,128)(2,1)S(1)}, bf16[32,512]{1,0:T(8,128)(2,1)S(1)}, u32[]{:S(2)}, u32[]{:S(2)}) collective-permute-start(bf16[32,512]{1,0:T(8,128)(2,1)S(1)} %get-tuple-element.60), channel_id=1, source_target_pairs={{0,3},{1,2},{2,1},{3,0},{4,7},{5,6},{6,5},{7,4},{8,11},{9,10},{10,... | collective-permute-start | bytes 98312 | tf_op jit(solution)/shard_map/ppermute | solution.py:366

commit v9 on v8

--- a/solution.py
+++ b/solution.py
@@ -53,13 +53,13 @@
 
 
 def prep_kernel(
-    vec_hbm, feat, src_hbm, dst_hbm, cell_hbm, p0, p1, far, blue, red, vectors, src, dst, cell, sems
+    vec_hbm, feat, src_hbm, dst_hbm, cell_hbm, p0, p1, p2, p3, blue, red, vectors, src, dst, cell, sems
 ):
     member, side = lax.axis_index("edges"), device_side()
-    pieces = (p0, p1, far.at[0], far.at[1])
+    pieces = (p0, p1, p2, p3)
     loads = []
-    width = p0.shape[1]
-    for k in range(4):
+    for k, piece in enumerate(pieces):
+        width = piece.shape[1]
         at = pl.multiple_of((member ^ k) * width, width)
         loads.append(pltpu.make_async_copy(vec_hbm.at[:, pl.ds(at, width)], vectors.at[k], sems.at[k]))
     high = feat.shape[0] - SPILL
@@ -102,13 +102,13 @@
         copy.wait()
 
 
-def relay_kernel(far, onward):
-    onward[...] = far[1]
-
-
-def field_kernel(p0, p1, far, p3, t0, to_blue, to_red, token, field):
+def pass_kernel(x, y):
+    y[...] = x[...]
+
+
+def field_kernel(p0, p1, p2, p3, t0, to_blue, to_red, token, field):
     member = lax.axis_index("edges")
-    for k, piece in enumerate((p0, p1, far.at[0], p3)):
+    for k, piece in enumerate((p0, p1, p2, p3)):
         high = piece.shape[0]
         field[pl.ds(pl.multiple_of((member ^ k) * high, high), high), :] = piece[...].astype(F32)
     t0[...] = field[...].T
@@ -363,17 +363,17 @@
 
     def exchange(pieces):
         return [pieces[0]] + [
-            lax.ppermute(pieces[k], "edges", [(i, i ^ k) for i in range(nedge)]) for k in (3, 2, 1)
-        ][::-1]
+            lax.ppermute(pieces[k], "edges", [(i, i ^ k) for i in range(nedge)]) for k in (1, 2, 3)
+        ]
 
     msg = shape((SPILL + ID_ROWS, nfeat), BF)
     piece = shape((high, nrow), BF)
     lines = (nown // 128, 128)
     edges = [x.reshape(lines) for x in (edge_src, edge_dst, edge_cell)]
-    own_piece, near, far, blue_msg, red_msg = call(
+    *pieces, blue_msg, red_msg = call(
         prep_kernel,
         "prep",
-        (piece, piece, shape((2, high, nrow), BF), msg, msg),
+        (piece,) * 4 + (msg, msg),
         [pltpu.VMEM((nedge, high, nrow), F32)]
         + [pltpu.VMEM(lines, jnp.int32)] * 3
         + [pltpu.SemaphoreType.DMA((9,))],
@@ -383,12 +383,9 @@
         in_hbm=range(5),
         limit=FULL,
     )
-    far = lax.ppermute(far, "edges", [(i, i ^ 2) for i in range(nedge)])
+    pieces = exchange(pieces)
     blue_msg, red_msg = swap(blue_msg, red_msg)
-    near = lax.ppermute(near, "edges", [(i, i ^ 1) for i in range(nedge)])
-    (onward,) = call(relay_kernel, "relay", (piece,), [], far, micros=0)
-    onward = lax.ppermute(onward, "edges", [(i, i ^ 1) for i in range(nedge)])
-    pieces = [own_piece, near, far, onward]
+    pieces[3:4] = call(pass_kernel, "pass", (piece,), [], pieces[3], micros=0)
     full, part = shape((nrow, VEC), F32), shape((HALO, VEC), BF)
     t0, to_blue, to_red, token = call(
         field_kernel, "field", (full, part, part, shape((8, VEC), F32)), [pltpu.VMEM((VEC, nrow), F32)], *pieces
@@ -408,7 +405,7 @@
         w_in,
         w_out,
         token,
-        micros=0,
+        micros=4,
     )
     spill_len = 2 * (SPILL + 64)
     (band,) = call(
@@ -421,7 +418,7 @@
         red_msg,
         *weights,
         alias={0: 0},
-        micros=3,
+        micros=0,
     )
 
     wide = pltpu.VMEM((2 * HALO, VEC), F32)

time: 49.8 us -> 49.4 us (level)
  starting transfers between devices: 25.1 us -> 17.8 us
  waiting for transfers between devices: 13.2 us -> 19.3 us
  local copies, waits for them, and re-layouts: 0.69 us -> 1.4 us
    ppermute x5, waiting for transfers between devices: 9.72 us -> 17 us  [swap(): lax.ppermute(first, axes, blue_pairs)]
    ppermute x5, starting transfers between devices: 19.6 us -> 12.7 us  [swap(): lax.ppermute(first, axes, blue_pairs)]
    ppermute x3 -> x0, starting transfers between devices: 3.59 us -> none  [the longest x1 3 us: per_device(): far = lax.ppermute(far, 'edges', [(i, i ^ 2) for i in range(nedge)])]
    ppermute x3 -> x6, starting transfers between devices: 1.93 us -> 5.08 us  [exchange(): lax.ppermute(pieces[k], 'edges', [(i, i ^ k) for i in range(nedge)])]
    ppermute x3 -> x0, waiting for transfers between devices: 1.13 us -> none  [the longest x1 1.06 us: per_device(): near = lax.ppermute(near, 'edges', [(i, i ^ 1) for i in range(nedge)])]
    unnamed x18, local copies, waits for them, and re-layouts: 0.69 us -> 1.4 us
    ppermute x3 -> x6, waiting for transfers between devices: 2.3 us -> 2.31 us  [exchange(): lax.ppermute(pieces[k], 'edges', [(i, i ^ k) for i in range(nedge)])]
  transfers between devices with their start and end apart: 16 -> 16, of which waited for: 6 -> 5; matrix products, arithmetic and copies ran while one was open for 0% -> 0% of each run, Pallas kernels for 12% -> 12%
where the time goes in v9:
time: 49.4 us; the launch traced here: 49.2 us
  waiting for transfers between devices  19.3 us (39%)
  starting transfers between devices  17.8 us (36%)
  Pallas kernels  10.4 us (21%)
  local copies, waits for them, and re-layouts  1.4 us (3%)
    ppermute x5, waiting for transfers between devices, swap(): lax.ppermute(first, axes, blue_pairs)  17 us
    ppermute x5, starting transfers between devices, swap(): lax.ppermute(first, axes, blue_pairs)  12.7 us
    pallas_call x13, Pallas kernels, call(): pl.pallas_call(kernel, name=name, out_shape=outs, in_specs=spaces, out_sp...  10.4 us
    ppermute x6, starting transfers between devices, exchange(): lax.ppermute(pieces[k], 'edges', [(i, i ^ k) for i in range(nedge)])  5.08 us
    ppermute x6, waiting for transfers between devices, exchange(): lax.ppermute(pieces[k], 'edges', [(i, i ^ k) for i in range(nedge)])  2.31 us
    unnamed x18, local copies, waits for them, and re-layouts  1.4 us
  transfers between devices with their start and end apart: 16, of which 5 were waited for; matrix products, arithmetic and copies ran while one was open for 0% of the time, Pallas kernels for 12%

profile of v9, /device:TPU:0, one launch (start us, length us, event | category | flops | bytes accessed | tf_op | source)
XLA Modules:
  0.0 49.2 jit_solution(9364640961550725009)
XLA Ops:
  0.0 2.0 %prep.1 = (bf16[32,512]{1,0:T(8,128)(2,1)}, bf16[32,512]{1,0:T(8,128)(2,1)}, bf16[32,512]{1,0:T(8,128)(2,1)}, bf16[32,512]{1,0:T(8,128)(2,1)}, bf16[336,256]{1,0:T(8,128)(2,1)}, /*index=5*/bf16[336,256]{1,0:T(8,128)(2,1)}) custom-call(f32[32,2048]{1,0:T(8,128)} %vec_hbm.1, bf16[1280,256]{1,0:T(8,128)(2,1)} %feat.3, s32[10,128]{1,0:T(8,128)} %bitcast.3, ...), custom_call_target="tpu_custom_call" | custom-call | flops 1000000000 | tf_op jit(solution)/shard_map/prep/pallas_call | solution.py:335
  2.0 2.4 %collective-permute-start.2 = (bf16[32,512]{1,0:T(8,128)(2,1)}, bf16[32,512]{1,0:T(8,128)(2,1)S(1)}, u32[]{:S(2)}, u32[]{:S(2)}) collective-permute-start(bf16[32,512]{1,0:T(8,128)(2,1)} %get-tuple-element.37), channel_id=1, source_target_pairs={{0,3},{1,2},{2,1},{3,0},{4,7},{5,6},{6,5},{7,4},{8,11},{9,10},{10,... | collective-permute-start | bytes 98312 | tf_op jit(solution)/shard_map/ppermute | solution.py:366
  4.5 0.7 %collective-permute-start = (bf16[32,512]{1,0:T(8,128)(2,1)}, bf16[32,512]{1,0:T(8,128)(2,1)S(1)}, u32[]{:S(2)}, u32[]{:S(2)}) collective-permute-start(bf16[32,512]{1,0:T(8,128)(2,1)} %get-tuple-element.35), channel_id=1, source_target_pairs={{0,1},{1,0},{2,3},{3,2},{4,5},{5,4},{6,7},{7,6},{8,9},{9,8},{10,11... | collective-permute-start | bytes 98312 | tf_op jit(solution)/shard_map/ppermute | solution.py:366
  5.2 0.0 collective-permute-start.1
  5.2 5.3 %collective-permute-start.3 = (bf16[336,256]{1,0:T(8,128)(2,1)}, bf16[336,256]{1,0:T(8,128)(2,1)S(1)}, u32[]{:S(2)}, u32[]{:S(2)}) collective-permute-start(bf16[336,256]{1,0:T(8,128)(2,1)} %get-tuple-element.40), channel_id=1, source_target_pairs={{0,31},{1,2},{2,1},{3,4},{4,3},{5,6},{6,5},{7,8},{8,7},{9,10},{10,... | collective-permute-start | bytes 516104 | tf_op jit(solution)/shard_map/ppermute | solution.py:360
  10.5 0.0 collective-permute-start.4
  10.5 0.0 collective-permute-done.2.x
  10.5 0.0 collective-permute-done.p1
  10.5 0.0 collective-permute-done.1.p2
  10.5 0.7 %copy-done.8 = bf16[32,512]{1,0:T(8,128)(2,1)S(1)} copy-done((bf16[32,512]{1,0:T(8,128)(2,1)S(1)}, bf16[32,512]{1,0:T(8,128)(2,1)}, u32[]{:S(2)}) %copy-start.8) | copy-done | bytes 32792
  11.3 0.0 copy-start.4
  11.3 0.0 copy-start.5
  11.3 0.2 field.1
  11.5 0.0 copy-start.6
  11.5 1.5 %collective-permute-start.5 = (bf16[384,128]{1,0:T(8,128)(2,1)S(1)}, bf16[384,128]{1,0:T(8,128)(2,1)S(1)}, u32[]{:S(2)}, u32[]{:S(2)}) collective-permute-start(bf16[384,128]{1,0:T(8,128)(2,1)S(1)} %get-tuple-element.46), channel_id=1, source_target_pairs={{0,31},{1,2},{2,1},{3,4},{4,3},{5,6},{6,5},{7,8},{8,7},{9,10},{10,... | collective-permute-start | bytes 294920 | tf_op jit(solution)/shard_map/ppermute | solution.py:360
  13.0 0.0 collective-permute-start.6
  13.1 2.2 %own.1 = (bf16[2,256,1024]{2,1,0:T(8,128)(2,1)S(1)}, bf16[512,256]{1,0:T(8,128)(2,1)S(1)}, bf16[512,8]{1,0:T(8,128)(2,1)S(1)}, bf16[256,256]{1,0:T(8,128)(2,1)S(1)}) custom-call(bf16[1280,256]{1,0:T(8,128)(2,1)S(1)} %copy-done, s32[10,128]{1,0:T(8,128)S(1)} %bitcast.4, s32[10,128]{1,0:T(8,128)S(1)} %bitcast.6, s32[10,128]{1,0:T(8,128)S(1)} %bitcast.8, ...), custom_call_target="tpu_custom_call" | custom-call | flops 4000000000 | tf_op jit(solution)/shard_map/own/pallas_call | solution.py:335
  15.3 0.0 collective-permute-done.3.blue
  15.3 0.0 collective-permute-done.4.red
  15.3 1.8 %spill.1.band = bf16[2,256,1024]{2,1,0:T(8,128)(2,1)S(1)} custom-call(bf16[2,256,1024]{2,1,0:T(8,128)(2,1)S(1)} %get-tuple-element.39.own_band, bf16[336,256]{1,0:T(8,128)(2,1)S(1)} %collective-permute-done.3.blue, bf16[336,256]{1,0:T(8,128)(2,1)S(1)} %collective-permute-done.4.red, ...), custom_call_target="tpu_custom_call", output_to_operand_aliasing={{}: (0, {})} | custom-call | tf_op jit(solution)/shard_map/spill/pallas_call | solution.py:335
  17.1 2.1 %collective-permute-done.5.blue = bf16[384,128]{1,0:T(8,128)(2,1)S(1)} collective-permute-done((bf16[384,128]{1,0:T(8,128)(2,1)S(1)}, bf16[384,128]{1,0:T(8,128)(2,1)S(1)}, u32[]{:S(2)}, u32[]{:S(2)}) %collective-permute-start.5) | collective-permute-done | bytes 98336 | tf_op jit(solution)/shard_map/ppermute | solution.py:360
  19.2 0.0 collective-permute-done.6.red
  19.2 0.6 %first.1 = (f32[512,128]{1,0:T(8,128)S(1)}, bf16[384,128]{1,0:T(8,128)(2,1)S(1)}, bf16[384,128]{1,0:T(8,128)(2,1)S(1)}) custom-call(bf16[2,256,1024]{2,1,0:T(8,128)(2,1)S(1)} %spill.1.band, f32[512,128]{1,0:T(8,128)S(1)} %get-tuple-element.45.t0.before, bf16[384,128]{1,0:T(8,128)(2,1)S(1)} %collective-permute-done.5.blue, ...), custom_call_target="tpu_custom_call" | custom-call | flops 1000000000 | tf_op jit(solution)/shard_map/first/pallas_call | solution.py:335
  19.8 1.9 %collective-permute-start.7 = (bf16[384,128]{1,0:T(8,128)(2,1)S(1)}, bf16[384,128]{1,0:T(8,128)(2,1)S(1)}, u32[]{:S(2)}, u32[]{:S(2)}) collective-permute-start(bf16[384,128]{1,0:T(8,128)(2,1)S(1)} %get-tuple-element.49), channel_id=1, source_target_pairs={{0,31},{1,2},{2,1},{3,4},{4,3},{5,6},{6,5},{7,8},{8,7},{9,10},{10,... | collective-permute-start | bytes 294920 | tf_op jit(solution)/shard_map/ppermute | solution.py:360
  21.7 0.0 collective-permute-start.8
  21.7 0.3 inner.2.part
  22.0 5.5 %collective-permute-done.7.blue = bf16[384,128]{1,0:T(8,128)(2,1)S(1)} collective-permute-done((bf16[384,128]{1,0:T(8,128)(2,1)S(1)}, bf16[384,128]{1,0:T(8,128)(2,1)S(1)}, u32[]{:S(2)}, u32[]{:S(2)}) %collective-permute-start.7) | collective-permute-done | bytes 98336 | tf_op jit(solution)/shard_map/ppermute | solution.py:360
  27.5 0.0 collective-permute-done.8.red
  27.5 0.4 outer.2
  27.9 2.0 %collective-permute-start.9 = (bf16[384,128]{1,0:T(8,128)(2,1)S(1)}, bf16[384,128]{1,0:T(8,128)(2,1)S(1)}, u32[]{:S(2)}, u32[]{:S(2)}) collective-permute-start(bf16[384,128]{1,0:T(8,128)(2,1)S(1)} %get-tuple-element.52), channel_id=1, source_target_pairs={{0,31},{1,2},{2,1},{3,4},{4,3},{5,6},{6,5},{7,8},{8,7},{9,10},{10,... | collective-permute-start | bytes 294920 | tf_op jit(solution)/shard_map/ppermute | solution.py:360
  29.9 0.0 collective-permute-start.10
  29.9 0.3 inner.3.part
  30.3 5.4 %collective-permute-done.9.blue = bf16[384,128]{1,0:T(8,128)(2,1)S(1)} collective-permute-done((bf16[384,128]{1,0:T(8,128)(2,1)S(1)}, bf16[384,128]{1,0:T(8,128)(2,1)S(1)}, u32[]{:S(2)}, u32[]{:S(2)}) %collective-permute-start.9) | collective-permute-done | bytes 98336 | tf_op jit(solution)/shard_map/ppermute | solution.py:360
  35.6 0.0 collective-permute-done.10.red
  35.6 0.4 outer.3
  36.1 2.0 %collective-permute-start.11 = (bf16[384,128]{1,0:T(8,128)(2,1)S(1)}, bf16[384,128]{1,0:T(8,128)(2,1)S(1)}, u32[]{:S(2)}, u32[]{:S(2)}) collective-permute-start(bf16[384,128]{1,0:T(8,128)(2,1)S(1)} %get-tuple-element.57), channel_id=1, source_target_pairs={{0,31},{1,2},{2,1},{3,4},{4,3},{5,6},{6,5},{7,8},{8,7},{9,10},{10,... | collective-permute-start | bytes 294920 | tf_op jit(solution)/shard_map/ppermute | solution.py:360
  38.1 0.0 collective-permute-start.12
  38.1 0.7 %copy-done.7 = f32[5]{0:T(128)S(1)} copy-done((f32[5]{0:T(128)S(1)}, f32[5]{0:T(128)}, u32[]{:S(2)}) %copy-start.7) | copy-done | bytes 44
  38.7 0.9 %mix.1 = (f32[128,512]{1,0:T(8,128)S(1)}, f32[8,128]{1,0:T(8,128)S(1)}) custom-call(f32[5]{0:T(128)S(1)} %copy-done.7, bf16[2,256,1024]{2,1,0:T(8,128)(2,1)S(1)} %spill.1.band, f32[512,128]{1,0:T(8,128)S(1)} %get-tuple-element.45.t0.before, f32[512,128]{1,0:T(8,128)S(1)} %get-tuple-element.48.now.before.t1, f32[512,128]{1,0:T(8,128)S(1)} %get-tuple-element.51.now.t2, ...), custom_call_target="tpu_custom_call" | custom-call | flops 1000000000 | tf_op jit(solution)/shard_map/mix/pallas_call | solution.py:335
  39.7 4.1 %collective-permute-done.11.blue = bf16[384,128]{1,0:T(8,128)(2,1)S(1)} collective-permute-done((bf16[384,128]{1,0:T(8,128)(2,1)S(1)}, bf16[384,128]{1,0:T(8,128)(2,1)S(1)}, u32[]{:S(2)}, u32[]{:S(2)}) %collective-permute-start.11) | collective-permute-done | bytes 98336 | tf_op jit(solution)/shard_map/ppermute | solution.py:360
  43.8 0.0 collective-permute-done.12.red
  43.8 0.5 last.1
  44.3 0.1 collective-permute-start.13
  44.4 0.1 collective-permute-start.14
  44.4 1.8 %collective-permute-start.15 = (bf16[32,512]{1,0:T(8,128)(2,1)S(1)}, bf16[32,512]{1,0:T(8,128)(2,1)S(1)}, u32[]{:S(2)}, u32[]{:S(2)}) collective-permute-start(bf16[32,512]{1,0:T(8,128)(2,1)S(1)} %get-tuple-element.62), channel_id=1, source_target_pairs={{0,3},{1,2},{2,1},{3,0},{4,7},{5,6},{6,5},{7,4},{8,11},{9,10},{10,... | collective-permute-start | bytes 98312 | tf_op jit(solution)/shard_map/ppermute | solution.py:366
  46.2 0.0 collective-permute-done.13.p1
  46.2 2.3 %collective-permute-done.14.p2 = bf16[32,512]{1,0:T(8,128)(2,1)S(1)} collective-permute-done((bf16[32,512]{1,0:T(8,128)(2,1)S(1)}, bf16[32,512]{1,0:T(8,128)(2,1)S(1)}, u32[]{:S(2)}, u32[]{:S(2)}) %collective-permute-start.14) | collective-permute-done | bytes 32800 | tf_op jit(solution)/shard_map/ppermute | solution.py:366
  48.5 0.7 %join.1 = f32[32,2048]{1,0:T(8,128)} custom-call(bf16[32,512]{1,0:T(8,128)(2,1)S(1)} %get-tuple-element.59.p0, bf16[32,512]{1,0:T(8,128)(2,1)S(1)} %collective-permute-done.13.p1, bf16[32,512]{1,0:T(8,128)(2,1)S(1)} %collective-permute-done.14.p2, bf16[32,512]{1,0:T(8,128)(2,1)S(1)} %collective-permute-done.15.p3), custom_call_target="tpu_custom_call" | custom-call | flops 1000000000 | tf_op jit(solution)/shard_map/join/pallas_call | solution.py:335
  (15 shorter events, 0.0 us)
Async XLA Ops:
  2.0 8.5 %collective-permute-start.2 = (bf16[32,512]{1,0:T(8,128)(2,1)}, bf16[32,512]{1,0:T(8,128)(2,1)S(1)}, u32[]{:S(2)}, u32[]{:S(2)}) collective-permute-start(bf16[32,512]{1,0:T(8,128)(2,1)} %get-tuple-element.37), channel_id=1, source_target_pairs={{0,3},{1,2},{2,1},{3,0},{4,7},{5,6},{6,5},{7,4},{8,11},{9,10},{10,... | collective-permute-start | bytes 98312 | tf_op jit(solution)/shard_map/ppermute | solution.py:366
  4.5 6.0 %collective-permute-start = (bf16[32,512]{1,0:T(8,128)(2,1)}, bf16[32,512]{1,0:T(8,128)(2,1)S(1)}, u32[]{:S(2)}, u32[]{:S(2)}) collective-permute-start(bf16[32,512]{1,0:T(8,128)(2,1)} %get-tuple-element.35), channel_id=1, source_target_pairs={{0,1},{1,0},{2,3},{3,2},{4,5},{5,4},{6,7},{7,6},{8,9},{9,8},{10,11... | collective-permute-start | bytes 98312 | tf_op jit(solution)/shard_map/ppermute | solution.py:366
  5.2 5.4 %collective-permute-start.1 = (bf16[32,512]{1,0:T(8,128)(2,1)}, bf16[32,512]{1,0:T(8,128)(2,1)S(1)}, u32[]{:S(2)}, u32[]{:S(2)}) collective-permute-start(bf16[32,512]{1,0:T(8,128)(2,1)} %get-tuple-element.36), channel_id=1, source_target_pairs={{0,2},{1,3},{2,0},{3,1},{4,6},{5,7},{6,4},{7,5},{8,10},{9,11},{10,... | collective-permute-start | bytes 98312 | tf_op jit(solution)/shard_map/ppermute | solution.py:366
  5.2 10.1 %collective-permute-start.3 = (bf16[336,256]{1,0:T(8,128)(2,1)}, bf16[336,256]{1,0:T(8,128)(2,1)S(1)}, u32[]{:S(2)}, u32[]{:S(2)}) collective-permute-start(bf16[336,256]{1,0:T(8,128)(2,1)} %get-tuple-element.40), channel_id=1, source_target_pairs={{0,31},{1,2},{2,1},{3,4},{4,3},{5,6},{6,5},{7,8},{8,7},{9,10},{10,... | collective-permute-start | bytes 516104 | tf_op jit(solution)/shard_map/ppermute | solution.py:360
  10.5 0.8 %copy-start.8 = (bf16[32,512]{1,0:T(8,128)(2,1)S(1)}, bf16[32,512]{1,0:T(8,128)(2,1)}, u32[]{:S(2)}) copy-start(bf16[32,512]{1,0:T(8,128)(2,1)} %get-tuple-element.34.p0) | copy-start | bytes 98308
  10.5 4.8 %collective-permute-start.4 = (bf16[336,256]{1,0:T(8,128)(2,1)}, bf16[336,256]{1,0:T(8,128)(2,1)S(1)}, u32[]{:S(2)}, u32[]{:S(2)}) collective-permute-start(bf16[336,256]{1,0:T(8,128)(2,1)} %get-tuple-element.41), channel_id=1, source_target_pairs={{0,1},{1,0},{2,3},{3,2},{4,5},{5,4},{6,7},{7,6},{8,9},{9,8},{10,11... | collective-permute-start | bytes 516104 | tf_op jit(solution)/shard_map/ppermute | solution.py:361
  11.3 1.8 %copy-start = (bf16[1280,256]{1,0:T(8,128)(2,1)S(1)}, bf16[1280,256]{1,0:T(8,128)(2,1)}, u32[]{:S(2)}) copy-start(bf16[1280,256]{1,0:T(8,128)(2,1)} %feat.3) | copy-start | bytes 1966084
  11.3 1.8 %copy-start.1 = (bf16[256,512]{1,0:T(8,128)(2,1)S(1)}, bf16[256,512]{1,0:T(8,128)(2,1)}, u32[]{:S(2)}) copy-start(bf16[256,512]{1,0:T(8,128)(2,1)} %w_in.1) | copy-start | bytes 786436
  11.3 1.8 %copy-start.2 = (bf16[256,256]{1,0:T(8,128)(2,1)S(1)}, bf16[256,256]{1,0:T(8,128)(2,1)}, u32[]{:S(2)}) copy-start(bf16[256,256]{1,0:T(8,128)(2,1)} %w_out.1) | copy-start | bytes 393220
  11.3 1.8 %copy-start.3 = (s32[1280]{0:T(1024)S(1)}, s32[1280]{0:T(1024)}, u32[]{:S(2)}) copy-start(s32[1280]{0:T(1024)} %param.10) | copy-start | bytes 15364
  11.3 1.8 %copy-start.4 = (s32[1280]{0:T(1024)S(1)}, s32[1280]{0:T(1024)}, u32[]{:S(2)}) copy-start(s32[1280]{0:T(1024)} %param.11) | copy-start | bytes 15364
  11.3 1.8 %copy-start.5 = (s32[1280]{0:T(1024)S(1)}, s32[1280]{0:T(1024)}, u32[]{:S(2)}) copy-start(s32[1280]{0:T(1024)} %param.12) | copy-start | bytes 15364
  11.5 1.6 %copy-start.6 = (bf16[3,512]{1,0:T(4,128)(2,1)S(1)}, bf16[3,512]{1,0:T(4,128)(2,1)}, u32[]{:S(2)}) copy-start(bf16[3,512]{1,0:T(4,128)(2,1)} %cell_bias.1) | copy-start | bytes 9220
  11.5 7.7 %collective-permute-start.5 = (bf16[384,128]{1,0:T(8,128)(2,1)S(1)}, bf16[384,128]{1,0:T(8,128)(2,1)S(1)}, u32[]{:S(2)}, u32[]{:S(2)}) collective-permute-start(bf16[384,128]{1,0:T(8,128)(2,1)S(1)} %get-tuple-element.46), channel_id=1, source_target_pairs={{0,31},{1,2},{2,1},{3,4},{4,3},{5,6},{6,5},{7,8},{8,7},{9,10},{10,... | collective-permute-start | bytes 294920 | tf_op jit(solution)/shard_map/ppermute | solution.py:360
  13.0 6.2 %collective-permute-start.6 = (bf16[384,128]{1,0:T(8,128)(2,1)S(1)}, bf16[384,128]{1,0:T(8,128)(2,1)S(1)}, u32[]{:S(2)}, u32[]{:S(2)}) collective-permute-start(bf16[384,128]{1,0:T(8,128)(2,1)S(1)} %get-tuple-element.47), channel_id=1, source_target_pairs={{0,1},{1,0},{2,3},{3,2},{4,5},{5,4},{6,7},{7,6},{8,9},{9,8},{10,11... | collective-permute-start | bytes 294920 | tf_op jit(solution)/shard_map/ppermute | solution.py:361
  19.8 7.7 %collective-permute-start.7 = (bf16[384,128]{1,0:T(8,128)(2,1)S(1)}, bf16[384,128]{1,0:T(8,128)(2,1)S(1)}, u32[]{:S(2)}, u32[]{:S(2)}) collective-permute-start(bf16[384,128]{1,0:T(8,128)(2,1)S(1)} %get-tuple-element.49), channel_id=1, source_target_pairs={{0,31},{1,2},{2,1},{3,4},{4,3},{5,6},{6,5},{7,8},{8,7},{9,10},{10,... | collective-permute-start | bytes 294920 | tf_op jit(solution)/shard_map/ppermute | solution.py:360
  21.7 5.8 %collective-permute-start.8 = (bf16[384,128]{1,0:T(8,128)(2,1)S(1)}, bf16[384,128]{1,0:T(8,128)(2,1)S(1)}, u32[]{:S(2)}, u32[]{:S(2)}) collective-permute-start(bf16[384,128]{1,0:T(8,128)(2,1)S(1)} %get-tuple-element.50), channel_id=1, source_target_pairs={{0,1},{1,0},{2,3},{3,2},{4,5},{5,4},{6,7},{7,6},{8,9},{9,8},{10,11... | collective-permute-start | bytes 294920 | tf_op jit(solution)/shard_map/ppermute | solution.py:361
  27.9 7.7 %collective-permute-start.9 = (bf16[384,128]{1,0:T(8,128)(2,1)S(1)}, bf16[384,128]{1,0:T(8,128)(2,1)S(1)}, u32[]{:S(2)}, u32[]{:S(2)}) collective-permute-start(bf16[384,128]{1,0:T(8,128)(2,1)S(1)} %get-tuple-element.52), channel_id=1, source_target_pairs={{0,31},{1,2},{2,1},{3,4},{4,3},{5,6},{6,5},{7,8},{8,7},{9,10},{10,... | collective-permute-start | bytes 294920 | tf_op jit(solution)/shard_map/ppermute | solution.py:360
  29.9 5.7 %collective-permute-start.10 = (bf16[384,128]{1,0:T(8,128)(2,1)S(1)}, bf16[384,128]{1,0:T(8,128)(2,1)S(1)}, u32[]{:S(2)}, u32[]{:S(2)}) collective-permute-start(bf16[384,128]{1,0:T(8,128)(2,1)S(1)} %get-tuple-element.53), channel_id=1, source_target_pairs={{0,1},{1,0},{2,3},{3,2},{4,5},{5,4},{6,7},{7,6},{8,9},{9,8},{10,11... | collective-permute-start | bytes 294920 | tf_op jit(solution)/shard_map/ppermute | solution.py:361
  36.1 7.7 %collective-permute-start.11 = (bf16[384,128]{1,0:T(8,128)(2,1)S(1)}, bf16[384,128]{1,0:T(8,128)(2,1)S(1)}, u32[]{:S(2)}, u32[]{:S(2)}) collective-permute-start(bf16[384,128]{1,0:T(8,128)(2,1)S(1)} %get-tuple-element.57), channel_id=1, source_target_pairs={{0,31},{1,2},{2,1},{3,4},{4,3},{5,6},{6,5},{7,8},{8,7},{9,10},{10,... | collective-permute-start | bytes 294920 | tf_op jit(solution)/shard_map/ppermute | solution.py:360
  38.1 0.7 %copy-start.7 = (f32[5]{0:T(128)S(1)}, f32[5]{0:T(128)}, u32[]{:S(2)}) copy-start(f32[5]{0:T(128)} %coef.1) | copy-start | bytes 64
  38.1 5.7 %collective-permute-start.12 = (bf16[384,128]{1,0:T(8,128)(2,1)S(1)}, bf16[384,128]{1,0:T(8,128)(2,1)S(1)}, u32[]{:S(2)}, u32[]{:S(2)}) collective-permute-start(bf16[384,128]{1,0:T(8,128)(2,1)S(1)} %get-tuple-element.58), channel_id=1, source_target_pairs={{0,1},{1,0},{2,3},{3,2},{4,5},{5,4},{6,7},{7,6},{8,9},{9,8},{10,11... | collective-permute-start | bytes 294920 | tf_op jit(solution)/shard_map/ppermute | solution.py:361
  44.3 1.9 %collective-permute-start.13 = (bf16[32,512]{1,0:T(8,128)(2,1)S(1)}, bf16[32,512]{1,0:T(8,128)(2,1)S(1)}, u32[]{:S(2)}, u32[]{:S(2)}) collective-permute-start(bf16[32,512]{1,0:T(8,128)(2,1)S(1)} %get-tuple-element.60), channel_id=1, source_target_pairs={{0,1},{1,0},{2,3},{3,2},{4,5},{5,4},{6,7},{7,6},{8,9},{9,8},{10,11... | collective-permute-start | bytes 98312 | tf_op jit(solution)/shard_map/ppermute | solution.py:366
  44.4 4.2 %collective-permute-start.14 = (bf16[32,512]{1,0:T(8,128)(2,1)S(1)}, bf16[32,512]{1,0:T(8,128)(2,1)S(1)}, u32[]{:S(2)}, u32[]{:S(2)}) collective-permute-start(bf16[32,512]{1,0:T(8,128)(2,1)S(1)} %get-tuple-element.61), channel_id=1, source_target_pairs={{0,2},{1,3},{2,0},{3,1},{4,6},{5,7},{6,4},{7,5},{8,10},{9,11},{10,... | collective-permute-start | bytes 98312 | tf_op jit(solution)/shard_map/ppermute | solution.py:366
  44.4 4.1 %collective-permute-start.15 = (bf16[32,512]{1,0:T(8,128)(2,1)S(1)}, bf16[32,512]{1,0:T(8,128)(2,1)S(1)}, u32[]{:S(2)}, u32[]{:S(2)}) collective-permute-start(bf16[32,512]{1,0:T(8,128)(2,1)S(1)} %get-tuple-element.62), channel_id=1, source_target_pairs={{0,3},{1,2},{2,1},{3,0},{4,7},{5,6},{6,5},{7,4},{8,11},{9,10},{10,... | collective-permute-start | bytes 98312 | tf_op jit(solution)/shard_map/ppermute | solution.py:366

commit v10 on v9

--- a/solution.py
+++ b/solution.py
@@ -53,13 +53,13 @@
 
 
 def prep_kernel(
-    vec_hbm, feat, src_hbm, dst_hbm, cell_hbm, p0, p1, p2, p3, blue, red, vectors, src, dst, cell, sems
+    vec_hbm, feat, src_hbm, dst_hbm, cell_hbm, p0, p2, p3, blue, red, vectors, src, dst, cell, sems
 ):
     member, side = lax.axis_index("edges"), device_side()
-    pieces = (p0, p1, p2, p3)
+    pieces = (p0, None, p2, p3)
     loads = []
-    for k, piece in enumerate(pieces):
-        width = piece.shape[1]
+    high_rows, width = p0.shape
+    for k in range(4):
         at = pl.multiple_of((member ^ k) * width, width)
         loads.append(pltpu.make_async_copy(vec_hbm.at[:, pl.ds(at, width)], vectors.at[k], sems.at[k]))
     high = feat.shape[0] - SPILL
@@ -97,7 +97,12 @@
         msg[SPILL : SPILL + ID_ROWS, 128:256] = none
     for k, piece in enumerate(pieces):
         loads[k].wait()
-        piece[...] = vectors[k].astype(BF)
+        if k == 1:
+            for n in range(width // red.shape[1]):
+                at = SPILL + ID_ROWS + n * high_rows
+                red[at : at + high_rows, :] = vectors[k, :, n * red.shape[1] : (n + 1) * red.shape[1]].astype(BF)
+        else:
+            piece[...] = vectors[k].astype(BF)
     for copy in copies:
         copy.wait()
 
@@ -106,11 +111,16 @@
     y[...] = x[...]
 
 
-def field_kernel(p0, p1, p2, p3, t0, to_blue, to_red, token, field):
+def field_kernel(p0, near, p2, p3, t0, to_blue, to_red, token, field):
     member = lax.axis_index("edges")
-    for k, piece in enumerate((p0, p1, p2, p3)):
-        high = piece.shape[0]
+    high = p0.shape[0]
+    for k, piece in ((0, p0), (2, p2), (3, p3)):
         field[pl.ds(pl.multiple_of((member ^ k) * high, high), high), :] = piece[...].astype(F32)
+    rows = pl.ds(pl.multiple_of((member ^ 1) * high, high), high)
+    width = near.shape[1]
+    for n in range(field.shape[1] // width):
+        at = SPILL + ID_ROWS + n * high
+        field[rows, n * width : (n + 1) * width] = near[at : at + high, :].astype(F32)
     t0[...] = field[...].T
     token[...] = jnp.zeros(token.shape, F32)
     put_sends(t0, to_blue, to_red)
@@ -202,7 +212,8 @@
     even = device_side() == 0
     nfeat = spill.shape[1]
     rows = spill.shape[0] // 2
-    left, right = [jnp.where(even, x, y) for x, y in ((blue[...], red[...]), (red[...], blue[...]))]
+    near = red[0 : SPILL + ID_ROWS, :]
+    left, right = [jnp.where(even, x, y) for x, y in ((blue[...], near), (near, blue[...]))]
     spill[0:64, :] = jnp.zeros((64, nfeat), BF)
     spill[64 : rows + SPILL, :] = jnp.concatenate([left[0:SPILL], right[0:SPILL]], axis=0)
     spill[rows + SPILL :, :] = jnp.zeros((64, nfeat), BF)
@@ -370,10 +381,11 @@
     piece = shape((high, nrow), BF)
     lines = (nown // 128, 128)
     edges = [x.reshape(lines) for x in (edge_src, edge_dst, edge_cell)]
-    *pieces, blue_msg, red_msg = call(
+    near_msg = shape((SPILL + ID_ROWS + high * nrow // nfeat, nfeat), BF)
+    own_piece, straight, across, blue_msg, near = call(
         prep_kernel,
         "prep",
-        (piece,) * 4 + (msg, msg),
+        (piece,) * 3 + (msg, near_msg),
         [pltpu.VMEM((nedge, high, nrow), F32)]
         + [pltpu.VMEM(lines, jnp.int32)] * 3
         + [pltpu.SemaphoreType.DMA((9,))],
@@ -383,9 +395,12 @@
         in_hbm=range(5),
         limit=FULL,
     )
-    pieces = exchange(pieces)
-    blue_msg, red_msg = swap(blue_msg, red_msg)
-    pieces[3:4] = call(pass_kernel, "pass", (piece,), [], pieces[3], micros=0)
+    across = lax.ppermute(across, "edges", [(i, i ^ 3) for i in range(nedge)])
+    straight = lax.ppermute(straight, "edges", [(i, i ^ 2) for i in range(nedge)])
+    near = lax.ppermute(near, axes, red_pairs)
+    blue_msg = lax.ppermute(blue_msg, axes, blue_pairs)
+    (across,) = call(pass_kernel, "pass", (piece,), [], across, micros=0)
+    pieces = [own_piece, near, straight, across]
     full, part = shape((nrow, VEC), F32), shape((HALO, VEC), BF)
     t0, to_blue, to_red, token = call(
         field_kernel, "field", (full, part, part, shape((8, VEC), F32)), [pltpu.VMEM((VEC, nrow), F32)], *pieces
@@ -415,7 +430,7 @@
         [pltpu.VMEM((ORB * ORB, spill_len), BF), pltpu.VMEM((spill_len, nfeat), BF)],
         band,
         blue_msg,
-        red_msg,
+        near,
         *weights,
         alias={0: 0},
         micros=0,

time: 49.4 us -> 49 us (level)
  starting transfers between devices: 17.8 us -> 20.5 us
  waiting for transfers between devices: 19.3 us -> 16.9 us
  local copies, waits for them, and re-layouts: 1.4 us -> 0.7 us
    ppermute x0 -> x4, starting transfers between devices: none -> 8.54 us  [the longest x1 5.37 us: per_device(): blue_msg = lax.ppermute(blue_msg, axes, blue_pairs)]
    ppermute x6 -> x3, starting transfers between devices: 5.08 us -> 1.93 us  [exchange(): lax.ppermute(pieces[k], 'edges', [(i, i ^ k) for i in range(nedge)])]
    ppermute x5 -> x4, starting transfers between devices: 12.7 us -> 10 us  [swap(): lax.ppermute(first, axes, blue_pairs)]
    ppermute x5 -> x4, waiting for transfers between devices: 17 us -> 14.5 us  [swap(): lax.ppermute(first, axes, blue_pairs)]
    unnamed x18, local copies, waits for them, and re-layouts: 1.4 us -> 0.7 us
    ppermute x6 -> x3, waiting for transfers between devices: 2.31 us -> 2.3 us  [exchange(): lax.ppermute(pieces[k], 'edges', [(i, i ^ k) for i in range(nedge)])]
  transfers between devices with their start and end apart: 16 -> 15, of which waited for: 5 -> 5; matrix products, arithmetic and copies ran while one was open for 0% -> 0% of each run, Pallas kernels for 12% -> 12%
where the time goes in v10:
time: 49 us; the launch traced here: 48.8 us
  starting transfers between devices  20.5 us (42%)
  waiting for transfers between devices  16.9 us (34%)
  Pallas kernels  10.5 us (21%)
  local copies, waits for them, and re-layouts  0.7 us (1%)
    ppermute x4, waiting for transfers between devices, swap(): lax.ppermute(first, axes, blue_pairs)  14.5 us
    pallas_call x13, Pallas kernels, call(): pl.pallas_call(kernel, name=name, out_shape=outs, in_specs=spaces, out_sp...  10.5 us
    ppermute x4, starting transfers between devices, swap(): lax.ppermute(first, axes, blue_pairs)  10 us
    ppermute x1, starting transfers between devices, per_device(): blue_msg = lax.ppermute(blue_msg, axes, blue_pairs)  5.37 us
    ppermute x1, starting transfers between devices, per_device(): across = lax.ppermute(across, 'edges', [(i, i ^ 3) for i in range(nedge)])  2.61 us
    ppermute x3, waiting for transfers between devices, exchange(): lax.ppermute(pieces[k], 'edges', [(i, i ^ k) for i in range(nedge)])  2.3 us
    ppermute x3, starting transfers between devices, exchange(): lax.ppermute(pieces[k], 'edges', [(i, i ^ k) for i in range(nedge)])  1.93 us
  transfers between devices with their start and end apart: 15, of which 5 were waited for; matrix products, arithmetic and copies ran while one was open for 0% of the time, Pallas kernels for 12%

profile of v10, /device:TPU:0, one launch (start us, length us, event | category | flops | bytes accessed | tf_op | source)
XLA Modules:
  0.0 48.8 jit_solution(16593652723449249909)
XLA Ops:
  0.0 2.0 %prep.1 = (bf16[32,512]{1,0:T(8,128)(2,1)}, bf16[32,512]{1,0:T(8,128)(2,1)}, bf16[32,512]{1,0:T(8,128)(2,1)}, bf16[336,256]{1,0:T(8,128)(2,1)}, bf16[400,256]{1,0:T(8,128)(2,1)}) custom-call(f32[32,2048]{1,0:T(8,128)} %vec_hbm.1, bf16[1280,256]{1,0:T(8,128)(2,1)} %feat.3, s32[10,128]{1,0:T(8,128)} %bitcast.3, s32[10,128]{1,0:T(8,128)} %bitcast.5, ...), custom_call_target="tpu_custom_call" | custom-call | flops 1000000000 | tf_op jit(solution)/shard_map/prep/pallas_call | solution.py:346
  2.0 0.5 %collective-permute-start = (bf16[400,256]{1,0:T(8,128)(2,1)}, bf16[400,256]{1,0:T(8,128)(2,1)S(1)}, u32[]{:S(2)}, u32[]{:S(2)}) collective-permute-start(bf16[400,256]{1,0:T(8,128)(2,1)} %get-tuple-element.34), channel_id=1, source_target_pairs={{0,1},{1,0},{2,3},{3,2},{4,5},{5,4},{6,7},{7,6},{8,9},{9,8},{10,11... | collective-permute-start | bytes 614408 | tf_op jit(solution)/shard_map/ppermute | solution.py:400
  2.5 2.6 %collective-permute-start.2 = (bf16[32,512]{1,0:T(8,128)(2,1)}, bf16[32,512]{1,0:T(8,128)(2,1)S(1)}, u32[]{:S(2)}, u32[]{:S(2)}) collective-permute-start(bf16[32,512]{1,0:T(8,128)(2,1)} %get-tuple-element.36), channel_id=1, source_target_pairs={{0,3},{1,2},{2,1},{3,0},{4,7},{5,6},{6,5},{7,4},{8,11},{9,10},{10,... | collective-permute-start | bytes 98312 | tf_op jit(solution)/shard_map/ppermute | solution.py:398
  5.2 0.0 collective-permute-start.1
  5.2 5.4 %collective-permute-start.3 = (bf16[336,256]{1,0:T(8,128)(2,1)}, bf16[336,256]{1,0:T(8,128)(2,1)S(1)}, u32[]{:S(2)}, u32[]{:S(2)}) collective-permute-start(bf16[336,256]{1,0:T(8,128)(2,1)} %get-tuple-element.39), channel_id=1, source_target_pairs={{0,31},{1,2},{2,1},{3,4},{4,3},{5,6},{6,5},{7,8},{8,7},{9,10},{10,... | collective-permute-start | bytes 516104 | tf_op jit(solution)/shard_map/ppermute | solution.py:401
  10.6 0.0 collective-permute-done.2.x
  10.6 0.0 collective-permute-done.1.p2
  10.6 0.0 collective-permute-done.near.red
  10.6 0.0 copy-start
  10.6 0.0 copy-start.1
  10.6 0.0 copy-start.2
  10.6 0.0 copy-start.3
  10.7 0.0 copy-start.4
  10.7 0.0 copy-start.5
  10.7 0.2 field.1
  10.9 0.0 copy-start.6
  10.9 2.3 %collective-permute-start.4 = (bf16[384,128]{1,0:T(8,128)(2,1)S(1)}, bf16[384,128]{1,0:T(8,128)(2,1)S(1)}, u32[]{:S(2)}, u32[]{:S(2)}) collective-permute-start(bf16[384,128]{1,0:T(8,128)(2,1)S(1)} %get-tuple-element.44), channel_id=1, source_target_pairs={{0,31},{1,2},{2,1},{3,4},{4,3},{5,6},{6,5},{7,8},{8,7},{9,10},{10,... | collective-permute-start | bytes 294920 | tf_op jit(solution)/shard_map/ppermute | solution.py:371
  13.2 0.0 collective-permute-start.5
  13.2 2.2 %own.1 = (bf16[2,256,1024]{2,1,0:T(8,128)(2,1)S(1)}, bf16[512,256]{1,0:T(8,128)(2,1)S(1)}, bf16[512,8]{1,0:T(8,128)(2,1)S(1)}, bf16[256,256]{1,0:T(8,128)(2,1)S(1)}) custom-call(bf16[1280,256]{1,0:T(8,128)(2,1)S(1)} %copy-done, s32[10,128]{1,0:T(8,128)S(1)} %bitcast.4, s32[10,128]{1,0:T(8,128)S(1)} %bitcast.6, s32[10,128]{1,0:T(8,128)S(1)} %bitcast.8, ...), custom_call_target="tpu_custom_call" | custom-call | flops 4000000000 | tf_op jit(solution)/shard_map/own/pallas_call | solution.py:346
  15.4 0.0 collective-permute-done.3.blue
  15.4 1.8 %spill.1.band = bf16[2,256,1024]{2,1,0:T(8,128)(2,1)S(1)} custom-call(bf16[2,256,1024]{2,1,0:T(8,128)(2,1)S(1)} %get-tuple-element.38.own_band, bf16[336,256]{1,0:T(8,128)(2,1)S(1)} %collective-permute-done.3.blue, bf16[400,256]{1,0:T(8,128)(2,1)S(1)} %collective-permute-done.near.red, ...), custom_call_target="tpu_custom_call", output_to_operand_aliasing={{}: (0, {})} | custom-call | tf_op jit(solution)/shard_map/spill/pallas_call | solution.py:346
  17.2 1.4 %collective-permute-done.4.blue = bf16[384,128]{1,0:T(8,128)(2,1)S(1)} collective-permute-done((bf16[384,128]{1,0:T(8,128)(2,1)S(1)}, bf16[384,128]{1,0:T(8,128)(2,1)S(1)}, u32[]{:S(2)}, u32[]{:S(2)}) %collective-permute-start.4) | collective-permute-done | bytes 98336 | tf_op jit(solution)/shard_map/ppermute | solution.py:371
  18.6 0.0 collective-permute-done.5.red
  18.6 0.6 %first.1 = (f32[512,128]{1,0:T(8,128)S(1)}, bf16[384,128]{1,0:T(8,128)(2,1)S(1)}, bf16[384,128]{1,0:T(8,128)(2,1)S(1)}) custom-call(bf16[2,256,1024]{2,1,0:T(8,128)(2,1)S(1)} %spill.1.band, f32[512,128]{1,0:T(8,128)S(1)} %get-tuple-element.43.t0.before, bf16[384,128]{1,0:T(8,128)(2,1)S(1)} %collective-permute-done.4.blue, ...), custom_call_target="tpu_custom_call" | custom-call | flops 1000000000 | tf_op jit(solution)/shard_map/first/pallas_call | solution.py:346
  19.2 2.6 %collective-permute-start.6 = (bf16[384,128]{1,0:T(8,128)(2,1)S(1)}, bf16[384,128]{1,0:T(8,128)(2,1)S(1)}, u32[]{:S(2)}, u32[]{:S(2)}) collective-permute-start(bf16[384,128]{1,0:T(8,128)(2,1)S(1)} %get-tuple-element.47), channel_id=1, source_target_pairs={{0,31},{1,2},{2,1},{3,4},{4,3},{5,6},{6,5},{7,8},{8,7},{9,10},{10,... | collective-permute-start | bytes 294920 | tf_op jit(solution)/shard_map/ppermute | solution.py:371
  21.8 0.0 collective-permute-start.7
  21.8 0.3 inner.2.part
  22.1 4.9 %collective-permute-done.6.blue = bf16[384,128]{1,0:T(8,128)(2,1)S(1)} collective-permute-done((bf16[384,128]{1,0:T(8,128)(2,1)S(1)}, bf16[384,128]{1,0:T(8,128)(2,1)S(1)}, u32[]{:S(2)}, u32[]{:S(2)}) %collective-permute-start.6) | collective-permute-done | bytes 98336 | tf_op jit(solution)/shard_map/ppermute | solution.py:371
  27.0 0.0 collective-permute-done.7.red
  27.0 0.4 outer.2
  27.5 2.6 %collective-permute-start.8 = (bf16[384,128]{1,0:T(8,128)(2,1)S(1)}, bf16[384,128]{1,0:T(8,128)(2,1)S(1)}, u32[]{:S(2)}, u32[]{:S(2)}) collective-permute-start(bf16[384,128]{1,0:T(8,128)(2,1)S(1)} %get-tuple-element.50), channel_id=1, source_target_pairs={{0,31},{1,2},{2,1},{3,4},{4,3},{5,6},{6,5},{7,8},{8,7},{9,10},{10,... | collective-permute-start | bytes 294920 | tf_op jit(solution)/shard_map/ppermute | solution.py:371
  30.1 0.0 collective-permute-start.9
  30.1 0.3 inner.3.part
  30.4 4.8 %collective-permute-done.8.blue = bf16[384,128]{1,0:T(8,128)(2,1)S(1)} collective-permute-done((bf16[384,128]{1,0:T(8,128)(2,1)S(1)}, bf16[384,128]{1,0:T(8,128)(2,1)S(1)}, u32[]{:S(2)}, u32[]{:S(2)}) %collective-permute-start.8) | collective-permute-done | bytes 98336 | tf_op jit(solution)/shard_map/ppermute | solution.py:371
  35.2 0.0 collective-permute-done.9.red
  35.2 0.4 outer.3
  35.6 2.6 %collective-permute-start.10 = (bf16[384,128]{1,0:T(8,128)(2,1)S(1)}, bf16[384,128]{1,0:T(8,128)(2,1)S(1)}, u32[]{:S(2)}, u32[]{:S(2)}) collective-permute-start(bf16[384,128]{1,0:T(8,128)(2,1)S(1)} %get-tuple-element.55), channel_id=1, source_target_pairs={{0,31},{1,2},{2,1},{3,4},{4,3},{5,6},{6,5},{7,8},{8,7},{9,10},{10,... | collective-permute-start | bytes 294920 | tf_op jit(solution)/shard_map/ppermute | solution.py:371
  38.2 0.7 %copy-done.7 = f32[5]{0:T(128)S(1)} copy-done((f32[5]{0:T(128)S(1)}, f32[5]{0:T(128)}, u32[]{:S(2)}) %copy-start.7) | copy-done | bytes 44
  38.8 1.0 %mix.1 = (f32[128,512]{1,0:T(8,128)S(1)}, f32[8,128]{1,0:T(8,128)S(1)}) custom-call(f32[5]{0:T(128)S(1)} %copy-done.7, bf16[2,256,1024]{2,1,0:T(8,128)(2,1)S(1)} %spill.1.band, f32[512,128]{1,0:T(8,128)S(1)} %get-tuple-element.43.t0.before, f32[512,128]{1,0:T(8,128)S(1)} %get-tuple-element.46.now.before.t1, f32[512,128]{1,0:T(8,128)S(1)} %get-tuple-element.49.now.t2, ...), custom_call_target="tpu_custom_call" | custom-call | flops 1000000000 | tf_op jit(solution)/shard_map/mix/pallas_call | solution.py:346
  39.8 3.5 %collective-permute-done.10.blue = bf16[384,128]{1,0:T(8,128)(2,1)S(1)} collective-permute-done((bf16[384,128]{1,0:T(8,128)(2,1)S(1)}, bf16[384,128]{1,0:T(8,128)(2,1)S(1)}, u32[]{:S(2)}, u32[]{:S(2)}) %collective-permute-start.10) | collective-permute-done | bytes 98336 | tf_op jit(solution)/shard_map/ppermute | solution.py:371
  43.3 0.0 collective-permute-done.11.red
  43.3 0.5 last.1
  43.8 0.1 collective-permute-start.12
  43.9 0.1 collective-permute-start.13
  44.0 1.8 %collective-permute-start.14 = (bf16[32,512]{1,0:T(8,128)(2,1)S(1)}, bf16[32,512]{1,0:T(8,128)(2,1)S(1)}, u32[]{:S(2)}, u32[]{:S(2)}) collective-permute-start(bf16[32,512]{1,0:T(8,128)(2,1)S(1)} %get-tuple-element.60), channel_id=1, source_target_pairs={{0,3},{1,2},{2,1},{3,0},{4,7},{5,6},{6,5},{7,4},{8,11},{9,10},{10,... | collective-permute-start | bytes 98312 | tf_op jit(solution)/shard_map/ppermute | solution.py:377
  45.7 0.0 collective-permute-done.12.p1
  45.7 2.3 %collective-permute-done.13.p2 = bf16[32,512]{1,0:T(8,128)(2,1)S(1)} collective-permute-done((bf16[32,512]{1,0:T(8,128)(2,1)S(1)}, bf16[32,512]{1,0:T(8,128)(2,1)S(1)}, u32[]{:S(2)}, u32[]{:S(2)}) %collective-permute-start.13) | collective-permute-done | bytes 32800 | tf_op jit(solution)/shard_map/ppermute | solution.py:377
  48.0 0.7 %join.1 = f32[32,2048]{1,0:T(8,128)} custom-call(bf16[32,512]{1,0:T(8,128)(2,1)S(1)} %get-tuple-element.57.p0, bf16[32,512]{1,0:T(8,128)(2,1)S(1)} %collective-permute-done.12.p1, bf16[32,512]{1,0:T(8,128)(2,1)S(1)} %collective-permute-done.13.p2, bf16[32,512]{1,0:T(8,128)(2,1)S(1)} %collective-permute-done.14.p3), custom_call_target="tpu_custom_call" | custom-call | flops 1000000000 | tf_op jit(solution)/shard_map/join/pallas_call | solution.py:346
  (13 shorter events, 0.0 us)
Async XLA Ops:
  2.0 8.6 %collective-permute-start = (bf16[400,256]{1,0:T(8,128)(2,1)}, bf16[400,256]{1,0:T(8,128)(2,1)S(1)}, u32[]{:S(2)}, u32[]{:S(2)}) collective-permute-start(bf16[400,256]{1,0:T(8,128)(2,1)} %get-tuple-element.34), channel_id=1, source_target_pairs={{0,1},{1,0},{2,3},{3,2},{4,5},{5,4},{6,7},{7,6},{8,9},{9,8},{10,11... | collective-permute-start | bytes 614408 | tf_op jit(solution)/shard_map/ppermute | solution.py:400
  2.5 8.0 %collective-permute-start.2 = (bf16[32,512]{1,0:T(8,128)(2,1)}, bf16[32,512]{1,0:T(8,128)(2,1)S(1)}, u32[]{:S(2)}, u32[]{:S(2)}) collective-permute-start(bf16[32,512]{1,0:T(8,128)(2,1)} %get-tuple-element.36), channel_id=1, source_target_pairs={{0,3},{1,2},{2,1},{3,0},{4,7},{5,6},{6,5},{7,4},{8,11},{9,10},{10,... | collective-permute-start | bytes 98312 | tf_op jit(solution)/shard_map/ppermute | solution.py:398
  5.2 5.4 %collective-permute-start.1 = (bf16[32,512]{1,0:T(8,128)(2,1)}, bf16[32,512]{1,0:T(8,128)(2,1)S(1)}, u32[]{:S(2)}, u32[]{:S(2)}) collective-permute-start(bf16[32,512]{1,0:T(8,128)(2,1)} %get-tuple-element.35), channel_id=1, source_target_pairs={{0,2},{1,3},{2,0},{3,1},{4,6},{5,7},{6,4},{7,5},{8,10},{9,11},{10,... | collective-permute-start | bytes 98312 | tf_op jit(solution)/shard_map/ppermute | solution.py:399
  5.2 5.4 %copy-start.8 = (bf16[32,512]{1,0:T(8,128)(2,1)S(1)}, bf16[32,512]{1,0:T(8,128)(2,1)}, u32[]{:S(2)}) copy-start(bf16[32,512]{1,0:T(8,128)(2,1)} %get-tuple-element.33.p0) | copy-start | bytes 98308
  5.2 10.2 %collective-permute-start.3 = (bf16[336,256]{1,0:T(8,128)(2,1)}, bf16[336,256]{1,0:T(8,128)(2,1)S(1)}, u32[]{:S(2)}, u32[]{:S(2)}) collective-permute-start(bf16[336,256]{1,0:T(8,128)(2,1)} %get-tuple-element.39), channel_id=1, source_target_pairs={{0,31},{1,2},{2,1},{3,4},{4,3},{5,6},{6,5},{7,8},{8,7},{9,10},{10,... | collective-permute-start | bytes 516104 | tf_op jit(solution)/shard_map/ppermute | solution.py:401
  10.6 2.6 %copy-start = (bf16[1280,256]{1,0:T(8,128)(2,1)S(1)}, bf16[1280,256]{1,0:T(8,128)(2,1)}, u32[]{:S(2)}) copy-start(bf16[1280,256]{1,0:T(8,128)(2,1)} %feat.3) | copy-start | bytes 1966084
  10.6 2.5 %copy-start.1 = (bf16[256,512]{1,0:T(8,128)(2,1)S(1)}, bf16[256,512]{1,0:T(8,128)(2,1)}, u32[]{:S(2)}) copy-start(bf16[256,512]{1,0:T(8,128)(2,1)} %w_in.1) | copy-start | bytes 786436
  10.6 2.5 %copy-start.2 = (bf16[256,256]{1,0:T(8,128)(2,1)S(1)}, bf16[256,256]{1,0:T(8,128)(2,1)}, u32[]{:S(2)}) copy-start(bf16[256,256]{1,0:T(8,128)(2,1)} %w_out.1) | copy-start | bytes 393220
  10.6 2.5 %copy-start.3 = (s32[1280]{0:T(1024)S(1)}, s32[1280]{0:T(1024)}, u32[]{:S(2)}) copy-start(s32[1280]{0:T(1024)} %param.10) | copy-start | bytes 15364
  10.7 2.5 %copy-start.4 = (s32[1280]{0:T(1024)S(1)}, s32[1280]{0:T(1024)}, u32[]{:S(2)}) copy-start(s32[1280]{0:T(1024)} %param.11) | copy-start | bytes 15364
  10.7 2.5 %copy-start.5 = (s32[1280]{0:T(1024)S(1)}, s32[1280]{0:T(1024)}, u32[]{:S(2)}) copy-start(s32[1280]{0:T(1024)} %param.12) | copy-start | bytes 15364
  10.9 2.3 %copy-start.6 = (bf16[3,512]{1,0:T(4,128)(2,1)S(1)}, bf16[3,512]{1,0:T(4,128)(2,1)}, u32[]{:S(2)}) copy-start(bf16[3,512]{1,0:T(4,128)(2,1)} %cell_bias.1) | copy-start | bytes 9220
  10.9 7.7 %collective-permute-start.4 = (bf16[384,128]{1,0:T(8,128)(2,1)S(1)}, bf16[384,128]{1,0:T(8,128)(2,1)S(1)}, u32[]{:S(2)}, u32[]{:S(2)}) collective-permute-start(bf16[384,128]{1,0:T(8,128)(2,1)S(1)} %get-tuple-element.44), channel_id=1, source_target_pairs={{0,31},{1,2},{2,1},{3,4},{4,3},{5,6},{6,5},{7,8},{8,7},{9,10},{10,... | collective-permute-start | bytes 294920 | tf_op jit(solution)/shard_map/ppermute | solution.py:371
  13.2 5.4 %collective-permute-start.5 = (bf16[384,128]{1,0:T(8,128)(2,1)S(1)}, bf16[384,128]{1,0:T(8,128)(2,1)S(1)}, u32[]{:S(2)}, u32[]{:S(2)}) collective-permute-start(bf16[384,128]{1,0:T(8,128)(2,1)S(1)} %get-tuple-element.45), channel_id=1, source_target_pairs={{0,1},{1,0},{2,3},{3,2},{4,5},{5,4},{6,7},{7,6},{8,9},{9,8},{10,11... | collective-permute-start | bytes 294920 | tf_op jit(solution)/shard_map/ppermute | solution.py:372
  19.2 7.8 %collective-permute-start.6 = (bf16[384,128]{1,0:T(8,128)(2,1)S(1)}, bf16[384,128]{1,0:T(8,128)(2,1)S(1)}, u32[]{:S(2)}, u32[]{:S(2)}) collective-permute-start(bf16[384,128]{1,0:T(8,128)(2,1)S(1)} %get-tuple-element.47), channel_id=1, source_target_pairs={{0,31},{1,2},{2,1},{3,4},{4,3},{5,6},{6,5},{7,8},{8,7},{9,10},{10,... | collective-permute-start | bytes 294920 | tf_op jit(solution)/shard_map/ppermute | solution.py:371
  21.8 5.2 %collective-permute-start.7 = (bf16[384,128]{1,0:T(8,128)(2,1)S(1)}, bf16[384,128]{1,0:T(8,128)(2,1)S(1)}, u32[]{:S(2)}, u32[]{:S(2)}) collective-permute-start(bf16[384,128]{1,0:T(8,128)(2,1)S(1)} %get-tuple-element.48), channel_id=1, source_target_pairs={{0,1},{1,0},{2,3},{3,2},{4,5},{5,4},{6,7},{7,6},{8,9},{9,8},{10,11... | collective-permute-start | bytes 294920 | tf_op jit(solution)/shard_map/ppermute | solution.py:372
  27.5 7.7 %collective-permute-start.8 = (bf16[384,128]{1,0:T(8,128)(2,1)S(1)}, bf16[384,128]{1,0:T(8,128)(2,1)S(1)}, u32[]{:S(2)}, u32[]{:S(2)}) collective-permute-start(bf16[384,128]{1,0:T(8,128)(2,1)S(1)} %get-tuple-element.50), channel_id=1, source_target_pairs={{0,31},{1,2},{2,1},{3,4},{4,3},{5,6},{6,5},{7,8},{8,7},{9,10},{10,... | collective-permute-start | bytes 294920 | tf_op jit(solution)/shard_map/ppermute | solution.py:371
  30.1 5.1 %collective-permute-start.9 = (bf16[384,128]{1,0:T(8,128)(2,1)S(1)}, bf16[384,128]{1,0:T(8,128)(2,1)S(1)}, u32[]{:S(2)}, u32[]{:S(2)}) collective-permute-start(bf16[384,128]{1,0:T(8,128)(2,1)S(1)} %get-tuple-element.51), channel_id=1, source_target_pairs={{0,1},{1,0},{2,3},{3,2},{4,5},{5,4},{6,7},{7,6},{8,9},{9,8},{10,11... | collective-permute-start | bytes 294920 | tf_op jit(solution)/shard_map/ppermute | solution.py:372
  35.6 7.7 %collective-permute-start.10 = (bf16[384,128]{1,0:T(8,128)(2,1)S(1)}, bf16[384,128]{1,0:T(8,128)(2,1)S(1)}, u32[]{:S(2)}, u32[]{:S(2)}) collective-permute-start(bf16[384,128]{1,0:T(8,128)(2,1)S(1)} %get-tuple-element.55), channel_id=1, source_target_pairs={{0,31},{1,2},{2,1},{3,4},{4,3},{5,6},{6,5},{7,8},{8,7},{9,10},{10,... | collective-permute-start | bytes 294920 | tf_op jit(solution)/shard_map/ppermute | solution.py:371
  38.2 0.7 %copy-start.7 = (f32[5]{0:T(128)S(1)}, f32[5]{0:T(128)}, u32[]{:S(2)}) copy-start(f32[5]{0:T(128)} %coef.1) | copy-start | bytes 64
  38.2 5.1 %collective-permute-start.11 = (bf16[384,128]{1,0:T(8,128)(2,1)S(1)}, bf16[384,128]{1,0:T(8,128)(2,1)S(1)}, u32[]{:S(2)}, u32[]{:S(2)}) collective-permute-start(bf16[384,128]{1,0:T(8,128)(2,1)S(1)} %get-tuple-element.56), channel_id=1, source_target_pairs={{0,1},{1,0},{2,3},{3,2},{4,5},{5,4},{6,7},{7,6},{8,9},{9,8},{10,11... | collective-permute-start | bytes 294920 | tf_op jit(solution)/shard_map/ppermute | solution.py:372
  43.8 1.9 %collective-permute-start.12 = (bf16[32,512]{1,0:T(8,128)(2,1)S(1)}, bf16[32,512]{1,0:T(8,128)(2,1)S(1)}, u32[]{:S(2)}, u32[]{:S(2)}) collective-permute-start(bf16[32,512]{1,0:T(8,128)(2,1)S(1)} %get-tuple-element.58), channel_id=1, source_target_pairs={{0,1},{1,0},{2,3},{3,2},{4,5},{5,4},{6,7},{7,6},{8,9},{9,8},{10,11... | collective-permute-start | bytes 98312 | tf_op jit(solution)/shard_map/ppermute | solution.py:377
  43.9 4.2 %collective-permute-start.13 = (bf16[32,512]{1,0:T(8,128)(2,1)S(1)}, bf16[32,512]{1,0:T(8,128)(2,1)S(1)}, u32[]{:S(2)}, u32[]{:S(2)}) collective-permute-start(bf16[32,512]{1,0:T(8,128)(2,1)S(1)} %get-tuple-element.59), channel_id=1, source_target_pairs={{0,2},{1,3},{2,0},{3,1},{4,6},{5,7},{6,4},{7,5},{8,10},{9,11},{10,... | collective-permute-start | bytes 98312 | tf_op jit(solution)/shard_map/ppermute | solution.py:377
  44.0 4.1 %collective-permute-start.14 = (bf16[32,512]{1,0:T(8,128)(2,1)S(1)}, bf16[32,512]{1,0:T(8,128)(2,1)S(1)}, u32[]{:S(2)}, u32[]{:S(2)}) collective-permute-start(bf16[32,512]{1,0:T(8,128)(2,1)S(1)} %get-tuple-element.60), channel_id=1, source_target_pairs={{0,3},{1,2},{2,1},{3,0},{4,7},{5,6},{6,5},{7,4},{8,11},{9,10},{10,... | collective-permute-start | bytes 98312 | tf_op jit(solution)/shard_map/ppermute | solution.py:377

commit v11 on v10

--- a/solution.py
+++ b/solution.py
@@ -143,8 +143,8 @@
     span = atom.shape[1]
     column = (iota((WIN_ATOMS, span), 0).astype(F32) == target).astype(BF)
     onehot = [
-        jnp.broadcast_to((atom == float(s)).astype(F32), (WIN_ATOMS, span)).astype(BF) * column
-        for s in range(first, first + GROUP)
+        jnp.broadcast_to((atom == as_float(first + s)).astype(F32), (WIN_ATOMS, span)).astype(BF) * column
+        for s in range(GROUP)
     ]
     return nt_dot(blocks, jnp.concatenate(onehot, axis=0))
 
@@ -155,6 +155,8 @@
     for sp in range(GROUP // 2):
         s = first + 2 * sp
         pair, at_row = s // PAIR_ATOMS, s % PAIR_ATOMS * ORB
+        if not isinstance(s, int):
+            at_row = pl.multiple_of(at_row, 2 * ORB)
         for m in range(ORB // 4):
             x = [
                 dense[(4 * m + i) * ORB : (4 * m + i + 1) * ORB, sp * 128 : sp * 128 + 128].astype(BF)
@@ -169,7 +171,7 @@
                     jnp.where(even, u[0], pltpu.roll(u[1], ATOM_Q, 1)),
                     jnp.where(even, pltpu.roll(u[0], 128 - ATOM_Q, 1), u[1]),
                 )
-                rows = slice(at_row + half * ORB, at_row + (half + 1) * ORB)
+                rows = pl.ds(at_row + half * ORB, ORB)
                 for n, value in enumerate(both):
                     lo = n * HALF + m * 128
                     if base is not None:
@@ -184,7 +186,38 @@
     return jnp.where((target >= 0.0) & (target < float(ATOM_Q)), target, outside)
 
 
-def own_kernel(feat, src, dst, cell, cell_bias, w_in, w_out, _, band, w_in_t, bias_t, w_out_t, blk, bias8, rows):
+def as_float(x):
+    return float(x) if isinstance(x, int) else x.astype(F32)
+
+
+def place(message, is_left, rows):
+    nfeat = rows.shape[1]
+    gap = rows.shape[0] - SPILL
+    rows[0:gap, :] = jnp.zeros((gap, nfeat), BF)
+    rows[SPILL : SPILL + gap, :] = jnp.zeros((gap, nfeat), BF)
+    rows[pl.ds(pl.multiple_of(jnp.where(is_left, gap, 0), 64), SPILL), :] = message[0:SPILL, :]
+    block = message[SPILL : SPILL + ID_ROWS, 0:128].astype(F32)
+    return [row_of(block[3 * k : 3 * k + 3]) for k in range(3)]
+
+
+def add_message(band, blocks, atom, column, is_left):
+    mine = (atom >= 0.0) & (atom < float(ATOM_Q))
+    highest = jnp.max(jnp.where(mine, atom, -1.0)).astype(jnp.int32)
+    lowest = jnp.min(jnp.where(mine, atom, float(ATOM_Q))).astype(jnp.int32)
+    for k in range(NEAR):
+        first = jnp.where(is_left, k * GROUP, ATOM_Q - (NEAR - k) * GROUP)
+        put_dense(band, dense_of(blocks[...], atom, column, first), first, band)
+    for k in range(ATOM_Q // GROUP - NEAR):
+        first = jnp.where(is_left, (NEAR + k) * GROUP, k * GROUP)
+
+        @pl.when(jnp.where(is_left, highest >= first, lowest < first + GROUP))
+        def _(first=first):
+            put_dense(band, dense_of(blocks[...], atom, column, first), first, band)
+
+
+def own_kernel(
+    feat, src, dst, cell, near, cell_bias, w_in, w_out, _, band, w_in_t, bias_t, w_out_t, blk, blk2, bias8, rows, more
+):
     nfeat, width = w_in.shape
     nblk = w_out.shape[1]
     eye = (iota((width, width), 0) == iota((width, width), 1)).astype(BF)
@@ -200,52 +233,24 @@
     atom = row_of(ids[0])
     rows[0:1, :] = atom
     rows[1:2, :] = column_of(atom, row_of(ids[1]))
+    is_left = device_side() == 1
+    other = place(near, is_left, more)
     blk[...] = pair_blocks(feat[...], row_of(ids[2]), w_in_t, bias_t, w_out_t)
+    blk2[...] = pair_blocks(more[...], other[2], w_in_t, bias_t, w_out_t)
     for first in range(0, ATOM_Q, GROUP):
         start = jnp.sum((ids[0] < float(first)).astype(F32)).astype(jnp.int32)
         at = pl.multiple_of(jnp.minimum(start // 128 * 128, own - GROUP_SPAN), 128)
         span = pl.ds(at, GROUP_SPAN)
         put_dense(band, dense_of(blk[:, span], rows[0:1, span], rows[1:2, span], first), first)
-
-
-def spill_kernel(own_band, blue, red, w_in_t, bias_t, w_out_t, band, blk, spill):
-    even = device_side() == 0
-    nfeat = spill.shape[1]
-    rows = spill.shape[0] // 2
-    near = red[0 : SPILL + ID_ROWS, :]
-    left, right = [jnp.where(even, x, y) for x, y in ((blue[...], near), (near, blue[...]))]
-    spill[0:64, :] = jnp.zeros((64, nfeat), BF)
-    spill[64 : rows + SPILL, :] = jnp.concatenate([left[0:SPILL], right[0:SPILL]], axis=0)
-    spill[rows + SPILL :, :] = jnp.zeros((64, nfeat), BF)
-    ids = []
-    for msg in (left, right):
-        block = msg[SPILL : SPILL + ID_ROWS, 0:128].astype(F32)
-        ids.append([row_of(block[3 * k : 3 * k + 3]) for k in range(3)])
-    atoms = [x[0] for x in ids]
-    cols = [column_of(x[0], x[1]) for x in ids]
-    mine = [(a >= 0.0) & (a < float(ATOM_Q)) for a in atoms]
-    highest = jnp.max(jnp.where(mine[0], atoms[0], -1.0)).astype(jnp.int32)
-    lowest = jnp.min(jnp.where(mine[1], atoms[1], float(ATOM_Q))).astype(jnp.int32)
-    cells = jnp.concatenate([x[2] for x in ids], axis=1)
-    blk[...] = pair_blocks(spill[...], cells, w_in_t, bias_t, w_out_t)
-    spans = [slice(0, rows), slice(rows, 2 * rows)]
-    ngroup = ATOM_Q // GROUP
-    for g in range(ngroup):
-        first = g * GROUP
-        sides = [m for m in range(2) if (g < NEAR, g >= ngroup - NEAR)[m]]
-        if sides:
-            (m,) = sides
-            put_dense(band, dense_of(blk[:, spans[m]], atoms[m], cols[m], first), first, own_band)
-        else:
-            pair, at = first // PAIR_ATOMS, first % PAIR_ATOMS * ORB
-            band[pair, at : at + GROUP * ORB, :] = own_band[pair, at : at + GROUP * ORB, :]
-    for m, far in ((0, range(NEAR, ngroup)), (1, range(ngroup - NEAR))):
-        for g in far:
-            first = g * GROUP
-
-            @pl.when(highest >= first if m == 0 else lowest < first + GROUP)
-            def _(m=m, first=first):
-                put_dense(band, dense_of(blk[:, spans[m]], atoms[m], cols[m], first), first, band)
+    add_message(band, blk2, other[0], column_of(other[0], other[1]), is_left)
+
+
+def spill_kernel(own_band, blue, w_in_t, bias_t, w_out_t, band, blk, more):
+    is_left = device_side() == 0
+    ids = place(blue, is_left, more)
+    blk[...] = pair_blocks(more[...], ids[2], w_in_t, bias_t, w_out_t)
+    band[...] = own_band[...]
+    add_message(band, blk, ids[0], column_of(ids[0], ids[1]), is_left)
 
 
 def own_part(band, field):
@@ -284,11 +289,10 @@
     return [slice(k * height, (k + 1) * height) for k in range(band.shape[0])]
 
 
-def first_kernel(band, t0, blue, red, t1, to_blue, to_red, wide):
-    inner, outer = own_part(band, t0), halo_part(band, blue, red, wide)
+def start_kernel(band, now, part):
+    inner = own_part(band, now)
     for k, span in enumerate(spans_of(band)):
-        t1[span, :] = inner[k] + outer[k]
-    put_sends(t1, to_blue, to_red)
+        part[span, :] = inner[k]
 
 
 def inner_kernel(band, before, now, part):
@@ -297,10 +301,10 @@
         part[span, :] = 2.0 * inner[k] - before[span, :]
 
 
-def outer_kernel(band, part, blue, red, after, to_blue, to_red, wide):
+def outer_kernel(scale, band, part, blue, red, after, to_blue, to_red, wide):
     outer = halo_part(band, blue, red, wide)
     for k, span in enumerate(spans_of(band)):
-        after[span, :] = 2.0 * outer[k] + part[span, :]
+        after[span, :] = scale * outer[k] + part[span, :]
     put_sends(after, to_blue, to_red)
 
 
@@ -407,43 +411,57 @@
     )
     blue, red = swap(to_blue, to_red)
 
+    wide_spill = SPILL + 64
     band_shape = shape((ATOM_Q // PAIR_ATOMS, PAIR_ATOMS * ORB, WIN_ATOMS * ORB), BF)
     width = w_in.shape[1]
     band, *weights = call(
         own_kernel,
         "own",
         (band_shape, shape((width, nfeat), BF), shape((width, 8), BF), shape((ORB * ORB, HID), BF)),
-        [pltpu.VMEM((ORB * ORB, nown), BF), pltpu.VMEM((8, width), F32), pltpu.VMEM((8, nown), F32)],
+        [
+            pltpu.VMEM((ORB * ORB, nown), BF),
+            pltpu.VMEM((ORB * ORB, wide_spill), BF),
+            pltpu.VMEM((8, width), F32),
+            pltpu.VMEM((8, nown), F32),
+            pltpu.VMEM((wide_spill, nfeat), BF),
+        ],
         features,
         *edges,
+        near,
         cell_bias,
         w_in,
         w_out,
         token,
         micros=4,
     )
-    spill_len = 2 * (SPILL + 64)
     (band,) = call(
         spill_kernel,
         "spill",
         (band_shape,),
-        [pltpu.VMEM((ORB * ORB, spill_len), BF), pltpu.VMEM((spill_len, nfeat), BF)],
+        [pltpu.VMEM((ORB * ORB, wide_spill), BF), pltpu.VMEM((wide_spill, nfeat), BF)],
         band,
         blue_msg,
-        near,
         *weights,
         alias={0: 0},
         micros=0,
     )
 
     wide = pltpu.VMEM((2 * HALO, VEC), F32)
-    t1, to_blue, to_red = call(first_kernel, "first", (full, part, part), [wide], band, t0, blue, red)
-    fields = [t0, t1]
-    for _ in range(2, STEPS):
-        blue, red = swap(to_blue, to_red)
-        (inner,) = call(inner_kernel, "inner", (full,), [], band, fields[-2], fields[-1])
+    fields = [t0]
+    for step in range(1, STEPS):
+        if step > 1:
+            blue, red = swap(to_blue, to_red)
+        inner, name = (start_kernel, "start") if step == 1 else (inner_kernel, "inner")
+        (inner,) = call(inner, name, (full,), [], band, *fields[-2:])
         following, to_blue, to_red = call(
-            outer_kernel, "outer", (full, part, part), [wide], band, inner, blue, red
+            functools.partial(outer_kernel, 1.0 if step == 1 else 2.0),
+            "outer",
+            (full, part, part),
+            [wide],
+            band,
+            inner,
+            blue,
+            red,
         )
         fields.append(following)
     blue, red = swap(to_blue, to_red)

time: 49 us -> 48.8 us (level)
  waiting for transfers between devices: 16.9 us -> 14.1 us
  starting transfers between devices: 20.5 us -> 22.1 us
  Pallas kernels: 10.5 us -> 11.6 us
    ppermute x4, waiting for transfers between devices: 14.5 us -> 11.8 us  [swap(): lax.ppermute(first, axes, blue_pairs)]
    ppermute x4, starting transfers between devices: 10 us -> 11.6 us  [swap(): lax.ppermute(first, axes, blue_pairs)]
    pallas_call x13 -> x14, Pallas kernels: 10.5 us -> 11.6 us  [call(): pl.pallas_call(kernel, name=name, out_shape=outs, in_specs=spaces, out_sp...]
  transfers between devices with their start and end apart: 15 -> 15, of which waited for: 5 -> 5; matrix products, arithmetic and copies ran while one was open for 0% -> 0% of each run, Pallas kernels for 12% -> 14%
where the time goes in v11:
time: 48.8 us; the launch traced here: 48.6 us
  starting transfers between devices  22.1 us (45%)
  waiting for transfers between devices  14.1 us (29%)
  Pallas kernels  11.6 us (24%)
  local copies, waits for them, and re-layouts  0.7 us (1%)
    ppermute x4, waiting for transfers between devices, swap(): lax.ppermute(first, axes, blue_pairs)  11.8 us
    ppermute x4, starting transfers between devices, swap(): lax.ppermute(first, axes, blue_pairs)  11.6 us
    pallas_call x14, Pallas kernels, call(): pl.pallas_call(kernel, name=name, out_shape=outs, in_specs=spaces, out_sp...  11.6 us
    ppermute x1, starting transfers between devices, per_device(): blue_msg = lax.ppermute(blue_msg, axes, blue_pairs)  5.37 us
    ppermute x1, starting transfers between devices, per_device(): across = lax.ppermute(across, 'edges', [(i, i ^ 3) for i in range(nedge)])  2.61 us
    ppermute x3, waiting for transfers between devices, exchange(): lax.ppermute(pieces[k], 'edges', [(i, i ^ k) for i in range(nedge)])  2.3 us
    ppermute x3, starting transfers between devices, exchange(): lax.ppermute(pieces[k], 'edges', [(i, i ^ k) for i in range(nedge)])  1.93 us
  transfers between devices with their start and end apart: 15, of which 5 were waited for; matrix products, arithmetic and copies ran while one was open for 0% of the time, Pallas kernels for 14%

profile of v11, /device:TPU:0, one launch (start us, length us, event | category | flops | bytes accessed | tf_op | source)
XLA Modules:
  0.0 48.6 jit_solution(15904122581153272481)
XLA Ops:
  0.0 2.0 %prep.1 = (bf16[32,512]{1,0:T(8,128)(2,1)}, bf16[32,512]{1,0:T(8,128)(2,1)}, bf16[32,512]{1,0:T(8,128)(2,1)}, bf16[336,256]{1,0:T(8,128)(2,1)}, bf16[400,256]{1,0:T(8,128)(2,1)}) custom-call(f32[32,2048]{1,0:T(8,128)} %vec_hbm.1, bf16[1280,256]{1,0:T(8,128)(2,1)} %feat.3, s32[10,128]{1,0:T(8,128)} %bitcast.3, s32[10,128]{1,0:T(8,128)} %bitcast.5, ...), custom_call_target="tpu_custom_call" | custom-call | flops 1000000000 | tf_op jit(solution)/shard_map/prep/pallas_call | solution.py:350
  2.0 0.5 %collective-permute-start = (bf16[400,256]{1,0:T(8,128)(2,1)}, bf16[400,256]{1,0:T(8,128)(2,1)S(1)}, u32[]{:S(2)}, u32[]{:S(2)}) collective-permute-start(bf16[400,256]{1,0:T(8,128)(2,1)} %get-tuple-element.33), channel_id=1, source_target_pairs={{0,1},{1,0},{2,3},{3,2},{4,5},{5,4},{6,7},{7,6},{8,9},{9,8},{10,11... | collective-permute-start | bytes 614408 | tf_op jit(solution)/shard_map/ppermute | solution.py:404
  2.5 2.6 %collective-permute-start.2 = (bf16[32,512]{1,0:T(8,128)(2,1)}, bf16[32,512]{1,0:T(8,128)(2,1)S(1)}, u32[]{:S(2)}, u32[]{:S(2)}) collective-permute-start(bf16[32,512]{1,0:T(8,128)(2,1)} %get-tuple-element.36), channel_id=1, source_target_pairs={{0,3},{1,2},{2,1},{3,0},{4,7},{5,6},{6,5},{7,4},{8,11},{9,10},{10,... | collective-permute-start | bytes 98312 | tf_op jit(solution)/shard_map/ppermute | solution.py:402
  5.2 0.0 collective-permute-start.1
  5.2 5.4 %collective-permute-start.3 = (bf16[336,256]{1,0:T(8,128)(2,1)}, bf16[336,256]{1,0:T(8,128)(2,1)S(1)}, u32[]{:S(2)}, u32[]{:S(2)}) collective-permute-start(bf16[336,256]{1,0:T(8,128)(2,1)} %get-tuple-element.39), channel_id=1, source_target_pairs={{0,31},{1,2},{2,1},{3,4},{4,3},{5,6},{6,5},{7,8},{8,7},{9,10},{10,... | collective-permute-start | bytes 516104 | tf_op jit(solution)/shard_map/ppermute | solution.py:405
  10.6 0.0 collective-permute-done.2.x
  10.6 0.0 collective-permute-done.1.p2
  10.6 0.0 collective-permute-done.near
  10.6 0.0 copy-start
  10.6 0.0 copy-start.1
  10.6 0.0 copy-start.2
  10.6 0.0 copy-start.3
  10.7 0.0 copy-start.4
  10.7 0.0 copy-start.5
  10.7 0.2 field.1
  10.9 0.0 copy-start.6
  10.9 2.3 %collective-permute-start.4 = (bf16[384,128]{1,0:T(8,128)(2,1)S(1)}, bf16[384,128]{1,0:T(8,128)(2,1)S(1)}, u32[]{:S(2)}, u32[]{:S(2)}) collective-permute-start(bf16[384,128]{1,0:T(8,128)(2,1)S(1)} %get-tuple-element.44), channel_id=1, source_target_pairs={{0,31},{1,2},{2,1},{3,4},{4,3},{5,6},{6,5},{7,8},{8,7},{9,10},{10,... | collective-permute-start | bytes 294920 | tf_op jit(solution)/shard_map/ppermute | solution.py:375
  13.2 0.0 collective-permute-start.5
  13.2 3.2 %own.1 = (bf16[2,256,1024]{2,1,0:T(8,128)(2,1)S(1)}, bf16[512,256]{1,0:T(8,128)(2,1)S(1)}, bf16[512,8]{1,0:T(8,128)(2,1)S(1)}, bf16[256,256]{1,0:T(8,128)(2,1)S(1)}) custom-call(bf16[1280,256]{1,0:T(8,128)(2,1)S(1)} %copy-done, s32[10,128]{1,0:T(8,128)S(1)} %bitcast.4, s32[10,128]{1,0:T(8,128)S(1)} %bitcast.6, s32[10,128]{1,0:T(8,128)S(1)} %bitcast.8, ...), custom_call_target="tpu_custom_call" | custom-call | flops 4000000000 | tf_op jit(solution)/shard_map/own/pallas_call | solution.py:350
  16.4 0.0 collective-permute-done.3.blue
  16.4 1.7 %spill.1.band = bf16[2,256,1024]{2,1,0:T(8,128)(2,1)S(1)} custom-call(bf16[2,256,1024]{2,1,0:T(8,128)(2,1)S(1)} %get-tuple-element.38.own_band, bf16[336,256]{1,0:T(8,128)(2,1)S(1)} %collective-permute-done.3.blue, bf16[512,256]{1,0:T(8,128)(2,1)S(1)} %get-tuple-element.40.w_in_t, ...), custom_call_target="tpu_custom_call", output_to_operand_aliasing={{}: (0, {})} | custom-call | tf_op jit(solution)/shard_map/spill/pallas_call | solution.py:350
  18.1 0.3 start.1.part
  18.5 0.1 collective-permute-done.4.blue
  18.6 0.0 collective-permute-done.5.red
  18.6 0.4 outer.3
  19.0 3.1 %collective-permute-start.6 = (bf16[384,128]{1,0:T(8,128)(2,1)S(1)}, bf16[384,128]{1,0:T(8,128)(2,1)S(1)}, u32[]{:S(2)}, u32[]{:S(2)}) collective-permute-start(bf16[384,128]{1,0:T(8,128)(2,1)S(1)} %get-tuple-element.47), channel_id=1, source_target_pairs={{0,31},{1,2},{2,1},{3,4},{4,3},{5,6},{6,5},{7,8},{8,7},{9,10},{10,... | collective-permute-start | bytes 294920 | tf_op jit(solution)/shard_map/ppermute | solution.py:375
  22.1 0.3 inner.2.part
  22.5 4.3 %collective-permute-done.6.blue = bf16[384,128]{1,0:T(8,128)(2,1)S(1)} collective-permute-done((bf16[384,128]{1,0:T(8,128)(2,1)S(1)}, bf16[384,128]{1,0:T(8,128)(2,1)S(1)}, u32[]{:S(2)}, u32[]{:S(2)}) %collective-permute-start.6) | collective-permute-done | bytes 98336 | tf_op jit(solution)/shard_map/ppermute | solution.py:375
  26.8 0.4 outer.4
  27.2 3.1 %collective-permute-start.8 = (bf16[384,128]{1,0:T(8,128)(2,1)S(1)}, bf16[384,128]{1,0:T(8,128)(2,1)S(1)}, u32[]{:S(2)}, u32[]{:S(2)}) collective-permute-start(bf16[384,128]{1,0:T(8,128)(2,1)S(1)} %get-tuple-element.50), channel_id=1, source_target_pairs={{0,31},{1,2},{2,1},{3,4},{4,3},{5,6},{6,5},{7,8},{8,7},{9,10},{10,... | collective-permute-start | bytes 294920 | tf_op jit(solution)/shard_map/ppermute | solution.py:375
  30.3 0.0 collective-permute-start.9
  30.3 0.3 inner.3.part
  30.7 4.2 %collective-permute-done.8.blue = bf16[384,128]{1,0:T(8,128)(2,1)S(1)} collective-permute-done((bf16[384,128]{1,0:T(8,128)(2,1)S(1)}, bf16[384,128]{1,0:T(8,128)(2,1)S(1)}, u32[]{:S(2)}, u32[]{:S(2)}) %collective-permute-start.8) | collective-permute-done | bytes 98336 | tf_op jit(solution)/shard_map/ppermute | solution.py:375
  34.9 0.0 collective-permute-done.9.red
  34.9 0.4 outer.5
  35.4 3.1 %collective-permute-start.10 = (bf16[384,128]{1,0:T(8,128)(2,1)S(1)}, bf16[384,128]{1,0:T(8,128)(2,1)S(1)}, u32[]{:S(2)}, u32[]{:S(2)}) collective-permute-start(bf16[384,128]{1,0:T(8,128)(2,1)S(1)} %get-tuple-element.55), channel_id=1, source_target_pairs={{0,31},{1,2},{2,1},{3,4},{4,3},{5,6},{6,5},{7,8},{8,7},{9,10},{10,... | collective-permute-start | bytes 294920 | tf_op jit(solution)/shard_map/ppermute | solution.py:375
  38.5 0.0 collective-permute-start.11
  38.5 0.7 %copy-done.7 = f32[5]{0:T(128)S(1)} copy-done((f32[5]{0:T(128)S(1)}, f32[5]{0:T(128)}, u32[]{:S(2)}) %copy-start.7) | copy-done | bytes 44
  39.1 0.9 %mix.1 = (f32[128,512]{1,0:T(8,128)S(1)}, f32[8,128]{1,0:T(8,128)S(1)}) custom-call(f32[5]{0:T(128)S(1)} %copy-done.7, bf16[2,256,1024]{2,1,0:T(8,128)(2,1)S(1)} %spill.1.band, f32[512,128]{1,0:T(8,128)S(1)} %get-tuple-element.43.now.before.t0, f32[512,128]{1,0:T(8,128)S(1)} %get-tuple-element.46.now.before.t1, f32[512,128]{1,0:T(8,128)S(1)} %get-tuple-element.49.now.t2, ...), custom_call_target="tpu_custom_call" | custom-call | flops 1000000000 | tf_op jit(solution)/shard_map/mix/pallas_call | solution.py:350
  40.1 3.1 %collective-permute-done.10.blue = bf16[384,128]{1,0:T(8,128)(2,1)S(1)} collective-permute-done((bf16[384,128]{1,0:T(8,128)(2,1)S(1)}, bf16[384,128]{1,0:T(8,128)(2,1)S(1)}, u32[]{:S(2)}, u32[]{:S(2)}) %collective-permute-start.10) | collective-permute-done | bytes 98336 | tf_op jit(solution)/shard_map/ppermute | solution.py:375
  43.2 0.0 collective-permute-done.11.red
  43.2 0.5 last.1
  43.7 0.1 collective-permute-start.12
  43.7 0.1 collective-permute-start.13
  43.8 1.8 %collective-permute-start.14 = (bf16[32,512]{1,0:T(8,128)(2,1)S(1)}, bf16[32,512]{1,0:T(8,128)(2,1)S(1)}, u32[]{:S(2)}, u32[]{:S(2)}) collective-permute-start(bf16[32,512]{1,0:T(8,128)(2,1)S(1)} %get-tuple-element.60), channel_id=1, source_target_pairs={{0,3},{1,2},{2,1},{3,0},{4,7},{5,6},{6,5},{7,4},{8,11},{9,10},{10,... | collective-permute-start | bytes 98312 | tf_op jit(solution)/shard_map/ppermute | solution.py:381
  45.6 2.3 %collective-permute-done.13.p2 = bf16[32,512]{1,0:T(8,128)(2,1)S(1)} collective-permute-done((bf16[32,512]{1,0:T(8,128)(2,1)S(1)}, bf16[32,512]{1,0:T(8,128)(2,1)S(1)}, u32[]{:S(2)}, u32[]{:S(2)}) %collective-permute-start.13) | collective-permute-done | bytes 32800 | tf_op jit(solution)/shard_map/ppermute | solution.py:381
  47.9 0.0 collective-permute-done.14.p3
  47.9 0.7 %join.1 = f32[32,2048]{1,0:T(8,128)} custom-call(bf16[32,512]{1,0:T(8,128)(2,1)S(1)} %get-tuple-element.57.p0, bf16[32,512]{1,0:T(8,128)(2,1)S(1)} %collective-permute-done.12.p1, bf16[32,512]{1,0:T(8,128)(2,1)S(1)} %collective-permute-done.13.p2, bf16[32,512]{1,0:T(8,128)(2,1)S(1)} %collective-permute-done.14.p3), custom_call_target="tpu_custom_call" | custom-call | flops 1000000000 | tf_op jit(solution)/shard_map/join/pallas_call | solution.py:350
  (14 shorter events, 0.0 us)
Async XLA Ops:
  2.0 8.6 %collective-permute-start = (bf16[400,256]{1,0:T(8,128)(2,1)}, bf16[400,256]{1,0:T(8,128)(2,1)S(1)}, u32[]{:S(2)}, u32[]{:S(2)}) collective-permute-start(bf16[400,256]{1,0:T(8,128)(2,1)} %get-tuple-element.33), channel_id=1, source_target_pairs={{0,1},{1,0},{2,3},{3,2},{4,5},{5,4},{6,7},{7,6},{8,9},{9,8},{10,11... | collective-permute-start | bytes 614408 | tf_op jit(solution)/shard_map/ppermute | solution.py:404
  2.5 8.0 %collective-permute-start.2 = (bf16[32,512]{1,0:T(8,128)(2,1)}, bf16[32,512]{1,0:T(8,128)(2,1)S(1)}, u32[]{:S(2)}, u32[]{:S(2)}) collective-permute-start(bf16[32,512]{1,0:T(8,128)(2,1)} %get-tuple-element.36), channel_id=1, source_target_pairs={{0,3},{1,2},{2,1},{3,0},{4,7},{5,6},{6,5},{7,4},{8,11},{9,10},{10,... | collective-permute-start | bytes 98312 | tf_op jit(solution)/shard_map/ppermute | solution.py:402
  5.2 5.4 %collective-permute-start.1 = (bf16[32,512]{1,0:T(8,128)(2,1)}, bf16[32,512]{1,0:T(8,128)(2,1)S(1)}, u32[]{:S(2)}, u32[]{:S(2)}) collective-permute-start(bf16[32,512]{1,0:T(8,128)(2,1)} %get-tuple-element.35), channel_id=1, source_target_pairs={{0,2},{1,3},{2,0},{3,1},{4,6},{5,7},{6,4},{7,5},{8,10},{9,11},{10,... | collective-permute-start | bytes 98312 | tf_op jit(solution)/shard_map/ppermute | solution.py:403
  5.2 5.4 %copy-start.8 = (bf16[32,512]{1,0:T(8,128)(2,1)S(1)}, bf16[32,512]{1,0:T(8,128)(2,1)}, u32[]{:S(2)}) copy-start(bf16[32,512]{1,0:T(8,128)(2,1)} %get-tuple-element.34.p0) | copy-start | bytes 98308
  5.2 11.2 %collective-permute-start.3 = (bf16[336,256]{1,0:T(8,128)(2,1)}, bf16[336,256]{1,0:T(8,128)(2,1)S(1)}, u32[]{:S(2)}, u32[]{:S(2)}) collective-permute-start(bf16[336,256]{1,0:T(8,128)(2,1)} %get-tuple-element.39), channel_id=1, source_target_pairs={{0,31},{1,2},{2,1},{3,4},{4,3},{5,6},{6,5},{7,8},{8,7},{9,10},{10,... | collective-permute-start | bytes 516104 | tf_op jit(solution)/shard_map/ppermute | solution.py:405
  10.6 2.6 %copy-start = (bf16[1280,256]{1,0:T(8,128)(2,1)S(1)}, bf16[1280,256]{1,0:T(8,128)(2,1)}, u32[]{:S(2)}) copy-start(bf16[1280,256]{1,0:T(8,128)(2,1)} %feat.3) | copy-start | bytes 1966084
  10.6 2.5 %copy-start.1 = (bf16[256,512]{1,0:T(8,128)(2,1)S(1)}, bf16[256,512]{1,0:T(8,128)(2,1)}, u32[]{:S(2)}) copy-start(bf16[256,512]{1,0:T(8,128)(2,1)} %w_in.1) | copy-start | bytes 786436
  10.6 2.5 %copy-start.2 = (bf16[256,256]{1,0:T(8,128)(2,1)S(1)}, bf16[256,256]{1,0:T(8,128)(2,1)}, u32[]{:S(2)}) copy-start(bf16[256,256]{1,0:T(8,128)(2,1)} %w_out.1) | copy-start | bytes 393220
  10.6 2.5 %copy-start.3 = (s32[1280]{0:T(1024)S(1)}, s32[1280]{0:T(1024)}, u32[]{:S(2)}) copy-start(s32[1280]{0:T(1024)} %param.10) | copy-start | bytes 15364
  10.7 2.5 %copy-start.4 = (s32[1280]{0:T(1024)S(1)}, s32[1280]{0:T(1024)}, u32[]{:S(2)}) copy-start(s32[1280]{0:T(1024)} %param.11) | copy-start | bytes 15364
  10.7 2.5 %copy-start.5 = (s32[1280]{0:T(1024)S(1)}, s32[1280]{0:T(1024)}, u32[]{:S(2)}) copy-start(s32[1280]{0:T(1024)} %param.12) | copy-start | bytes 15364
  10.9 2.3 %copy-start.6 = (bf16[3,512]{1,0:T(4,128)(2,1)S(1)}, bf16[3,512]{1,0:T(4,128)(2,1)}, u32[]{:S(2)}) copy-start(bf16[3,512]{1,0:T(4,128)(2,1)} %cell_bias.1) | copy-start | bytes 9220
  10.9 7.7 %collective-permute-start.4 = (bf16[384,128]{1,0:T(8,128)(2,1)S(1)}, bf16[384,128]{1,0:T(8,128)(2,1)S(1)}, u32[]{:S(2)}, u32[]{:S(2)}) collective-permute-start(bf16[384,128]{1,0:T(8,128)(2,1)S(1)} %get-tuple-element.44), channel_id=1, source_target_pairs={{0,31},{1,2},{2,1},{3,4},{4,3},{5,6},{6,5},{7,8},{8,7},{9,10},{10,... | collective-permute-start | bytes 294920 | tf_op jit(solution)/shard_map/ppermute | solution.py:375
  13.2 5.4 %collective-permute-start.5 = (bf16[384,128]{1,0:T(8,128)(2,1)S(1)}, bf16[384,128]{1,0:T(8,128)(2,1)S(1)}, u32[]{:S(2)}, u32[]{:S(2)}) collective-permute-start(bf16[384,128]{1,0:T(8,128)(2,1)S(1)} %get-tuple-element.45), channel_id=1, source_target_pairs={{0,1},{1,0},{2,3},{3,2},{4,5},{5,4},{6,7},{7,6},{8,9},{9,8},{10,11... | collective-permute-start | bytes 294920 | tf_op jit(solution)/shard_map/ppermute | solution.py:376
  19.0 7.7 %collective-permute-start.6 = (bf16[384,128]{1,0:T(8,128)(2,1)S(1)}, bf16[384,128]{1,0:T(8,128)(2,1)S(1)}, u32[]{:S(2)}, u32[]{:S(2)}) collective-permute-start(bf16[384,128]{1,0:T(8,128)(2,1)S(1)} %get-tuple-element.47), channel_id=1, source_target_pairs={{0,31},{1,2},{2,1},{3,4},{4,3},{5,6},{6,5},{7,8},{8,7},{9,10},{10,... | collective-permute-start | bytes 294920 | tf_op jit(solution)/shard_map/ppermute | solution.py:375
  22.1 4.6 %collective-permute-start.7 = (bf16[384,128]{1,0:T(8,128)(2,1)S(1)}, bf16[384,128]{1,0:T(8,128)(2,1)S(1)}, u32[]{:S(2)}, u32[]{:S(2)}) collective-permute-start(bf16[384,128]{1,0:T(8,128)(2,1)S(1)} %get-tuple-element.48), channel_id=1, source_target_pairs={{0,1},{1,0},{2,3},{3,2},{4,5},{5,4},{6,7},{7,6},{8,9},{9,8},{10,11... | collective-permute-start | bytes 294920 | tf_op jit(solution)/shard_map/ppermute | solution.py:376
  27.2 7.7 %collective-permute-start.8 = (bf16[384,128]{1,0:T(8,128)(2,1)S(1)}, bf16[384,128]{1,0:T(8,128)(2,1)S(1)}, u32[]{:S(2)}, u32[]{:S(2)}) collective-permute-start(bf16[384,128]{1,0:T(8,128)(2,1)S(1)} %get-tuple-element.50), channel_id=1, source_target_pairs={{0,31},{1,2},{2,1},{3,4},{4,3},{5,6},{6,5},{7,8},{8,7},{9,10},{10,... | collective-permute-start | bytes 294920 | tf_op jit(solution)/shard_map/ppermute | solution.py:375
  30.3 4.6 %collective-permute-start.9 = (bf16[384,128]{1,0:T(8,128)(2,1)S(1)}, bf16[384,128]{1,0:T(8,128)(2,1)S(1)}, u32[]{:S(2)}, u32[]{:S(2)}) collective-permute-start(bf16[384,128]{1,0:T(8,128)(2,1)S(1)} %get-tuple-element.51), channel_id=1, source_target_pairs={{0,1},{1,0},{2,3},{3,2},{4,5},{5,4},{6,7},{7,6},{8,9},{9,8},{10,11... | collective-permute-start | bytes 294920 | tf_op jit(solution)/shard_map/ppermute | solution.py:376
  35.4 7.8 %collective-permute-start.10 = (bf16[384,128]{1,0:T(8,128)(2,1)S(1)}, bf16[384,128]{1,0:T(8,128)(2,1)S(1)}, u32[]{:S(2)}, u32[]{:S(2)}) collective-permute-start(bf16[384,128]{1,0:T(8,128)(2,1)S(1)} %get-tuple-element.55), channel_id=1, source_target_pairs={{0,31},{1,2},{2,1},{3,4},{4,3},{5,6},{6,5},{7,8},{8,7},{9,10},{10,... | collective-permute-start | bytes 294920 | tf_op jit(solution)/shard_map/ppermute | solution.py:375
  38.5 0.7 %copy-start.7 = (f32[5]{0:T(128)S(1)}, f32[5]{0:T(128)}, u32[]{:S(2)}) copy-start(f32[5]{0:T(128)} %coef.1) | copy-start | bytes 64
  38.5 4.7 %collective-permute-start.11 = (bf16[384,128]{1,0:T(8,128)(2,1)S(1)}, bf16[384,128]{1,0:T(8,128)(2,1)S(1)}, u32[]{:S(2)}, u32[]{:S(2)}) collective-permute-start(bf16[384,128]{1,0:T(8,128)(2,1)S(1)} %get-tuple-element.56), channel_id=1, source_target_pairs={{0,1},{1,0},{2,3},{3,2},{4,5},{5,4},{6,7},{7,6},{8,9},{9,8},{10,11... | collective-permute-start | bytes 294920 | tf_op jit(solution)/shard_map/ppermute | solution.py:376
  43.7 1.9 %collective-permute-start.12 = (bf16[32,512]{1,0:T(8,128)(2,1)S(1)}, bf16[32,512]{1,0:T(8,128)(2,1)S(1)}, u32[]{:S(2)}, u32[]{:S(2)}) collective-permute-start(bf16[32,512]{1,0:T(8,128)(2,1)S(1)} %get-tuple-element.58), channel_id=1, source_target_pairs={{0,1},{1,0},{2,3},{3,2},{4,5},{5,4},{6,7},{7,6},{8,9},{9,8},{10,11... | collective-permute-start | bytes 98312 | tf_op jit(solution)/shard_map/ppermute | solution.py:381
  43.7 4.2 %collective-permute-start.13 = (bf16[32,512]{1,0:T(8,128)(2,1)S(1)}, bf16[32,512]{1,0:T(8,128)(2,1)S(1)}, u32[]{:S(2)}, u32[]{:S(2)}) collective-permute-start(bf16[32,512]{1,0:T(8,128)(2,1)S(1)} %get-tuple-element.59), channel_id=1, source_target_pairs={{0,2},{1,3},{2,0},{3,1},{4,6},{5,7},{6,4},{7,5},{8,10},{9,11},{10,... | collective-permute-start | bytes 98312 | tf_op jit(solution)/shard_map/ppermute | solution.py:381
  43.8 4.1 %collective-permute-start.14 = (bf16[32,512]{1,0:T(8,128)(2,1)S(1)}, bf16[32,512]{1,0:T(8,128)(2,1)S(1)}, u32[]{:S(2)}, u32[]{:S(2)}) collective-permute-start(bf16[32,512]{1,0:T(8,128)(2,1)S(1)} %get-tuple-element.60), channel_id=1, source_target_pairs={{0,3},{1,2},{2,1},{3,0},{4,7},{5,6},{6,5},{7,4},{8,11},{9,10},{10,... | collective-permute-start | bytes 98312 | tf_op jit(solution)/shard_map/ppermute | solution.py:381

commit v12 on v11

--- a/solution.py
+++ b/solution.py
@@ -190,33 +190,43 @@
     return float(x) if isinstance(x, int) else x.astype(F32)
 
 
-def place(message, is_left, rows):
+def place(message, is_left, rows, lists):
     nfeat = rows.shape[1]
     gap = rows.shape[0] - SPILL
     rows[0:gap, :] = jnp.zeros((gap, nfeat), BF)
     rows[SPILL : SPILL + gap, :] = jnp.zeros((gap, nfeat), BF)
     rows[pl.ds(pl.multiple_of(jnp.where(is_left, gap, 0), 64), SPILL), :] = message[0:SPILL, :]
     block = message[SPILL : SPILL + ID_ROWS, 0:128].astype(F32)
-    return [row_of(block[3 * k : 3 * k + 3]) for k in range(3)]
-
-
-def add_message(band, blocks, atom, column, is_left):
+    atom, offset, cell = [row_of(block[3 * k : 3 * k + 3]) for k in range(3)]
+    lists[0:1, :] = atom
+    lists[1:2, :] = column_of(atom, offset)
+    return cell
+
+
+def near_groups(is_left):
+    ngroup = ATOM_Q // GROUP
+    return range(NEAR) if is_left else range(ngroup - NEAR, ngroup)
+
+
+def add_far(band, blocks, lists, left):
+    atom = lists[0:1, :]
     mine = (atom >= 0.0) & (atom < float(ATOM_Q))
-    highest = jnp.max(jnp.where(mine, atom, -1.0)).astype(jnp.int32)
-    lowest = jnp.min(jnp.where(mine, atom, float(ATOM_Q))).astype(jnp.int32)
-    for k in range(NEAR):
-        first = jnp.where(is_left, k * GROUP, ATOM_Q - (NEAR - k) * GROUP)
-        put_dense(band, dense_of(blocks[...], atom, column, first), first, band)
-    for k in range(ATOM_Q // GROUP - NEAR):
-        first = jnp.where(is_left, (NEAR + k) * GROUP, k * GROUP)
-
-        @pl.when(jnp.where(is_left, highest >= first, lowest < first + GROUP))
-        def _(first=first):
-            put_dense(band, dense_of(blocks[...], atom, column, first), first, band)
+    reach = float(NEAR * GROUP)
+    beyond = (left & (atom >= reach)) | (jnp.logical_not(left) & (atom < ATOM_Q - reach))
+    any_far = jnp.max(jnp.where(mine & beyond, 1.0, 0.0)) > 0.5
+    for is_left in (True, False):
+
+        @pl.when(any_far & (left == is_left))
+        def _(is_left=is_left):
+            for g in range(ATOM_Q // GROUP):
+                if g not in near_groups(is_left):
+                    first = g * GROUP
+                    dense = dense_of(blocks[...], lists[0:1, :], lists[1:2, :], first)
+                    put_dense(band, dense, first, band)
 
 
 def own_kernel(
-    feat, src, dst, cell, near, cell_bias, w_in, w_out, _, band, w_in_t, bias_t, w_out_t, blk, blk2, bias8, rows, more
+    feat, src, dst, cell, near, cell_bias, w_in, w_out, _, band, w_in_t, bias_t, w_out_t, blk, blk2, bias8, rows, more, lists
 ):
     nfeat, width = w_in.shape
     nblk = w_out.shape[1]
@@ -234,23 +244,45 @@
     rows[0:1, :] = atom
     rows[1:2, :] = column_of(atom, row_of(ids[1]))
     is_left = device_side() == 1
-    other = place(near, is_left, more)
+    cells = place(near, is_left, more, lists)
     blk[...] = pair_blocks(feat[...], row_of(ids[2]), w_in_t, bias_t, w_out_t)
-    blk2[...] = pair_blocks(more[...], other[2], w_in_t, bias_t, w_out_t)
+    blk2[...] = pair_blocks(more[...], cells, w_in_t, bias_t, w_out_t)
+    spans = []
     for first in range(0, ATOM_Q, GROUP):
         start = jnp.sum((ids[0] < float(first)).astype(F32)).astype(jnp.int32)
-        at = pl.multiple_of(jnp.minimum(start // 128 * 128, own - GROUP_SPAN), 128)
-        span = pl.ds(at, GROUP_SPAN)
-        put_dense(band, dense_of(blk[:, span], rows[0:1, span], rows[1:2, span], first), first)
-    add_message(band, blk2, other[0], column_of(other[0], other[1]), is_left)
-
-
-def spill_kernel(own_band, blue, w_in_t, bias_t, w_out_t, band, blk, more):
+        spans.append(pl.ds(pl.multiple_of(jnp.minimum(start // 128 * 128, own - GROUP_SPAN), 128), GROUP_SPAN))
+    for left in (True, False):
+
+        @pl.when(is_left == left)
+        def _(left=left):
+            for g, span in enumerate(spans):
+                first = g * GROUP
+                dense = dense_of(blk[:, span], rows[0:1, span], rows[1:2, span], first)
+                if g in near_groups(left):
+                    dense = dense + dense_of(blk2[...], lists[0:1, :], lists[1:2, :], first)
+                put_dense(band, dense, first)
+
+    add_far(band, blk2, lists, is_left)
+
+
+def spill_kernel(own_band, blue, w_in_t, bias_t, w_out_t, band, blk, more, lists):
     is_left = device_side() == 0
-    ids = place(blue, is_left, more)
-    blk[...] = pair_blocks(more[...], ids[2], w_in_t, bias_t, w_out_t)
-    band[...] = own_band[...]
-    add_message(band, blk, ids[0], column_of(ids[0], ids[1]), is_left)
+    cells = place(blue, is_left, more, lists)
+    blk[...] = pair_blocks(more[...], cells, w_in_t, bias_t, w_out_t)
+    for left in (True, False):
+
+        @pl.when(is_left == left)
+        def _(left=left):
+            for g in range(ATOM_Q // GROUP):
+                first = g * GROUP
+                if g in near_groups(left):
+                    dense = dense_of(blk[...], lists[0:1, :], lists[1:2, :], first)
+                    put_dense(band, dense, first, own_band)
+                else:
+                    pair, at = first // PAIR_ATOMS, first % PAIR_ATOMS * ORB
+                    band[pair, at : at + GROUP * ORB, :] = own_band[pair, at : at + GROUP * ORB, :]
+
+    add_far(band, blk, lists, is_left)
 
 
 def own_part(band, field):
@@ -424,6 +456,7 @@
             pltpu.VMEM((8, width), F32),
             pltpu.VMEM((8, nown), F32),
             pltpu.VMEM((wide_spill, nfeat), BF),
+            pltpu.VMEM((8, wide_spill), F32),
         ],
         features,
         *edges,
@@ -438,7 +471,11 @@
         spill_kernel,
         "spill",
         (band_shape,),
-        [pltpu.VMEM((ORB * ORB, wide_spill), BF), pltpu.VMEM((wide_spill, nfeat), BF)],
+        [
+            pltpu.VMEM((ORB * ORB, wide_spill), BF),
+            pltpu.VMEM((wide_spill, nfeat), BF),
+            pltpu.VMEM((8, wide_spill), F32),
+        ],
         band,
         blue_msg,
         *weights,

time: 48.8 us -> 48.8 us (level)
  waiting for transfers between devices: 14.1 us -> 14.7 us
  starting transfers between devices: 22.1 us -> 21.6 us
    ppermute x4, waiting for transfers between devices: 11.8 us -> 12.4 us  [swap(): lax.ppermute(first, axes, blue_pairs)]
where the time goes in v12:
time: 48.8 us; the launch traced here: 48.6 us
  starting transfers between devices  21.6 us (44%)
  waiting for transfers between devices  14.7 us (30%)
  Pallas kernels  11.4 us (23%)
  local copies, waits for them, and re-layouts  0.7 us (1%)
    ppermute x4, waiting for transfers between devices, swap(): lax.ppermute(first, axes, blue_pairs)  12.4 us
    pallas_call x14, Pallas kernels, call(): pl.pallas_call(kernel, name=name, out_shape=outs, in_specs=spaces, out_sp...  11.4 us
    ppermute x4, starting transfers between devices, swap(): lax.ppermute(first, axes, blue_pairs)  11.1 us
    ppermute x1, starting transfers between devices, per_device(): blue_msg = lax.ppermute(blue_msg, axes, blue_pairs)  5.37 us
    ppermute x1, starting transfers between devices, per_device(): across = lax.ppermute(across, 'edges', [(i, i ^ 3) for i in range(nedge)])  2.61 us
    ppermute x3, waiting for transfers between devices, exchange(): lax.ppermute(pieces[k], 'edges', [(i, i ^ k) for i in range(nedge)])  2.3 us
    ppermute x3, starting transfers between devices, exchange(): lax.ppermute(pieces[k], 'edges', [(i, i ^ k) for i in range(nedge)])  1.93 us
  transfers between devices with their start and end apart: 15, of which 5 were waited for; matrix products, arithmetic and copies ran while one was open for 0% of the time, Pallas kernels for 14%

profile of v12, /device:TPU:0, one launch (start us, length us, event | category | flops | bytes accessed | tf_op | source)
XLA Modules:
  0.0 48.6 jit_solution(11749155970791584141)
XLA Ops:
  0.0 2.0 %prep.1 = (bf16[32,512]{1,0:T(8,128)(2,1)}, bf16[32,512]{1,0:T(8,128)(2,1)}, bf16[32,512]{1,0:T(8,128)(2,1)}, bf16[336,256]{1,0:T(8,128)(2,1)}, bf16[400,256]{1,0:T(8,128)(2,1)}) custom-call(f32[32,2048]{1,0:T(8,128)} %vec_hbm.1, bf16[1280,256]{1,0:T(8,128)(2,1)} %feat.3, s32[10,128]{1,0:T(8,128)} %bitcast.3, s32[10,128]{1,0:T(8,128)} %bitcast.5, ...), custom_call_target="tpu_custom_call" | custom-call | flops 1000000000 | tf_op jit(solution)/shard_map/prep/pallas_call | solution.py:382
  2.0 0.5 %collective-permute-start = (bf16[400,256]{1,0:T(8,128)(2,1)}, bf16[400,256]{1,0:T(8,128)(2,1)S(1)}, u32[]{:S(2)}, u32[]{:S(2)}) collective-permute-start(bf16[400,256]{1,0:T(8,128)(2,1)} %get-tuple-element.33), channel_id=1, source_target_pairs={{0,1},{1,0},{2,3},{3,2},{4,5},{5,4},{6,7},{7,6},{8,9},{9,8},{10,11... | collective-permute-start | bytes 614408 | tf_op jit(solution)/shard_map/ppermute | solution.py:436
  2.5 2.6 %collective-permute-start.2 = (bf16[32,512]{1,0:T(8,128)(2,1)}, bf16[32,512]{1,0:T(8,128)(2,1)S(1)}, u32[]{:S(2)}, u32[]{:S(2)}) collective-permute-start(bf16[32,512]{1,0:T(8,128)(2,1)} %get-tuple-element.36), channel_id=1, source_target_pairs={{0,3},{1,2},{2,1},{3,0},{4,7},{5,6},{6,5},{7,4},{8,11},{9,10},{10,... | collective-permute-start | bytes 98312 | tf_op jit(solution)/shard_map/ppermute | solution.py:434
  5.2 0.0 collective-permute-start.1
  5.2 5.4 %collective-permute-start.3 = (bf16[336,256]{1,0:T(8,128)(2,1)}, bf16[336,256]{1,0:T(8,128)(2,1)S(1)}, u32[]{:S(2)}, u32[]{:S(2)}) collective-permute-start(bf16[336,256]{1,0:T(8,128)(2,1)} %get-tuple-element.39), channel_id=1, source_target_pairs={{0,31},{1,2},{2,1},{3,4},{4,3},{5,6},{6,5},{7,8},{8,7},{9,10},{10,... | collective-permute-start | bytes 516104 | tf_op jit(solution)/shard_map/ppermute | solution.py:437
  10.6 0.0 collective-permute-done.2.x
  10.6 0.0 collective-permute-done.1.p2
  10.6 0.0 collective-permute-done.near
  10.6 0.0 copy-start
  10.6 0.0 copy-start.1
  10.6 0.0 copy-start.2
  10.6 0.0 copy-start.3
  10.7 0.0 copy-start.4
  10.7 0.0 copy-start.5
  10.7 0.2 field.1
  10.9 0.0 copy-start.6
  10.9 2.3 %collective-permute-start.4 = (bf16[384,128]{1,0:T(8,128)(2,1)S(1)}, bf16[384,128]{1,0:T(8,128)(2,1)S(1)}, u32[]{:S(2)}, u32[]{:S(2)}) collective-permute-start(bf16[384,128]{1,0:T(8,128)(2,1)S(1)} %get-tuple-element.44), channel_id=1, source_target_pairs={{0,31},{1,2},{2,1},{3,4},{4,3},{5,6},{6,5},{7,8},{8,7},{9,10},{10,... | collective-permute-start | bytes 294920 | tf_op jit(solution)/shard_map/ppermute | solution.py:407
  13.2 0.0 collective-permute-start.5
  13.2 3.1 %own.1 = (bf16[2,256,1024]{2,1,0:T(8,128)(2,1)S(1)}, bf16[512,256]{1,0:T(8,128)(2,1)S(1)}, bf16[512,8]{1,0:T(8,128)(2,1)S(1)}, bf16[256,256]{1,0:T(8,128)(2,1)S(1)}) custom-call(bf16[1280,256]{1,0:T(8,128)(2,1)S(1)} %copy-done, s32[10,128]{1,0:T(8,128)S(1)} %bitcast.4, s32[10,128]{1,0:T(8,128)S(1)} %bitcast.6, s32[10,128]{1,0:T(8,128)S(1)} %bitcast.8, ...), custom_call_target="tpu_custom_call" | custom-call | flops 4000000000 | tf_op jit(solution)/shard_map/own/pallas_call | solution.py:382
  16.3 0.0 collective-permute-done.3.blue
  16.3 1.6 %spill.1.band = bf16[2,256,1024]{2,1,0:T(8,128)(2,1)S(1)} custom-call(bf16[2,256,1024]{2,1,0:T(8,128)(2,1)S(1)} %get-tuple-element.38.own_band, bf16[336,256]{1,0:T(8,128)(2,1)S(1)} %collective-permute-done.3.blue, bf16[512,256]{1,0:T(8,128)(2,1)S(1)} %get-tuple-element.40.w_in_t, ...), custom_call_target="tpu_custom_call", output_to_operand_aliasing={{}: (0, {})} | custom-call | tf_op jit(solution)/shard_map/spill/pallas_call | solution.py:382
  18.0 0.3 start.1.part
  18.3 0.3 collective-permute-done.4.blue
  18.6 0.0 collective-permute-done.5.red
  18.6 0.4 outer.3
  19.0 3.0 %collective-permute-start.6 = (bf16[384,128]{1,0:T(8,128)(2,1)S(1)}, bf16[384,128]{1,0:T(8,128)(2,1)S(1)}, u32[]{:S(2)}, u32[]{:S(2)}) collective-permute-start(bf16[384,128]{1,0:T(8,128)(2,1)S(1)} %get-tuple-element.47), channel_id=1, source_target_pairs={{0,31},{1,2},{2,1},{3,4},{4,3},{5,6},{6,5},{7,8},{8,7},{9,10},{10,... | collective-permute-start | bytes 294920 | tf_op jit(solution)/shard_map/ppermute | solution.py:407
  22.0 0.0 collective-permute-start.7
  22.0 0.3 inner.2.part
  22.3 4.4 %collective-permute-done.6.blue = bf16[384,128]{1,0:T(8,128)(2,1)S(1)} collective-permute-done((bf16[384,128]{1,0:T(8,128)(2,1)S(1)}, bf16[384,128]{1,0:T(8,128)(2,1)S(1)}, u32[]{:S(2)}, u32[]{:S(2)}) %collective-permute-start.6) | collective-permute-done | bytes 98336 | tf_op jit(solution)/shard_map/ppermute | solution.py:407
  26.8 0.0 collective-permute-done.7.red
  26.8 0.4 outer.4
  27.2 3.0 %collective-permute-start.8 = (bf16[384,128]{1,0:T(8,128)(2,1)S(1)}, bf16[384,128]{1,0:T(8,128)(2,1)S(1)}, u32[]{:S(2)}, u32[]{:S(2)}) collective-permute-start(bf16[384,128]{1,0:T(8,128)(2,1)S(1)} %get-tuple-element.50), channel_id=1, source_target_pairs={{0,31},{1,2},{2,1},{3,4},{4,3},{5,6},{6,5},{7,8},{8,7},{9,10},{10,... | collective-permute-start | bytes 294920 | tf_op jit(solution)/shard_map/ppermute | solution.py:407
  30.2 0.3 inner.3.part
  30.5 4.4 %collective-permute-done.8.blue = bf16[384,128]{1,0:T(8,128)(2,1)S(1)} collective-permute-done((bf16[384,128]{1,0:T(8,128)(2,1)S(1)}, bf16[384,128]{1,0:T(8,128)(2,1)S(1)}, u32[]{:S(2)}, u32[]{:S(2)}) %collective-permute-start.8) | collective-permute-done | bytes 98336 | tf_op jit(solution)/shard_map/ppermute | solution.py:407
  34.9 0.0 collective-permute-done.9.red
  34.9 0.4 outer.5
  35.4 3.0 %collective-permute-start.10 = (bf16[384,128]{1,0:T(8,128)(2,1)S(1)}, bf16[384,128]{1,0:T(8,128)(2,1)S(1)}, u32[]{:S(2)}, u32[]{:S(2)}) collective-permute-start(bf16[384,128]{1,0:T(8,128)(2,1)S(1)} %get-tuple-element.55), channel_id=1, source_target_pairs={{0,31},{1,2},{2,1},{3,4},{4,3},{5,6},{6,5},{7,8},{8,7},{9,10},{10,... | collective-permute-start | bytes 294920 | tf_op jit(solution)/shard_map/ppermute | solution.py:407
  38.3 0.7 %copy-done.7 = f32[5]{0:T(128)S(1)} copy-done((f32[5]{0:T(128)S(1)}, f32[5]{0:T(128)}, u32[]{:S(2)}) %copy-start.7) | copy-done | bytes 44
  39.0 0.9 %mix.1 = (f32[128,512]{1,0:T(8,128)S(1)}, f32[8,128]{1,0:T(8,128)S(1)}) custom-call(f32[5]{0:T(128)S(1)} %copy-done.7, bf16[2,256,1024]{2,1,0:T(8,128)(2,1)S(1)} %spill.1.band, f32[512,128]{1,0:T(8,128)S(1)} %get-tuple-element.43.now.before.t0, f32[512,128]{1,0:T(8,128)S(1)} %get-tuple-element.46.now.before.t1, f32[512,128]{1,0:T(8,128)S(1)} %get-tuple-element.49.now.t2, ...), custom_call_target="tpu_custom_call" | custom-call | flops 1000000000 | tf_op jit(solution)/shard_map/mix/pallas_call | solution.py:382
  39.9 3.3 %collective-permute-done.10.blue = bf16[384,128]{1,0:T(8,128)(2,1)S(1)} collective-permute-done((bf16[384,128]{1,0:T(8,128)(2,1)S(1)}, bf16[384,128]{1,0:T(8,128)(2,1)S(1)}, u32[]{:S(2)}, u32[]{:S(2)}) %collective-permute-start.10) | collective-permute-done | bytes 98336 | tf_op jit(solution)/shard_map/ppermute | solution.py:407
  43.2 0.0 collective-permute-done.11.red
  43.2 0.5 last.1
  43.7 0.1 collective-permute-start.12
  43.8 0.1 collective-permute-start.13
  43.8 1.8 %collective-permute-start.14 = (bf16[32,512]{1,0:T(8,128)(2,1)S(1)}, bf16[32,512]{1,0:T(8,128)(2,1)S(1)}, u32[]{:S(2)}, u32[]{:S(2)}) collective-permute-start(bf16[32,512]{1,0:T(8,128)(2,1)S(1)} %get-tuple-element.60), channel_id=1, source_target_pairs={{0,3},{1,2},{2,1},{3,0},{4,7},{5,6},{6,5},{7,4},{8,11},{9,10},{10,... | collective-permute-start | bytes 98312 | tf_op jit(solution)/shard_map/ppermute | solution.py:413
  45.6 0.0 collective-permute-done.12.p1
  45.6 2.3 %collective-permute-done.13.p2 = bf16[32,512]{1,0:T(8,128)(2,1)S(1)} collective-permute-done((bf16[32,512]{1,0:T(8,128)(2,1)S(1)}, bf16[32,512]{1,0:T(8,128)(2,1)S(1)}, u32[]{:S(2)}, u32[]{:S(2)}) %collective-permute-start.13) | collective-permute-done | bytes 32800 | tf_op jit(solution)/shard_map/ppermute | solution.py:413
  47.9 0.7 %join.1 = f32[32,2048]{1,0:T(8,128)} custom-call(bf16[32,512]{1,0:T(8,128)(2,1)S(1)} %get-tuple-element.57.p0, bf16[32,512]{1,0:T(8,128)(2,1)S(1)} %collective-permute-done.12.p1, bf16[32,512]{1,0:T(8,128)(2,1)S(1)} %collective-permute-done.13.p2, bf16[32,512]{1,0:T(8,128)(2,1)S(1)} %collective-permute-done.14.p3), custom_call_target="tpu_custom_call" | custom-call | flops 1000000000 | tf_op jit(solution)/shard_map/join/pallas_call | solution.py:382
  (14 shorter events, 0.0 us)
Async XLA Ops:
  2.0 8.6 %collective-permute-start = (bf16[400,256]{1,0:T(8,128)(2,1)}, bf16[400,256]{1,0:T(8,128)(2,1)S(1)}, u32[]{:S(2)}, u32[]{:S(2)}) collective-permute-start(bf16[400,256]{1,0:T(8,128)(2,1)} %get-tuple-element.33), channel_id=1, source_target_pairs={{0,1},{1,0},{2,3},{3,2},{4,5},{5,4},{6,7},{7,6},{8,9},{9,8},{10,11... | collective-permute-start | bytes 614408 | tf_op jit(solution)/shard_map/ppermute | solution.py:436
  2.5 8.0 %collective-permute-start.2 = (bf16[32,512]{1,0:T(8,128)(2,1)}, bf16[32,512]{1,0:T(8,128)(2,1)S(1)}, u32[]{:S(2)}, u32[]{:S(2)}) collective-permute-start(bf16[32,512]{1,0:T(8,128)(2,1)} %get-tuple-element.36), channel_id=1, source_target_pairs={{0,3},{1,2},{2,1},{3,0},{4,7},{5,6},{6,5},{7,4},{8,11},{9,10},{10,... | collective-permute-start | bytes 98312 | tf_op jit(solution)/shard_map/ppermute | solution.py:434
  5.2 5.4 %collective-permute-start.1 = (bf16[32,512]{1,0:T(8,128)(2,1)}, bf16[32,512]{1,0:T(8,128)(2,1)S(1)}, u32[]{:S(2)}, u32[]{:S(2)}) collective-permute-start(bf16[32,512]{1,0:T(8,128)(2,1)} %get-tuple-element.35), channel_id=1, source_target_pairs={{0,2},{1,3},{2,0},{3,1},{4,6},{5,7},{6,4},{7,5},{8,10},{9,11},{10,... | collective-permute-start | bytes 98312 | tf_op jit(solution)/shard_map/ppermute | solution.py:435
  5.2 5.4 %copy-start.8 = (bf16[32,512]{1,0:T(8,128)(2,1)S(1)}, bf16[32,512]{1,0:T(8,128)(2,1)}, u32[]{:S(2)}) copy-start(bf16[32,512]{1,0:T(8,128)(2,1)} %get-tuple-element.34.p0) | copy-start | bytes 98308
  5.2 11.1 %collective-permute-start.3 = (bf16[336,256]{1,0:T(8,128)(2,1)}, bf16[336,256]{1,0:T(8,128)(2,1)S(1)}, u32[]{:S(2)}, u32[]{:S(2)}) collective-permute-start(bf16[336,256]{1,0:T(8,128)(2,1)} %get-tuple-element.39), channel_id=1, source_target_pairs={{0,31},{1,2},{2,1},{3,4},{4,3},{5,6},{6,5},{7,8},{8,7},{9,10},{10,... | collective-permute-start | bytes 516104 | tf_op jit(solution)/shard_map/ppermute | solution.py:437
  10.6 2.6 %copy-start = (bf16[1280,256]{1,0:T(8,128)(2,1)S(1)}, bf16[1280,256]{1,0:T(8,128)(2,1)}, u32[]{:S(2)}) copy-start(bf16[1280,256]{1,0:T(8,128)(2,1)} %feat.3) | copy-start | bytes 1966084
  10.6 2.5 %copy-start.1 = (bf16[256,512]{1,0:T(8,128)(2,1)S(1)}, bf16[256,512]{1,0:T(8,128)(2,1)}, u32[]{:S(2)}) copy-start(bf16[256,512]{1,0:T(8,128)(2,1)} %w_in.1) | copy-start | bytes 786436
  10.6 2.5 %copy-start.2 = (bf16[256,256]{1,0:T(8,128)(2,1)S(1)}, bf16[256,256]{1,0:T(8,128)(2,1)}, u32[]{:S(2)}) copy-start(bf16[256,256]{1,0:T(8,128)(2,1)} %w_out.1) | copy-start | bytes 393220
  10.6 2.5 %copy-start.3 = (s32[1280]{0:T(1024)S(1)}, s32[1280]{0:T(1024)}, u32[]{:S(2)}) copy-start(s32[1280]{0:T(1024)} %param.10) | copy-start | bytes 15364
  10.7 2.5 %copy-start.4 = (s32[1280]{0:T(1024)S(1)}, s32[1280]{0:T(1024)}, u32[]{:S(2)}) copy-start(s32[1280]{0:T(1024)} %param.11) | copy-start | bytes 15364
  10.7 2.5 %copy-start.5 = (s32[1280]{0:T(1024)S(1)}, s32[1280]{0:T(1024)}, u32[]{:S(2)}) copy-start(s32[1280]{0:T(1024)} %param.12) | copy-start | bytes 15364
  10.9 2.3 %copy-start.6 = (bf16[3,512]{1,0:T(4,128)(2,1)S(1)}, bf16[3,512]{1,0:T(4,128)(2,1)}, u32[]{:S(2)}) copy-start(bf16[3,512]{1,0:T(4,128)(2,1)} %cell_bias.1) | copy-start | bytes 9220
  10.9 7.7 %collective-permute-start.4 = (bf16[384,128]{1,0:T(8,128)(2,1)S(1)}, bf16[384,128]{1,0:T(8,128)(2,1)S(1)}, u32[]{:S(2)}, u32[]{:S(2)}) collective-permute-start(bf16[384,128]{1,0:T(8,128)(2,1)S(1)} %get-tuple-element.44), channel_id=1, source_target_pairs={{0,31},{1,2},{2,1},{3,4},{4,3},{5,6},{6,5},{7,8},{8,7},{9,10},{10,... | collective-permute-start | bytes 294920 | tf_op jit(solution)/shard_map/ppermute | solution.py:407
  13.2 5.4 %collective-permute-start.5 = (bf16[384,128]{1,0:T(8,128)(2,1)S(1)}, bf16[384,128]{1,0:T(8,128)(2,1)S(1)}, u32[]{:S(2)}, u32[]{:S(2)}) collective-permute-start(bf16[384,128]{1,0:T(8,128)(2,1)S(1)} %get-tuple-element.45), channel_id=1, source_target_pairs={{0,1},{1,0},{2,3},{3,2},{4,5},{5,4},{6,7},{7,6},{8,9},{9,8},{10,11... | collective-permute-start | bytes 294920 | tf_op jit(solution)/shard_map/ppermute | solution.py:408
  19.0 7.7 %collective-permute-start.6 = (bf16[384,128]{1,0:T(8,128)(2,1)S(1)}, bf16[384,128]{1,0:T(8,128)(2,1)S(1)}, u32[]{:S(2)}, u32[]{:S(2)}) collective-permute-start(bf16[384,128]{1,0:T(8,128)(2,1)S(1)} %get-tuple-element.47), channel_id=1, source_target_pairs={{0,31},{1,2},{2,1},{3,4},{4,3},{5,6},{6,5},{7,8},{8,7},{9,10},{10,... | collective-permute-start | bytes 294920 | tf_op jit(solution)/shard_map/ppermute | solution.py:407
  22.0 4.8 %collective-permute-start.7 = (bf16[384,128]{1,0:T(8,128)(2,1)S(1)}, bf16[384,128]{1,0:T(8,128)(2,1)S(1)}, u32[]{:S(2)}, u32[]{:S(2)}) collective-permute-start(bf16[384,128]{1,0:T(8,128)(2,1)S(1)} %get-tuple-element.48), channel_id=1, source_target_pairs={{0,1},{1,0},{2,3},{3,2},{4,5},{5,4},{6,7},{7,6},{8,9},{9,8},{10,11... | collective-permute-start | bytes 294920 | tf_op jit(solution)/shard_map/ppermute | solution.py:408
  27.2 7.7 %collective-permute-start.8 = (bf16[384,128]{1,0:T(8,128)(2,1)S(1)}, bf16[384,128]{1,0:T(8,128)(2,1)S(1)}, u32[]{:S(2)}, u32[]{:S(2)}) collective-permute-start(bf16[384,128]{1,0:T(8,128)(2,1)S(1)} %get-tuple-element.50), channel_id=1, source_target_pairs={{0,31},{1,2},{2,1},{3,4},{4,3},{5,6},{6,5},{7,8},{8,7},{9,10},{10,... | collective-permute-start | bytes 294920 | tf_op jit(solution)/shard_map/ppermute | solution.py:407
  30.2 4.8 %collective-permute-start.9 = (bf16[384,128]{1,0:T(8,128)(2,1)S(1)}, bf16[384,128]{1,0:T(8,128)(2,1)S(1)}, u32[]{:S(2)}, u32[]{:S(2)}) collective-permute-start(bf16[384,128]{1,0:T(8,128)(2,1)S(1)} %get-tuple-element.51), channel_id=1, source_target_pairs={{0,1},{1,0},{2,3},{3,2},{4,5},{5,4},{6,7},{7,6},{8,9},{9,8},{10,11... | collective-permute-start | bytes 294920 | tf_op jit(solution)/shard_map/ppermute | solution.py:408
  35.4 7.8 %collective-permute-start.10 = (bf16[384,128]{1,0:T(8,128)(2,1)S(1)}, bf16[384,128]{1,0:T(8,128)(2,1)S(1)}, u32[]{:S(2)}, u32[]{:S(2)}) collective-permute-start(bf16[384,128]{1,0:T(8,128)(2,1)S(1)} %get-tuple-element.55), channel_id=1, source_target_pairs={{0,31},{1,2},{2,1},{3,4},{4,3},{5,6},{6,5},{7,8},{8,7},{9,10},{10,... | collective-permute-start | bytes 294920 | tf_op jit(solution)/shard_map/ppermute | solution.py:407
  38.3 0.7 %copy-start.7 = (f32[5]{0:T(128)S(1)}, f32[5]{0:T(128)}, u32[]{:S(2)}) copy-start(f32[5]{0:T(128)} %coef.1) | copy-start | bytes 64
  38.3 4.9 %collective-permute-start.11 = (bf16[384,128]{1,0:T(8,128)(2,1)S(1)}, bf16[384,128]{1,0:T(8,128)(2,1)S(1)}, u32[]{:S(2)}, u32[]{:S(2)}) collective-permute-start(bf16[384,128]{1,0:T(8,128)(2,1)S(1)} %get-tuple-element.56), channel_id=1, source_target_pairs={{0,1},{1,0},{2,3},{3,2},{4,5},{5,4},{6,7},{7,6},{8,9},{9,8},{10,11... | collective-permute-start | bytes 294920 | tf_op jit(solution)/shard_map/ppermute | solution.py:408
  43.7 1.9 %collective-permute-start.12 = (bf16[32,512]{1,0:T(8,128)(2,1)S(1)}, bf16[32,512]{1,0:T(8,128)(2,1)S(1)}, u32[]{:S(2)}, u32[]{:S(2)}) collective-permute-start(bf16[32,512]{1,0:T(8,128)(2,1)S(1)} %get-tuple-element.58), channel_id=1, source_target_pairs={{0,1},{1,0},{2,3},{3,2},{4,5},{5,4},{6,7},{7,6},{8,9},{9,8},{10,11... | collective-permute-start | bytes 98312 | tf_op jit(solution)/shard_map/ppermute | solution.py:413
  43.8 4.2 %collective-permute-start.13 = (bf16[32,512]{1,0:T(8,128)(2,1)S(1)}, bf16[32,512]{1,0:T(8,128)(2,1)S(1)}, u32[]{:S(2)}, u32[]{:S(2)}) collective-permute-start(bf16[32,512]{1,0:T(8,128)(2,1)S(1)} %get-tuple-element.59), channel_id=1, source_target_pairs={{0,2},{1,3},{2,0},{3,1},{4,6},{5,7},{6,4},{7,5},{8,10},{9,11},{10,... | collective-permute-start | bytes 98312 | tf_op jit(solution)/shard_map/ppermute | solution.py:413
  43.8 4.1 %collective-permute-start.14 = (bf16[32,512]{1,0:T(8,128)(2,1)S(1)}, bf16[32,512]{1,0:T(8,128)(2,1)S(1)}, u32[]{:S(2)}, u32[]{:S(2)}) collective-permute-start(bf16[32,512]{1,0:T(8,128)(2,1)S(1)} %get-tuple-element.60), channel_id=1, source_target_pairs={{0,3},{1,2},{2,1},{3,0},{4,7},{5,6},{6,5},{7,4},{8,11},{9,10},{10,... | collective-permute-start | bytes 98312 | tf_op jit(solution)/shard_map/ppermute | solution.py:413

commit v13 on v12

--- a/solution.py
+++ b/solution.py
@@ -200,41 +200,31 @@
     atom, offset, cell = [row_of(block[3 * k : 3 * k + 3]) for k in range(3)]
     lists[0:1, :] = atom
     lists[1:2, :] = column_of(atom, offset)
-    return cell
-
-
-def near_groups(is_left):
-    ngroup = ATOM_Q // GROUP
-    return range(NEAR) if is_left else range(ngroup - NEAR, ngroup)
-
-
-def add_far(band, blocks, lists, left):
-    atom = lists[0:1, :]
-    mine = (atom >= 0.0) & (atom < float(ATOM_Q))
-    reach = float(NEAR * GROUP)
-    beyond = (left & (atom >= reach)) | (jnp.logical_not(left) & (atom < ATOM_Q - reach))
-    any_far = jnp.max(jnp.where(mine & beyond, 1.0, 0.0)) > 0.5
-    for is_left in (True, False):
-
-        @pl.when(any_far & (left == is_left))
-        def _(is_left=is_left):
-            for g in range(ATOM_Q // GROUP):
-                if g not in near_groups(is_left):
-                    first = g * GROUP
-                    dense = dense_of(blocks[...], lists[0:1, :], lists[1:2, :], first)
-                    put_dense(band, dense, first, band)
+    middle = (atom >= float(NEAR * GROUP)) & (atom < float(ATOM_Q - NEAR * GROUP))
+    return cell, jnp.max(jnp.where(middle, 1.0, 0.0)) > 0.5
+
+
+def at_ends(g):
+    return g < NEAR or g >= ATOM_Q // GROUP - NEAR
+
+
+def add_middle(band, blocks, lists, any_middle):
+    @pl.when(any_middle)
+    def _():
+        for g in range(ATOM_Q // GROUP):
+            if not at_ends(g):
+                dense = dense_of(blocks[...], lists[0:1, :], lists[1:2, :], g * GROUP)
+                put_dense(band, dense, g * GROUP, band)
 
 
 def own_kernel(
     feat, src, dst, cell, near, cell_bias, w_in, w_out, _, band, w_in_t, bias_t, w_out_t, blk, blk2, bias8, rows, more, lists
 ):
-    nfeat, width = w_in.shape
     nblk = w_out.shape[1]
-    eye = (iota((width, width), 0) == iota((width, width), 1)).astype(BF)
-    w_in_t[...] = nt_dot(eye, w_in[...]).astype(BF)
+    w_in_t[...] = w_in[...].astype(F32).T.astype(BF)
     bias8[...] = jnp.zeros(bias8.shape, F32)
     bias8[0:3, :] = cell_bias[...].astype(F32)
-    bias_t[...] = nt_dot(eye, bias8[...].astype(BF)).astype(BF)
+    bias_t[...] = bias8[...].T.astype(BF)
     row, col = iota((nblk, nblk), 0), iota((nblk, nblk), 1)
     swap = (col == (row % ORB) * ORB + row // ORB).astype(BF)
     w_out_t[...] = nt_dot(swap, w_out[...]).astype(BF)
@@ -244,45 +234,35 @@
     rows[0:1, :] = atom
     rows[1:2, :] = column_of(atom, row_of(ids[1]))
     is_left = device_side() == 1
-    cells = place(near, is_left, more, lists)
+    cells, any_middle = place(near, is_left, more, lists)
     blk[...] = pair_blocks(feat[...], row_of(ids[2]), w_in_t, bias_t, w_out_t)
     blk2[...] = pair_blocks(more[...], cells, w_in_t, bias_t, w_out_t)
     spans = []
     for first in range(0, ATOM_Q, GROUP):
         start = jnp.sum((ids[0] < float(first)).astype(F32)).astype(jnp.int32)
         spans.append(pl.ds(pl.multiple_of(jnp.minimum(start // 128 * 128, own - GROUP_SPAN), 128), GROUP_SPAN))
-    for left in (True, False):
-
-        @pl.when(is_left == left)
-        def _(left=left):
-            for g, span in enumerate(spans):
-                first = g * GROUP
-                dense = dense_of(blk[:, span], rows[0:1, span], rows[1:2, span], first)
-                if g in near_groups(left):
-                    dense = dense + dense_of(blk2[...], lists[0:1, :], lists[1:2, :], first)
-                put_dense(band, dense, first)
-
-    add_far(band, blk2, lists, is_left)
+    for g, span in enumerate(spans):
+        first = g * GROUP
+        dense = dense_of(blk[:, span], rows[0:1, span], rows[1:2, span], first)
+        if at_ends(g):
+            dense = dense + dense_of(blk2[...], lists[0:1, :], lists[1:2, :], first)
+        put_dense(band, dense, first)
+    add_middle(band, blk2, lists, any_middle)
 
 
 def spill_kernel(own_band, blue, w_in_t, bias_t, w_out_t, band, blk, more, lists):
     is_left = device_side() == 0
-    cells = place(blue, is_left, more, lists)
+    cells, any_middle = place(blue, is_left, more, lists)
     blk[...] = pair_blocks(more[...], cells, w_in_t, bias_t, w_out_t)
-    for left in (True, False):
-
-        @pl.when(is_left == left)
-        def _(left=left):
-            for g in range(ATOM_Q // GROUP):
-                first = g * GROUP
-                if g in near_groups(left):
-                    dense = dense_of(blk[...], lists[0:1, :], lists[1:2, :], first)
-                    put_dense(band, dense, first, own_band)
-                else:
-                    pair, at = first // PAIR_ATOMS, first % PAIR_ATOMS * ORB
-                    band[pair, at : at + GROUP * ORB, :] = own_band[pair, at : at + GROUP * ORB, :]
-
-    add_far(band, blk, lists, is_left)
+    for g in range(ATOM_Q // GROUP):
+        first = g * GROUP
+        if at_ends(g):
+            dense = dense_of(blk[...], lists[0:1, :], lists[1:2, :], first)
+            put_dense(band, dense, first, own_band)
+        else:
+            pair, at = first // PAIR_ATOMS, first % PAIR_ATOMS * ORB
+            band[pair, at : at + GROUP * ORB, :] = own_band[pair, at : at + GROUP * ORB, :]
+    add_middle(band, blk, lists, any_middle)
 
 
 def own_part(band, field):

time: 48.8 us -> 48.8 us (level)
  waiting for transfers between devices: 14.7 us -> 15.9 us
  starting transfers between devices: 21.6 us -> 20.7 us
    ppermute x4, waiting for transfers between devices: 12.4 us -> 13.6 us  [swap(): lax.ppermute(first, axes, blue_pairs)]
    ppermute x4, starting transfers between devices: 11.1 us -> 10.2 us  [swap(): lax.ppermute(first, axes, blue_pairs)]
where the time goes in v13:
time: 48.8 us; the launch traced here: 48.6 us
  starting transfers between devices  20.7 us (42%)
  waiting for transfers between devices  15.9 us (33%)
  Pallas kernels  11.1 us (23%)
  local copies, waits for them, and re-layouts  0.7 us (1%)
    ppermute x4, waiting for transfers between devices, swap(): lax.ppermute(first, axes, blue_pairs)  13.6 us
    pallas_call x14, Pallas kernels, call(): pl.pallas_call(kernel, name=name, out_shape=outs, in_specs=spaces, out_sp...  11.1 us
    ppermute x4, starting transfers between devices, swap(): lax.ppermute(first, axes, blue_pairs)  10.2 us
    ppermute x1, starting transfers between devices, per_device(): blue_msg = lax.ppermute(blue_msg, axes, blue_pairs)  5.37 us
    ppermute x1, starting transfers between devices, per_device(): across = lax.ppermute(across, 'edges', [(i, i ^ 3) for i in range(nedge)])  2.61 us
    ppermute x3, waiting for transfers between devices, exchange(): lax.ppermute(pieces[k], 'edges', [(i, i ^ k) for i in range(nedge)])  2.3 us
    ppermute x3, starting transfers between devices, exchange(): lax.ppermute(pieces[k], 'edges', [(i, i ^ k) for i in range(nedge)])  1.93 us
  transfers between devices with their start and end apart: 15, of which 5 were waited for; matrix products, arithmetic and copies ran while one was open for 0% of the time, Pallas kernels for 14%

profile of v13, /device:TPU:0, one launch (start us, length us, event | category | flops | bytes accessed | tf_op | source)
XLA Modules:
  0.0 48.6 jit_solution(14078796493963271315)
XLA Ops:
  0.0 2.0 %prep.1 = (bf16[32,512]{1,0:T(8,128)(2,1)}, bf16[32,512]{1,0:T(8,128)(2,1)}, bf16[32,512]{1,0:T(8,128)(2,1)}, bf16[336,256]{1,0:T(8,128)(2,1)}, bf16[400,256]{1,0:T(8,128)(2,1)}) custom-call(f32[32,2048]{1,0:T(8,128)} %vec_hbm.1, bf16[1280,256]{1,0:T(8,128)(2,1)} %feat.3, s32[10,128]{1,0:T(8,128)} %bitcast.3, s32[10,128]{1,0:T(8,128)} %bitcast.5, ...), custom_call_target="tpu_custom_call" | custom-call | flops 1000000000 | tf_op jit(solution)/shard_map/prep/pallas_call | solution.py:362
  2.0 0.5 %collective-permute-start = (bf16[400,256]{1,0:T(8,128)(2,1)}, bf16[400,256]{1,0:T(8,128)(2,1)S(1)}, u32[]{:S(2)}, u32[]{:S(2)}) collective-permute-start(bf16[400,256]{1,0:T(8,128)(2,1)} %get-tuple-element.33), channel_id=1, source_target_pairs={{0,1},{1,0},{2,3},{3,2},{4,5},{5,4},{6,7},{7,6},{8,9},{9,8},{10,11... | collective-permute-start | bytes 614408 | tf_op jit(solution)/shard_map/ppermute | solution.py:416
  2.5 2.6 %collective-permute-start.2 = (bf16[32,512]{1,0:T(8,128)(2,1)}, bf16[32,512]{1,0:T(8,128)(2,1)S(1)}, u32[]{:S(2)}, u32[]{:S(2)}) collective-permute-start(bf16[32,512]{1,0:T(8,128)(2,1)} %get-tuple-element.36), channel_id=1, source_target_pairs={{0,3},{1,2},{2,1},{3,0},{4,7},{5,6},{6,5},{7,4},{8,11},{9,10},{10,... | collective-permute-start | bytes 98312 | tf_op jit(solution)/shard_map/ppermute | solution.py:414
  5.2 0.0 collective-permute-start.1
  5.2 5.4 %collective-permute-start.3 = (bf16[336,256]{1,0:T(8,128)(2,1)}, bf16[336,256]{1,0:T(8,128)(2,1)S(1)}, u32[]{:S(2)}, u32[]{:S(2)}) collective-permute-start(bf16[336,256]{1,0:T(8,128)(2,1)} %get-tuple-element.39), channel_id=1, source_target_pairs={{0,31},{1,2},{2,1},{3,4},{4,3},{5,6},{6,5},{7,8},{8,7},{9,10},{10,... | collective-permute-start | bytes 516104 | tf_op jit(solution)/shard_map/ppermute | solution.py:417
  10.6 0.0 collective-permute-done.2.x
  10.6 0.0 collective-permute-done.1.p2
  10.6 0.0 collective-permute-done.near
  10.6 0.0 copy-start
  10.6 0.0 copy-start.1
  10.6 0.0 copy-start.2
  10.6 0.0 copy-start.3
  10.7 0.0 copy-start.4
  10.7 0.0 copy-start.5
  10.7 0.2 field.1
  10.9 0.0 copy-start.6
  10.9 2.3 %collective-permute-start.4 = (bf16[384,128]{1,0:T(8,128)(2,1)S(1)}, bf16[384,128]{1,0:T(8,128)(2,1)S(1)}, u32[]{:S(2)}, u32[]{:S(2)}) collective-permute-start(bf16[384,128]{1,0:T(8,128)(2,1)S(1)} %get-tuple-element.44), channel_id=1, source_target_pairs={{0,31},{1,2},{2,1},{3,4},{4,3},{5,6},{6,5},{7,8},{8,7},{9,10},{10,... | collective-permute-start | bytes 294920 | tf_op jit(solution)/shard_map/ppermute | solution.py:387
  13.2 0.0 collective-permute-start.5
  13.2 2.9 %own.1 = (bf16[2,256,1024]{2,1,0:T(8,128)(2,1)S(1)}, bf16[512,256]{1,0:T(8,128)(2,1)S(1)}, bf16[512,8]{1,0:T(8,128)(2,1)S(1)}, bf16[256,256]{1,0:T(8,128)(2,1)S(1)}) custom-call(bf16[1280,256]{1,0:T(8,128)(2,1)S(1)} %copy-done, s32[10,128]{1,0:T(8,128)S(1)} %bitcast.4, s32[10,128]{1,0:T(8,128)S(1)} %bitcast.6, s32[10,128]{1,0:T(8,128)S(1)} %bitcast.8, ...), custom_call_target="tpu_custom_call" | custom-call | flops 4000000000 | tf_op jit(solution)/shard_map/own/pallas_call | solution.py:362
  16.1 0.0 collective-permute-done.3.blue
  16.1 1.5 %spill.1.band = bf16[2,256,1024]{2,1,0:T(8,128)(2,1)S(1)} custom-call(bf16[2,256,1024]{2,1,0:T(8,128)(2,1)S(1)} %get-tuple-element.38.own_band, bf16[336,256]{1,0:T(8,128)(2,1)S(1)} %collective-permute-done.3.blue, bf16[512,256]{1,0:T(8,128)(2,1)S(1)} %get-tuple-element.40.w_in_t, ...), custom_call_target="tpu_custom_call", output_to_operand_aliasing={{}: (0, {})} | custom-call | tf_op jit(solution)/shard_map/spill/pallas_call | solution.py:362
  17.7 0.3 start.1.part
  18.0 0.6 %collective-permute-done.4.blue = bf16[384,128]{1,0:T(8,128)(2,1)S(1)} collective-permute-done((bf16[384,128]{1,0:T(8,128)(2,1)S(1)}, bf16[384,128]{1,0:T(8,128)(2,1)S(1)}, u32[]{:S(2)}, u32[]{:S(2)}) %collective-permute-start.4) | collective-permute-done | bytes 98336 | tf_op jit(solution)/shard_map/ppermute | solution.py:387
  18.6 0.0 collective-permute-done.5.red
  18.6 0.4 outer.3
  19.0 2.7 %collective-permute-start.6 = (bf16[384,128]{1,0:T(8,128)(2,1)S(1)}, bf16[384,128]{1,0:T(8,128)(2,1)S(1)}, u32[]{:S(2)}, u32[]{:S(2)}) collective-permute-start(bf16[384,128]{1,0:T(8,128)(2,1)S(1)} %get-tuple-element.47), channel_id=1, source_target_pairs={{0,31},{1,2},{2,1},{3,4},{4,3},{5,6},{6,5},{7,8},{8,7},{9,10},{10,... | collective-permute-start | bytes 294920 | tf_op jit(solution)/shard_map/ppermute | solution.py:387
  21.7 0.0 collective-permute-start.7
  21.7 0.3 inner.2.part
  22.1 4.8 %collective-permute-done.6.blue = bf16[384,128]{1,0:T(8,128)(2,1)S(1)} collective-permute-done((bf16[384,128]{1,0:T(8,128)(2,1)S(1)}, bf16[384,128]{1,0:T(8,128)(2,1)S(1)}, u32[]{:S(2)}, u32[]{:S(2)}) %collective-permute-start.6) | collective-permute-done | bytes 98336 | tf_op jit(solution)/shard_map/ppermute | solution.py:387
  26.8 0.0 collective-permute-done.7.red
  26.8 0.4 outer.4
  27.3 2.6 %collective-permute-start.8 = (bf16[384,128]{1,0:T(8,128)(2,1)S(1)}, bf16[384,128]{1,0:T(8,128)(2,1)S(1)}, u32[]{:S(2)}, u32[]{:S(2)}) collective-permute-start(bf16[384,128]{1,0:T(8,128)(2,1)S(1)} %get-tuple-element.50), channel_id=1, source_target_pairs={{0,31},{1,2},{2,1},{3,4},{4,3},{5,6},{6,5},{7,8},{8,7},{9,10},{10,... | collective-permute-start | bytes 294920 | tf_op jit(solution)/shard_map/ppermute | solution.py:387
  29.9 0.0 collective-permute-start.9
  29.9 0.3 inner.3.part
  30.2 4.7 %collective-permute-done.8.blue = bf16[384,128]{1,0:T(8,128)(2,1)S(1)} collective-permute-done((bf16[384,128]{1,0:T(8,128)(2,1)S(1)}, bf16[384,128]{1,0:T(8,128)(2,1)S(1)}, u32[]{:S(2)}, u32[]{:S(2)}) %collective-permute-start.8) | collective-permute-done | bytes 98336 | tf_op jit(solution)/shard_map/ppermute | solution.py:387
  35.0 0.0 collective-permute-done.9.red
  35.0 0.4 outer.5
  35.4 2.6 %collective-permute-start.10 = (bf16[384,128]{1,0:T(8,128)(2,1)S(1)}, bf16[384,128]{1,0:T(8,128)(2,1)S(1)}, u32[]{:S(2)}, u32[]{:S(2)}) collective-permute-start(bf16[384,128]{1,0:T(8,128)(2,1)S(1)} %get-tuple-element.55), channel_id=1, source_target_pairs={{0,31},{1,2},{2,1},{3,4},{4,3},{5,6},{6,5},{7,8},{8,7},{9,10},{10,... | collective-permute-start | bytes 294920 | tf_op jit(solution)/shard_map/ppermute | solution.py:387
  38.0 0.7 %copy-done.7 = f32[5]{0:T(128)S(1)} copy-done((f32[5]{0:T(128)S(1)}, f32[5]{0:T(128)}, u32[]{:S(2)}) %copy-start.7) | copy-done | bytes 44
  38.7 0.9 %mix.1 = (f32[128,512]{1,0:T(8,128)S(1)}, f32[8,128]{1,0:T(8,128)S(1)}) custom-call(f32[5]{0:T(128)S(1)} %copy-done.7, bf16[2,256,1024]{2,1,0:T(8,128)(2,1)S(1)} %spill.1.band, f32[512,128]{1,0:T(8,128)S(1)} %get-tuple-element.43.now.before.t0, f32[512,128]{1,0:T(8,128)S(1)} %get-tuple-element.46.now.before.t1, f32[512,128]{1,0:T(8,128)S(1)} %get-tuple-element.49.now.t2, ...), custom_call_target="tpu_custom_call" | custom-call | flops 1000000000 | tf_op jit(solution)/shard_map/mix/pallas_call | solution.py:362
  39.6 3.5 %collective-permute-done.10.blue = bf16[384,128]{1,0:T(8,128)(2,1)S(1)} collective-permute-done((bf16[384,128]{1,0:T(8,128)(2,1)S(1)}, bf16[384,128]{1,0:T(8,128)(2,1)S(1)}, u32[]{:S(2)}, u32[]{:S(2)}) %collective-permute-start.10) | collective-permute-done | bytes 98336 | tf_op jit(solution)/shard_map/ppermute | solution.py:387
  43.1 0.5 last.1
  43.6 0.1 collective-permute-start.12
  43.7 0.1 collective-permute-start.13
  43.8 1.8 %collective-permute-start.14 = (bf16[32,512]{1,0:T(8,128)(2,1)S(1)}, bf16[32,512]{1,0:T(8,128)(2,1)S(1)}, u32[]{:S(2)}, u32[]{:S(2)}) collective-permute-start(bf16[32,512]{1,0:T(8,128)(2,1)S(1)} %get-tuple-element.60), channel_id=1, source_target_pairs={{0,3},{1,2},{2,1},{3,0},{4,7},{5,6},{6,5},{7,4},{8,11},{9,10},{10,... | collective-permute-start | bytes 98312 | tf_op jit(solution)/shard_map/ppermute | solution.py:393
  45.5 2.3 %collective-permute-done.13.p2 = bf16[32,512]{1,0:T(8,128)(2,1)S(1)} collective-permute-done((bf16[32,512]{1,0:T(8,128)(2,1)S(1)}, bf16[32,512]{1,0:T(8,128)(2,1)S(1)}, u32[]{:S(2)}, u32[]{:S(2)}) %collective-permute-start.13) | collective-permute-done | bytes 32800 | tf_op jit(solution)/shard_map/ppermute | solution.py:393
  47.8 0.0 collective-permute-done.14.p3
  47.8 0.7 %join.1 = f32[32,2048]{1,0:T(8,128)} custom-call(bf16[32,512]{1,0:T(8,128)(2,1)S(1)} %get-tuple-element.57.p0, bf16[32,512]{1,0:T(8,128)(2,1)S(1)} %collective-permute-done.12.p1, bf16[32,512]{1,0:T(8,128)(2,1)S(1)} %collective-permute-done.13.p2, bf16[32,512]{1,0:T(8,128)(2,1)S(1)} %collective-permute-done.14.p3), custom_call_target="tpu_custom_call" | custom-call | flops 1000000000 | tf_op jit(solution)/shard_map/join/pallas_call | solution.py:362
  (14 shorter events, 0.0 us)
Async XLA Ops:
  2.0 8.6 %collective-permute-start = (bf16[400,256]{1,0:T(8,128)(2,1)}, bf16[400,256]{1,0:T(8,128)(2,1)S(1)}, u32[]{:S(2)}, u32[]{:S(2)}) collective-permute-start(bf16[400,256]{1,0:T(8,128)(2,1)} %get-tuple-element.33), channel_id=1, source_target_pairs={{0,1},{1,0},{2,3},{3,2},{4,5},{5,4},{6,7},{7,6},{8,9},{9,8},{10,11... | collective-permute-start | bytes 614408 | tf_op jit(solution)/shard_map/ppermute | solution.py:416
  2.5 8.0 %collective-permute-start.2 = (bf16[32,512]{1,0:T(8,128)(2,1)}, bf16[32,512]{1,0:T(8,128)(2,1)S(1)}, u32[]{:S(2)}, u32[]{:S(2)}) collective-permute-start(bf16[32,512]{1,0:T(8,128)(2,1)} %get-tuple-element.36), channel_id=1, source_target_pairs={{0,3},{1,2},{2,1},{3,0},{4,7},{5,6},{6,5},{7,4},{8,11},{9,10},{10,... | collective-permute-start | bytes 98312 | tf_op jit(solution)/shard_map/ppermute | solution.py:414
  5.2 5.4 %collective-permute-start.1 = (bf16[32,512]{1,0:T(8,128)(2,1)}, bf16[32,512]{1,0:T(8,128)(2,1)S(1)}, u32[]{:S(2)}, u32[]{:S(2)}) collective-permute-start(bf16[32,512]{1,0:T(8,128)(2,1)} %get-tuple-element.35), channel_id=1, source_target_pairs={{0,2},{1,3},{2,0},{3,1},{4,6},{5,7},{6,4},{7,5},{8,10},{9,11},{10,... | collective-permute-start | bytes 98312 | tf_op jit(solution)/shard_map/ppermute | solution.py:415
  5.2 5.4 %copy-start.8 = (bf16[32,512]{1,0:T(8,128)(2,1)S(1)}, bf16[32,512]{1,0:T(8,128)(2,1)}, u32[]{:S(2)}) copy-start(bf16[32,512]{1,0:T(8,128)(2,1)} %get-tuple-element.34.p0) | copy-start | bytes 98308
  5.2 10.9 %collective-permute-start.3 = (bf16[336,256]{1,0:T(8,128)(2,1)}, bf16[336,256]{1,0:T(8,128)(2,1)S(1)}, u32[]{:S(2)}, u32[]{:S(2)}) collective-permute-start(bf16[336,256]{1,0:T(8,128)(2,1)} %get-tuple-element.39), channel_id=1, source_target_pairs={{0,31},{1,2},{2,1},{3,4},{4,3},{5,6},{6,5},{7,8},{8,7},{9,10},{10,... | collective-permute-start | bytes 516104 | tf_op jit(solution)/shard_map/ppermute | solution.py:417
  10.6 2.6 %copy-start = (bf16[1280,256]{1,0:T(8,128)(2,1)S(1)}, bf16[1280,256]{1,0:T(8,128)(2,1)}, u32[]{:S(2)}) copy-start(bf16[1280,256]{1,0:T(8,128)(2,1)} %feat.3) | copy-start | bytes 1966084
  10.6 2.5 %copy-start.1 = (bf16[256,512]{1,0:T(8,128)(2,1)S(1)}, bf16[256,512]{1,0:T(8,128)(2,1)}, u32[]{:S(2)}) copy-start(bf16[256,512]{1,0:T(8,128)(2,1)} %w_in.1) | copy-start | bytes 786436
  10.6 2.5 %copy-start.2 = (bf16[256,256]{1,0:T(8,128)(2,1)S(1)}, bf16[256,256]{1,0:T(8,128)(2,1)}, u32[]{:S(2)}) copy-start(bf16[256,256]{1,0:T(8,128)(2,1)} %w_out.1) | copy-start | bytes 393220
  10.6 2.5 %copy-start.3 = (s32[1280]{0:T(1024)S(1)}, s32[1280]{0:T(1024)}, u32[]{:S(2)}) copy-start(s32[1280]{0:T(1024)} %param.10) | copy-start | bytes 15364
  10.7 2.5 %copy-start.4 = (s32[1280]{0:T(1024)S(1)}, s32[1280]{0:T(1024)}, u32[]{:S(2)}) copy-start(s32[1280]{0:T(1024)} %param.11) | copy-start | bytes 15364
  10.7 2.5 %copy-start.5 = (s32[1280]{0:T(1024)S(1)}, s32[1280]{0:T(1024)}, u32[]{:S(2)}) copy-start(s32[1280]{0:T(1024)} %param.12) | copy-start | bytes 15364
  10.9 2.3 %copy-start.6 = (bf16[3,512]{1,0:T(4,128)(2,1)S(1)}, bf16[3,512]{1,0:T(4,128)(2,1)}, u32[]{:S(2)}) copy-start(bf16[3,512]{1,0:T(4,128)(2,1)} %cell_bias.1) | copy-start | bytes 9220
  10.9 7.7 %collective-permute-start.4 = (bf16[384,128]{1,0:T(8,128)(2,1)S(1)}, bf16[384,128]{1,0:T(8,128)(2,1)S(1)}, u32[]{:S(2)}, u32[]{:S(2)}) collective-permute-start(bf16[384,128]{1,0:T(8,128)(2,1)S(1)} %get-tuple-element.44), channel_id=1, source_target_pairs={{0,31},{1,2},{2,1},{3,4},{4,3},{5,6},{6,5},{7,8},{8,7},{9,10},{10,... | collective-permute-start | bytes 294920 | tf_op jit(solution)/shard_map/ppermute | solution.py:387
  13.2 5.4 %collective-permute-start.5 = (bf16[384,128]{1,0:T(8,128)(2,1)S(1)}, bf16[384,128]{1,0:T(8,128)(2,1)S(1)}, u32[]{:S(2)}, u32[]{:S(2)}) collective-permute-start(bf16[384,128]{1,0:T(8,128)(2,1)S(1)} %get-tuple-element.45), channel_id=1, source_target_pairs={{0,1},{1,0},{2,3},{3,2},{4,5},{5,4},{6,7},{7,6},{8,9},{9,8},{10,11... | collective-permute-start | bytes 294920 | tf_op jit(solution)/shard_map/ppermute | solution.py:388
  19.0 7.8 %collective-permute-start.6 = (bf16[384,128]{1,0:T(8,128)(2,1)S(1)}, bf16[384,128]{1,0:T(8,128)(2,1)S(1)}, u32[]{:S(2)}, u32[]{:S(2)}) collective-permute-start(bf16[384,128]{1,0:T(8,128)(2,1)S(1)} %get-tuple-element.47), channel_id=1, source_target_pairs={{0,31},{1,2},{2,1},{3,4},{4,3},{5,6},{6,5},{7,8},{8,7},{9,10},{10,... | collective-permute-start | bytes 294920 | tf_op jit(solution)/shard_map/ppermute | solution.py:387
  21.7 5.1 %collective-permute-start.7 = (bf16[384,128]{1,0:T(8,128)(2,1)S(1)}, bf16[384,128]{1,0:T(8,128)(2,1)S(1)}, u32[]{:S(2)}, u32[]{:S(2)}) collective-permute-start(bf16[384,128]{1,0:T(8,128)(2,1)S(1)} %get-tuple-element.48), channel_id=1, source_target_pairs={{0,1},{1,0},{2,3},{3,2},{4,5},{5,4},{6,7},{7,6},{8,9},{9,8},{10,11... | collective-permute-start | bytes 294920 | tf_op jit(solution)/shard_map/ppermute | solution.py:388
  27.3 7.7 %collective-permute-start.8 = (bf16[384,128]{1,0:T(8,128)(2,1)S(1)}, bf16[384,128]{1,0:T(8,128)(2,1)S(1)}, u32[]{:S(2)}, u32[]{:S(2)}) collective-permute-start(bf16[384,128]{1,0:T(8,128)(2,1)S(1)} %get-tuple-element.50), channel_id=1, source_target_pairs={{0,31},{1,2},{2,1},{3,4},{4,3},{5,6},{6,5},{7,8},{8,7},{9,10},{10,... | collective-permute-start | bytes 294920 | tf_op jit(solution)/shard_map/ppermute | solution.py:387
  29.9 5.1 %collective-permute-start.9 = (bf16[384,128]{1,0:T(8,128)(2,1)S(1)}, bf16[384,128]{1,0:T(8,128)(2,1)S(1)}, u32[]{:S(2)}, u32[]{:S(2)}) collective-permute-start(bf16[384,128]{1,0:T(8,128)(2,1)S(1)} %get-tuple-element.51), channel_id=1, source_target_pairs={{0,1},{1,0},{2,3},{3,2},{4,5},{5,4},{6,7},{7,6},{8,9},{9,8},{10,11... | collective-permute-start | bytes 294920 | tf_op jit(solution)/shard_map/ppermute | solution.py:388
  35.4 7.7 %collective-permute-start.10 = (bf16[384,128]{1,0:T(8,128)(2,1)S(1)}, bf16[384,128]{1,0:T(8,128)(2,1)S(1)}, u32[]{:S(2)}, u32[]{:S(2)}) collective-permute-start(bf16[384,128]{1,0:T(8,128)(2,1)S(1)} %get-tuple-element.55), channel_id=1, source_target_pairs={{0,31},{1,2},{2,1},{3,4},{4,3},{5,6},{6,5},{7,8},{8,7},{9,10},{10,... | collective-permute-start | bytes 294920 | tf_op jit(solution)/shard_map/ppermute | solution.py:387
  38.0 0.7 %copy-start.7 = (f32[5]{0:T(128)S(1)}, f32[5]{0:T(128)}, u32[]{:S(2)}) copy-start(f32[5]{0:T(128)} %coef.1) | copy-start | bytes 64
  38.0 5.1 %collective-permute-start.11 = (bf16[384,128]{1,0:T(8,128)(2,1)S(1)}, bf16[384,128]{1,0:T(8,128)(2,1)S(1)}, u32[]{:S(2)}, u32[]{:S(2)}) collective-permute-start(bf16[384,128]{1,0:T(8,128)(2,1)S(1)} %get-tuple-element.56), channel_id=1, source_target_pairs={{0,1},{1,0},{2,3},{3,2},{4,5},{5,4},{6,7},{7,6},{8,9},{9,8},{10,11... | collective-permute-start | bytes 294920 | tf_op jit(solution)/shard_map/ppermute | solution.py:388
  43.6 1.9 %collective-permute-start.12 = (bf16[32,512]{1,0:T(8,128)(2,1)S(1)}, bf16[32,512]{1,0:T(8,128)(2,1)S(1)}, u32[]{:S(2)}, u32[]{:S(2)}) collective-permute-start(bf16[32,512]{1,0:T(8,128)(2,1)S(1)} %get-tuple-element.58), channel_id=1, source_target_pairs={{0,1},{1,0},{2,3},{3,2},{4,5},{5,4},{6,7},{7,6},{8,9},{9,8},{10,11... | collective-permute-start | bytes 98312 | tf_op jit(solution)/shard_map/ppermute | solution.py:393
  43.7 4.2 %collective-permute-start.13 = (bf16[32,512]{1,0:T(8,128)(2,1)S(1)}, bf16[32,512]{1,0:T(8,128)(2,1)S(1)}, u32[]{:S(2)}, u32[]{:S(2)}) collective-permute-start(bf16[32,512]{1,0:T(8,128)(2,1)S(1)} %get-tuple-element.59), channel_id=1, source_target_pairs={{0,2},{1,3},{2,0},{3,1},{4,6},{5,7},{6,4},{7,5},{8,10},{9,11},{10,... | collective-permute-start | bytes 98312 | tf_op jit(solution)/shard_map/ppermute | solution.py:393
  43.8 4.1 %collective-permute-start.14 = (bf16[32,512]{1,0:T(8,128)(2,1)S(1)}, bf16[32,512]{1,0:T(8,128)(2,1)S(1)}, u32[]{:S(2)}, u32[]{:S(2)}) collective-permute-start(bf16[32,512]{1,0:T(8,128)(2,1)S(1)} %get-tuple-element.60), channel_id=1, source_target_pairs={{0,3},{1,2},{2,1},{3,0},{4,7},{5,6},{6,5},{7,4},{8,11},{9,10},{10,... | collective-permute-start | bytes 98312 | tf_op jit(solution)/shard_map/ppermute | solution.py:393

commit v14 on v13

--- a/solution.py
+++ b/solution.py
@@ -53,27 +53,50 @@
 
 
 def prep_kernel(
-    vec_hbm, feat, src_hbm, dst_hbm, cell_hbm, p0, p2, p3, blue, red, vectors, src, dst, cell, sems
+    vec_hbm,
+    feat,
+    src_hbm,
+    dst_hbm,
+    cell_hbm,
+    p0,
+    p2,
+    p3,
+    blue,
+    red,
+    vectors,
+    halves,
+    sends,
+    msgs,
+    src,
+    dst,
+    cell,
+    sems,
+    out_sems,
 ):
     member, side = lax.axis_index("edges"), device_side()
-    pieces = (p0, None, p2, p3)
+    high_rows, width = p0.shape
+    nfeat = feat.shape[1]
+    lists = [
+        pltpu.make_async_copy(x, y, sems.at[6 + n])
+        for n, (x, y) in enumerate(((src_hbm, src), (dst_hbm, dst), (cell_hbm, cell)))
+    ]
     loads = []
-    high_rows, width = p0.shape
     for k in range(4):
         at = pl.multiple_of((member ^ k) * width, width)
         loads.append(pltpu.make_async_copy(vec_hbm.at[:, pl.ds(at, width)], vectors.at[k], sems.at[k]))
     high = feat.shape[0] - SPILL
     off = pl.multiple_of(side * high, 64)
     copies = [
-        pltpu.make_async_copy(feat.at[pl.ds(off, SPILL)], blue.at[pl.ds(0, SPILL)], sems.at[4]),
-        pltpu.make_async_copy(
-            feat.at[pl.ds(pl.multiple_of(high - off, 64), SPILL)], red.at[pl.ds(0, SPILL)], sems.at[5]
-        ),
+        pltpu.make_async_copy(feat.at[pl.ds(off, SPILL)], halves.at[0], sems.at[4]),
+        pltpu.make_async_copy(feat.at[pl.ds(pl.multiple_of(high - off, 64), SPILL)], halves.at[1], sems.at[5]),
     ]
-    lists = [
-        pltpu.make_async_copy(x, y, sems.at[6 + n])
-        for n, (x, y) in enumerate(((src_hbm, src), (dst_hbm, dst), (cell_hbm, cell)))
-    ]
+    outs = []
+
+    def send(x, y):
+        copy = pltpu.make_async_copy(x, y, out_sems.at[len(outs)])
+        copy.start()
+        outs.append(copy)
+
     for copy in lists + loads + copies:
         copy.start()
     for copy in lists:
@@ -89,21 +112,25 @@
     low_ids = jnp.concatenate(starts + [pad], axis=0)
     high_ids = jnp.concatenate(ends + [pad], axis=0)
     none = jnp.zeros((ID_ROWS, 128), BF)
-    for msg, ids_of in (
-        (blue, jnp.where(side == 0, low_ids, high_ids)),
-        (red, jnp.where(side == 0, high_ids, low_ids)),
-    ):
-        msg[SPILL : SPILL + ID_ROWS, 0:128] = ids_of.astype(BF)
-        msg[SPILL : SPILL + ID_ROWS, 128:256] = none
-    for k, piece in enumerate(pieces):
+    for n, ids_of in enumerate((jnp.where(side == 0, low_ids, high_ids), jnp.where(side == 0, high_ids, low_ids))):
+        msgs[n, 0:ID_ROWS, 0:128] = ids_of.astype(BF)
+        msgs[n, 0:ID_ROWS, 128:256] = none
+    send(msgs.at[0, pl.ds(0, ID_ROWS)], blue.at[pl.ds(SPILL, ID_ROWS)])
+    for k in (3, 2, 1, 0):
         loads[k].wait()
         if k == 1:
-            for n in range(width // red.shape[1]):
-                at = SPILL + ID_ROWS + n * high_rows
-                red[at : at + high_rows, :] = vectors[k, :, n * red.shape[1] : (n + 1) * red.shape[1]].astype(BF)
+            for n in range(width // nfeat):
+                at = ID_ROWS + n * high_rows
+                msgs[1, at : at + high_rows, :] = vectors[k, :, n * nfeat : (n + 1) * nfeat].astype(BF)
+            rest = red.shape[0] - SPILL
+            send(msgs.at[1, pl.ds(0, rest)], red.at[pl.ds(SPILL, rest)])
         else:
-            piece[...] = vectors[k].astype(BF)
-    for copy in copies:
+            sends[k] = vectors[k].astype(BF)
+            send(sends.at[k], {0: p0, 2: p2, 3: p3}[k])
+    for n, msg in ((1, red), (0, blue)):
+        copies[n].wait()
+        send(halves.at[n], msg.at[pl.ds(0, SPILL)])
+    for copy in outs:
         copy.wait()
 
 
@@ -402,13 +429,19 @@
         prep_kernel,
         "prep",
         (piece,) * 3 + (msg, near_msg),
-        [pltpu.VMEM((nedge, high, nrow), F32)]
+        [
+            pltpu.VMEM((nedge, high, nrow), F32),
+            pltpu.VMEM((2, SPILL, nfeat), BF),
+            pltpu.VMEM((nedge, high, nrow), BF),
+            pltpu.VMEM((2, near_msg.shape[0] - SPILL, nfeat), BF),
+        ]
         + [pltpu.VMEM(lines, jnp.int32)] * 3
-        + [pltpu.SemaphoreType.DMA((9,))],
+        + [pltpu.SemaphoreType.DMA((9,)), pltpu.SemaphoreType.DMA((7,))],
         vectors,
         features,
         *edges,
         in_hbm=range(5),
+        out_hbm=range(5),
         limit=FULL,
     )
     across = lax.ppermute(across, "edges", [(i, i ^ 3) for i in range(nedge)])

time: 48.8 us -> 48.8 us (level)
  no operation moved by 1% of the time
where the time goes in v14:
time: 48.8 us; the launch traced here: 48.6 us
  starting transfers between devices  20.7 us (42%)
  waiting for transfers between devices  15.9 us (33%)
  Pallas kernels  11.1 us (23%)
  local copies, waits for them, and re-layouts  0.7 us (1%)
    ppermute x4, waiting for transfers between devices, swap(): lax.ppermute(first, axes, blue_pairs)  13.6 us
    pallas_call x14, Pallas kernels, call(): pl.pallas_call(kernel, name=name, out_shape=outs, in_specs=spaces, out_sp...  11.1 us
    ppermute x4, starting transfers between devices, swap(): lax.ppermute(first, axes, blue_pairs)  10.2 us
    ppermute x1, starting transfers between devices, per_device(): blue_msg = lax.ppermute(blue_msg, axes, blue_pairs)  5.37 us
    ppermute x1, starting transfers between devices, per_device(): across = lax.ppermute(across, 'edges', [(i, i ^ 3) for i in range(nedge)])  2.61 us
    ppermute x3, waiting for transfers between devices, exchange(): lax.ppermute(pieces[k], 'edges', [(i, i ^ k) for i in range(nedge)])  2.3 us
    ppermute x3, starting transfers between devices, exchange(): lax.ppermute(pieces[k], 'edges', [(i, i ^ k) for i in range(nedge)])  1.93 us
  transfers between devices with their start and end apart: 15, of which 5 were waited for; matrix products, arithmetic and copies ran while one was open for 0% of the time, Pallas kernels for 14%

profile of v14, /device:TPU:0, one launch (start us, length us, event | category | flops | bytes accessed | tf_op | source)
XLA Modules:
  0.0 48.6 jit_solution(18319644865464186582)
XLA Ops:
  0.0 2.0 %prep.1 = (bf16[32,512]{1,0:T(8,128)(2,1)}, bf16[32,512]{1,0:T(8,128)(2,1)}, bf16[32,512]{1,0:T(8,128)(2,1)}, bf16[336,256]{1,0:T(8,128)(2,1)}, bf16[400,256]{1,0:T(8,128)(2,1)}) custom-call(f32[32,2048]{1,0:T(8,128)} %vec_hbm.1, bf16[1280,256]{1,0:T(8,128)(2,1)} %feat.3, s32[10,128]{1,0:T(8,128)} %bitcast.3, s32[10,128]{1,0:T(8,128)} %bitcast.5, ...), custom_call_target="tpu_custom_call" | custom-call | flops 1000000000 | tf_op jit(solution)/shard_map/prep/pallas_call | solution.py:389
  2.0 0.5 %collective-permute-start = (bf16[400,256]{1,0:T(8,128)(2,1)}, bf16[400,256]{1,0:T(8,128)(2,1)S(1)}, u32[]{:S(2)}, u32[]{:S(2)}) collective-permute-start(bf16[400,256]{1,0:T(8,128)(2,1)} %get-tuple-element.33), channel_id=1, source_target_pairs={{0,1},{1,0},{2,3},{3,2},{4,5},{5,4},{6,7},{7,6},{8,9},{9,8},{10,11... | collective-permute-start | bytes 614408 | tf_op jit(solution)/shard_map/ppermute | solution.py:449
  2.6 2.6 %collective-permute-start.2 = (bf16[32,512]{1,0:T(8,128)(2,1)}, bf16[32,512]{1,0:T(8,128)(2,1)S(1)}, u32[]{:S(2)}, u32[]{:S(2)}) collective-permute-start(bf16[32,512]{1,0:T(8,128)(2,1)} %get-tuple-element.36), channel_id=1, source_target_pairs={{0,3},{1,2},{2,1},{3,0},{4,7},{5,6},{6,5},{7,4},{8,11},{9,10},{10,... | collective-permute-start | bytes 98312 | tf_op jit(solution)/shard_map/ppermute | solution.py:447
  5.2 0.0 collective-permute-start.1
  5.2 5.4 %collective-permute-start.3 = (bf16[336,256]{1,0:T(8,128)(2,1)}, bf16[336,256]{1,0:T(8,128)(2,1)S(1)}, u32[]{:S(2)}, u32[]{:S(2)}) collective-permute-start(bf16[336,256]{1,0:T(8,128)(2,1)} %get-tuple-element.39), channel_id=1, source_target_pairs={{0,31},{1,2},{2,1},{3,4},{4,3},{5,6},{6,5},{7,8},{8,7},{9,10},{10,... | collective-permute-start | bytes 516104 | tf_op jit(solution)/shard_map/ppermute | solution.py:450
  10.6 0.0 collective-permute-done.2.x
  10.6 0.0 collective-permute-done.1.p2
  10.6 0.0 collective-permute-done.near
  10.6 0.0 copy-start
  10.6 0.0 copy-start.1
  10.6 0.0 copy-start.2
  10.7 0.0 copy-start.3
  10.7 0.0 copy-start.4
  10.7 0.0 copy-start.5
  10.7 0.2 field.1
  10.9 0.0 copy-start.6
  10.9 2.3 %collective-permute-start.4 = (bf16[384,128]{1,0:T(8,128)(2,1)S(1)}, bf16[384,128]{1,0:T(8,128)(2,1)S(1)}, u32[]{:S(2)}, u32[]{:S(2)}) collective-permute-start(bf16[384,128]{1,0:T(8,128)(2,1)S(1)} %get-tuple-element.44), channel_id=1, source_target_pairs={{0,31},{1,2},{2,1},{3,4},{4,3},{5,6},{6,5},{7,8},{8,7},{9,10},{10,... | collective-permute-start | bytes 294920 | tf_op jit(solution)/shard_map/ppermute | solution.py:414
  13.2 0.0 collective-permute-start.5
  13.2 2.9 %own.1 = (bf16[2,256,1024]{2,1,0:T(8,128)(2,1)S(1)}, bf16[512,256]{1,0:T(8,128)(2,1)S(1)}, bf16[512,8]{1,0:T(8,128)(2,1)S(1)}, bf16[256,256]{1,0:T(8,128)(2,1)S(1)}) custom-call(bf16[1280,256]{1,0:T(8,128)(2,1)S(1)} %copy-done, s32[10,128]{1,0:T(8,128)S(1)} %bitcast.4, s32[10,128]{1,0:T(8,128)S(1)} %bitcast.6, s32[10,128]{1,0:T(8,128)S(1)} %bitcast.8, ...), custom_call_target="tpu_custom_call" | custom-call | flops 4000000000 | tf_op jit(solution)/shard_map/own/pallas_call | solution.py:389
  16.2 0.0 collective-permute-done.3.blue
  16.2 1.5 %spill.1.band = bf16[2,256,1024]{2,1,0:T(8,128)(2,1)S(1)} custom-call(bf16[2,256,1024]{2,1,0:T(8,128)(2,1)S(1)} %get-tuple-element.38.own_band, bf16[336,256]{1,0:T(8,128)(2,1)S(1)} %collective-permute-done.3.blue, bf16[512,256]{1,0:T(8,128)(2,1)S(1)} %get-tuple-element.40.w_in_t, ...), custom_call_target="tpu_custom_call", output_to_operand_aliasing={{}: (0, {})} | custom-call | tf_op jit(solution)/shard_map/spill/pallas_call | solution.py:389
  17.7 0.3 start.1.part
  18.0 0.6 %collective-permute-done.4.blue = bf16[384,128]{1,0:T(8,128)(2,1)S(1)} collective-permute-done((bf16[384,128]{1,0:T(8,128)(2,1)S(1)}, bf16[384,128]{1,0:T(8,128)(2,1)S(1)}, u32[]{:S(2)}, u32[]{:S(2)}) %collective-permute-start.4) | collective-permute-done | bytes 98336 | tf_op jit(solution)/shard_map/ppermute | solution.py:414
  18.6 0.0 collective-permute-done.5.red
  18.6 0.4 outer.3
  19.1 2.7 %collective-permute-start.6 = (bf16[384,128]{1,0:T(8,128)(2,1)S(1)}, bf16[384,128]{1,0:T(8,128)(2,1)S(1)}, u32[]{:S(2)}, u32[]{:S(2)}) collective-permute-start(bf16[384,128]{1,0:T(8,128)(2,1)S(1)} %get-tuple-element.47), channel_id=1, source_target_pairs={{0,31},{1,2},{2,1},{3,4},{4,3},{5,6},{6,5},{7,8},{8,7},{9,10},{10,... | collective-permute-start | bytes 294920 | tf_op jit(solution)/shard_map/ppermute | solution.py:414
  21.7 0.0 collective-permute-start.7
  21.7 0.3 inner.2.part
  22.1 4.8 %collective-permute-done.6.blue = bf16[384,128]{1,0:T(8,128)(2,1)S(1)} collective-permute-done((bf16[384,128]{1,0:T(8,128)(2,1)S(1)}, bf16[384,128]{1,0:T(8,128)(2,1)S(1)}, u32[]{:S(2)}, u32[]{:S(2)}) %collective-permute-start.6) | collective-permute-done | bytes 98336 | tf_op jit(solution)/shard_map/ppermute | solution.py:414
  26.8 0.0 collective-permute-done.7.red
  26.8 0.4 outer.4
  27.3 2.6 %collective-permute-start.8 = (bf16[384,128]{1,0:T(8,128)(2,1)S(1)}, bf16[384,128]{1,0:T(8,128)(2,1)S(1)}, u32[]{:S(2)}, u32[]{:S(2)}) collective-permute-start(bf16[384,128]{1,0:T(8,128)(2,1)S(1)} %get-tuple-element.50), channel_id=1, source_target_pairs={{0,31},{1,2},{2,1},{3,4},{4,3},{5,6},{6,5},{7,8},{8,7},{9,10},{10,... | collective-permute-start | bytes 294920 | tf_op jit(solution)/shard_map/ppermute | solution.py:414
  29.9 0.0 collective-permute-start.9
  29.9 0.3 inner.3.part
  30.3 4.7 %collective-permute-done.8.blue = bf16[384,128]{1,0:T(8,128)(2,1)S(1)} collective-permute-done((bf16[384,128]{1,0:T(8,128)(2,1)S(1)}, bf16[384,128]{1,0:T(8,128)(2,1)S(1)}, u32[]{:S(2)}, u32[]{:S(2)}) %collective-permute-start.8) | collective-permute-done | bytes 98336 | tf_op jit(solution)/shard_map/ppermute | solution.py:414
  35.0 0.0 collective-permute-done.9.red
  35.0 0.4 outer.5
  35.4 2.6 %collective-permute-start.10 = (bf16[384,128]{1,0:T(8,128)(2,1)S(1)}, bf16[384,128]{1,0:T(8,128)(2,1)S(1)}, u32[]{:S(2)}, u32[]{:S(2)}) collective-permute-start(bf16[384,128]{1,0:T(8,128)(2,1)S(1)} %get-tuple-element.55), channel_id=1, source_target_pairs={{0,31},{1,2},{2,1},{3,4},{4,3},{5,6},{6,5},{7,8},{8,7},{9,10},{10,... | collective-permute-start | bytes 294920 | tf_op jit(solution)/shard_map/ppermute | solution.py:414
  38.1 0.7 %copy-done.7 = f32[5]{0:T(128)S(1)} copy-done((f32[5]{0:T(128)S(1)}, f32[5]{0:T(128)}, u32[]{:S(2)}) %copy-start.7) | copy-done | bytes 44
  38.7 0.9 %mix.1 = (f32[128,512]{1,0:T(8,128)S(1)}, f32[8,128]{1,0:T(8,128)S(1)}) custom-call(f32[5]{0:T(128)S(1)} %copy-done.7, bf16[2,256,1024]{2,1,0:T(8,128)(2,1)S(1)} %spill.1.band, f32[512,128]{1,0:T(8,128)S(1)} %get-tuple-element.43.now.before.t0, f32[512,128]{1,0:T(8,128)S(1)} %get-tuple-element.46.now.before.t1, f32[512,128]{1,0:T(8,128)S(1)} %get-tuple-element.49.now.t2, ...), custom_call_target="tpu_custom_call" | custom-call | flops 1000000000 | tf_op jit(solution)/shard_map/mix/pallas_call | solution.py:389
  39.7 3.5 %collective-permute-done.10.blue = bf16[384,128]{1,0:T(8,128)(2,1)S(1)} collective-permute-done((bf16[384,128]{1,0:T(8,128)(2,1)S(1)}, bf16[384,128]{1,0:T(8,128)(2,1)S(1)}, u32[]{:S(2)}, u32[]{:S(2)}) %collective-permute-start.10) | collective-permute-done | bytes 98336 | tf_op jit(solution)/shard_map/ppermute | solution.py:414
  43.1 0.5 last.1
  43.6 0.1 collective-permute-start.12
  43.7 0.1 collective-permute-start.13
  43.8 1.8 %collective-permute-start.14 = (bf16[32,512]{1,0:T(8,128)(2,1)S(1)}, bf16[32,512]{1,0:T(8,128)(2,1)S(1)}, u32[]{:S(2)}, u32[]{:S(2)}) collective-permute-start(bf16[32,512]{1,0:T(8,128)(2,1)S(1)} %get-tuple-element.60), channel_id=1, source_target_pairs={{0,3},{1,2},{2,1},{3,0},{4,7},{5,6},{6,5},{7,4},{8,11},{9,10},{10,... | collective-permute-start | bytes 98312 | tf_op jit(solution)/shard_map/ppermute | solution.py:420
  45.6 0.0 collective-permute-done.12.p1
  45.6 2.3 %collective-permute-done.13.p2 = bf16[32,512]{1,0:T(8,128)(2,1)S(1)} collective-permute-done((bf16[32,512]{1,0:T(8,128)(2,1)S(1)}, bf16[32,512]{1,0:T(8,128)(2,1)S(1)}, u32[]{:S(2)}, u32[]{:S(2)}) %collective-permute-start.13) | collective-permute-done | bytes 32800 | tf_op jit(solution)/shard_map/ppermute | solution.py:420
  47.9 0.7 %join.1 = f32[32,2048]{1,0:T(8,128)} custom-call(bf16[32,512]{1,0:T(8,128)(2,1)S(1)} %get-tuple-element.57.p0, bf16[32,512]{1,0:T(8,128)(2,1)S(1)} %collective-permute-done.12.p1, bf16[32,512]{1,0:T(8,128)(2,1)S(1)} %collective-permute-done.13.p2, bf16[32,512]{1,0:T(8,128)(2,1)S(1)} %collective-permute-done.14.p3), custom_call_target="tpu_custom_call" | custom-call | flops 1000000000 | tf_op jit(solution)/shard_map/join/pallas_call | solution.py:389
  (14 shorter events, 0.0 us)
Async XLA Ops:
  2.0 8.6 %collective-permute-start = (bf16[400,256]{1,0:T(8,128)(2,1)}, bf16[400,256]{1,0:T(8,128)(2,1)S(1)}, u32[]{:S(2)}, u32[]{:S(2)}) collective-permute-start(bf16[400,256]{1,0:T(8,128)(2,1)} %get-tuple-element.33), channel_id=1, source_target_pairs={{0,1},{1,0},{2,3},{3,2},{4,5},{5,4},{6,7},{7,6},{8,9},{9,8},{10,11... | collective-permute-start | bytes 614408 | tf_op jit(solution)/shard_map/ppermute | solution.py:449
  2.6 8.0 %collective-permute-start.2 = (bf16[32,512]{1,0:T(8,128)(2,1)}, bf16[32,512]{1,0:T(8,128)(2,1)S(1)}, u32[]{:S(2)}, u32[]{:S(2)}) collective-permute-start(bf16[32,512]{1,0:T(8,128)(2,1)} %get-tuple-element.36), channel_id=1, source_target_pairs={{0,3},{1,2},{2,1},{3,0},{4,7},{5,6},{6,5},{7,4},{8,11},{9,10},{10,... | collective-permute-start | bytes 98312 | tf_op jit(solution)/shard_map/ppermute | solution.py:447
  5.2 5.4 %collective-permute-start.1 = (bf16[32,512]{1,0:T(8,128)(2,1)}, bf16[32,512]{1,0:T(8,128)(2,1)S(1)}, u32[]{:S(2)}, u32[]{:S(2)}) collective-permute-start(bf16[32,512]{1,0:T(8,128)(2,1)} %get-tuple-element.35), channel_id=1, source_target_pairs={{0,2},{1,3},{2,0},{3,1},{4,6},{5,7},{6,4},{7,5},{8,10},{9,11},{10,... | collective-permute-start | bytes 98312 | tf_op jit(solution)/shard_map/ppermute | solution.py:448
  5.2 5.4 %copy-start.8 = (bf16[32,512]{1,0:T(8,128)(2,1)S(1)}, bf16[32,512]{1,0:T(8,128)(2,1)}, u32[]{:S(2)}) copy-start(bf16[32,512]{1,0:T(8,128)(2,1)} %get-tuple-element.34.p0) | copy-start | bytes 98308
  5.2 10.9 %collective-permute-start.3 = (bf16[336,256]{1,0:T(8,128)(2,1)}, bf16[336,256]{1,0:T(8,128)(2,1)S(1)}, u32[]{:S(2)}, u32[]{:S(2)}) collective-permute-start(bf16[336,256]{1,0:T(8,128)(2,1)} %get-tuple-element.39), channel_id=1, source_target_pairs={{0,31},{1,2},{2,1},{3,4},{4,3},{5,6},{6,5},{7,8},{8,7},{9,10},{10,... | collective-permute-start | bytes 516104 | tf_op jit(solution)/shard_map/ppermute | solution.py:450
  10.6 2.6 %copy-start = (bf16[1280,256]{1,0:T(8,128)(2,1)S(1)}, bf16[1280,256]{1,0:T(8,128)(2,1)}, u32[]{:S(2)}) copy-start(bf16[1280,256]{1,0:T(8,128)(2,1)} %feat.3) | copy-start | bytes 1966084
  10.6 2.5 %copy-start.1 = (bf16[256,512]{1,0:T(8,128)(2,1)S(1)}, bf16[256,512]{1,0:T(8,128)(2,1)}, u32[]{:S(2)}) copy-start(bf16[256,512]{1,0:T(8,128)(2,1)} %w_in.1) | copy-start | bytes 786436
  10.6 2.5 %copy-start.2 = (bf16[256,256]{1,0:T(8,128)(2,1)S(1)}, bf16[256,256]{1,0:T(8,128)(2,1)}, u32[]{:S(2)}) copy-start(bf16[256,256]{1,0:T(8,128)(2,1)} %w_out.1) | copy-start | bytes 393220
  10.7 2.5 %copy-start.3 = (s32[1280]{0:T(1024)S(1)}, s32[1280]{0:T(1024)}, u32[]{:S(2)}) copy-start(s32[1280]{0:T(1024)} %param.10) | copy-start | bytes 15364
  10.7 2.5 %copy-start.4 = (s32[1280]{0:T(1024)S(1)}, s32[1280]{0:T(1024)}, u32[]{:S(2)}) copy-start(s32[1280]{0:T(1024)} %param.11) | copy-start | bytes 15364
  10.7 2.5 %copy-start.5 = (s32[1280]{0:T(1024)S(1)}, s32[1280]{0:T(1024)}, u32[]{:S(2)}) copy-start(s32[1280]{0:T(1024)} %param.12) | copy-start | bytes 15364
  10.9 2.3 %copy-start.6 = (bf16[3,512]{1,0:T(4,128)(2,1)S(1)}, bf16[3,512]{1,0:T(4,128)(2,1)}, u32[]{:S(2)}) copy-start(bf16[3,512]{1,0:T(4,128)(2,1)} %cell_bias.1) | copy-start | bytes 9220
  10.9 7.7 %collective-permute-start.4 = (bf16[384,128]{1,0:T(8,128)(2,1)S(1)}, bf16[384,128]{1,0:T(8,128)(2,1)S(1)}, u32[]{:S(2)}, u32[]{:S(2)}) collective-permute-start(bf16[384,128]{1,0:T(8,128)(2,1)S(1)} %get-tuple-element.44), channel_id=1, source_target_pairs={{0,31},{1,2},{2,1},{3,4},{4,3},{5,6},{6,5},{7,8},{8,7},{9,10},{10,... | collective-permute-start | bytes 294920 | tf_op jit(solution)/shard_map/ppermute | solution.py:414
  13.2 5.4 %collective-permute-start.5 = (bf16[384,128]{1,0:T(8,128)(2,1)S(1)}, bf16[384,128]{1,0:T(8,128)(2,1)S(1)}, u32[]{:S(2)}, u32[]{:S(2)}) collective-permute-start(bf16[384,128]{1,0:T(8,128)(2,1)S(1)} %get-tuple-element.45), channel_id=1, source_target_pairs={{0,1},{1,0},{2,3},{3,2},{4,5},{5,4},{6,7},{7,6},{8,9},{9,8},{10,11... | collective-permute-start | bytes 294920 | tf_op jit(solution)/shard_map/ppermute | solution.py:415
  19.1 7.8 %collective-permute-start.6 = (bf16[384,128]{1,0:T(8,128)(2,1)S(1)}, bf16[384,128]{1,0:T(8,128)(2,1)S(1)}, u32[]{:S(2)}, u32[]{:S(2)}) collective-permute-start(bf16[384,128]{1,0:T(8,128)(2,1)S(1)} %get-tuple-element.47), channel_id=1, source_target_pairs={{0,31},{1,2},{2,1},{3,4},{4,3},{5,6},{6,5},{7,8},{8,7},{9,10},{10,... | collective-permute-start | bytes 294920 | tf_op jit(solution)/shard_map/ppermute | solution.py:414
  21.7 5.1 %collective-permute-start.7 = (bf16[384,128]{1,0:T(8,128)(2,1)S(1)}, bf16[384,128]{1,0:T(8,128)(2,1)S(1)}, u32[]{:S(2)}, u32[]{:S(2)}) collective-permute-start(bf16[384,128]{1,0:T(8,128)(2,1)S(1)} %get-tuple-element.48), channel_id=1, source_target_pairs={{0,1},{1,0},{2,3},{3,2},{4,5},{5,4},{6,7},{7,6},{8,9},{9,8},{10,11... | collective-permute-start | bytes 294920 | tf_op jit(solution)/shard_map/ppermute | solution.py:415
  27.3 7.7 %collective-permute-start.8 = (bf16[384,128]{1,0:T(8,128)(2,1)S(1)}, bf16[384,128]{1,0:T(8,128)(2,1)S(1)}, u32[]{:S(2)}, u32[]{:S(2)}) collective-permute-start(bf16[384,128]{1,0:T(8,128)(2,1)S(1)} %get-tuple-element.50), channel_id=1, source_target_pairs={{0,31},{1,2},{2,1},{3,4},{4,3},{5,6},{6,5},{7,8},{8,7},{9,10},{10,... | collective-permute-start | bytes 294920 | tf_op jit(solution)/shard_map/ppermute | solution.py:414
  29.9 5.1 %collective-permute-start.9 = (bf16[384,128]{1,0:T(8,128)(2,1)S(1)}, bf16[384,128]{1,0:T(8,128)(2,1)S(1)}, u32[]{:S(2)}, u32[]{:S(2)}) collective-permute-start(bf16[384,128]{1,0:T(8,128)(2,1)S(1)} %get-tuple-element.51), channel_id=1, source_target_pairs={{0,1},{1,0},{2,3},{3,2},{4,5},{5,4},{6,7},{7,6},{8,9},{9,8},{10,11... | collective-permute-start | bytes 294920 | tf_op jit(solution)/shard_map/ppermute | solution.py:415
  35.4 7.7 %collective-permute-start.10 = (bf16[384,128]{1,0:T(8,128)(2,1)S(1)}, bf16[384,128]{1,0:T(8,128)(2,1)S(1)}, u32[]{:S(2)}, u32[]{:S(2)}) collective-permute-start(bf16[384,128]{1,0:T(8,128)(2,1)S(1)} %get-tuple-element.55), channel_id=1, source_target_pairs={{0,31},{1,2},{2,1},{3,4},{4,3},{5,6},{6,5},{7,8},{8,7},{9,10},{10,... | collective-permute-start | bytes 294920 | tf_op jit(solution)/shard_map/ppermute | solution.py:414
  38.1 0.7 %copy-start.7 = (f32[5]{0:T(128)S(1)}, f32[5]{0:T(128)}, u32[]{:S(2)}) copy-start(f32[5]{0:T(128)} %coef.1) | copy-start | bytes 64
  38.1 5.1 %collective-permute-start.11 = (bf16[384,128]{1,0:T(8,128)(2,1)S(1)}, bf16[384,128]{1,0:T(8,128)(2,1)S(1)}, u32[]{:S(2)}, u32[]{:S(2)}) collective-permute-start(bf16[384,128]{1,0:T(8,128)(2,1)S(1)} %get-tuple-element.56), channel_id=1, source_target_pairs={{0,1},{1,0},{2,3},{3,2},{4,5},{5,4},{6,7},{7,6},{8,9},{9,8},{10,11... | collective-permute-start | bytes 294920 | tf_op jit(solution)/shard_map/ppermute | solution.py:415
  43.6 1.9 %collective-permute-start.12 = (bf16[32,512]{1,0:T(8,128)(2,1)S(1)}, bf16[32,512]{1,0:T(8,128)(2,1)S(1)}, u32[]{:S(2)}, u32[]{:S(2)}) collective-permute-start(bf16[32,512]{1,0:T(8,128)(2,1)S(1)} %get-tuple-element.58), channel_id=1, source_target_pairs={{0,1},{1,0},{2,3},{3,2},{4,5},{5,4},{6,7},{7,6},{8,9},{9,8},{10,11... | collective-permute-start | bytes 98312 | tf_op jit(solution)/shard_map/ppermute | solution.py:420
  43.7 4.2 %collective-permute-start.13 = (bf16[32,512]{1,0:T(8,128)(2,1)S(1)}, bf16[32,512]{1,0:T(8,128)(2,1)S(1)}, u32[]{:S(2)}, u32[]{:S(2)}) collective-permute-start(bf16[32,512]{1,0:T(8,128)(2,1)S(1)} %get-tuple-element.59), channel_id=1, source_target_pairs={{0,2},{1,3},{2,0},{3,1},{4,6},{5,7},{6,4},{7,5},{8,10},{9,11},{10,... | collective-permute-start | bytes 98312 | tf_op jit(solution)/shard_map/ppermute | solution.py:420
  43.8 4.1 %collective-permute-start.14 = (bf16[32,512]{1,0:T(8,128)(2,1)S(1)}, bf16[32,512]{1,0:T(8,128)(2,1)S(1)}, u32[]{:S(2)}, u32[]{:S(2)}) collective-permute-start(bf16[32,512]{1,0:T(8,128)(2,1)S(1)} %get-tuple-element.60), channel_id=1, source_target_pairs={{0,3},{1,2},{2,1},{3,0},{4,7},{5,6},{6,5},{7,4},{8,11},{9,10},{10,... | collective-permute-start | bytes 98312 | tf_op jit(solution)/shard_map/ppermute | solution.py:420

commit v15 on v13

--- a/solution.py
+++ b/solution.py
@@ -52,32 +52,22 @@
     return [x.astype(F32) for x in (rel, shift * TILE_ATOMS + (dst & 7), cell)]
 
 
-def prep_kernel(
-    vec_hbm, feat, src_hbm, dst_hbm, cell_hbm, p0, p2, p3, blue, red, vectors, src, dst, cell, sems
-):
-    member, side = lax.axis_index("edges"), device_side()
-    pieces = (p0, None, p2, p3)
-    loads = []
-    high_rows, width = p0.shape
-    for k in range(4):
+def split_kernel(vectors, p0, p1, p2, p3):
+    member = lax.axis_index("edges")
+    for k, piece in enumerate((p0, p1, p2, p3)):
+        width = piece.shape[1]
         at = pl.multiple_of((member ^ k) * width, width)
-        loads.append(pltpu.make_async_copy(vec_hbm.at[:, pl.ds(at, width)], vectors.at[k], sems.at[k]))
+        piece[...] = vectors[:, pl.ds(at, width)].astype(BF)
+
+
+def message_kernel(feat, src, dst, cell, p1, blue, red):
+    side = device_side()
+    high_rows, width = p1.shape
+    nfeat = feat.shape[1]
     high = feat.shape[0] - SPILL
     off = pl.multiple_of(side * high, 64)
-    copies = [
-        pltpu.make_async_copy(feat.at[pl.ds(off, SPILL)], blue.at[pl.ds(0, SPILL)], sems.at[4]),
-        pltpu.make_async_copy(
-            feat.at[pl.ds(pl.multiple_of(high - off, 64), SPILL)], red.at[pl.ds(0, SPILL)], sems.at[5]
-        ),
-    ]
-    lists = [
-        pltpu.make_async_copy(x, y, sems.at[6 + n])
-        for n, (x, y) in enumerate(((src_hbm, src), (dst_hbm, dst), (cell_hbm, cell)))
-    ]
-    for copy in lists + loads + copies:
-        copy.start()
-    for copy in lists:
-        copy.wait()
+    blue[0:SPILL, :] = feat[pl.ds(off, SPILL), :]
+    red[0:SPILL, :] = feat[pl.ds(pl.multiple_of(high - off, 64), SPILL), :]
     three = edge_ids(src[...], dst[...], cell[...])
     lane, line = iota((3, 128), 1), iota((3, 128), 0)
     nrow = src.shape[0]
@@ -95,16 +85,9 @@
     ):
         msg[SPILL : SPILL + ID_ROWS, 0:128] = ids_of.astype(BF)
         msg[SPILL : SPILL + ID_ROWS, 128:256] = none
-    for k, piece in enumerate(pieces):
-        loads[k].wait()
-        if k == 1:
-            for n in range(width // red.shape[1]):
-                at = SPILL + ID_ROWS + n * high_rows
-                red[at : at + high_rows, :] = vectors[k, :, n * red.shape[1] : (n + 1) * red.shape[1]].astype(BF)
-        else:
-            piece[...] = vectors[k].astype(BF)
-    for copy in copies:
-        copy.wait()
+    for n in range(width // nfeat):
+        at = SPILL + ID_ROWS + n * high_rows
+        red[at : at + high_rows, :] = p1[:, n * nfeat : (n + 1) * nfeat]
 
 
 def pass_kernel(x, y):
@@ -398,18 +381,11 @@
     lines = (nown // 128, 128)
     edges = [x.reshape(lines) for x in (edge_src, edge_dst, edge_cell)]
     near_msg = shape((SPILL + ID_ROWS + high * nrow // nfeat, nfeat), BF)
-    own_piece, straight, across, blue_msg, near = call(
-        prep_kernel,
-        "prep",
-        (piece,) * 3 + (msg, near_msg),
-        [pltpu.VMEM((nedge, high, nrow), F32)]
-        + [pltpu.VMEM(lines, jnp.int32)] * 3
-        + [pltpu.SemaphoreType.DMA((9,))],
-        vectors,
-        features,
-        *edges,
-        in_hbm=range(5),
-        limit=FULL,
+    own_piece, beside, straight, across = call(
+        split_kernel, "split", (piece,) * 4, [], vectors, micros=1
+    )
+    blue_msg, near = call(
+        message_kernel, "message", (msg, near_msg), [], features, *edges, beside, micros=0
     )
     across = lax.ppermute(across, "edges", [(i, i ^ 3) for i in range(nedge)])
     straight = lax.ppermute(straight, "edges", [(i, i ^ 2) for i in range(nedge)])

time: 48.8 us -> 48.6 us (level)
  Pallas kernels: 11.1 us -> 9.06 us
  local copies, waits for them, and re-layouts: 0.7 us -> 2.43 us
  waiting for transfers between devices: 15.9 us -> 16.7 us
  starting transfers between devices: 20.7 us -> 20 us
    pallas_call x14 -> x15, Pallas kernels: 11.1 us -> 9.06 us  [call(): pl.pallas_call(kernel, name=name, out_shape=outs, in_specs=spaces, out_sp...]
    unnamed x18, local copies, waits for them, and re-layouts: 0.7 us -> 2.43 us
    ppermute x4, waiting for transfers between devices: 13.6 us -> 14.4 us  [swap(): lax.ppermute(first, axes, blue_pairs)]
    ppermute x4, starting transfers between devices: 10.2 us -> 9.53 us  [swap(): lax.ppermute(first, axes, blue_pairs)]
  transfers between devices with their start and end apart: 15 -> 15, of which waited for: 5 -> 5; matrix products, arithmetic and copies ran while one was open for 0% -> 0% of each run, Pallas kernels for 14% -> 13%
where the time goes in v15:
time: 48.6 us; the launch traced here: 48.3 us
  starting transfers between devices  20 us (41%)
  waiting for transfers between devices  16.7 us (34%)
  Pallas kernels  9.06 us (19%)
  local copies, waits for them, and re-layouts  2.43 us (5%)
    ppermute x4, waiting for transfers between devices, swap(): lax.ppermute(first, axes, blue_pairs)  14.4 us
    ppermute x4, starting transfers between devices, swap(): lax.ppermute(first, axes, blue_pairs)  9.53 us
    pallas_call x15, Pallas kernels, call(): pl.pallas_call(kernel, name=name, out_shape=outs, in_specs=spaces, out_sp...  9.06 us
    ppermute x1, starting transfers between devices, per_device(): blue_msg = lax.ppermute(blue_msg, axes, blue_pairs)  5.37 us
    ppermute x1, starting transfers between devices, per_device(): across = lax.ppermute(across, 'edges', [(i, i ^ 3) for i in range(nedge)])  2.61 us
    unnamed x18, local copies, waits for them, and re-layouts  2.43 us
    ppermute x3, waiting for transfers between devices, exchange(): lax.ppermute(pieces[k], 'edges', [(i, i ^ k) for i in range(nedge)])  2.3 us
    ppermute x3, starting transfers between devices, exchange(): lax.ppermute(pieces[k], 'edges', [(i, i ^ k) for i in range(nedge)])  1.93 us
  transfers between devices with their start and end apart: 15, of which 5 were waited for; matrix products, arithmetic and copies ran while one was open for 0% of the time, Pallas kernels for 13%

profile of v15, /device:TPU:0, one launch (start us, length us, event | category | flops | bytes accessed | tf_op | source)
XLA Modules:
  0.0 48.3 jit_solution(12082081008701053444)
XLA Ops:
  0.0 1.0 %copy-done.4 = f32[32,2048]{1,0:T(8,128)S(1)} copy-done((f32[32,2048]{1,0:T(8,128)S(1)}, f32[32,2048]{1,0:T(8,128)}, u32[]{:S(2)}) %copy-start.4) | copy-done | bytes 262168
  1.0 0.1 copy-done
  1.2 0.6 %copy-done.1 = s32[1280]{0:T(1024)S(1)} copy-done((s32[1280]{0:T(1024)S(1)}, s32[1280]{0:T(1024)}, u32[]{:S(2)}) %copy-start.1) | copy-done | bytes 5144
  1.8 0.0 copy-done.2
  1.8 0.0 copy-done.3
  1.8 0.5 %collective-permute-start = (bf16[400,256]{1,0:T(8,128)(2,1)S(1)}, bf16[400,256]{1,0:T(8,128)(2,1)S(1)}, u32[]{:S(2)}, u32[]{:S(2)}) collective-permute-start(bf16[400,256]{1,0:T(8,128)(2,1)S(1)} %get-tuple-element.35), channel_id=1, source_target_pairs={{0,1},{1,0},{2,3},{3,2},{4,5},{5,4},{6,7},{7,6},{8,9},{9,8},{10,11... | collective-permute-start | bytes 614408 | tf_op jit(solution)/shard_map/ppermute | solution.py:392
  2.3 2.6 %collective-permute-start.2 = (bf16[32,512]{1,0:T(8,128)(2,1)S(1)}, bf16[32,512]{1,0:T(8,128)(2,1)S(1)}, u32[]{:S(2)}, u32[]{:S(2)}) collective-permute-start(bf16[32,512]{1,0:T(8,128)(2,1)S(1)} %get-tuple-element.38), channel_id=1, source_target_pairs={{0,3},{1,2},{2,1},{3,0},{4,7},{5,6},{6,5},{7,4},{8,11},{9,10},{10,... | collective-permute-start | bytes 98312 | tf_op jit(solution)/shard_map/ppermute | solution.py:390
  5.0 0.0 collective-permute-start.1
  5.0 5.4 %collective-permute-start.3 = (bf16[336,256]{1,0:T(8,128)(2,1)S(1)}, bf16[336,256]{1,0:T(8,128)(2,1)S(1)}, u32[]{:S(2)}, u32[]{:S(2)}) collective-permute-start(bf16[336,256]{1,0:T(8,128)(2,1)S(1)} %get-tuple-element.41), channel_id=1, source_target_pairs={{0,31},{1,2},{2,1},{3,4},{4,3},{5,6},{6,5},{7,8},{8,7},{9,10},{10,... | collective-permute-start | bytes 516104 | tf_op jit(solution)/shard_map/ppermute | solution.py:393
  10.4 0.0 collective-permute-done.2.x
  10.4 0.0 collective-permute-done.1.p2
  10.4 0.0 collective-permute-done.near
  10.4 0.0 copy-start.5
  10.4 0.0 copy-start.6
  10.4 0.2 field.1
  10.6 0.0 copy-start.7
  10.6 2.1 %collective-permute-start.4 = (bf16[384,128]{1,0:T(8,128)(2,1)S(1)}, bf16[384,128]{1,0:T(8,128)(2,1)S(1)}, u32[]{:S(2)}, u32[]{:S(2)}) collective-permute-start(bf16[384,128]{1,0:T(8,128)(2,1)S(1)} %get-tuple-element.46), channel_id=1, source_target_pairs={{0,31},{1,2},{2,1},{3,4},{4,3},{5,6},{6,5},{7,8},{8,7},{9,10},{10,... | collective-permute-start | bytes 294920 | tf_op jit(solution)/shard_map/ppermute | solution.py:370
  12.7 0.0 collective-permute-start.5
  12.7 2.8 %own.1 = (bf16[2,256,1024]{2,1,0:T(8,128)(2,1)S(1)}, bf16[512,256]{1,0:T(8,128)(2,1)S(1)}, bf16[512,8]{1,0:T(8,128)(2,1)S(1)}, bf16[256,256]{1,0:T(8,128)(2,1)S(1)}) custom-call(bf16[1280,256]{1,0:T(8,128)(2,1)S(1)} %copy-done, s32[10,128]{1,0:T(8,128)S(1)} %bitcast.4, s32[10,128]{1,0:T(8,128)S(1)} %bitcast.6, s32[10,128]{1,0:T(8,128)S(1)} %bitcast.8, ...), custom_call_target="tpu_custom_call" | custom-call | flops 4000000000 | tf_op jit(solution)/shard_map/own/pallas_call | solution.py:345
  15.6 0.0 collective-permute-done.3.blue
  15.6 1.5 %spill.1.band = bf16[2,256,1024]{2,1,0:T(8,128)(2,1)S(1)} custom-call(bf16[2,256,1024]{2,1,0:T(8,128)(2,1)S(1)} %get-tuple-element.40.own_band, bf16[336,256]{1,0:T(8,128)(2,1)S(1)} %collective-permute-done.3.blue, bf16[512,256]{1,0:T(8,128)(2,1)S(1)} %get-tuple-element.42.w_in_t, ...), custom_call_target="tpu_custom_call", output_to_operand_aliasing={{}: (0, {})} | custom-call | tf_op jit(solution)/shard_map/spill/pallas_call | solution.py:345
  17.1 0.3 start.1.part
  17.4 0.9 %collective-permute-done.4.blue = bf16[384,128]{1,0:T(8,128)(2,1)S(1)} collective-permute-done((bf16[384,128]{1,0:T(8,128)(2,1)S(1)}, bf16[384,128]{1,0:T(8,128)(2,1)S(1)}, u32[]{:S(2)}, u32[]{:S(2)}) %collective-permute-start.4) | collective-permute-done | bytes 98336 | tf_op jit(solution)/shard_map/ppermute | solution.py:370
  18.3 0.0 collective-permute-done.5.red
  18.3 0.4 outer.3
  18.8 2.5 %collective-permute-start.6 = (bf16[384,128]{1,0:T(8,128)(2,1)S(1)}, bf16[384,128]{1,0:T(8,128)(2,1)S(1)}, u32[]{:S(2)}, u32[]{:S(2)}) collective-permute-start(bf16[384,128]{1,0:T(8,128)(2,1)S(1)} %get-tuple-element.49), channel_id=1, source_target_pairs={{0,31},{1,2},{2,1},{3,4},{4,3},{5,6},{6,5},{7,8},{8,7},{9,10},{10,... | collective-permute-start | bytes 294920 | tf_op jit(solution)/shard_map/ppermute | solution.py:370
  21.3 0.0 collective-permute-start.7
  21.3 0.3 inner.2.part
  21.6 4.9 %collective-permute-done.6.blue = bf16[384,128]{1,0:T(8,128)(2,1)S(1)} collective-permute-done((bf16[384,128]{1,0:T(8,128)(2,1)S(1)}, bf16[384,128]{1,0:T(8,128)(2,1)S(1)}, u32[]{:S(2)}, u32[]{:S(2)}) %collective-permute-start.6) | collective-permute-done | bytes 98336 | tf_op jit(solution)/shard_map/ppermute | solution.py:370
  26.6 0.0 collective-permute-done.7.red
  26.6 0.4 outer.4
  27.0 2.5 %collective-permute-start.8 = (bf16[384,128]{1,0:T(8,128)(2,1)S(1)}, bf16[384,128]{1,0:T(8,128)(2,1)S(1)}, u32[]{:S(2)}, u32[]{:S(2)}) collective-permute-start(bf16[384,128]{1,0:T(8,128)(2,1)S(1)} %get-tuple-element.52), channel_id=1, source_target_pairs={{0,31},{1,2},{2,1},{3,4},{4,3},{5,6},{6,5},{7,8},{8,7},{9,10},{10,... | collective-permute-start | bytes 294920 | tf_op jit(solution)/shard_map/ppermute | solution.py:370
  29.5 0.3 inner.3.part
  29.8 4.9 %collective-permute-done.8.blue = bf16[384,128]{1,0:T(8,128)(2,1)S(1)} collective-permute-done((bf16[384,128]{1,0:T(8,128)(2,1)S(1)}, bf16[384,128]{1,0:T(8,128)(2,1)S(1)}, u32[]{:S(2)}, u32[]{:S(2)}) %collective-permute-start.8) | collective-permute-done | bytes 98336 | tf_op jit(solution)/shard_map/ppermute | solution.py:370
  34.7 0.0 collective-permute-done.9.red
  34.7 0.4 outer.5
  35.2 2.5 %collective-permute-start.10 = (bf16[384,128]{1,0:T(8,128)(2,1)S(1)}, bf16[384,128]{1,0:T(8,128)(2,1)S(1)}, u32[]{:S(2)}, u32[]{:S(2)}) collective-permute-start(bf16[384,128]{1,0:T(8,128)(2,1)S(1)} %get-tuple-element.57), channel_id=1, source_target_pairs={{0,31},{1,2},{2,1},{3,4},{4,3},{5,6},{6,5},{7,8},{8,7},{9,10},{10,... | collective-permute-start | bytes 294920 | tf_op jit(solution)/shard_map/ppermute | solution.py:370
  37.7 0.7 %copy-done.8 = f32[5]{0:T(128)S(1)} copy-done((f32[5]{0:T(128)S(1)}, f32[5]{0:T(128)}, u32[]{:S(2)}) %copy-start.8) | copy-done | bytes 44
  38.3 1.0 %mix.1 = (f32[128,512]{1,0:T(8,128)S(1)}, f32[8,128]{1,0:T(8,128)S(1)}) custom-call(f32[5]{0:T(128)S(1)} %copy-done.8, bf16[2,256,1024]{2,1,0:T(8,128)(2,1)S(1)} %spill.1.band, f32[512,128]{1,0:T(8,128)S(1)} %get-tuple-element.45.now.before.t0, f32[512,128]{1,0:T(8,128)S(1)} %get-tuple-element.48.now.before.t1, f32[512,128]{1,0:T(8,128)S(1)} %get-tuple-element.51.now.t2, ...), custom_call_target="tpu_custom_call" | custom-call | flops 1000000000 | tf_op jit(solution)/shard_map/mix/pallas_call | solution.py:345
  39.3 3.6 %collective-permute-done.10.blue = bf16[384,128]{1,0:T(8,128)(2,1)S(1)} collective-permute-done((bf16[384,128]{1,0:T(8,128)(2,1)S(1)}, bf16[384,128]{1,0:T(8,128)(2,1)S(1)}, u32[]{:S(2)}, u32[]{:S(2)}) %collective-permute-start.10) | collective-permute-done | bytes 98336 | tf_op jit(solution)/shard_map/ppermute | solution.py:370
  42.9 0.0 collective-permute-done.11.red
  42.9 0.5 last.1
  43.4 0.1 collective-permute-start.12
  43.4 0.1 collective-permute-start.13
  43.5 1.8 %collective-permute-start.14 = (bf16[32,512]{1,0:T(8,128)(2,1)S(1)}, bf16[32,512]{1,0:T(8,128)(2,1)S(1)}, u32[]{:S(2)}, u32[]{:S(2)}) collective-permute-start(bf16[32,512]{1,0:T(8,128)(2,1)S(1)} %get-tuple-element.62), channel_id=1, source_target_pairs={{0,3},{1,2},{2,1},{3,0},{4,7},{5,6},{6,5},{7,4},{8,11},{9,10},{10,... | collective-permute-start | bytes 98312 | tf_op jit(solution)/shard_map/ppermute | solution.py:376
  45.3 2.3 %collective-permute-done.13.p2 = bf16[32,512]{1,0:T(8,128)(2,1)S(1)} collective-permute-done((bf16[32,512]{1,0:T(8,128)(2,1)S(1)}, bf16[32,512]{1,0:T(8,128)(2,1)S(1)}, u32[]{:S(2)}, u32[]{:S(2)}) %collective-permute-start.13) | collective-permute-done | bytes 32800 | tf_op jit(solution)/shard_map/ppermute | solution.py:376
  47.6 0.0 collective-permute-done.14.p3
  47.6 0.7 %join.1 = f32[32,2048]{1,0:T(8,128)} custom-call(bf16[32,512]{1,0:T(8,128)(2,1)S(1)} %get-tuple-element.59.p0, bf16[32,512]{1,0:T(8,128)(2,1)S(1)} %collective-permute-done.12.p1, bf16[32,512]{1,0:T(8,128)(2,1)S(1)} %collective-permute-done.13.p2, bf16[32,512]{1,0:T(8,128)(2,1)S(1)} %collective-permute-done.14.p3), custom_call_target="tpu_custom_call" | custom-call | flops 1000000000 | tf_op jit(solution)/shard_map/join/pallas_call | solution.py:345
  (15 shorter events, 0.1 us)
Async XLA Ops:
  0.0 1.2 %copy-start = (bf16[1280,256]{1,0:T(8,128)(2,1)S(1)}, bf16[1280,256]{1,0:T(8,128)(2,1)}, u32[]{:S(2)}) copy-start(bf16[1280,256]{1,0:T(8,128)(2,1)} %feat.3) | copy-start | bytes 1966084
  0.0 1.0 %copy-start.4 = (f32[32,2048]{1,0:T(8,128)S(1)}, f32[32,2048]{1,0:T(8,128)}, u32[]{:S(2)}) copy-start(f32[32,2048]{1,0:T(8,128)} %vectors.1) | copy-start | bytes 786436
  1.0 0.7 %copy-start.1 = (s32[1280]{0:T(1024)S(1)}, s32[1280]{0:T(1024)}, u32[]{:S(2)}) copy-start(s32[1280]{0:T(1024)} %param.10) | copy-start | bytes 15364
  1.0 0.7 %copy-start.2 = (s32[1280]{0:T(1024)S(1)}, s32[1280]{0:T(1024)}, u32[]{:S(2)}) copy-start(s32[1280]{0:T(1024)} %param.11) | copy-start | bytes 15364
  1.0 0.8 %copy-start.3 = (s32[1280]{0:T(1024)S(1)}, s32[1280]{0:T(1024)}, u32[]{:S(2)}) copy-start(s32[1280]{0:T(1024)} %param.12) | copy-start | bytes 15364
  1.8 8.6 %collective-permute-start = (bf16[400,256]{1,0:T(8,128)(2,1)S(1)}, bf16[400,256]{1,0:T(8,128)(2,1)S(1)}, u32[]{:S(2)}, u32[]{:S(2)}) collective-permute-start(bf16[400,256]{1,0:T(8,128)(2,1)S(1)} %get-tuple-element.35), channel_id=1, source_target_pairs={{0,1},{1,0},{2,3},{3,2},{4,5},{5,4},{6,7},{7,6},{8,9},{9,8},{10,11... | collective-permute-start | bytes 614408 | tf_op jit(solution)/shard_map/ppermute | solution.py:392
  2.3 8.0 %collective-permute-start.2 = (bf16[32,512]{1,0:T(8,128)(2,1)S(1)}, bf16[32,512]{1,0:T(8,128)(2,1)S(1)}, u32[]{:S(2)}, u32[]{:S(2)}) collective-permute-start(bf16[32,512]{1,0:T(8,128)(2,1)S(1)} %get-tuple-element.38), channel_id=1, source_target_pairs={{0,3},{1,2},{2,1},{3,0},{4,7},{5,6},{6,5},{7,4},{8,11},{9,10},{10,... | collective-permute-start | bytes 98312 | tf_op jit(solution)/shard_map/ppermute | solution.py:390
  5.0 5.4 %collective-permute-start.1 = (bf16[32,512]{1,0:T(8,128)(2,1)S(1)}, bf16[32,512]{1,0:T(8,128)(2,1)S(1)}, u32[]{:S(2)}, u32[]{:S(2)}) collective-permute-start(bf16[32,512]{1,0:T(8,128)(2,1)S(1)} %get-tuple-element.37), channel_id=1, source_target_pairs={{0,2},{1,3},{2,0},{3,1},{4,6},{5,7},{6,4},{7,5},{8,10},{9,11},{10,... | collective-permute-start | bytes 98312 | tf_op jit(solution)/shard_map/ppermute | solution.py:391
  5.0 10.6 %collective-permute-start.3 = (bf16[336,256]{1,0:T(8,128)(2,1)S(1)}, bf16[336,256]{1,0:T(8,128)(2,1)S(1)}, u32[]{:S(2)}, u32[]{:S(2)}) collective-permute-start(bf16[336,256]{1,0:T(8,128)(2,1)S(1)} %get-tuple-element.41), channel_id=1, source_target_pairs={{0,31},{1,2},{2,1},{3,4},{4,3},{5,6},{6,5},{7,8},{8,7},{9,10},{10,... | collective-permute-start | bytes 516104 | tf_op jit(solution)/shard_map/ppermute | solution.py:393
  10.4 2.3 %copy-start.5 = (bf16[256,512]{1,0:T(8,128)(2,1)S(1)}, bf16[256,512]{1,0:T(8,128)(2,1)}, u32[]{:S(2)}) copy-start(bf16[256,512]{1,0:T(8,128)(2,1)} %w_in.1) | copy-start | bytes 786436
  10.4 2.3 %copy-start.6 = (bf16[256,256]{1,0:T(8,128)(2,1)S(1)}, bf16[256,256]{1,0:T(8,128)(2,1)}, u32[]{:S(2)}) copy-start(bf16[256,256]{1,0:T(8,128)(2,1)} %w_out.1) | copy-start | bytes 393220
  10.6 2.1 %copy-start.7 = (bf16[3,512]{1,0:T(4,128)(2,1)S(1)}, bf16[3,512]{1,0:T(4,128)(2,1)}, u32[]{:S(2)}) copy-start(bf16[3,512]{1,0:T(4,128)(2,1)} %cell_bias.1) | copy-start | bytes 9220
  10.6 7.7 %collective-permute-start.4 = (bf16[384,128]{1,0:T(8,128)(2,1)S(1)}, bf16[384,128]{1,0:T(8,128)(2,1)S(1)}, u32[]{:S(2)}, u32[]{:S(2)}) collective-permute-start(bf16[384,128]{1,0:T(8,128)(2,1)S(1)} %get-tuple-element.46), channel_id=1, source_target_pairs={{0,31},{1,2},{2,1},{3,4},{4,3},{5,6},{6,5},{7,8},{8,7},{9,10},{10,... | collective-permute-start | bytes 294920 | tf_op jit(solution)/shard_map/ppermute | solution.py:370
  12.7 5.6 %collective-permute-start.5 = (bf16[384,128]{1,0:T(8,128)(2,1)S(1)}, bf16[384,128]{1,0:T(8,128)(2,1)S(1)}, u32[]{:S(2)}, u32[]{:S(2)}) collective-permute-start(bf16[384,128]{1,0:T(8,128)(2,1)S(1)} %get-tuple-element.47), channel_id=1, source_target_pairs={{0,1},{1,0},{2,3},{3,2},{4,5},{5,4},{6,7},{7,6},{8,9},{9,8},{10,11... | collective-permute-start | bytes 294920 | tf_op jit(solution)/shard_map/ppermute | solution.py:371
  18.8 7.8 %collective-permute-start.6 = (bf16[384,128]{1,0:T(8,128)(2,1)S(1)}, bf16[384,128]{1,0:T(8,128)(2,1)S(1)}, u32[]{:S(2)}, u32[]{:S(2)}) collective-permute-start(bf16[384,128]{1,0:T(8,128)(2,1)S(1)} %get-tuple-element.49), channel_id=1, source_target_pairs={{0,31},{1,2},{2,1},{3,4},{4,3},{5,6},{6,5},{7,8},{8,7},{9,10},{10,... | collective-permute-start | bytes 294920 | tf_op jit(solution)/shard_map/ppermute | solution.py:370
  21.3 5.3 %collective-permute-start.7 = (bf16[384,128]{1,0:T(8,128)(2,1)S(1)}, bf16[384,128]{1,0:T(8,128)(2,1)S(1)}, u32[]{:S(2)}, u32[]{:S(2)}) collective-permute-start(bf16[384,128]{1,0:T(8,128)(2,1)S(1)} %get-tuple-element.50), channel_id=1, source_target_pairs={{0,1},{1,0},{2,3},{3,2},{4,5},{5,4},{6,7},{7,6},{8,9},{9,8},{10,11... | collective-permute-start | bytes 294920 | tf_op jit(solution)/shard_map/ppermute | solution.py:371
  27.0 7.7 %collective-permute-start.8 = (bf16[384,128]{1,0:T(8,128)(2,1)S(1)}, bf16[384,128]{1,0:T(8,128)(2,1)S(1)}, u32[]{:S(2)}, u32[]{:S(2)}) collective-permute-start(bf16[384,128]{1,0:T(8,128)(2,1)S(1)} %get-tuple-element.52), channel_id=1, source_target_pairs={{0,31},{1,2},{2,1},{3,4},{4,3},{5,6},{6,5},{7,8},{8,7},{9,10},{10,... | collective-permute-start | bytes 294920 | tf_op jit(solution)/shard_map/ppermute | solution.py:370
  29.5 5.2 %collective-permute-start.9 = (bf16[384,128]{1,0:T(8,128)(2,1)S(1)}, bf16[384,128]{1,0:T(8,128)(2,1)S(1)}, u32[]{:S(2)}, u32[]{:S(2)}) collective-permute-start(bf16[384,128]{1,0:T(8,128)(2,1)S(1)} %get-tuple-element.53), channel_id=1, source_target_pairs={{0,1},{1,0},{2,3},{3,2},{4,5},{5,4},{6,7},{7,6},{8,9},{9,8},{10,11... | collective-permute-start | bytes 294920 | tf_op jit(solution)/shard_map/ppermute | solution.py:371
  35.2 7.7 %collective-permute-start.10 = (bf16[384,128]{1,0:T(8,128)(2,1)S(1)}, bf16[384,128]{1,0:T(8,128)(2,1)S(1)}, u32[]{:S(2)}, u32[]{:S(2)}) collective-permute-start(bf16[384,128]{1,0:T(8,128)(2,1)S(1)} %get-tuple-element.57), channel_id=1, source_target_pairs={{0,31},{1,2},{2,1},{3,4},{4,3},{5,6},{6,5},{7,8},{8,7},{9,10},{10,... | collective-permute-start | bytes 294920 | tf_op jit(solution)/shard_map/ppermute | solution.py:370
  37.6 0.7 %copy-start.8 = (f32[5]{0:T(128)S(1)}, f32[5]{0:T(128)}, u32[]{:S(2)}) copy-start(f32[5]{0:T(128)} %coef.1) | copy-start | bytes 64
  37.6 5.2 %collective-permute-start.11 = (bf16[384,128]{1,0:T(8,128)(2,1)S(1)}, bf16[384,128]{1,0:T(8,128)(2,1)S(1)}, u32[]{:S(2)}, u32[]{:S(2)}) collective-permute-start(bf16[384,128]{1,0:T(8,128)(2,1)S(1)} %get-tuple-element.58), channel_id=1, source_target_pairs={{0,1},{1,0},{2,3},{3,2},{4,5},{5,4},{6,7},{7,6},{8,9},{9,8},{10,11... | collective-permute-start | bytes 294920 | tf_op jit(solution)/shard_map/ppermute | solution.py:371
  43.4 1.9 %collective-permute-start.12 = (bf16[32,512]{1,0:T(8,128)(2,1)S(1)}, bf16[32,512]{1,0:T(8,128)(2,1)S(1)}, u32[]{:S(2)}, u32[]{:S(2)}) collective-permute-start(bf16[32,512]{1,0:T(8,128)(2,1)S(1)} %get-tuple-element.60), channel_id=1, source_target_pairs={{0,1},{1,0},{2,3},{3,2},{4,5},{5,4},{6,7},{7,6},{8,9},{9,8},{10,11... | collective-permute-start | bytes 98312 | tf_op jit(solution)/shard_map/ppermute | solution.py:376
  43.4 4.2 %collective-permute-start.13 = (bf16[32,512]{1,0:T(8,128)(2,1)S(1)}, bf16[32,512]{1,0:T(8,128)(2,1)S(1)}, u32[]{:S(2)}, u32[]{:S(2)}) collective-permute-start(bf16[32,512]{1,0:T(8,128)(2,1)S(1)} %get-tuple-element.61), channel_id=1, source_target_pairs={{0,2},{1,3},{2,0},{3,1},{4,6},{5,7},{6,4},{7,5},{8,10},{9,11},{10,... | collective-permute-start | bytes 98312 | tf_op jit(solution)/shard_map/ppermute | solution.py:376
  43.5 4.1 %collective-permute-start.14 = (bf16[32,512]{1,0:T(8,128)(2,1)S(1)}, bf16[32,512]{1,0:T(8,128)(2,1)S(1)}, u32[]{:S(2)}, u32[]{:S(2)}) collective-permute-start(bf16[32,512]{1,0:T(8,128)(2,1)S(1)} %get-tuple-element.62), channel_id=1, source_target_pairs={{0,3},{1,2},{2,1},{3,0},{4,7},{5,6},{6,5},{7,4},{8,11},{9,10},{10,... | collective-permute-start | bytes 98312 | tf_op jit(solution)/shard_map/ppermute | solution.py:376

commit v16 on v15

--- a/solution.py
+++ b/solution.py
@@ -52,7 +52,11 @@
     return [x.astype(F32) for x in (rel, shift * TILE_ATOMS + (dst & 7), cell)]
 
 
-def split_kernel(vectors, p0, p1, p2, p3):
+def tick_kernel(token):
+    token[...] = jnp.zeros(token.shape, F32)
+
+
+def split_kernel(vectors, _, src, dst, cell, p0, p1, p2, p3):
     member = lax.axis_index("edges")
     for k, piece in enumerate((p0, p1, p2, p3)):
         width = piece.shape[1]
@@ -381,8 +385,9 @@
     lines = (nown // 128, 128)
     edges = [x.reshape(lines) for x in (edge_src, edge_dst, edge_cell)]
     near_msg = shape((SPILL + ID_ROWS + high * nrow // nfeat, nfeat), BF)
+    (tick,) = call(tick_kernel, "tick", (shape((8, VEC), F32),), [], micros=5)
     own_piece, beside, straight, across = call(
-        split_kernel, "split", (piece,) * 4, [], vectors, micros=1
+        split_kernel, "split", (piece,) * 4, [], vectors, tick, *edges, micros=0
     )
     blue_msg, near = call(
         message_kernel, "message", (msg, near_msg), [], features, *edges, beside, micros=0

time: 48.6 us -> 47.9 us (0.986)
  local copies, waits for them, and re-layouts: 2.43 us -> 1.84 us
    unnamed x18, local copies, waits for them, and re-layouts: 2.43 us -> 1.84 us
    pallas_call x15 -> x16, Pallas kernels: 9.06 us -> 9.17 us  [call(): pl.pallas_call(kernel, name=name, out_shape=outs, in_specs=spaces, out_sp...]
  transfers between devices with their start and end apart: 15 -> 15, of which waited for: 5 -> 5; matrix products, arithmetic and copies ran while one was open for 0% -> 0% of each run, Pallas kernels for 13% -> 14%
where the time goes in v16:
time: 47.9 us; the launch traced here: 47.8 us
  starting transfers between devices  20.3 us (42%)
  waiting for transfers between devices  16.3 us (34%)
  Pallas kernels  9.17 us (19%)
  local copies, waits for them, and re-layouts  1.84 us (4%)
    ppermute x4, waiting for transfers between devices, swap(): lax.ppermute(first, axes, blue_pairs)  14 us
    ppermute x4, starting transfers between devices, swap(): lax.ppermute(first, axes, blue_pairs)  9.77 us
    pallas_call x16, Pallas kernels, call(): pl.pallas_call(kernel, name=name, out_shape=outs, in_specs=spaces, out_sp...  9.17 us
    ppermute x1, starting transfers between devices, per_device(): blue_msg = lax.ppermute(blue_msg, axes, blue_pairs)  5.37 us
    ppermute x1, starting transfers between devices, per_device(): across = lax.ppermute(across, 'edges', [(i, i ^ 3) for i in range(nedge)])  2.61 us
    ppermute x3, waiting for transfers between devices, exchange(): lax.ppermute(pieces[k], 'edges', [(i, i ^ k) for i in range(nedge)])  2.3 us
    ppermute x3, starting transfers between devices, exchange(): lax.ppermute(pieces[k], 'edges', [(i, i ^ k) for i in range(nedge)])  1.93 us
    unnamed x18, local copies, waits for them, and re-layouts  1.84 us
  transfers between devices with their start and end apart: 15, of which 5 were waited for; matrix products, arithmetic and copies ran while one was open for 0% of the time, Pallas kernels for 14%

profile of v16, /device:TPU:0, one launch (start us, length us, event | category | flops | bytes accessed | tf_op | source)
XLA Modules:
  0.0 47.8 jit_solution(5765799771338027733)
XLA Ops:
  0.0 0.9 %copy-done.1 = f32[32,2048]{1,0:T(8,128)S(1)} copy-done((f32[32,2048]{1,0:T(8,128)S(1)}, f32[32,2048]{1,0:T(8,128)}, u32[]{:S(2)}) %copy-start.1) | copy-done | bytes 262168
  1.0 0.2 copy-done
  1.3 0.5 %collective-permute-start = (bf16[400,256]{1,0:T(8,128)(2,1)S(1)}, bf16[400,256]{1,0:T(8,128)(2,1)S(1)}, u32[]{:S(2)}, u32[]{:S(2)}) collective-permute-start(bf16[400,256]{1,0:T(8,128)(2,1)S(1)} %get-tuple-element.35), channel_id=1, source_target_pairs={{0,1},{1,0},{2,3},{3,2},{4,5},{5,4},{6,7},{7,6},{8,9},{9,8},{10,11... | collective-permute-start | bytes 614408 | tf_op jit(solution)/shard_map/ppermute | solution.py:397
  1.8 2.6 %collective-permute-start.2 = (bf16[32,512]{1,0:T(8,128)(2,1)S(1)}, bf16[32,512]{1,0:T(8,128)(2,1)S(1)}, u32[]{:S(2)}, u32[]{:S(2)}) collective-permute-start(bf16[32,512]{1,0:T(8,128)(2,1)S(1)} %get-tuple-element.38), channel_id=1, source_target_pairs={{0,3},{1,2},{2,1},{3,0},{4,7},{5,6},{6,5},{7,4},{8,11},{9,10},{10,... | collective-permute-start | bytes 98312 | tf_op jit(solution)/shard_map/ppermute | solution.py:395
  4.4 0.0 collective-permute-start.1
  4.4 5.4 %collective-permute-start.3 = (bf16[336,256]{1,0:T(8,128)(2,1)S(1)}, bf16[336,256]{1,0:T(8,128)(2,1)S(1)}, u32[]{:S(2)}, u32[]{:S(2)}) collective-permute-start(bf16[336,256]{1,0:T(8,128)(2,1)S(1)} %get-tuple-element.41), channel_id=1, source_target_pairs={{0,31},{1,2},{2,1},{3,4},{4,3},{5,6},{6,5},{7,8},{8,7},{9,10},{10,... | collective-permute-start | bytes 516104 | tf_op jit(solution)/shard_map/ppermute | solution.py:398
  9.8 0.0 collective-permute-done.2.x
  9.8 0.0 collective-permute-done.1.p2
  9.8 0.0 collective-permute-done.near
  9.8 0.0 copy-start.5
  9.8 0.0 copy-start.6
  9.9 0.2 field.1
  10.1 0.0 copy-start.7
  10.1 2.1 %collective-permute-start.4 = (bf16[384,128]{1,0:T(8,128)(2,1)S(1)}, bf16[384,128]{1,0:T(8,128)(2,1)S(1)}, u32[]{:S(2)}, u32[]{:S(2)}) collective-permute-start(bf16[384,128]{1,0:T(8,128)(2,1)S(1)} %get-tuple-element.46), channel_id=1, source_target_pairs={{0,31},{1,2},{2,1},{3,4},{4,3},{5,6},{6,5},{7,8},{8,7},{9,10},{10,... | collective-permute-start | bytes 294920 | tf_op jit(solution)/shard_map/ppermute | solution.py:374
  12.1 0.0 collective-permute-start.5
  12.1 2.9 %own.1 = (bf16[2,256,1024]{2,1,0:T(8,128)(2,1)S(1)}, bf16[512,256]{1,0:T(8,128)(2,1)S(1)}, bf16[512,8]{1,0:T(8,128)(2,1)S(1)}, bf16[256,256]{1,0:T(8,128)(2,1)S(1)}) custom-call(bf16[1280,256]{1,0:T(8,128)(2,1)S(1)} %copy-done, s32[10,128]{1,0:T(8,128)S(1)} %bitcast.5, s32[10,128]{1,0:T(8,128)S(1)} %bitcast.8, s32[10,128]{1,0:T(8,128)S(1)} %bitcast.11, ...), custom_call_target="tpu_custom_call" | custom-call | flops 4000000000 | tf_op jit(solution)/shard_map/own/pallas_call | solution.py:349
  15.1 0.0 collective-permute-done.3.blue
  15.1 1.5 %spill.1.band = bf16[2,256,1024]{2,1,0:T(8,128)(2,1)S(1)} custom-call(bf16[2,256,1024]{2,1,0:T(8,128)(2,1)S(1)} %get-tuple-element.40.own_band, bf16[336,256]{1,0:T(8,128)(2,1)S(1)} %collective-permute-done.3.blue, bf16[512,256]{1,0:T(8,128)(2,1)S(1)} %get-tuple-element.42.w_in_t, ...), custom_call_target="tpu_custom_call", output_to_operand_aliasing={{}: (0, {})} | custom-call | tf_op jit(solution)/shard_map/spill/pallas_call | solution.py:349
  16.6 0.3 start.1.part
  16.9 0.8 %collective-permute-done.4.blue = bf16[384,128]{1,0:T(8,128)(2,1)S(1)} collective-permute-done((bf16[384,128]{1,0:T(8,128)(2,1)S(1)}, bf16[384,128]{1,0:T(8,128)(2,1)S(1)}, u32[]{:S(2)}, u32[]{:S(2)}) %collective-permute-start.4) | collective-permute-done | bytes 98336 | tf_op jit(solution)/shard_map/ppermute | solution.py:374
  17.8 0.0 collective-permute-done.5.red
  17.8 0.4 outer.3
  18.2 2.6 %collective-permute-start.6 = (bf16[384,128]{1,0:T(8,128)(2,1)S(1)}, bf16[384,128]{1,0:T(8,128)(2,1)S(1)}, u32[]{:S(2)}, u32[]{:S(2)}) collective-permute-start(bf16[384,128]{1,0:T(8,128)(2,1)S(1)} %get-tuple-element.49), channel_id=1, source_target_pairs={{0,31},{1,2},{2,1},{3,4},{4,3},{5,6},{6,5},{7,8},{8,7},{9,10},{10,... | collective-permute-start | bytes 294920 | tf_op jit(solution)/shard_map/ppermute | solution.py:374
  20.8 0.0 collective-permute-start.7
  20.8 0.3 inner.2.part
  21.2 4.9 %collective-permute-done.6.blue = bf16[384,128]{1,0:T(8,128)(2,1)S(1)} collective-permute-done((bf16[384,128]{1,0:T(8,128)(2,1)S(1)}, bf16[384,128]{1,0:T(8,128)(2,1)S(1)}, u32[]{:S(2)}, u32[]{:S(2)}) %collective-permute-start.6) | collective-permute-done | bytes 98336 | tf_op jit(solution)/shard_map/ppermute | solution.py:374
  26.0 0.0 collective-permute-done.7.red
  26.0 0.4 outer.4
  26.5 2.6 %collective-permute-start.8 = (bf16[384,128]{1,0:T(8,128)(2,1)S(1)}, bf16[384,128]{1,0:T(8,128)(2,1)S(1)}, u32[]{:S(2)}, u32[]{:S(2)}) collective-permute-start(bf16[384,128]{1,0:T(8,128)(2,1)S(1)} %get-tuple-element.52), channel_id=1, source_target_pairs={{0,31},{1,2},{2,1},{3,4},{4,3},{5,6},{6,5},{7,8},{8,7},{9,10},{10,... | collective-permute-start | bytes 294920 | tf_op jit(solution)/shard_map/ppermute | solution.py:374
  29.0 0.0 collective-permute-start.9
  29.0 0.3 inner.3.part
  29.4 4.8 %collective-permute-done.8.blue = bf16[384,128]{1,0:T(8,128)(2,1)S(1)} collective-permute-done((bf16[384,128]{1,0:T(8,128)(2,1)S(1)}, bf16[384,128]{1,0:T(8,128)(2,1)S(1)}, u32[]{:S(2)}, u32[]{:S(2)}) %collective-permute-start.8) | collective-permute-done | bytes 98336 | tf_op jit(solution)/shard_map/ppermute | solution.py:374
  34.2 0.0 collective-permute-done.9.red
  34.2 0.4 outer.5
  34.6 2.6 %collective-permute-start.10 = (bf16[384,128]{1,0:T(8,128)(2,1)S(1)}, bf16[384,128]{1,0:T(8,128)(2,1)S(1)}, u32[]{:S(2)}, u32[]{:S(2)}) collective-permute-start(bf16[384,128]{1,0:T(8,128)(2,1)S(1)} %get-tuple-element.57), channel_id=1, source_target_pairs={{0,31},{1,2},{2,1},{3,4},{4,3},{5,6},{6,5},{7,8},{8,7},{9,10},{10,... | collective-permute-start | bytes 294920 | tf_op jit(solution)/shard_map/ppermute | solution.py:374
  37.2 0.0 collective-permute-start.11
  37.2 0.7 %copy-done.8 = f32[5]{0:T(128)S(1)} copy-done((f32[5]{0:T(128)S(1)}, f32[5]{0:T(128)}, u32[]{:S(2)}) %copy-start.8) | copy-done | bytes 44
  37.8 1.0 %mix.1 = (f32[128,512]{1,0:T(8,128)S(1)}, f32[8,128]{1,0:T(8,128)S(1)}) custom-call(f32[5]{0:T(128)S(1)} %copy-done.8, bf16[2,256,1024]{2,1,0:T(8,128)(2,1)S(1)} %spill.1.band, f32[512,128]{1,0:T(8,128)S(1)} %get-tuple-element.45.now.before.t0, f32[512,128]{1,0:T(8,128)S(1)} %get-tuple-element.48.now.before.t1, f32[512,128]{1,0:T(8,128)S(1)} %get-tuple-element.51.now.t2, ...), custom_call_target="tpu_custom_call" | custom-call | flops 1000000000 | tf_op jit(solution)/shard_map/mix/pallas_call | solution.py:349
  38.8 3.5 %collective-permute-done.10.blue = bf16[384,128]{1,0:T(8,128)(2,1)S(1)} collective-permute-done((bf16[384,128]{1,0:T(8,128)(2,1)S(1)}, bf16[384,128]{1,0:T(8,128)(2,1)S(1)}, u32[]{:S(2)}, u32[]{:S(2)}) %collective-permute-start.10) | collective-permute-done | bytes 98336 | tf_op jit(solution)/shard_map/ppermute | solution.py:374
  42.3 0.0 collective-permute-done.11.red
  42.3 0.5 %last.1 = (bf16[32,512]{1,0:T(8,128)(2,1)S(1)}, bf16[32,512]{1,0:T(8,128)(2,1)S(1)}, bf16[32,512]{1,0:T(8,128)(2,1)S(1)}, bf16[32,512]{1,0:T(8,128)(2,1)S(1)}) custom-call(f32[8,128]{1,0:T(8,128)S(1)} %get-tuple-element.55.final, bf16[2,256,1024]{2,1,0:T(8,128)(2,1)S(1)} %spill.1.band, f32[128,512]{1,0:T(8,128)S(1)} %get-tuple-element.56.base, ...), custom_call_target="tpu_custom_call" | custom-call | flops 1000000000 | tf_op jit(solution)/shard_map/last/pallas_call | solution.py:349
  42.8 0.1 collective-permute-start.12
  42.9 0.1 collective-permute-start.13
  43.0 1.8 %collective-permute-start.14 = (bf16[32,512]{1,0:T(8,128)(2,1)S(1)}, bf16[32,512]{1,0:T(8,128)(2,1)S(1)}, u32[]{:S(2)}, u32[]{:S(2)}) collective-permute-start(bf16[32,512]{1,0:T(8,128)(2,1)S(1)} %get-tuple-element.62), channel_id=1, source_target_pairs={{0,3},{1,2},{2,1},{3,0},{4,7},{5,6},{6,5},{7,4},{8,11},{9,10},{10,... | collective-permute-start | bytes 98312 | tf_op jit(solution)/shard_map/ppermute | solution.py:380
  44.8 0.0 collective-permute-done.12.p1
  44.8 2.3 %collective-permute-done.13.p2 = bf16[32,512]{1,0:T(8,128)(2,1)S(1)} collective-permute-done((bf16[32,512]{1,0:T(8,128)(2,1)S(1)}, bf16[32,512]{1,0:T(8,128)(2,1)S(1)}, u32[]{:S(2)}, u32[]{:S(2)}) %collective-permute-start.13) | collective-permute-done | bytes 32800 | tf_op jit(solution)/shard_map/ppermute | solution.py:380
  47.1 0.0 collective-permute-done.14.p3
  47.1 0.7 %join.1 = f32[32,2048]{1,0:T(8,128)} custom-call(bf16[32,512]{1,0:T(8,128)(2,1)S(1)} %get-tuple-element.59.p0, bf16[32,512]{1,0:T(8,128)(2,1)S(1)} %collective-permute-done.12.p1, bf16[32,512]{1,0:T(8,128)(2,1)S(1)} %collective-permute-done.13.p2, bf16[32,512]{1,0:T(8,128)(2,1)S(1)} %collective-permute-done.14.p3), custom_call_target="tpu_custom_call" | custom-call | flops 1000000000 | tf_op jit(solution)/shard_map/join/pallas_call | solution.py:349
  (16 shorter events, 0.1 us)
Async XLA Ops:
  0.0 0.9 %copy-start.1 = (f32[32,2048]{1,0:T(8,128)S(1)}, f32[32,2048]{1,0:T(8,128)}, u32[]{:S(2)}) copy-start(f32[32,2048]{1,0:T(8,128)} %vectors.1) | copy-start | bytes 786436
  0.0 1.0 %copy-start.2 = (s32[1280]{0:T(1024)S(1)}, s32[1280]{0:T(1024)}, u32[]{:S(2)}) copy-start(s32[1280]{0:T(1024)} %param.10) | copy-start | bytes 15364
  0.0 1.0 %copy-start.3 = (s32[1280]{0:T(1024)S(1)}, s32[1280]{0:T(1024)}, u32[]{:S(2)}) copy-start(s32[1280]{0:T(1024)} %param.11) | copy-start | bytes 15364
  0.0 1.0 %copy-start.4 = (s32[1280]{0:T(1024)S(1)}, s32[1280]{0:T(1024)}, u32[]{:S(2)}) copy-start(s32[1280]{0:T(1024)} %param.12) | copy-start | bytes 15364
  0.0 1.2 %copy-start = (bf16[1280,256]{1,0:T(8,128)(2,1)S(1)}, bf16[1280,256]{1,0:T(8,128)(2,1)}, u32[]{:S(2)}) copy-start(bf16[1280,256]{1,0:T(8,128)(2,1)} %feat.3) | copy-start | bytes 1966084
  1.3 8.6 %collective-permute-start = (bf16[400,256]{1,0:T(8,128)(2,1)S(1)}, bf16[400,256]{1,0:T(8,128)(2,1)S(1)}, u32[]{:S(2)}, u32[]{:S(2)}) collective-permute-start(bf16[400,256]{1,0:T(8,128)(2,1)S(1)} %get-tuple-element.35), channel_id=1, source_target_pairs={{0,1},{1,0},{2,3},{3,2},{4,5},{5,4},{6,7},{7,6},{8,9},{9,8},{10,11... | collective-permute-start | bytes 614408 | tf_op jit(solution)/shard_map/ppermute | solution.py:397
  1.8 8.0 %collective-permute-start.2 = (bf16[32,512]{1,0:T(8,128)(2,1)S(1)}, bf16[32,512]{1,0:T(8,128)(2,1)S(1)}, u32[]{:S(2)}, u32[]{:S(2)}) collective-permute-start(bf16[32,512]{1,0:T(8,128)(2,1)S(1)} %get-tuple-element.38), channel_id=1, source_target_pairs={{0,3},{1,2},{2,1},{3,0},{4,7},{5,6},{6,5},{7,4},{8,11},{9,10},{10,... | collective-permute-start | bytes 98312 | tf_op jit(solution)/shard_map/ppermute | solution.py:395
  4.4 5.4 %collective-permute-start.1 = (bf16[32,512]{1,0:T(8,128)(2,1)S(1)}, bf16[32,512]{1,0:T(8,128)(2,1)S(1)}, u32[]{:S(2)}, u32[]{:S(2)}) collective-permute-start(bf16[32,512]{1,0:T(8,128)(2,1)S(1)} %get-tuple-element.37), channel_id=1, source_target_pairs={{0,2},{1,3},{2,0},{3,1},{4,6},{5,7},{6,4},{7,5},{8,10},{9,11},{10,... | collective-permute-start | bytes 98312 | tf_op jit(solution)/shard_map/ppermute | solution.py:396
  4.4 10.6 %collective-permute-start.3 = (bf16[336,256]{1,0:T(8,128)(2,1)S(1)}, bf16[336,256]{1,0:T(8,128)(2,1)S(1)}, u32[]{:S(2)}, u32[]{:S(2)}) collective-permute-start(bf16[336,256]{1,0:T(8,128)(2,1)S(1)} %get-tuple-element.41), channel_id=1, source_target_pairs={{0,31},{1,2},{2,1},{3,4},{4,3},{5,6},{6,5},{7,8},{8,7},{9,10},{10,... | collective-permute-start | bytes 516104 | tf_op jit(solution)/shard_map/ppermute | solution.py:398
  9.8 2.3 %copy-start.5 = (bf16[256,512]{1,0:T(8,128)(2,1)S(1)}, bf16[256,512]{1,0:T(8,128)(2,1)}, u32[]{:S(2)}) copy-start(bf16[256,512]{1,0:T(8,128)(2,1)} %w_in.1) | copy-start | bytes 786436
  9.8 2.3 %copy-start.6 = (bf16[256,256]{1,0:T(8,128)(2,1)S(1)}, bf16[256,256]{1,0:T(8,128)(2,1)}, u32[]{:S(2)}) copy-start(bf16[256,256]{1,0:T(8,128)(2,1)} %w_out.1) | copy-start | bytes 393220
  10.1 2.1 %copy-start.7 = (bf16[3,512]{1,0:T(4,128)(2,1)S(1)}, bf16[3,512]{1,0:T(4,128)(2,1)}, u32[]{:S(2)}) copy-start(bf16[3,512]{1,0:T(4,128)(2,1)} %cell_bias.1) | copy-start | bytes 9220
  10.1 7.7 %collective-permute-start.4 = (bf16[384,128]{1,0:T(8,128)(2,1)S(1)}, bf16[384,128]{1,0:T(8,128)(2,1)S(1)}, u32[]{:S(2)}, u32[]{:S(2)}) collective-permute-start(bf16[384,128]{1,0:T(8,128)(2,1)S(1)} %get-tuple-element.46), channel_id=1, source_target_pairs={{0,31},{1,2},{2,1},{3,4},{4,3},{5,6},{6,5},{7,8},{8,7},{9,10},{10,... | collective-permute-start | bytes 294920 | tf_op jit(solution)/shard_map/ppermute | solution.py:374
  12.1 5.6 %collective-permute-start.5 = (bf16[384,128]{1,0:T(8,128)(2,1)S(1)}, bf16[384,128]{1,0:T(8,128)(2,1)S(1)}, u32[]{:S(2)}, u32[]{:S(2)}) collective-permute-start(bf16[384,128]{1,0:T(8,128)(2,1)S(1)} %get-tuple-element.47), channel_id=1, source_target_pairs={{0,1},{1,0},{2,3},{3,2},{4,5},{5,4},{6,7},{7,6},{8,9},{9,8},{10,11... | collective-permute-start | bytes 294920 | tf_op jit(solution)/shard_map/ppermute | solution.py:375
  18.2 7.8 %collective-permute-start.6 = (bf16[384,128]{1,0:T(8,128)(2,1)S(1)}, bf16[384,128]{1,0:T(8,128)(2,1)S(1)}, u32[]{:S(2)}, u32[]{:S(2)}) collective-permute-start(bf16[384,128]{1,0:T(8,128)(2,1)S(1)} %get-tuple-element.49), channel_id=1, source_target_pairs={{0,31},{1,2},{2,1},{3,4},{4,3},{5,6},{6,5},{7,8},{8,7},{9,10},{10,... | collective-permute-start | bytes 294920 | tf_op jit(solution)/shard_map/ppermute | solution.py:374
  20.8 5.2 %collective-permute-start.7 = (bf16[384,128]{1,0:T(8,128)(2,1)S(1)}, bf16[384,128]{1,0:T(8,128)(2,1)S(1)}, u32[]{:S(2)}, u32[]{:S(2)}) collective-permute-start(bf16[384,128]{1,0:T(8,128)(2,1)S(1)} %get-tuple-element.50), channel_id=1, source_target_pairs={{0,1},{1,0},{2,3},{3,2},{4,5},{5,4},{6,7},{7,6},{8,9},{9,8},{10,11... | collective-permute-start | bytes 294920 | tf_op jit(solution)/shard_map/ppermute | solution.py:375
  26.5 7.7 %collective-permute-start.8 = (bf16[384,128]{1,0:T(8,128)(2,1)S(1)}, bf16[384,128]{1,0:T(8,128)(2,1)S(1)}, u32[]{:S(2)}, u32[]{:S(2)}) collective-permute-start(bf16[384,128]{1,0:T(8,128)(2,1)S(1)} %get-tuple-element.52), channel_id=1, source_target_pairs={{0,31},{1,2},{2,1},{3,4},{4,3},{5,6},{6,5},{7,8},{8,7},{9,10},{10,... | collective-permute-start | bytes 294920 | tf_op jit(solution)/shard_map/ppermute | solution.py:374
  29.0 5.1 %collective-permute-start.9 = (bf16[384,128]{1,0:T(8,128)(2,1)S(1)}, bf16[384,128]{1,0:T(8,128)(2,1)S(1)}, u32[]{:S(2)}, u32[]{:S(2)}) collective-permute-start(bf16[384,128]{1,0:T(8,128)(2,1)S(1)} %get-tuple-element.53), channel_id=1, source_target_pairs={{0,1},{1,0},{2,3},{3,2},{4,5},{5,4},{6,7},{7,6},{8,9},{9,8},{10,11... | collective-permute-start | bytes 294920 | tf_op jit(solution)/shard_map/ppermute | solution.py:375
  34.6 7.7 %collective-permute-start.10 = (bf16[384,128]{1,0:T(8,128)(2,1)S(1)}, bf16[384,128]{1,0:T(8,128)(2,1)S(1)}, u32[]{:S(2)}, u32[]{:S(2)}) collective-permute-start(bf16[384,128]{1,0:T(8,128)(2,1)S(1)} %get-tuple-element.57), channel_id=1, source_target_pairs={{0,31},{1,2},{2,1},{3,4},{4,3},{5,6},{6,5},{7,8},{8,7},{9,10},{10,... | collective-permute-start | bytes 294920 | tf_op jit(solution)/shard_map/ppermute | solution.py:374
  37.2 0.7 %copy-start.8 = (f32[5]{0:T(128)S(1)}, f32[5]{0:T(128)}, u32[]{:S(2)}) copy-start(f32[5]{0:T(128)} %coef.1) | copy-start | bytes 64
  37.2 5.1 %collective-permute-start.11 = (bf16[384,128]{1,0:T(8,128)(2,1)S(1)}, bf16[384,128]{1,0:T(8,128)(2,1)S(1)}, u32[]{:S(2)}, u32[]{:S(2)}) collective-permute-start(bf16[384,128]{1,0:T(8,128)(2,1)S(1)} %get-tuple-element.58), channel_id=1, source_target_pairs={{0,1},{1,0},{2,3},{3,2},{4,5},{5,4},{6,7},{7,6},{8,9},{9,8},{10,11... | collective-permute-start | bytes 294920 | tf_op jit(solution)/shard_map/ppermute | solution.py:375
  42.8 1.9 %collective-permute-start.12 = (bf16[32,512]{1,0:T(8,128)(2,1)S(1)}, bf16[32,512]{1,0:T(8,128)(2,1)S(1)}, u32[]{:S(2)}, u32[]{:S(2)}) collective-permute-start(bf16[32,512]{1,0:T(8,128)(2,1)S(1)} %get-tuple-element.60), channel_id=1, source_target_pairs={{0,1},{1,0},{2,3},{3,2},{4,5},{5,4},{6,7},{7,6},{8,9},{9,8},{10,11... | collective-permute-start | bytes 98312 | tf_op jit(solution)/shard_map/ppermute | solution.py:380
  42.9 4.2 %collective-permute-start.13 = (bf16[32,512]{1,0:T(8,128)(2,1)S(1)}, bf16[32,512]{1,0:T(8,128)(2,1)S(1)}, u32[]{:S(2)}, u32[]{:S(2)}) collective-permute-start(bf16[32,512]{1,0:T(8,128)(2,1)S(1)} %get-tuple-element.61), channel_id=1, source_target_pairs={{0,2},{1,3},{2,0},{3,1},{4,6},{5,7},{6,4},{7,5},{8,10},{9,11},{10,... | collective-permute-start | bytes 98312 | tf_op jit(solution)/shard_map/ppermute | solution.py:380
  43.0 4.1 %collective-permute-start.14 = (bf16[32,512]{1,0:T(8,128)(2,1)S(1)}, bf16[32,512]{1,0:T(8,128)(2,1)S(1)}, u32[]{:S(2)}, u32[]{:S(2)}) collective-permute-start(bf16[32,512]{1,0:T(8,128)(2,1)S(1)} %get-tuple-element.62), channel_id=1, source_target_pairs={{0,3},{1,2},{2,1},{3,0},{4,7},{5,6},{6,5},{7,4},{8,11},{9,10},{10,... | collective-permute-start | bytes 98312 | tf_op jit(solution)/shard_map/ppermute | solution.py:380

commit v17 on v16

--- a/solution.py
+++ b/solution.py
@@ -259,9 +259,9 @@
 
 
 def halo_part(band, blue, red, wide):
-    even = device_side() == 0
-    wide[0:HALO, :] = jnp.where(even, blue[...], red[...]).astype(F32)
-    wide[HALO : 2 * HALO, :] = jnp.where(even, red[...], blue[...]).astype(F32)
+    off = pl.multiple_of(device_side() * HALO, HALO)
+    wide[pl.ds(off, HALO), :] = blue[...].astype(F32)
+    wide[pl.ds(pl.multiple_of(HALO - off, HALO), HALO), :] = red[...].astype(F32)
     atoms = BAND * TILE_ATOMS
     pieces = [[], []]
     for q in range(ORB):
@@ -377,8 +377,8 @@
 
     def exchange(pieces):
         return [pieces[0]] + [
-            lax.ppermute(pieces[k], "edges", [(i, i ^ k) for i in range(nedge)]) for k in (1, 2, 3)
-        ]
+            lax.ppermute(pieces[k], "edges", [(i, i ^ k) for i in range(nedge)]) for k in (3, 2, 1)
+        ][::-1]
 
     msg = shape((SPILL + ID_ROWS, nfeat), BF)
     piece = shape((high, nrow), BF)
@@ -484,7 +484,9 @@
         blue,
         red,
     )
-    (result,) = call(join_kernel, "join", (shape((high, ncol), F32),), [], *exchange(pieces))
+    pieces = exchange(pieces)
+    pieces[3:] = call(pass_kernel, "pass", (piece,), [], pieces[3], micros=1)
+    (result,) = call(join_kernel, "join", (shape((high, ncol), F32),), [], *pieces)
     return result
 
 

time: 47.9 us -> 47.8 us (level)
    pallas_call x16 -> x17, Pallas kernels: 9.17 us -> 9.1 us  [call(): pl.pallas_call(kernel, name=name, out_shape=outs, in_specs=spaces, out_sp...]
  transfers between devices with their start and end apart: 15 -> 15, of which waited for: 5 -> 6; matrix products, arithmetic and copies ran while one was open for 0% -> 0% of each run, Pallas kernels for 14% -> 14%
where the time goes in v17:
time: 47.8 us; the launch traced here: 47.6 us
  starting transfers between devices  20.5 us (43%)
  waiting for transfers between devices  16 us (33%)
  Pallas kernels  9.1 us (19%)
  local copies, waits for them, and re-layouts  1.84 us (4%)
    ppermute x4, waiting for transfers between devices, swap(): lax.ppermute(first, axes, blue_pairs)  14.1 us
    ppermute x4, starting transfers between devices, swap(): lax.ppermute(first, axes, blue_pairs)  9.75 us
    pallas_call x17, Pallas kernels, call(): pl.pallas_call(kernel, name=name, out_shape=outs, in_specs=spaces, out_sp...  9.1 us
    ppermute x1, starting transfers between devices, per_device(): blue_msg = lax.ppermute(blue_msg, axes, blue_pairs)  5.37 us
    ppermute x1, starting transfers between devices, per_device(): across = lax.ppermute(across, 'edges', [(i, i ^ 3) for i in range(nedge)])  2.61 us
    ppermute x3, starting transfers between devices, exchange(): lax.ppermute(pieces[k], 'edges', [(i, i ^ k) for i in range(nedge)])  2.19 us
    ppermute x3, waiting for transfers between devices, exchange(): lax.ppermute(pieces[k], 'edges', [(i, i ^ k) for i in range(nedge)])  1.93 us
    unnamed x18, local copies, waits for them, and re-layouts  1.84 us
  transfers between devices with their start and end apart: 15, of which 6 were waited for; matrix products, arithmetic and copies ran while one was open for 0% of the time, Pallas kernels for 14%

profile of v17, /device:TPU:0, one launch (start us, length us, event | category | flops | bytes accessed | tf_op | source)
XLA Modules:
  0.0 47.6 jit_solution(8647828394797430252)
XLA Ops:
  0.0 0.9 %copy-done.1 = f32[32,2048]{1,0:T(8,128)S(1)} copy-done((f32[32,2048]{1,0:T(8,128)S(1)}, f32[32,2048]{1,0:T(8,128)}, u32[]{:S(2)}) %copy-start.1) | copy-done | bytes 262168
  1.0 0.2 copy-done
  1.3 0.5 %collective-permute-start = (bf16[400,256]{1,0:T(8,128)(2,1)S(1)}, bf16[400,256]{1,0:T(8,128)(2,1)S(1)}, u32[]{:S(2)}, u32[]{:S(2)}) collective-permute-start(bf16[400,256]{1,0:T(8,128)(2,1)S(1)} %get-tuple-element.35), channel_id=1, source_target_pairs={{0,1},{1,0},{2,3},{3,2},{4,5},{5,4},{6,7},{7,6},{8,9},{9,8},{10,11... | collective-permute-start | bytes 614408 | tf_op jit(solution)/shard_map/ppermute | solution.py:397
  1.8 2.6 %collective-permute-start.2 = (bf16[32,512]{1,0:T(8,128)(2,1)S(1)}, bf16[32,512]{1,0:T(8,128)(2,1)S(1)}, u32[]{:S(2)}, u32[]{:S(2)}) collective-permute-start(bf16[32,512]{1,0:T(8,128)(2,1)S(1)} %get-tuple-element.38), channel_id=1, source_target_pairs={{0,3},{1,2},{2,1},{3,0},{4,7},{5,6},{6,5},{7,4},{8,11},{9,10},{10,... | collective-permute-start | bytes 98312 | tf_op jit(solution)/shard_map/ppermute | solution.py:395
  4.4 0.0 collective-permute-start.1
  4.4 5.4 %collective-permute-start.3 = (bf16[336,256]{1,0:T(8,128)(2,1)S(1)}, bf16[336,256]{1,0:T(8,128)(2,1)S(1)}, u32[]{:S(2)}, u32[]{:S(2)}) collective-permute-start(bf16[336,256]{1,0:T(8,128)(2,1)S(1)} %get-tuple-element.41), channel_id=1, source_target_pairs={{0,31},{1,2},{2,1},{3,4},{4,3},{5,6},{6,5},{7,8},{8,7},{9,10},{10,... | collective-permute-start | bytes 516104 | tf_op jit(solution)/shard_map/ppermute | solution.py:398
  9.8 0.0 collective-permute-done.2.x
  9.8 0.0 collective-permute-done.1.p2
  9.8 0.0 collective-permute-done.near
  9.8 0.0 copy-start.5
  9.8 0.0 copy-start.6
  9.9 0.2 field.1
  10.1 0.0 copy-start.7
  10.1 2.1 %collective-permute-start.4 = (bf16[384,128]{1,0:T(8,128)(2,1)S(1)}, bf16[384,128]{1,0:T(8,128)(2,1)S(1)}, u32[]{:S(2)}, u32[]{:S(2)}) collective-permute-start(bf16[384,128]{1,0:T(8,128)(2,1)S(1)} %get-tuple-element.46), channel_id=1, source_target_pairs={{0,31},{1,2},{2,1},{3,4},{4,3},{5,6},{6,5},{7,8},{8,7},{9,10},{10,... | collective-permute-start | bytes 294920 | tf_op jit(solution)/shard_map/ppermute | solution.py:374
  12.1 0.0 collective-permute-start.5
  12.1 2.9 %own.1 = (bf16[2,256,1024]{2,1,0:T(8,128)(2,1)S(1)}, bf16[512,256]{1,0:T(8,128)(2,1)S(1)}, bf16[512,8]{1,0:T(8,128)(2,1)S(1)}, bf16[256,256]{1,0:T(8,128)(2,1)S(1)}) custom-call(bf16[1280,256]{1,0:T(8,128)(2,1)S(1)} %copy-done, s32[10,128]{1,0:T(8,128)S(1)} %bitcast.5, s32[10,128]{1,0:T(8,128)S(1)} %bitcast.8, s32[10,128]{1,0:T(8,128)S(1)} %bitcast.11, ...), custom_call_target="tpu_custom_call" | custom-call | flops 4000000000 | tf_op jit(solution)/shard_map/own/pallas_call | solution.py:349
  15.1 0.0 collective-permute-done.3.blue
  15.1 1.5 %spill.1.band = bf16[2,256,1024]{2,1,0:T(8,128)(2,1)S(1)} custom-call(bf16[2,256,1024]{2,1,0:T(8,128)(2,1)S(1)} %get-tuple-element.40.own_band, bf16[336,256]{1,0:T(8,128)(2,1)S(1)} %collective-permute-done.3.blue, bf16[512,256]{1,0:T(8,128)(2,1)S(1)} %get-tuple-element.42.w_in_t, ...), custom_call_target="tpu_custom_call", output_to_operand_aliasing={{}: (0, {})} | custom-call | tf_op jit(solution)/shard_map/spill/pallas_call | solution.py:349
  16.6 0.3 start.1.part
  16.9 0.8 %collective-permute-done.4.blue = bf16[384,128]{1,0:T(8,128)(2,1)S(1)} collective-permute-done((bf16[384,128]{1,0:T(8,128)(2,1)S(1)}, bf16[384,128]{1,0:T(8,128)(2,1)S(1)}, u32[]{:S(2)}, u32[]{:S(2)}) %collective-permute-start.4) | collective-permute-done | bytes 98336 | tf_op jit(solution)/shard_map/ppermute | solution.py:374
  17.8 0.0 collective-permute-done.5.red
  17.8 0.4 outer.3
  18.2 2.6 %collective-permute-start.6 = (bf16[384,128]{1,0:T(8,128)(2,1)S(1)}, bf16[384,128]{1,0:T(8,128)(2,1)S(1)}, u32[]{:S(2)}, u32[]{:S(2)}) collective-permute-start(bf16[384,128]{1,0:T(8,128)(2,1)S(1)} %get-tuple-element.49), channel_id=1, source_target_pairs={{0,31},{1,2},{2,1},{3,4},{4,3},{5,6},{6,5},{7,8},{8,7},{9,10},{10,... | collective-permute-start | bytes 294920 | tf_op jit(solution)/shard_map/ppermute | solution.py:374
  20.8 0.0 collective-permute-start.7
  20.8 0.3 inner.2.part
  21.2 4.9 %collective-permute-done.6.blue = bf16[384,128]{1,0:T(8,128)(2,1)S(1)} collective-permute-done((bf16[384,128]{1,0:T(8,128)(2,1)S(1)}, bf16[384,128]{1,0:T(8,128)(2,1)S(1)}, u32[]{:S(2)}, u32[]{:S(2)}) %collective-permute-start.6) | collective-permute-done | bytes 98336 | tf_op jit(solution)/shard_map/ppermute | solution.py:374
  26.0 0.0 collective-permute-done.7.red
  26.0 0.4 outer.4
  26.4 2.5 %collective-permute-start.8 = (bf16[384,128]{1,0:T(8,128)(2,1)S(1)}, bf16[384,128]{1,0:T(8,128)(2,1)S(1)}, u32[]{:S(2)}, u32[]{:S(2)}) collective-permute-start(bf16[384,128]{1,0:T(8,128)(2,1)S(1)} %get-tuple-element.52), channel_id=1, source_target_pairs={{0,31},{1,2},{2,1},{3,4},{4,3},{5,6},{6,5},{7,8},{8,7},{9,10},{10,... | collective-permute-start | bytes 294920 | tf_op jit(solution)/shard_map/ppermute | solution.py:374
  29.0 0.0 collective-permute-start.9
  29.0 0.3 inner.3.part
  29.3 4.8 %collective-permute-done.8.blue = bf16[384,128]{1,0:T(8,128)(2,1)S(1)} collective-permute-done((bf16[384,128]{1,0:T(8,128)(2,1)S(1)}, bf16[384,128]{1,0:T(8,128)(2,1)S(1)}, u32[]{:S(2)}, u32[]{:S(2)}) %collective-permute-start.8) | collective-permute-done | bytes 98336 | tf_op jit(solution)/shard_map/ppermute | solution.py:374
  34.1 0.0 collective-permute-done.9.red
  34.1 0.4 outer.5
  34.6 2.5 %collective-permute-start.10 = (bf16[384,128]{1,0:T(8,128)(2,1)S(1)}, bf16[384,128]{1,0:T(8,128)(2,1)S(1)}, u32[]{:S(2)}, u32[]{:S(2)}) collective-permute-start(bf16[384,128]{1,0:T(8,128)(2,1)S(1)} %get-tuple-element.57), channel_id=1, source_target_pairs={{0,31},{1,2},{2,1},{3,4},{4,3},{5,6},{6,5},{7,8},{8,7},{9,10},{10,... | collective-permute-start | bytes 294920 | tf_op jit(solution)/shard_map/ppermute | solution.py:374
  37.1 0.0 collective-permute-start.11
  37.1 0.7 %copy-done.8 = f32[5]{0:T(128)S(1)} copy-done((f32[5]{0:T(128)S(1)}, f32[5]{0:T(128)}, u32[]{:S(2)}) %copy-start.8) | copy-done | bytes 44
  37.8 0.9 %mix.1 = (f32[128,512]{1,0:T(8,128)S(1)}, f32[8,128]{1,0:T(8,128)S(1)}) custom-call(f32[5]{0:T(128)S(1)} %copy-done.8, bf16[2,256,1024]{2,1,0:T(8,128)(2,1)S(1)} %spill.1.band, f32[512,128]{1,0:T(8,128)S(1)} %get-tuple-element.45.now.before.t0, f32[512,128]{1,0:T(8,128)S(1)} %get-tuple-element.48.now.before.t1, f32[512,128]{1,0:T(8,128)S(1)} %get-tuple-element.51.now.t2, ...), custom_call_target="tpu_custom_call" | custom-call | flops 1000000000 | tf_op jit(solution)/shard_map/mix/pallas_call | solution.py:349
  38.7 3.6 %collective-permute-done.10.blue = bf16[384,128]{1,0:T(8,128)(2,1)S(1)} collective-permute-done((bf16[384,128]{1,0:T(8,128)(2,1)S(1)}, bf16[384,128]{1,0:T(8,128)(2,1)S(1)}, u32[]{:S(2)}, u32[]{:S(2)}) %collective-permute-start.10) | collective-permute-done | bytes 98336 | tf_op jit(solution)/shard_map/ppermute | solution.py:374
  42.3 0.0 collective-permute-done.11.red
  42.3 0.5 last.1
  42.8 0.1 collective-permute-start.14
  42.8 0.1 collective-permute-start.12
  42.9 2.0 %collective-permute-start.13 = (bf16[32,512]{1,0:T(8,128)(2,1)S(1)}, bf16[32,512]{1,0:T(8,128)(2,1)S(1)}, u32[]{:S(2)}, u32[]{:S(2)}) collective-permute-start(bf16[32,512]{1,0:T(8,128)(2,1)S(1)} %get-tuple-element.61), channel_id=1, source_target_pairs={{0,2},{1,3},{2,0},{3,1},{4,6},{5,7},{6,4},{7,5},{8,10},{9,11},{10,... | collective-permute-start | bytes 98312 | tf_op jit(solution)/shard_map/ppermute | solution.py:380
  45.0 1.2 %collective-permute-done.14.x = bf16[32,512]{1,0:T(8,128)(2,1)S(1)} collective-permute-done((bf16[32,512]{1,0:T(8,128)(2,1)S(1)}, bf16[32,512]{1,0:T(8,128)(2,1)S(1)}, u32[]{:S(2)}, u32[]{:S(2)}) %collective-permute-start.14) | collective-permute-done | bytes 32800 | tf_op jit(solution)/shard_map/ppermute | solution.py:380
  46.2 0.0 collective-permute-done.12.p1
  46.2 0.7 %collective-permute-done.13.p2 = bf16[32,512]{1,0:T(8,128)(2,1)S(1)} collective-permute-done((bf16[32,512]{1,0:T(8,128)(2,1)S(1)}, bf16[32,512]{1,0:T(8,128)(2,1)S(1)}, u32[]{:S(2)}, u32[]{:S(2)}) %collective-permute-start.13) | collective-permute-done | bytes 32800 | tf_op jit(solution)/shard_map/ppermute | solution.py:380
  46.9 0.7 %join.1 = f32[32,2048]{1,0:T(8,128)} custom-call(bf16[32,512]{1,0:T(8,128)(2,1)S(1)} %get-tuple-element.59.p0, bf16[32,512]{1,0:T(8,128)(2,1)S(1)} %collective-permute-done.12.p1, bf16[32,512]{1,0:T(8,128)(2,1)S(1)} %collective-permute-done.13.p2, bf16[32,512]{1,0:T(8,128)(2,1)S(1)} %pass.3.p3), custom_call_target="tpu_custom_call" | custom-call | flops 1000000000 | tf_op jit(solution)/shard_map/join/pallas_call | solution.py:349
  (17 shorter events, 0.1 us)
Async XLA Ops:
  0.0 0.9 %copy-start.1 = (f32[32,2048]{1,0:T(8,128)S(1)}, f32[32,2048]{1,0:T(8,128)}, u32[]{:S(2)}) copy-start(f32[32,2048]{1,0:T(8,128)} %vectors.1) | copy-start | bytes 786436
  0.0 1.0 %copy-start.2 = (s32[1280]{0:T(1024)S(1)}, s32[1280]{0:T(1024)}, u32[]{:S(2)}) copy-start(s32[1280]{0:T(1024)} %param.10) | copy-start | bytes 15364
  0.0 1.0 %copy-start.3 = (s32[1280]{0:T(1024)S(1)}, s32[1280]{0:T(1024)}, u32[]{:S(2)}) copy-start(s32[1280]{0:T(1024)} %param.11) | copy-start | bytes 15364
  0.0 1.0 %copy-start.4 = (s32[1280]{0:T(1024)S(1)}, s32[1280]{0:T(1024)}, u32[]{:S(2)}) copy-start(s32[1280]{0:T(1024)} %param.12) | copy-start | bytes 15364
  0.0 1.2 %copy-start = (bf16[1280,256]{1,0:T(8,128)(2,1)S(1)}, bf16[1280,256]{1,0:T(8,128)(2,1)}, u32[]{:S(2)}) copy-start(bf16[1280,256]{1,0:T(8,128)(2,1)} %feat.3) | copy-start | bytes 1966084
  1.3 8.6 %collective-permute-start = (bf16[400,256]{1,0:T(8,128)(2,1)S(1)}, bf16[400,256]{1,0:T(8,128)(2,1)S(1)}, u32[]{:S(2)}, u32[]{:S(2)}) collective-permute-start(bf16[400,256]{1,0:T(8,128)(2,1)S(1)} %get-tuple-element.35), channel_id=1, source_target_pairs={{0,1},{1,0},{2,3},{3,2},{4,5},{5,4},{6,7},{7,6},{8,9},{9,8},{10,11... | collective-permute-start | bytes 614408 | tf_op jit(solution)/shard_map/ppermute | solution.py:397
  1.8 8.0 %collective-permute-start.2 = (bf16[32,512]{1,0:T(8,128)(2,1)S(1)}, bf16[32,512]{1,0:T(8,128)(2,1)S(1)}, u32[]{:S(2)}, u32[]{:S(2)}) collective-permute-start(bf16[32,512]{1,0:T(8,128)(2,1)S(1)} %get-tuple-element.38), channel_id=1, source_target_pairs={{0,3},{1,2},{2,1},{3,0},{4,7},{5,6},{6,5},{7,4},{8,11},{9,10},{10,... | collective-permute-start | bytes 98312 | tf_op jit(solution)/shard_map/ppermute | solution.py:395
  4.4 5.4 %collective-permute-start.1 = (bf16[32,512]{1,0:T(8,128)(2,1)S(1)}, bf16[32,512]{1,0:T(8,128)(2,1)S(1)}, u32[]{:S(2)}, u32[]{:S(2)}) collective-permute-start(bf16[32,512]{1,0:T(8,128)(2,1)S(1)} %get-tuple-element.37), channel_id=1, source_target_pairs={{0,2},{1,3},{2,0},{3,1},{4,6},{5,7},{6,4},{7,5},{8,10},{9,11},{10,... | collective-permute-start | bytes 98312 | tf_op jit(solution)/shard_map/ppermute | solution.py:396
  4.4 10.6 %collective-permute-start.3 = (bf16[336,256]{1,0:T(8,128)(2,1)S(1)}, bf16[336,256]{1,0:T(8,128)(2,1)S(1)}, u32[]{:S(2)}, u32[]{:S(2)}) collective-permute-start(bf16[336,256]{1,0:T(8,128)(2,1)S(1)} %get-tuple-element.41), channel_id=1, source_target_pairs={{0,31},{1,2},{2,1},{3,4},{4,3},{5,6},{6,5},{7,8},{8,7},{9,10},{10,... | collective-permute-start | bytes 516104 | tf_op jit(solution)/shard_map/ppermute | solution.py:398
  9.8 2.3 %copy-start.5 = (bf16[256,512]{1,0:T(8,128)(2,1)S(1)}, bf16[256,512]{1,0:T(8,128)(2,1)}, u32[]{:S(2)}) copy-start(bf16[256,512]{1,0:T(8,128)(2,1)} %w_in.1) | copy-start | bytes 786436
  9.8 2.3 %copy-start.6 = (bf16[256,256]{1,0:T(8,128)(2,1)S(1)}, bf16[256,256]{1,0:T(8,128)(2,1)}, u32[]{:S(2)}) copy-start(bf16[256,256]{1,0:T(8,128)(2,1)} %w_out.1) | copy-start | bytes 393220
  10.1 2.1 %copy-start.7 = (bf16[3,512]{1,0:T(4,128)(2,1)S(1)}, bf16[3,512]{1,0:T(4,128)(2,1)}, u32[]{:S(2)}) copy-start(bf16[3,512]{1,0:T(4,128)(2,1)} %cell_bias.1) | copy-start | bytes 9220
  10.1 7.7 %collective-permute-start.4 = (bf16[384,128]{1,0:T(8,128)(2,1)S(1)}, bf16[384,128]{1,0:T(8,128)(2,1)S(1)}, u32[]{:S(2)}, u32[]{:S(2)}) collective-permute-start(bf16[384,128]{1,0:T(8,128)(2,1)S(1)} %get-tuple-element.46), channel_id=1, source_target_pairs={{0,31},{1,2},{2,1},{3,4},{4,3},{5,6},{6,5},{7,8},{8,7},{9,10},{10,... | collective-permute-start | bytes 294920 | tf_op jit(solution)/shard_map/ppermute | solution.py:374
  12.1 5.6 %collective-permute-start.5 = (bf16[384,128]{1,0:T(8,128)(2,1)S(1)}, bf16[384,128]{1,0:T(8,128)(2,1)S(1)}, u32[]{:S(2)}, u32[]{:S(2)}) collective-permute-start(bf16[384,128]{1,0:T(8,128)(2,1)S(1)} %get-tuple-element.47), channel_id=1, source_target_pairs={{0,1},{1,0},{2,3},{3,2},{4,5},{5,4},{6,7},{7,6},{8,9},{9,8},{10,11... | collective-permute-start | bytes 294920 | tf_op jit(solution)/shard_map/ppermute | solution.py:375
  18.2 7.8 %collective-permute-start.6 = (bf16[384,128]{1,0:T(8,128)(2,1)S(1)}, bf16[384,128]{1,0:T(8,128)(2,1)S(1)}, u32[]{:S(2)}, u32[]{:S(2)}) collective-permute-start(bf16[384,128]{1,0:T(8,128)(2,1)S(1)} %get-tuple-element.49), channel_id=1, source_target_pairs={{0,31},{1,2},{2,1},{3,4},{4,3},{5,6},{6,5},{7,8},{8,7},{9,10},{10,... | collective-permute-start | bytes 294920 | tf_op jit(solution)/shard_map/ppermute | solution.py:374
  20.8 5.2 %collective-permute-start.7 = (bf16[384,128]{1,0:T(8,128)(2,1)S(1)}, bf16[384,128]{1,0:T(8,128)(2,1)S(1)}, u32[]{:S(2)}, u32[]{:S(2)}) collective-permute-start(bf16[384,128]{1,0:T(8,128)(2,1)S(1)} %get-tuple-element.50), channel_id=1, source_target_pairs={{0,1},{1,0},{2,3},{3,2},{4,5},{5,4},{6,7},{7,6},{8,9},{9,8},{10,11... | collective-permute-start | bytes 294920 | tf_op jit(solution)/shard_map/ppermute | solution.py:375
  26.4 7.7 %collective-permute-start.8 = (bf16[384,128]{1,0:T(8,128)(2,1)S(1)}, bf16[384,128]{1,0:T(8,128)(2,1)S(1)}, u32[]{:S(2)}, u32[]{:S(2)}) collective-permute-start(bf16[384,128]{1,0:T(8,128)(2,1)S(1)} %get-tuple-element.52), channel_id=1, source_target_pairs={{0,31},{1,2},{2,1},{3,4},{4,3},{5,6},{6,5},{7,8},{8,7},{9,10},{10,... | collective-permute-start | bytes 294920 | tf_op jit(solution)/shard_map/ppermute | solution.py:374
  29.0 5.2 %collective-permute-start.9 = (bf16[384,128]{1,0:T(8,128)(2,1)S(1)}, bf16[384,128]{1,0:T(8,128)(2,1)S(1)}, u32[]{:S(2)}, u32[]{:S(2)}) collective-permute-start(bf16[384,128]{1,0:T(8,128)(2,1)S(1)} %get-tuple-element.53), channel_id=1, source_target_pairs={{0,1},{1,0},{2,3},{3,2},{4,5},{5,4},{6,7},{7,6},{8,9},{9,8},{10,11... | collective-permute-start | bytes 294920 | tf_op jit(solution)/shard_map/ppermute | solution.py:375
  34.6 7.7 %collective-permute-start.10 = (bf16[384,128]{1,0:T(8,128)(2,1)S(1)}, bf16[384,128]{1,0:T(8,128)(2,1)S(1)}, u32[]{:S(2)}, u32[]{:S(2)}) collective-permute-start(bf16[384,128]{1,0:T(8,128)(2,1)S(1)} %get-tuple-element.57), channel_id=1, source_target_pairs={{0,31},{1,2},{2,1},{3,4},{4,3},{5,6},{6,5},{7,8},{8,7},{9,10},{10,... | collective-permute-start | bytes 294920 | tf_op jit(solution)/shard_map/ppermute | solution.py:374
  37.1 0.7 %copy-start.8 = (f32[5]{0:T(128)S(1)}, f32[5]{0:T(128)}, u32[]{:S(2)}) copy-start(f32[5]{0:T(128)} %coef.1) | copy-start | bytes 64
  37.1 5.2 %collective-permute-start.11 = (bf16[384,128]{1,0:T(8,128)(2,1)S(1)}, bf16[384,128]{1,0:T(8,128)(2,1)S(1)}, u32[]{:S(2)}, u32[]{:S(2)}) collective-permute-start(bf16[384,128]{1,0:T(8,128)(2,1)S(1)} %get-tuple-element.58), channel_id=1, source_target_pairs={{0,1},{1,0},{2,3},{3,2},{4,5},{5,4},{6,7},{7,6},{8,9},{9,8},{10,11... | collective-permute-start | bytes 294920 | tf_op jit(solution)/shard_map/ppermute | solution.py:375
  42.8 3.4 %collective-permute-start.14 = (bf16[32,512]{1,0:T(8,128)(2,1)S(1)}, bf16[32,512]{1,0:T(8,128)(2,1)S(1)}, u32[]{:S(2)}, u32[]{:S(2)}) collective-permute-start(bf16[32,512]{1,0:T(8,128)(2,1)S(1)} %get-tuple-element.62), channel_id=1, source_target_pairs={{0,3},{1,2},{2,1},{3,0},{4,7},{5,6},{6,5},{7,4},{8,11},{9,10},{10,... | collective-permute-start | bytes 98312 | tf_op jit(solution)/shard_map/ppermute | solution.py:380
  42.8 3.3 %collective-permute-start.12 = (bf16[32,512]{1,0:T(8,128)(2,1)S(1)}, bf16[32,512]{1,0:T(8,128)(2,1)S(1)}, u32[]{:S(2)}, u32[]{:S(2)}) collective-permute-start(bf16[32,512]{1,0:T(8,128)(2,1)S(1)} %get-tuple-element.60), channel_id=1, source_target_pairs={{0,1},{1,0},{2,3},{3,2},{4,5},{5,4},{6,7},{7,6},{8,9},{9,8},{10,11... | collective-permute-start | bytes 98312 | tf_op jit(solution)/shard_map/ppermute | solution.py:380
  42.9 4.0 %collective-permute-start.13 = (bf16[32,512]{1,0:T(8,128)(2,1)S(1)}, bf16[32,512]{1,0:T(8,128)(2,1)S(1)}, u32[]{:S(2)}, u32[]{:S(2)}) collective-permute-start(bf16[32,512]{1,0:T(8,128)(2,1)S(1)} %get-tuple-element.61), channel_id=1, source_target_pairs={{0,2},{1,3},{2,0},{3,1},{4,6},{5,7},{6,4},{7,5},{8,10},{9,11},{10,... | collective-permute-start | bytes 98312 | tf_op jit(solution)/shard_map/ppermute | solution.py:380

commit v18 on v17

--- a/solution.py
+++ b/solution.py
@@ -396,7 +396,7 @@
     straight = lax.ppermute(straight, "edges", [(i, i ^ 2) for i in range(nedge)])
     near = lax.ppermute(near, axes, red_pairs)
     blue_msg = lax.ppermute(blue_msg, axes, blue_pairs)
-    (across,) = call(pass_kernel, "pass", (piece,), [], across, micros=0)
+    (straight,) = call(pass_kernel, "pass", (piece,), [], straight, micros=0)
     pieces = [own_piece, near, straight, across]
     full, part = shape((nrow, VEC), F32), shape((HALO, VEC), BF)
     t0, to_blue, to_red, token = call(

time: 47.8 us -> 48 us (level)
  starting transfers between devices: 20.5 us -> 21.1 us
    ppermute x1, starting transfers between devices: 2.61 us -> 0.07 us  [per_device(): across = lax.ppermute(across, 'edges', [(i, i ^ 3) for i in range(nedge)])]
    ppermute x1, starting transfers between devices: 0.04 us -> 2.56 us  [per_device(): lax.ppermute(straight, 'edges', [(i, i ^ 2) for i in range(nedge)])]
where the time goes in v18:
time: 48 us; the launch traced here: 47.9 us
  starting transfers between devices  21.1 us (44%)
  waiting for transfers between devices  15.7 us (33%)
  Pallas kernels  9.1 us (19%)
  local copies, waits for them, and re-layouts  1.84 us (4%)
    ppermute x4, waiting for transfers between devices, swap(): lax.ppermute(first, axes, blue_pairs)  13.7 us
    ppermute x4, starting transfers between devices, swap(): lax.ppermute(first, axes, blue_pairs)  10.1 us
    pallas_call x17, Pallas kernels, call(): pl.pallas_call(kernel, name=name, out_shape=outs, in_specs=spaces, out_sp...  9.1 us
    ppermute x1, starting transfers between devices, per_device(): blue_msg = lax.ppermute(blue_msg, axes, blue_pairs)  5.67 us
    ppermute x1, starting transfers between devices, per_device(): lax.ppermute(straight, 'edges', [(i, i ^ 2) for i in range(nedge)])  2.56 us
    ppermute x3, starting transfers between devices, exchange(): lax.ppermute(pieces[k], 'edges', [(i, i ^ k) for i in range(nedge)])  2.19 us
    ppermute x3, waiting for transfers between devices, exchange(): lax.ppermute(pieces[k], 'edges', [(i, i ^ k) for i in range(nedge)])  1.93 us
    unnamed x18, local copies, waits for them, and re-layouts  1.84 us
  transfers between devices with their start and end apart: 15, of which 6 were waited for; matrix products, arithmetic and copies ran while one was open for 0% of the time, Pallas kernels for 14%

profile of v18, /device:TPU:0, one launch (start us, length us, event | category | flops | bytes accessed | tf_op | source)
XLA Modules:
  0.0 47.9 jit_solution(4841740992102390088)
XLA Ops:
  0.0 0.9 %copy-done.1 = f32[32,2048]{1,0:T(8,128)S(1)} copy-done((f32[32,2048]{1,0:T(8,128)S(1)}, f32[32,2048]{1,0:T(8,128)}, u32[]{:S(2)}) %copy-start.1) | copy-done | bytes 262168
  1.0 0.2 copy-done
  1.3 0.5 %collective-permute-start = (bf16[400,256]{1,0:T(8,128)(2,1)S(1)}, bf16[400,256]{1,0:T(8,128)(2,1)S(1)}, u32[]{:S(2)}, u32[]{:S(2)}) collective-permute-start(bf16[400,256]{1,0:T(8,128)(2,1)S(1)} %get-tuple-element.35), channel_id=1, source_target_pairs={{0,1},{1,0},{2,3},{3,2},{4,5},{5,4},{6,7},{7,6},{8,9},{9,8},{10,11... | collective-permute-start | bytes 614408 | tf_op jit(solution)/shard_map/ppermute | solution.py:397
  1.8 2.6 %collective-permute-start.1 = (bf16[32,512]{1,0:T(8,128)(2,1)S(1)}, bf16[32,512]{1,0:T(8,128)(2,1)S(1)}, u32[]{:S(2)}, u32[]{:S(2)}) collective-permute-start(bf16[32,512]{1,0:T(8,128)(2,1)S(1)} %get-tuple-element.37), channel_id=1, source_target_pairs={{0,2},{1,3},{2,0},{3,1},{4,6},{5,7},{6,4},{7,5},{8,10},{9,11},{10,... | collective-permute-start | bytes 98312 | tf_op jit(solution)/shard_map/ppermute | solution.py:396
  4.4 0.1 collective-permute-start.2
  4.4 5.7 %collective-permute-start.3 = (bf16[336,256]{1,0:T(8,128)(2,1)S(1)}, bf16[336,256]{1,0:T(8,128)(2,1)S(1)}, u32[]{:S(2)}, u32[]{:S(2)}) collective-permute-start(bf16[336,256]{1,0:T(8,128)(2,1)S(1)} %get-tuple-element.41), channel_id=1, source_target_pairs={{0,31},{1,2},{2,1},{3,4},{4,3},{5,6},{6,5},{7,8},{8,7},{9,10},{10,... | collective-permute-start | bytes 516104 | tf_op jit(solution)/shard_map/ppermute | solution.py:398
  10.1 0.0 collective-permute-done.1.x
  10.1 0.0 collective-permute-done.2.p3
  10.1 0.0 collective-permute-done.near
  10.1 0.0 copy-start.5
  10.1 0.0 copy-start.6
  10.1 0.2 field.1
  10.3 0.0 copy-start.7
  10.3 2.3 %collective-permute-start.4 = (bf16[384,128]{1,0:T(8,128)(2,1)S(1)}, bf16[384,128]{1,0:T(8,128)(2,1)S(1)}, u32[]{:S(2)}, u32[]{:S(2)}) collective-permute-start(bf16[384,128]{1,0:T(8,128)(2,1)S(1)} %get-tuple-element.46), channel_id=1, source_target_pairs={{0,31},{1,2},{2,1},{3,4},{4,3},{5,6},{6,5},{7,8},{8,7},{9,10},{10,... | collective-permute-start | bytes 294920 | tf_op jit(solution)/shard_map/ppermute | solution.py:374
  12.6 0.0 collective-permute-start.5
  12.7 2.9 %own.1 = (bf16[2,256,1024]{2,1,0:T(8,128)(2,1)S(1)}, bf16[512,256]{1,0:T(8,128)(2,1)S(1)}, bf16[512,8]{1,0:T(8,128)(2,1)S(1)}, bf16[256,256]{1,0:T(8,128)(2,1)S(1)}) custom-call(bf16[1280,256]{1,0:T(8,128)(2,1)S(1)} %copy-done, s32[10,128]{1,0:T(8,128)S(1)} %bitcast.5, s32[10,128]{1,0:T(8,128)S(1)} %bitcast.8, s32[10,128]{1,0:T(8,128)S(1)} %bitcast.11, ...), custom_call_target="tpu_custom_call" | custom-call | flops 4000000000 | tf_op jit(solution)/shard_map/own/pallas_call | solution.py:349
  15.6 0.0 collective-permute-done.3.blue
  15.6 1.5 %spill.1.band = bf16[2,256,1024]{2,1,0:T(8,128)(2,1)S(1)} custom-call(bf16[2,256,1024]{2,1,0:T(8,128)(2,1)S(1)} %get-tuple-element.40.own_band, bf16[336,256]{1,0:T(8,128)(2,1)S(1)} %collective-permute-done.3.blue, bf16[512,256]{1,0:T(8,128)(2,1)S(1)} %get-tuple-element.42.w_in_t, ...), custom_call_target="tpu_custom_call", output_to_operand_aliasing={{}: (0, {})} | custom-call | tf_op jit(solution)/shard_map/spill/pallas_call | solution.py:349
  17.1 0.3 start.1.part
  17.4 0.6 %collective-permute-done.4.blue = bf16[384,128]{1,0:T(8,128)(2,1)S(1)} collective-permute-done((bf16[384,128]{1,0:T(8,128)(2,1)S(1)}, bf16[384,128]{1,0:T(8,128)(2,1)S(1)}, u32[]{:S(2)}, u32[]{:S(2)}) %collective-permute-start.4) | collective-permute-done | bytes 98336 | tf_op jit(solution)/shard_map/ppermute | solution.py:374
  18.1 0.0 collective-permute-done.5.red
  18.1 0.4 outer.3
  18.5 2.6 %collective-permute-start.6 = (bf16[384,128]{1,0:T(8,128)(2,1)S(1)}, bf16[384,128]{1,0:T(8,128)(2,1)S(1)}, u32[]{:S(2)}, u32[]{:S(2)}) collective-permute-start(bf16[384,128]{1,0:T(8,128)(2,1)S(1)} %get-tuple-element.49), channel_id=1, source_target_pairs={{0,31},{1,2},{2,1},{3,4},{4,3},{5,6},{6,5},{7,8},{8,7},{9,10},{10,... | collective-permute-start | bytes 294920 | tf_op jit(solution)/shard_map/ppermute | solution.py:374
  21.1 0.0 collective-permute-start.7
  21.1 0.3 inner.2.part
  21.4 4.9 %collective-permute-done.6.blue = bf16[384,128]{1,0:T(8,128)(2,1)S(1)} collective-permute-done((bf16[384,128]{1,0:T(8,128)(2,1)S(1)}, bf16[384,128]{1,0:T(8,128)(2,1)S(1)}, u32[]{:S(2)}, u32[]{:S(2)}) %collective-permute-start.6) | collective-permute-done | bytes 98336 | tf_op jit(solution)/shard_map/ppermute | solution.py:374
  26.3 0.0 collective-permute-done.7.red
  26.3 0.4 outer.4
  26.7 2.6 %collective-permute-start.8 = (bf16[384,128]{1,0:T(8,128)(2,1)S(1)}, bf16[384,128]{1,0:T(8,128)(2,1)S(1)}, u32[]{:S(2)}, u32[]{:S(2)}) collective-permute-start(bf16[384,128]{1,0:T(8,128)(2,1)S(1)} %get-tuple-element.52), channel_id=1, source_target_pairs={{0,31},{1,2},{2,1},{3,4},{4,3},{5,6},{6,5},{7,8},{8,7},{9,10},{10,... | collective-permute-start | bytes 294920 | tf_op jit(solution)/shard_map/ppermute | solution.py:374
  29.3 0.0 collective-permute-start.9
  29.3 0.3 inner.3.part
  29.7 4.8 %collective-permute-done.8.blue = bf16[384,128]{1,0:T(8,128)(2,1)S(1)} collective-permute-done((bf16[384,128]{1,0:T(8,128)(2,1)S(1)}, bf16[384,128]{1,0:T(8,128)(2,1)S(1)}, u32[]{:S(2)}, u32[]{:S(2)}) %collective-permute-start.8) | collective-permute-done | bytes 98336 | tf_op jit(solution)/shard_map/ppermute | solution.py:374
  34.4 0.0 collective-permute-done.9.red
  34.4 0.4 outer.5
  34.9 2.6 %collective-permute-start.10 = (bf16[384,128]{1,0:T(8,128)(2,1)S(1)}, bf16[384,128]{1,0:T(8,128)(2,1)S(1)}, u32[]{:S(2)}, u32[]{:S(2)}) collective-permute-start(bf16[384,128]{1,0:T(8,128)(2,1)S(1)} %get-tuple-element.57), channel_id=1, source_target_pairs={{0,31},{1,2},{2,1},{3,4},{4,3},{5,6},{6,5},{7,8},{8,7},{9,10},{10,... | collective-permute-start | bytes 294920 | tf_op jit(solution)/shard_map/ppermute | solution.py:374
  37.4 0.0 collective-permute-start.11
  37.4 0.7 %copy-done.8 = f32[5]{0:T(128)S(1)} copy-done((f32[5]{0:T(128)S(1)}, f32[5]{0:T(128)}, u32[]{:S(2)}) %copy-start.8) | copy-done | bytes 44
  38.1 0.9 %mix.1 = (f32[128,512]{1,0:T(8,128)S(1)}, f32[8,128]{1,0:T(8,128)S(1)}) custom-call(f32[5]{0:T(128)S(1)} %copy-done.8, bf16[2,256,1024]{2,1,0:T(8,128)(2,1)S(1)} %spill.1.band, f32[512,128]{1,0:T(8,128)S(1)} %get-tuple-element.45.now.before.t0, f32[512,128]{1,0:T(8,128)S(1)} %get-tuple-element.48.now.before.t1, f32[512,128]{1,0:T(8,128)S(1)} %get-tuple-element.51.now.t2, ...), custom_call_target="tpu_custom_call" | custom-call | flops 1000000000 | tf_op jit(solution)/shard_map/mix/pallas_call | solution.py:349
  39.0 3.5 %collective-permute-done.10.blue = bf16[384,128]{1,0:T(8,128)(2,1)S(1)} collective-permute-done((bf16[384,128]{1,0:T(8,128)(2,1)S(1)}, bf16[384,128]{1,0:T(8,128)(2,1)S(1)}, u32[]{:S(2)}, u32[]{:S(2)}) %collective-permute-start.10) | collective-permute-done | bytes 98336 | tf_op jit(solution)/shard_map/ppermute | solution.py:374
  42.6 0.0 collective-permute-done.11.red
  42.6 0.5 last.1
  43.0 0.1 collective-permute-start.14
  43.1 0.1 collective-permute-start.12
  43.2 2.0 %collective-permute-start.13 = (bf16[32,512]{1,0:T(8,128)(2,1)S(1)}, bf16[32,512]{1,0:T(8,128)(2,1)S(1)}, u32[]{:S(2)}, u32[]{:S(2)}) collective-permute-start(bf16[32,512]{1,0:T(8,128)(2,1)S(1)} %get-tuple-element.61), channel_id=1, source_target_pairs={{0,2},{1,3},{2,0},{3,1},{4,6},{5,7},{6,4},{7,5},{8,10},{9,11},{10,... | collective-permute-start | bytes 98312 | tf_op jit(solution)/shard_map/ppermute | solution.py:380
  45.2 1.2 %collective-permute-done.14.x = bf16[32,512]{1,0:T(8,128)(2,1)S(1)} collective-permute-done((bf16[32,512]{1,0:T(8,128)(2,1)S(1)}, bf16[32,512]{1,0:T(8,128)(2,1)S(1)}, u32[]{:S(2)}, u32[]{:S(2)}) %collective-permute-start.14) | collective-permute-done | bytes 32800 | tf_op jit(solution)/shard_map/ppermute | solution.py:380
  46.4 0.0 collective-permute-done.12.p1
  46.5 0.7 %collective-permute-done.13.p2 = bf16[32,512]{1,0:T(8,128)(2,1)S(1)} collective-permute-done((bf16[32,512]{1,0:T(8,128)(2,1)S(1)}, bf16[32,512]{1,0:T(8,128)(2,1)S(1)}, u32[]{:S(2)}, u32[]{:S(2)}) %collective-permute-start.13) | collective-permute-done | bytes 32800 | tf_op jit(solution)/shard_map/ppermute | solution.py:380
  47.2 0.7 %join.1 = f32[32,2048]{1,0:T(8,128)} custom-call(bf16[32,512]{1,0:T(8,128)(2,1)S(1)} %get-tuple-element.59.p0, bf16[32,512]{1,0:T(8,128)(2,1)S(1)} %collective-permute-done.12.p1, bf16[32,512]{1,0:T(8,128)(2,1)S(1)} %collective-permute-done.13.p2, bf16[32,512]{1,0:T(8,128)(2,1)S(1)} %pass.3.p3), custom_call_target="tpu_custom_call" | custom-call | flops 1000000000 | tf_op jit(solution)/shard_map/join/pallas_call | solution.py:349
  (17 shorter events, 0.1 us)
Async XLA Ops:
  0.0 0.9 %copy-start.1 = (f32[32,2048]{1,0:T(8,128)S(1)}, f32[32,2048]{1,0:T(8,128)}, u32[]{:S(2)}) copy-start(f32[32,2048]{1,0:T(8,128)} %vectors.1) | copy-start | bytes 786436
  0.0 1.0 %copy-start.2 = (s32[1280]{0:T(1024)S(1)}, s32[1280]{0:T(1024)}, u32[]{:S(2)}) copy-start(s32[1280]{0:T(1024)} %param.10) | copy-start | bytes 15364
  0.0 1.0 %copy-start.3 = (s32[1280]{0:T(1024)S(1)}, s32[1280]{0:T(1024)}, u32[]{:S(2)}) copy-start(s32[1280]{0:T(1024)} %param.11) | copy-start | bytes 15364
  0.0 1.0 %copy-start.4 = (s32[1280]{0:T(1024)S(1)}, s32[1280]{0:T(1024)}, u32[]{:S(2)}) copy-start(s32[1280]{0:T(1024)} %param.12) | copy-start | bytes 15364
  0.0 1.2 %copy-start = (bf16[1280,256]{1,0:T(8,128)(2,1)S(1)}, bf16[1280,256]{1,0:T(8,128)(2,1)}, u32[]{:S(2)}) copy-start(bf16[1280,256]{1,0:T(8,128)(2,1)} %feat.3) | copy-start | bytes 1966084
  1.3 8.8 %collective-permute-start = (bf16[400,256]{1,0:T(8,128)(2,1)S(1)}, bf16[400,256]{1,0:T(8,128)(2,1)S(1)}, u32[]{:S(2)}, u32[]{:S(2)}) collective-permute-start(bf16[400,256]{1,0:T(8,128)(2,1)S(1)} %get-tuple-element.35), channel_id=1, source_target_pairs={{0,1},{1,0},{2,3},{3,2},{4,5},{5,4},{6,7},{7,6},{8,9},{9,8},{10,11... | collective-permute-start | bytes 614408 | tf_op jit(solution)/shard_map/ppermute | solution.py:397
  1.8 8.3 %collective-permute-start.1 = (bf16[32,512]{1,0:T(8,128)(2,1)S(1)}, bf16[32,512]{1,0:T(8,128)(2,1)S(1)}, u32[]{:S(2)}, u32[]{:S(2)}) collective-permute-start(bf16[32,512]{1,0:T(8,128)(2,1)S(1)} %get-tuple-element.37), channel_id=1, source_target_pairs={{0,2},{1,3},{2,0},{3,1},{4,6},{5,7},{6,4},{7,5},{8,10},{9,11},{10,... | collective-permute-start | bytes 98312 | tf_op jit(solution)/shard_map/ppermute | solution.py:396
  4.4 5.8 %collective-permute-start.2 = (bf16[32,512]{1,0:T(8,128)(2,1)S(1)}, bf16[32,512]{1,0:T(8,128)(2,1)S(1)}, u32[]{:S(2)}, u32[]{:S(2)}) collective-permute-start(bf16[32,512]{1,0:T(8,128)(2,1)S(1)} %get-tuple-element.38), channel_id=1, source_target_pairs={{0,3},{1,2},{2,1},{3,0},{4,7},{5,6},{6,5},{7,4},{8,11},{9,10},{10,... | collective-permute-start | bytes 98312 | tf_op jit(solution)/shard_map/ppermute | solution.py:395
  4.4 11.2 %collective-permute-start.3 = (bf16[336,256]{1,0:T(8,128)(2,1)S(1)}, bf16[336,256]{1,0:T(8,128)(2,1)S(1)}, u32[]{:S(2)}, u32[]{:S(2)}) collective-permute-start(bf16[336,256]{1,0:T(8,128)(2,1)S(1)} %get-tuple-element.41), channel_id=1, source_target_pairs={{0,31},{1,2},{2,1},{3,4},{4,3},{5,6},{6,5},{7,8},{8,7},{9,10},{10,... | collective-permute-start | bytes 516104 | tf_op jit(solution)/shard_map/ppermute | solution.py:398
  10.1 2.5 %copy-start.5 = (bf16[256,512]{1,0:T(8,128)(2,1)S(1)}, bf16[256,512]{1,0:T(8,128)(2,1)}, u32[]{:S(2)}) copy-start(bf16[256,512]{1,0:T(8,128)(2,1)} %w_in.1) | copy-start | bytes 786436
  10.1 2.5 %copy-start.6 = (bf16[256,256]{1,0:T(8,128)(2,1)S(1)}, bf16[256,256]{1,0:T(8,128)(2,1)}, u32[]{:S(2)}) copy-start(bf16[256,256]{1,0:T(8,128)(2,1)} %w_out.1) | copy-start | bytes 393220
  10.3 2.3 %copy-start.7 = (bf16[3,512]{1,0:T(4,128)(2,1)S(1)}, bf16[3,512]{1,0:T(4,128)(2,1)}, u32[]{:S(2)}) copy-start(bf16[3,512]{1,0:T(4,128)(2,1)} %cell_bias.1) | copy-start | bytes 9220
  10.3 7.7 %collective-permute-start.4 = (bf16[384,128]{1,0:T(8,128)(2,1)S(1)}, bf16[384,128]{1,0:T(8,128)(2,1)S(1)}, u32[]{:S(2)}, u32[]{:S(2)}) collective-permute-start(bf16[384,128]{1,0:T(8,128)(2,1)S(1)} %get-tuple-element.46), channel_id=1, source_target_pairs={{0,31},{1,2},{2,1},{3,4},{4,3},{5,6},{6,5},{7,8},{8,7},{9,10},{10,... | collective-permute-start | bytes 294920 | tf_op jit(solution)/shard_map/ppermute | solution.py:374
  12.6 5.4 %collective-permute-start.5 = (bf16[384,128]{1,0:T(8,128)(2,1)S(1)}, bf16[384,128]{1,0:T(8,128)(2,1)S(1)}, u32[]{:S(2)}, u32[]{:S(2)}) collective-permute-start(bf16[384,128]{1,0:T(8,128)(2,1)S(1)} %get-tuple-element.47), channel_id=1, source_target_pairs={{0,1},{1,0},{2,3},{3,2},{4,5},{5,4},{6,7},{7,6},{8,9},{9,8},{10,11... | collective-permute-start | bytes 294920 | tf_op jit(solution)/shard_map/ppermute | solution.py:375
  18.5 7.8 %collective-permute-start.6 = (bf16[384,128]{1,0:T(8,128)(2,1)S(1)}, bf16[384,128]{1,0:T(8,128)(2,1)S(1)}, u32[]{:S(2)}, u32[]{:S(2)}) collective-permute-start(bf16[384,128]{1,0:T(8,128)(2,1)S(1)} %get-tuple-element.49), channel_id=1, source_target_pairs={{0,31},{1,2},{2,1},{3,4},{4,3},{5,6},{6,5},{7,8},{8,7},{9,10},{10,... | collective-permute-start | bytes 294920 | tf_op jit(solution)/shard_map/ppermute | solution.py:374
  21.1 5.2 %collective-permute-start.7 = (bf16[384,128]{1,0:T(8,128)(2,1)S(1)}, bf16[384,128]{1,0:T(8,128)(2,1)S(1)}, u32[]{:S(2)}, u32[]{:S(2)}) collective-permute-start(bf16[384,128]{1,0:T(8,128)(2,1)S(1)} %get-tuple-element.50), channel_id=1, source_target_pairs={{0,1},{1,0},{2,3},{3,2},{4,5},{5,4},{6,7},{7,6},{8,9},{9,8},{10,11... | collective-permute-start | bytes 294920 | tf_op jit(solution)/shard_map/ppermute | solution.py:375
  26.7 7.7 %collective-permute-start.8 = (bf16[384,128]{1,0:T(8,128)(2,1)S(1)}, bf16[384,128]{1,0:T(8,128)(2,1)S(1)}, u32[]{:S(2)}, u32[]{:S(2)}) collective-permute-start(bf16[384,128]{1,0:T(8,128)(2,1)S(1)} %get-tuple-element.52), channel_id=1, source_target_pairs={{0,31},{1,2},{2,1},{3,4},{4,3},{5,6},{6,5},{7,8},{8,7},{9,10},{10,... | collective-permute-start | bytes 294920 | tf_op jit(solution)/shard_map/ppermute | solution.py:374
  29.3 5.1 %collective-permute-start.9 = (bf16[384,128]{1,0:T(8,128)(2,1)S(1)}, bf16[384,128]{1,0:T(8,128)(2,1)S(1)}, u32[]{:S(2)}, u32[]{:S(2)}) collective-permute-start(bf16[384,128]{1,0:T(8,128)(2,1)S(1)} %get-tuple-element.53), channel_id=1, source_target_pairs={{0,1},{1,0},{2,3},{3,2},{4,5},{5,4},{6,7},{7,6},{8,9},{9,8},{10,11... | collective-permute-start | bytes 294920 | tf_op jit(solution)/shard_map/ppermute | solution.py:375
  34.9 7.7 %collective-permute-start.10 = (bf16[384,128]{1,0:T(8,128)(2,1)S(1)}, bf16[384,128]{1,0:T(8,128)(2,1)S(1)}, u32[]{:S(2)}, u32[]{:S(2)}) collective-permute-start(bf16[384,128]{1,0:T(8,128)(2,1)S(1)} %get-tuple-element.57), channel_id=1, source_target_pairs={{0,31},{1,2},{2,1},{3,4},{4,3},{5,6},{6,5},{7,8},{8,7},{9,10},{10,... | collective-permute-start | bytes 294920 | tf_op jit(solution)/shard_map/ppermute | solution.py:374
  37.4 0.7 %copy-start.8 = (f32[5]{0:T(128)S(1)}, f32[5]{0:T(128)}, u32[]{:S(2)}) copy-start(f32[5]{0:T(128)} %coef.1) | copy-start | bytes 64
  37.4 5.1 %collective-permute-start.11 = (bf16[384,128]{1,0:T(8,128)(2,1)S(1)}, bf16[384,128]{1,0:T(8,128)(2,1)S(1)}, u32[]{:S(2)}, u32[]{:S(2)}) collective-permute-start(bf16[384,128]{1,0:T(8,128)(2,1)S(1)} %get-tuple-element.58), channel_id=1, source_target_pairs={{0,1},{1,0},{2,3},{3,2},{4,5},{5,4},{6,7},{7,6},{8,9},{9,8},{10,11... | collective-permute-start | bytes 294920 | tf_op jit(solution)/shard_map/ppermute | solution.py:375
  43.0 3.4 %collective-permute-start.14 = (bf16[32,512]{1,0:T(8,128)(2,1)S(1)}, bf16[32,512]{1,0:T(8,128)(2,1)S(1)}, u32[]{:S(2)}, u32[]{:S(2)}) collective-permute-start(bf16[32,512]{1,0:T(8,128)(2,1)S(1)} %get-tuple-element.62), channel_id=1, source_target_pairs={{0,3},{1,2},{2,1},{3,0},{4,7},{5,6},{6,5},{7,4},{8,11},{9,10},{10,... | collective-permute-start | bytes 98312 | tf_op jit(solution)/shard_map/ppermute | solution.py:380
  43.1 3.3 %collective-permute-start.12 = (bf16[32,512]{1,0:T(8,128)(2,1)S(1)}, bf16[32,512]{1,0:T(8,128)(2,1)S(1)}, u32[]{:S(2)}, u32[]{:S(2)}) collective-permute-start(bf16[32,512]{1,0:T(8,128)(2,1)S(1)} %get-tuple-element.60), channel_id=1, source_target_pairs={{0,1},{1,0},{2,3},{3,2},{4,5},{5,4},{6,7},{7,6},{8,9},{9,8},{10,11... | collective-permute-start | bytes 98312 | tf_op jit(solution)/shard_map/ppermute | solution.py:380
  43.2 4.0 %collective-permute-start.13 = (bf16[32,512]{1,0:T(8,128)(2,1)S(1)}, bf16[32,512]{1,0:T(8,128)(2,1)S(1)}, u32[]{:S(2)}, u32[]{:S(2)}) collective-permute-start(bf16[32,512]{1,0:T(8,128)(2,1)S(1)} %get-tuple-element.61), channel_id=1, source_target_pairs={{0,2},{1,3},{2,0},{3,1},{4,6},{5,7},{6,4},{7,5},{8,10},{9,11},{10,... | collective-permute-start | bytes 98312 | tf_op jit(solution)/shard_map/ppermute | solution.py:380

commit v19 on v17

--- a/solution.py
+++ b/solution.py
@@ -486,6 +486,7 @@
     )
     pieces = exchange(pieces)
     pieces[3:] = call(pass_kernel, "pass", (piece,), [], pieces[3], micros=1)
+    pieces[2:3] = call(pass_kernel, "pass", (piece,), [], pieces[2], micros=1)
     (result,) = call(join_kernel, "join", (shape((high, ncol), F32),), [], *pieces)
     return result
 

time: 47.8 us -> 47.8 us (level)
    pallas_call x17 -> x18, Pallas kernels: 9.1 us -> 9.1 us  [call(): pl.pallas_call(kernel, name=name, out_shape=outs, in_specs=spaces, out_sp...]
  transfers between devices with their start and end apart: 15 -> 15, of which waited for: 6 -> 5; matrix products, arithmetic and copies ran while one was open for 0% -> 0% of each run, Pallas kernels for 14% -> 14%
where the time goes in v19:
time: 47.8 us; the launch traced here: 47.7 us
  starting transfers between devices  20.5 us (43%)
  waiting for transfers between devices  16 us (33%)
  Pallas kernels  9.1 us (19%)
  local copies, waits for them, and re-layouts  1.84 us (4%)
    ppermute x4, waiting for transfers between devices, swap(): lax.ppermute(first, axes, blue_pairs)  14.1 us
    ppermute x4, starting transfers between devices, swap(): lax.ppermute(first, axes, blue_pairs)  9.75 us
    pallas_call x18, Pallas kernels, call(): pl.pallas_call(kernel, name=name, out_shape=outs, in_specs=spaces, out_sp...  9.1 us
    ppermute x1, starting transfers between devices, per_device(): blue_msg = lax.ppermute(blue_msg, axes, blue_pairs)  5.37 us
    ppermute x1, starting transfers between devices, per_device(): across = lax.ppermute(across, 'edges', [(i, i ^ 3) for i in range(nedge)])  2.61 us
    ppermute x3, starting transfers between devices, exchange(): lax.ppermute(pieces[k], 'edges', [(i, i ^ k) for i in range(nedge)])  2.19 us
    ppermute x3, waiting for transfers between devices, exchange(): lax.ppermute(pieces[k], 'edges', [(i, i ^ k) for i in range(nedge)])  1.95 us
    unnamed x18, local copies, waits for them, and re-layouts  1.84 us
  transfers between devices with their start and end apart: 15, of which 5 were waited for; matrix products, arithmetic and copies ran while one was open for 0% of the time, Pallas kernels for 14%

profile of v19, /device:TPU:0, one launch (start us, length us, event | category | flops | bytes accessed | tf_op | source)
XLA Modules:
  0.0 47.7 jit_solution(13894345928346888907)
XLA Ops:
  0.0 0.9 %copy-done.1 = f32[32,2048]{1,0:T(8,128)S(1)} copy-done((f32[32,2048]{1,0:T(8,128)S(1)}, f32[32,2048]{1,0:T(8,128)}, u32[]{:S(2)}) %copy-start.1) | copy-done | bytes 262168
  1.0 0.2 copy-done
  1.3 0.5 %collective-permute-start = (bf16[400,256]{1,0:T(8,128)(2,1)S(1)}, bf16[400,256]{1,0:T(8,128)(2,1)S(1)}, u32[]{:S(2)}, u32[]{:S(2)}) collective-permute-start(bf16[400,256]{1,0:T(8,128)(2,1)S(1)} %get-tuple-element.35), channel_id=1, source_target_pairs={{0,1},{1,0},{2,3},{3,2},{4,5},{5,4},{6,7},{7,6},{8,9},{9,8},{10,11... | collective-permute-start | bytes 614408 | tf_op jit(solution)/shard_map/ppermute | solution.py:397
  1.8 2.6 %collective-permute-start.2 = (bf16[32,512]{1,0:T(8,128)(2,1)S(1)}, bf16[32,512]{1,0:T(8,128)(2,1)S(1)}, u32[]{:S(2)}, u32[]{:S(2)}) collective-permute-start(bf16[32,512]{1,0:T(8,128)(2,1)S(1)} %get-tuple-element.38), channel_id=1, source_target_pairs={{0,3},{1,2},{2,1},{3,0},{4,7},{5,6},{6,5},{7,4},{8,11},{9,10},{10,... | collective-permute-start | bytes 98312 | tf_op jit(solution)/shard_map/ppermute | solution.py:395
  4.4 0.0 collective-permute-start.1
  4.4 5.4 %collective-permute-start.3 = (bf16[336,256]{1,0:T(8,128)(2,1)S(1)}, bf16[336,256]{1,0:T(8,128)(2,1)S(1)}, u32[]{:S(2)}, u32[]{:S(2)}) collective-permute-start(bf16[336,256]{1,0:T(8,128)(2,1)S(1)} %get-tuple-element.41), channel_id=1, source_target_pairs={{0,31},{1,2},{2,1},{3,4},{4,3},{5,6},{6,5},{7,8},{8,7},{9,10},{10,... | collective-permute-start | bytes 516104 | tf_op jit(solution)/shard_map/ppermute | solution.py:398
  9.8 0.0 collective-permute-done.2.x
  9.8 0.0 collective-permute-done.1.p2
  9.8 0.0 collective-permute-done.near
  9.8 0.0 copy-start.5
  9.8 0.0 copy-start.6
  9.9 0.2 field.1
  10.1 0.0 copy-start.7
  10.1 2.1 %collective-permute-start.4 = (bf16[384,128]{1,0:T(8,128)(2,1)S(1)}, bf16[384,128]{1,0:T(8,128)(2,1)S(1)}, u32[]{:S(2)}, u32[]{:S(2)}) collective-permute-start(bf16[384,128]{1,0:T(8,128)(2,1)S(1)} %get-tuple-element.46), channel_id=1, source_target_pairs={{0,31},{1,2},{2,1},{3,4},{4,3},{5,6},{6,5},{7,8},{8,7},{9,10},{10,... | collective-permute-start | bytes 294920 | tf_op jit(solution)/shard_map/ppermute | solution.py:374
  12.1 0.0 collective-permute-start.5
  12.1 2.9 %own.1 = (bf16[2,256,1024]{2,1,0:T(8,128)(2,1)S(1)}, bf16[512,256]{1,0:T(8,128)(2,1)S(1)}, bf16[512,8]{1,0:T(8,128)(2,1)S(1)}, bf16[256,256]{1,0:T(8,128)(2,1)S(1)}) custom-call(bf16[1280,256]{1,0:T(8,128)(2,1)S(1)} %copy-done, s32[10,128]{1,0:T(8,128)S(1)} %bitcast.5, s32[10,128]{1,0:T(8,128)S(1)} %bitcast.8, s32[10,128]{1,0:T(8,128)S(1)} %bitcast.11, ...), custom_call_target="tpu_custom_call" | custom-call | flops 4000000000 | tf_op jit(solution)/shard_map/own/pallas_call | solution.py:349
  15.1 0.0 collective-permute-done.3.blue
  15.1 1.5 %spill.1.band = bf16[2,256,1024]{2,1,0:T(8,128)(2,1)S(1)} custom-call(bf16[2,256,1024]{2,1,0:T(8,128)(2,1)S(1)} %get-tuple-element.40.own_band, bf16[336,256]{1,0:T(8,128)(2,1)S(1)} %collective-permute-done.3.blue, bf16[512,256]{1,0:T(8,128)(2,1)S(1)} %get-tuple-element.42.w_in_t, ...), custom_call_target="tpu_custom_call", output_to_operand_aliasing={{}: (0, {})} | custom-call | tf_op jit(solution)/shard_map/spill/pallas_call | solution.py:349
  16.6 0.3 start.1.part
  16.9 0.8 %collective-permute-done.4.blue = bf16[384,128]{1,0:T(8,128)(2,1)S(1)} collective-permute-done((bf16[384,128]{1,0:T(8,128)(2,1)S(1)}, bf16[384,128]{1,0:T(8,128)(2,1)S(1)}, u32[]{:S(2)}, u32[]{:S(2)}) %collective-permute-start.4) | collective-permute-done | bytes 98336 | tf_op jit(solution)/shard_map/ppermute | solution.py:374
  17.8 0.0 collective-permute-done.5.red
  17.8 0.4 outer.3
  18.2 2.6 %collective-permute-start.6 = (bf16[384,128]{1,0:T(8,128)(2,1)S(1)}, bf16[384,128]{1,0:T(8,128)(2,1)S(1)}, u32[]{:S(2)}, u32[]{:S(2)}) collective-permute-start(bf16[384,128]{1,0:T(8,128)(2,1)S(1)} %get-tuple-element.49), channel_id=1, source_target_pairs={{0,31},{1,2},{2,1},{3,4},{4,3},{5,6},{6,5},{7,8},{8,7},{9,10},{10,... | collective-permute-start | bytes 294920 | tf_op jit(solution)/shard_map/ppermute | solution.py:374
  20.8 0.0 collective-permute-start.7
  20.8 0.3 inner.2.part
  21.2 4.9 %collective-permute-done.6.blue = bf16[384,128]{1,0:T(8,128)(2,1)S(1)} collective-permute-done((bf16[384,128]{1,0:T(8,128)(2,1)S(1)}, bf16[384,128]{1,0:T(8,128)(2,1)S(1)}, u32[]{:S(2)}, u32[]{:S(2)}) %collective-permute-start.6) | collective-permute-done | bytes 98336 | tf_op jit(solution)/shard_map/ppermute | solution.py:374
  26.0 0.0 collective-permute-done.7.red
  26.0 0.4 outer.4
  26.4 2.5 %collective-permute-start.8 = (bf16[384,128]{1,0:T(8,128)(2,1)S(1)}, bf16[384,128]{1,0:T(8,128)(2,1)S(1)}, u32[]{:S(2)}, u32[]{:S(2)}) collective-permute-start(bf16[384,128]{1,0:T(8,128)(2,1)S(1)} %get-tuple-element.52), channel_id=1, source_target_pairs={{0,31},{1,2},{2,1},{3,4},{4,3},{5,6},{6,5},{7,8},{8,7},{9,10},{10,... | collective-permute-start | bytes 294920 | tf_op jit(solution)/shard_map/ppermute | solution.py:374
  29.0 0.0 collective-permute-start.9
  29.0 0.3 inner.3.part
  29.3 4.8 %collective-permute-done.8.blue = bf16[384,128]{1,0:T(8,128)(2,1)S(1)} collective-permute-done((bf16[384,128]{1,0:T(8,128)(2,1)S(1)}, bf16[384,128]{1,0:T(8,128)(2,1)S(1)}, u32[]{:S(2)}, u32[]{:S(2)}) %collective-permute-start.8) | collective-permute-done | bytes 98336 | tf_op jit(solution)/shard_map/ppermute | solution.py:374
  34.1 0.0 collective-permute-done.9.red
  34.1 0.4 outer.5
  34.6 2.5 %collective-permute-start.10 = (bf16[384,128]{1,0:T(8,128)(2,1)S(1)}, bf16[384,128]{1,0:T(8,128)(2,1)S(1)}, u32[]{:S(2)}, u32[]{:S(2)}) collective-permute-start(bf16[384,128]{1,0:T(8,128)(2,1)S(1)} %get-tuple-element.57), channel_id=1, source_target_pairs={{0,31},{1,2},{2,1},{3,4},{4,3},{5,6},{6,5},{7,8},{8,7},{9,10},{10,... | collective-permute-start | bytes 294920 | tf_op jit(solution)/shard_map/ppermute | solution.py:374
  37.1 0.0 collective-permute-start.11
  37.1 0.7 %copy-done.8 = f32[5]{0:T(128)S(1)} copy-done((f32[5]{0:T(128)S(1)}, f32[5]{0:T(128)}, u32[]{:S(2)}) %copy-start.8) | copy-done | bytes 44
  37.8 0.9 %mix.1 = (f32[128,512]{1,0:T(8,128)S(1)}, f32[8,128]{1,0:T(8,128)S(1)}) custom-call(f32[5]{0:T(128)S(1)} %copy-done.8, bf16[2,256,1024]{2,1,0:T(8,128)(2,1)S(1)} %spill.1.band, f32[512,128]{1,0:T(8,128)S(1)} %get-tuple-element.45.now.before.t0, f32[512,128]{1,0:T(8,128)S(1)} %get-tuple-element.48.now.before.t1, f32[512,128]{1,0:T(8,128)S(1)} %get-tuple-element.51.now.t2, ...), custom_call_target="tpu_custom_call" | custom-call | flops 1000000000 | tf_op jit(solution)/shard_map/mix/pallas_call | solution.py:349
  38.7 3.6 %collective-permute-done.10.blue = bf16[384,128]{1,0:T(8,128)(2,1)S(1)} collective-permute-done((bf16[384,128]{1,0:T(8,128)(2,1)S(1)}, bf16[384,128]{1,0:T(8,128)(2,1)S(1)}, u32[]{:S(2)}, u32[]{:S(2)}) %collective-permute-start.10) | collective-permute-done | bytes 98336 | tf_op jit(solution)/shard_map/ppermute | solution.py:374
  42.3 0.0 collective-permute-done.11.red
  42.3 0.5 last.1
  42.8 0.1 collective-permute-start.13
  42.8 0.1 collective-permute-start.12
  42.9 2.0 %collective-permute-start.14 = (bf16[32,512]{1,0:T(8,128)(2,1)S(1)}, bf16[32,512]{1,0:T(8,128)(2,1)S(1)}, u32[]{:S(2)}, u32[]{:S(2)}) collective-permute-start(bf16[32,512]{1,0:T(8,128)(2,1)S(1)} %get-tuple-element.62), channel_id=1, source_target_pairs={{0,3},{1,2},{2,1},{3,0},{4,7},{5,6},{6,5},{7,4},{8,11},{9,10},{10,... | collective-permute-start | bytes 98312 | tf_op jit(solution)/shard_map/ppermute | solution.py:380
  45.0 1.9 %collective-permute-done.13.x = bf16[32,512]{1,0:T(8,128)(2,1)S(1)} collective-permute-done((bf16[32,512]{1,0:T(8,128)(2,1)S(1)}, bf16[32,512]{1,0:T(8,128)(2,1)S(1)}, u32[]{:S(2)}, u32[]{:S(2)}) %collective-permute-start.13) | collective-permute-done | bytes 32800 | tf_op jit(solution)/shard_map/ppermute | solution.py:380
  46.9 0.0 collective-permute-done.14.x
  46.9 0.0 collective-permute-done.12.p1
  46.9 0.7 %join.1 = f32[32,2048]{1,0:T(8,128)} custom-call(bf16[32,512]{1,0:T(8,128)(2,1)S(1)} %get-tuple-element.59.p0, bf16[32,512]{1,0:T(8,128)(2,1)S(1)} %collective-permute-done.12.p1, bf16[32,512]{1,0:T(8,128)(2,1)S(1)} %pass.4.p2, bf16[32,512]{1,0:T(8,128)(2,1)S(1)} %pass.5.p3), custom_call_target="tpu_custom_call" | custom-call | flops 1000000000 | tf_op jit(solution)/shard_map/join/pallas_call | solution.py:349
  (18 shorter events, 0.1 us)
Async XLA Ops:
  0.0 0.9 %copy-start.1 = (f32[32,2048]{1,0:T(8,128)S(1)}, f32[32,2048]{1,0:T(8,128)}, u32[]{:S(2)}) copy-start(f32[32,2048]{1,0:T(8,128)} %vectors.1) | copy-start | bytes 786436
  0.0 1.0 %copy-start.2 = (s32[1280]{0:T(1024)S(1)}, s32[1280]{0:T(1024)}, u32[]{:S(2)}) copy-start(s32[1280]{0:T(1024)} %param.10) | copy-start | bytes 15364
  0.0 1.0 %copy-start.3 = (s32[1280]{0:T(1024)S(1)}, s32[1280]{0:T(1024)}, u32[]{:S(2)}) copy-start(s32[1280]{0:T(1024)} %param.11) | copy-start | bytes 15364
  0.0 1.0 %copy-start.4 = (s32[1280]{0:T(1024)S(1)}, s32[1280]{0:T(1024)}, u32[]{:S(2)}) copy-start(s32[1280]{0:T(1024)} %param.12) | copy-start | bytes 15364
  0.0 1.2 %copy-start = (bf16[1280,256]{1,0:T(8,128)(2,1)S(1)}, bf16[1280,256]{1,0:T(8,128)(2,1)}, u32[]{:S(2)}) copy-start(bf16[1280,256]{1,0:T(8,128)(2,1)} %feat.3) | copy-start | bytes 1966084
  1.3 8.6 %collective-permute-start = (bf16[400,256]{1,0:T(8,128)(2,1)S(1)}, bf16[400,256]{1,0:T(8,128)(2,1)S(1)}, u32[]{:S(2)}, u32[]{:S(2)}) collective-permute-start(bf16[400,256]{1,0:T(8,128)(2,1)S(1)} %get-tuple-element.35), channel_id=1, source_target_pairs={{0,1},{1,0},{2,3},{3,2},{4,5},{5,4},{6,7},{7,6},{8,9},{9,8},{10,11... | collective-permute-start | bytes 614408 | tf_op jit(solution)/shard_map/ppermute | solution.py:397
  1.8 8.0 %collective-permute-start.2 = (bf16[32,512]{1,0:T(8,128)(2,1)S(1)}, bf16[32,512]{1,0:T(8,128)(2,1)S(1)}, u32[]{:S(2)}, u32[]{:S(2)}) collective-permute-start(bf16[32,512]{1,0:T(8,128)(2,1)S(1)} %get-tuple-element.38), channel_id=1, source_target_pairs={{0,3},{1,2},{2,1},{3,0},{4,7},{5,6},{6,5},{7,4},{8,11},{9,10},{10,... | collective-permute-start | bytes 98312 | tf_op jit(solution)/shard_map/ppermute | solution.py:395
  4.4 5.4 %collective-permute-start.1 = (bf16[32,512]{1,0:T(8,128)(2,1)S(1)}, bf16[32,512]{1,0:T(8,128)(2,1)S(1)}, u32[]{:S(2)}, u32[]{:S(2)}) collective-permute-start(bf16[32,512]{1,0:T(8,128)(2,1)S(1)} %get-tuple-element.37), channel_id=1, source_target_pairs={{0,2},{1,3},{2,0},{3,1},{4,6},{5,7},{6,4},{7,5},{8,10},{9,11},{10,... | collective-permute-start | bytes 98312 | tf_op jit(solution)/shard_map/ppermute | solution.py:396
  4.4 10.6 %collective-permute-start.3 = (bf16[336,256]{1,0:T(8,128)(2,1)S(1)}, bf16[336,256]{1,0:T(8,128)(2,1)S(1)}, u32[]{:S(2)}, u32[]{:S(2)}) collective-permute-start(bf16[336,256]{1,0:T(8,128)(2,1)S(1)} %get-tuple-element.41), channel_id=1, source_target_pairs={{0,31},{1,2},{2,1},{3,4},{4,3},{5,6},{6,5},{7,8},{8,7},{9,10},{10,... | collective-permute-start | bytes 516104 | tf_op jit(solution)/shard_map/ppermute | solution.py:398
  9.8 2.3 %copy-start.5 = (bf16[256,512]{1,0:T(8,128)(2,1)S(1)}, bf16[256,512]{1,0:T(8,128)(2,1)}, u32[]{:S(2)}) copy-start(bf16[256,512]{1,0:T(8,128)(2,1)} %w_in.1) | copy-start | bytes 786436
  9.8 2.3 %copy-start.6 = (bf16[256,256]{1,0:T(8,128)(2,1)S(1)}, bf16[256,256]{1,0:T(8,128)(2,1)}, u32[]{:S(2)}) copy-start(bf16[256,256]{1,0:T(8,128)(2,1)} %w_out.1) | copy-start | bytes 393220
  10.1 2.1 %copy-start.7 = (bf16[3,512]{1,0:T(4,128)(2,1)S(1)}, bf16[3,512]{1,0:T(4,128)(2,1)}, u32[]{:S(2)}) copy-start(bf16[3,512]{1,0:T(4,128)(2,1)} %cell_bias.1) | copy-start | bytes 9220
  10.1 7.7 %collective-permute-start.4 = (bf16[384,128]{1,0:T(8,128)(2,1)S(1)}, bf16[384,128]{1,0:T(8,128)(2,1)S(1)}, u32[]{:S(2)}, u32[]{:S(2)}) collective-permute-start(bf16[384,128]{1,0:T(8,128)(2,1)S(1)} %get-tuple-element.46), channel_id=1, source_target_pairs={{0,31},{1,2},{2,1},{3,4},{4,3},{5,6},{6,5},{7,8},{8,7},{9,10},{10,... | collective-permute-start | bytes 294920 | tf_op jit(solution)/shard_map/ppermute | solution.py:374
  12.1 5.6 %collective-permute-start.5 = (bf16[384,128]{1,0:T(8,128)(2,1)S(1)}, bf16[384,128]{1,0:T(8,128)(2,1)S(1)}, u32[]{:S(2)}, u32[]{:S(2)}) collective-permute-start(bf16[384,128]{1,0:T(8,128)(2,1)S(1)} %get-tuple-element.47), channel_id=1, source_target_pairs={{0,1},{1,0},{2,3},{3,2},{4,5},{5,4},{6,7},{7,6},{8,9},{9,8},{10,11... | collective-permute-start | bytes 294920 | tf_op jit(solution)/shard_map/ppermute | solution.py:375
  18.2 7.8 %collective-permute-start.6 = (bf16[384,128]{1,0:T(8,128)(2,1)S(1)}, bf16[384,128]{1,0:T(8,128)(2,1)S(1)}, u32[]{:S(2)}, u32[]{:S(2)}) collective-permute-start(bf16[384,128]{1,0:T(8,128)(2,1)S(1)} %get-tuple-element.49), channel_id=1, source_target_pairs={{0,31},{1,2},{2,1},{3,4},{4,3},{5,6},{6,5},{7,8},{8,7},{9,10},{10,... | collective-permute-start | bytes 294920 | tf_op jit(solution)/shard_map/ppermute | solution.py:374
  20.8 5.2 %collective-permute-start.7 = (bf16[384,128]{1,0:T(8,128)(2,1)S(1)}, bf16[384,128]{1,0:T(8,128)(2,1)S(1)}, u32[]{:S(2)}, u32[]{:S(2)}) collective-permute-start(bf16[384,128]{1,0:T(8,128)(2,1)S(1)} %get-tuple-element.50), channel_id=1, source_target_pairs={{0,1},{1,0},{2,3},{3,2},{4,5},{5,4},{6,7},{7,6},{8,9},{9,8},{10,11... | collective-permute-start | bytes 294920 | tf_op jit(solution)/shard_map/ppermute | solution.py:375
  26.4 7.7 %collective-permute-start.8 = (bf16[384,128]{1,0:T(8,128)(2,1)S(1)}, bf16[384,128]{1,0:T(8,128)(2,1)S(1)}, u32[]{:S(2)}, u32[]{:S(2)}) collective-permute-start(bf16[384,128]{1,0:T(8,128)(2,1)S(1)} %get-tuple-element.52), channel_id=1, source_target_pairs={{0,31},{1,2},{2,1},{3,4},{4,3},{5,6},{6,5},{7,8},{8,7},{9,10},{10,... | collective-permute-start | bytes 294920 | tf_op jit(solution)/shard_map/ppermute | solution.py:374
  29.0 5.2 %collective-permute-start.9 = (bf16[384,128]{1,0:T(8,128)(2,1)S(1)}, bf16[384,128]{1,0:T(8,128)(2,1)S(1)}, u32[]{:S(2)}, u32[]{:S(2)}) collective-permute-start(bf16[384,128]{1,0:T(8,128)(2,1)S(1)} %get-tuple-element.53), channel_id=1, source_target_pairs={{0,1},{1,0},{2,3},{3,2},{4,5},{5,4},{6,7},{7,6},{8,9},{9,8},{10,11... | collective-permute-start | bytes 294920 | tf_op jit(solution)/shard_map/ppermute | solution.py:375
  34.6 7.7 %collective-permute-start.10 = (bf16[384,128]{1,0:T(8,128)(2,1)S(1)}, bf16[384,128]{1,0:T(8,128)(2,1)S(1)}, u32[]{:S(2)}, u32[]{:S(2)}) collective-permute-start(bf16[384,128]{1,0:T(8,128)(2,1)S(1)} %get-tuple-element.57), channel_id=1, source_target_pairs={{0,31},{1,2},{2,1},{3,4},{4,3},{5,6},{6,5},{7,8},{8,7},{9,10},{10,... | collective-permute-start | bytes 294920 | tf_op jit(solution)/shard_map/ppermute | solution.py:374
  37.1 0.7 %copy-start.8 = (f32[5]{0:T(128)S(1)}, f32[5]{0:T(128)}, u32[]{:S(2)}) copy-start(f32[5]{0:T(128)} %coef.1) | copy-start | bytes 64
  37.1 5.2 %collective-permute-start.11 = (bf16[384,128]{1,0:T(8,128)(2,1)S(1)}, bf16[384,128]{1,0:T(8,128)(2,1)S(1)}, u32[]{:S(2)}, u32[]{:S(2)}) collective-permute-start(bf16[384,128]{1,0:T(8,128)(2,1)S(1)} %get-tuple-element.58), channel_id=1, source_target_pairs={{0,1},{1,0},{2,3},{3,2},{4,5},{5,4},{6,7},{7,6},{8,9},{9,8},{10,11... | collective-permute-start | bytes 294920 | tf_op jit(solution)/shard_map/ppermute | solution.py:375
  42.8 4.2 %collective-permute-start.13 = (bf16[32,512]{1,0:T(8,128)(2,1)S(1)}, bf16[32,512]{1,0:T(8,128)(2,1)S(1)}, u32[]{:S(2)}, u32[]{:S(2)}) collective-permute-start(bf16[32,512]{1,0:T(8,128)(2,1)S(1)} %get-tuple-element.61), channel_id=1, source_target_pairs={{0,2},{1,3},{2,0},{3,1},{4,6},{5,7},{6,4},{7,5},{8,10},{9,11},{10,... | collective-permute-start | bytes 98312 | tf_op jit(solution)/shard_map/ppermute | solution.py:380
  42.8 4.1 %collective-permute-start.12 = (bf16[32,512]{1,0:T(8,128)(2,1)S(1)}, bf16[32,512]{1,0:T(8,128)(2,1)S(1)}, u32[]{:S(2)}, u32[]{:S(2)}) collective-permute-start(bf16[32,512]{1,0:T(8,128)(2,1)S(1)} %get-tuple-element.60), channel_id=1, source_target_pairs={{0,1},{1,0},{2,3},{3,2},{4,5},{5,4},{6,7},{7,6},{8,9},{9,8},{10,11... | collective-permute-start | bytes 98312 | tf_op jit(solution)/shard_map/ppermute | solution.py:380
  42.9 4.0 %collective-permute-start.14 = (bf16[32,512]{1,0:T(8,128)(2,1)S(1)}, bf16[32,512]{1,0:T(8,128)(2,1)S(1)}, u32[]{:S(2)}, u32[]{:S(2)}) collective-permute-start(bf16[32,512]{1,0:T(8,128)(2,1)S(1)} %get-tuple-element.62), channel_id=1, source_target_pairs={{0,3},{1,2},{2,1},{3,0},{4,7},{5,6},{6,5},{7,4},{8,11},{9,10},{10,... | collective-permute-start | bytes 98312 | tf_op jit(solution)/shard_map/ppermute | solution.py:380
